TPU v7x, 128 devices: a whole 4x4x4 slice. The times are simulated.
128 devices in a mesh: sec: 32 (over z, x, y_hi), tp: 4 (over y_lo, core).
Axes of the slice: x: 4, y: 4 (y_hi: 2, y_lo: 2; y = y_hi * 2 + y_lo), z: 4, core: 2. Of those that a mesh axis runs over, the one named last changes fastest.
Arguments:
- patches: bfloat16 [32768, 1280], P('sec'), may hold values from -48 to 48
- image_ids: int32 [32, 256], P('sec'), may hold values from 0 to 3, never falling along the last dimension, each value on 1 to 128 neighbouring positions
- qkv_weight: bfloat16 [3, 1280, 1280], P(None, None, 'tp'), may hold values from -0.15625 to 0.15625
- out_weight: bfloat16 [1280, 1280], P('tp'), may hold values from -0.15625 to 0.15625
- merge_gain: float32 [1280], replicated, may hold values from 0.5 to 1.5
- merge_weight: bfloat16 [5120, 8192], P('sec', 'tp'), may hold values from -0.078125 to 0.078125
- text_rows: bfloat16 [16384, 8192], P('sec', 'tp'), may hold values from -21 to 21
- image_refs: int32 [16384], P('sec'), may hold values from -1 to 8191, as said below
- llm_gain: float32 [8192], P('tp'), may hold values from 0.5 to 1.5
Outputs:
- prompt_states: bfloat16 [16384, 8192], P('sec', 'tp')
Inputs may be any that keep to these rules, and one draw needn't show every extreme that they name: `image_ids`: each image's rows form one run within its device's row of ids. `image_refs`: -1 marks a text row; any other value names one of the 8192 image rows, those of device s starting at s * 256. Each image row is named at most once. The 512 prompt rows of one device name at most 16 image rows of one device, and exactly 16 for some pairs of devices.
All inputs are finite; a program needn't handle non-finite values.
Results may differ from a plain program's by a relative error of at most 0.012.
Values may be sent and summed in bfloat16 or wider, within the bound.
No kernel may reach another device: no remote copies, remote signals or barrier semaphores. Data moves between devices by JAX's collectives and lax.ppermute only.
A program may use at most 128 MiB of HBM per device.

v0:
```python
import jax
import jax.numpy as jnp
from jax import lax
from jax.sharding import PartitionSpec as P

HEAD_DIM = 80
MERGE = 4


EPSILON = 1e-06


def vision_context(patches, image_ids, qkv_weight):
    row_count = patches.shape[0]
    projected = jnp.einsum(
        "pd,cde->cpe", patches, qkv_weight, preferred_element_type=jnp.float32
    ).astype(jnp.bfloat16)
    local_heads = projected.shape[2] // HEAD_DIM
    queries = projected[0].reshape(row_count, local_heads, HEAD_DIM)
    key_heads = projected[1].reshape(row_count, local_heads, HEAD_DIM)
    value_heads = projected[2].reshape(row_count, local_heads, HEAD_DIM)
    patch_ids = jnp.repeat(image_ids.reshape(-1), MERGE)
    block_rows = min(512, row_count)

    def one_block(block_index):
        first_row = block_index * block_rows
        query_part = lax.dynamic_slice_in_dim(queries, first_row, block_rows, 0)
        id_part = lax.dynamic_slice_in_dim(patch_ids, first_row, block_rows, 0)
        scores = jnp.einsum(
            "qhd,khd->hqk", query_part, key_heads, preferred_element_type=jnp.float32
        ) * HEAD_DIM ** (-0.5)
        same_image = id_part[:, None] == patch_ids[None, :]
        scores = jnp.where(same_image[None, :, :], scores, -1e30)
        highest = jnp.max(scores, axis=2, keepdims=True)
        weights = jnp.exp(scores - highest)
        attention = (weights / jnp.sum(weights, axis=2, keepdims=True)).astype(jnp.bfloat16)
        context = jnp.einsum(
            "hqk,khd->qhd", attention, value_heads, preferred_element_type=jnp.float32
        )
        return context.astype(jnp.bfloat16).reshape(block_rows, local_heads * HEAD_DIM)

    contexts = lax.map(one_block, jnp.arange(row_count // block_rows))
    return contexts.reshape(row_count, local_heads * HEAD_DIM)


def vision_norm(own_patches, attended_terms, merge_gain):
    attended = own_patches.astype(jnp.float32) + attended_terms
    moment = jnp.mean(attended * attended, axis=1, keepdims=True)
    return (attended * lax.rsqrt(moment + EPSILON) * merge_gain).astype(jnp.bfloat16)


def on_device(
    patches,
    image_ids,
    qkv_weight,
    out_weight,
    merge_gain,
    merge_weight,
    text_rows,
    image_refs,
    llm_gain,
):
    context = vision_context(patches, image_ids, qkv_weight)
    partial_terms = jnp.dot(context, out_weight, preferred_element_type=jnp.float32)
    attended_terms = lax.psum(partial_terms, "tp")
    normed = vision_norm(patches, attended_terms, merge_gain)
    merged = normed.reshape(normed.shape[0] // MERGE, MERGE * normed.shape[1])
    image_rows = jnp.dot(
        merged,
        lax.all_gather(merge_weight, "sec", axis=0, tiled=True),
        preferred_element_type=jnp.float32,
    ).astype(jnp.bfloat16)
    sections = lax.axis_size("sec")
    merged_rows = image_rows.shape[0]
    capacity = merged_rows // (sections // 2)
    usable = image_refs >= 0
    source_dev = jnp.where(usable, image_refs // merged_rows, 0)
    source_hits = ((source_dev[:, None] == jnp.arange(sections)[None, :]) & usable[:, None]).astype(
        jnp.int32
    )
    arrival = jnp.sum(jnp.cumsum(source_hits, axis=0) * source_hits, axis=1) - 1
    every_list = lax.all_gather(image_refs, "sec", axis=0, tiled=True).reshape(sections, -1)
    own_index = lax.axis_index("sec")
    wanted = (every_list >= 0) & (every_list // merged_rows == own_index)
    running = jnp.cumsum(wanted.astype(jnp.int32), axis=1) - 1
    spot_col = jnp.where(wanted, running, capacity)
    target_dev = jnp.broadcast_to(jnp.arange(sections)[:, None], every_list.shape)
    send_table = (
        jnp.full((sections, capacity), -1, jnp.int32)
        .at[target_dev, spot_col]
        .set(every_list % merged_rows, mode="drop")
    )
    filled = send_table >= 0
    outgoing = jnp.where(
        filled[:, :, None], image_rows[jnp.maximum(send_table, 0)], jnp.zeros((), jnp.bfloat16)
    )
    received = lax.all_to_all(outgoing, "sec", split_axis=0, concat_axis=0, tiled=True)
    arrived = received.reshape(sections * capacity, received.shape[2])
    picked = arrived[source_dev * capacity + jnp.maximum(arrival, 0)]
    prompt = jnp.where(usable[:, None], picked, text_rows)
    widened = prompt.astype(jnp.float32)
    squares = lax.psum(jnp.sum(widened * widened, axis=1), "tp")
    total_width = widened.shape[1] * lax.axis_size("tp")
    inverse = lax.rsqrt(squares / total_width + EPSILON)
    return (widened * inverse[:, None] * llm_gain[None, :]).astype(jnp.bfloat16)


def solution(mesh):
    return jax.shard_map(
        on_device,
        mesh=mesh,
        in_specs=(
            P("sec", None),
            P("sec", None),
            P(None, None, "tp"),
            P("tp", None),
            P(),
            P("sec", "tp"),
            P("sec", "tp"),
            P("sec"),
            P("tp"),
        ),
        out_specs=P("sec", "tp"),
        check_vma=False,
    )
```

profile of v0, /device:TPU:1, one launch (start us, length us, event | category | flops | bytes accessed | tf_op | source)
XLA Modules:
  0.0 342.1 jit_solution(6338063523229905883)
XLA Ops:
  7.4 0.9 broadcast_in_dim.84
  8.4 0.7 copy-done
  9.1 4.5 %convert_bitcast_fusion = bf16[3,1024,320]{1,2,0:T(8,128)(2,1)S(1)} fusion(bf16[3,1280,320]{1,2,0:T(8,128)(2,1)S(1)} %copy-done, bf16[1024,1280]{1,0:T(8,128)(2,1)} %param.11), kind=kOutput, calls=%fused_computation.37 | convolution fusion | flops 2517565440 | bytes 7045120 | tf_op jit(solution)/shard_map/pd,cde->cpe/dot_general | solution.py:15
  13.6 1.3 fusion.56
  14.8 28.9 %while.11 = (s32[]{:T(128)}, bf16[2,512,320]{1,2,0:T(8,128)(2,1)S(1)}, s32[2]{0:T(128)S(1)}, s32[1024]{0:T(1024)S(1)}, bf16[1024,4,80]{0,2,1:T(8,128)(2,1)}, /*i...) while((s32[]{:T(128)}, ...), condition=%wide.region_6.7_spmd.clone, body=%wide.region_3.6_spmd.clone.sunk | while | flops 684360704 | bytes 20487364 | solution.py:42
  15.1 0.7 dynamic_slice.29
  16.9 7.5 %fusion.74 = (f32[4,512]{1,0:T(4,128)S(1)}, f32[4,512,1024]{2,1,0:T(8,128)}) fusion(pred[512,1024]{1,0:T(8,128)(4,1)S(1)} %broadcast_compare_fusion.5, bf16[1024,4,80]{0,2,1:T(8,128)(2,1)} %get-tuple-element.172, bf16[1024,4,80]{0,2,1:T(8,128)(2,1)} %get-tuple-element.171, s32[]{:T(128)S(6)} %select_n.125), kind=kOutput, calls=%fused_computation.99.clone.1 | convolution fusion | flops 343933952 | bytes 9904132 | tf_op jit(solution)/shard_map/while/body/eval_jaxpr/sub | solution.py:35
  24.4 4.8 %fusion.75 = bf16[4,512,80]{1,2,0:T(8,128)(2,1)S(1)} fusion(bf16[1024,4,80]{0,2,1:T(8,128)(2,1)S(1)} %get-tuple-element.173, f32[4,512,1024]{2,1,0:T(8,128)} %get-tuple-element.141, f32[4,512]{1,0:T(4,128)S(1)} %get-tuple-element.142), kind=kOutput, calls=%fused_computation.13.clone.1 | convolution fusion | flops 339902464 | bytes 9379840 | tf_op jit(solution)/shard_map/while/body/eval_jaxpr/hqk,khd->qhd/dot_general | solution.py:37
  29.5 0.7 dynamic_slice.29
  31.3 7.5 %fusion.74 = (f32[4,512]{1,0:T(4,128)S(1)}, f32[4,512,1024]{2,1,0:T(8,128)}) fusion(pred[512,1024]{1,0:T(8,128)(4,1)S(1)} %broadcast_compare_fusion.5, bf16[1024,4,80]{0,2,1:T(8,128)(2,1)} %get-tuple-element.172, bf16[1024,4,80]{0,2,1:T(8,128)(2,1)} %get-tuple-element.171, s32[]{:T(128)S(6)} %select_n.125), kind=kOutput, calls=%fused_computation.99.clone.1 | convolution fusion | flops 343933952 | bytes 9904132 | tf_op jit(solution)/shard_map/while/body/eval_jaxpr/sub | solution.py:35
  38.8 4.8 %fusion.75 = bf16[4,512,80]{1,2,0:T(8,128)(2,1)S(1)} fusion(bf16[1024,4,80]{0,2,1:T(8,128)(2,1)S(1)} %get-tuple-element.173, f32[4,512,1024]{2,1,0:T(8,128)} %get-tuple-element.141, f32[4,512]{1,0:T(4,128)S(1)} %get-tuple-element.142), kind=kOutput, calls=%fused_computation.13.clone.1 | convolution fusion | flops 339902464 | bytes 9379840 | tf_op jit(solution)/shard_map/while/body/eval_jaxpr/hqk,khd->qhd/dot_general | solution.py:37
  43.8 4.0 %fusion.57 = f32[1024,1280]{1,0:T(8,128)} fusion(bf16[1024,320]{0,1:T(8,128)(2,1)S(1)} %bitcast.94, bf16[320,1280]{1,0:T(8,128)(2,1)S(1)} %copy-done.4), kind=kOutput, calls=%fused_computation.101 | convolution fusion | flops 838860800 | bytes 6717440 | tf_op jit(solution)/shard_map/dot_general | solution.py:64
  48.5 84.6 %all-gather = s32[32,1,512]{2,1,0:T(1,128)S(1)} all-gather(s32[1,1,512]{2,1,0:T(1,128)S(1)} %bitcast.108), channel_id=1, replica_groups=mesh['sec'=32,'tp'=4] {'sec'}, dimensions={0}, use_global_device_ids=true | all-gather | bytes 67584 | tf_op jit(solution)/shard_map/all_gather | solution.py:82
  133.1 1.2 reduce-window.14
  135.1 60.5 %scatter_custom_fusion = s32[512]{0:T(512)S(1)} fusion(s32[16384]{0:T(1024)S(1)} %bitcast.100, s32[16384]{0:T(1024)S(1)} %bitcast.101, s32[]{:T(128)} %constant.90.clone.1), kind=kCustom, calls=%fused_computation.94 | custom fusion | bytes 2052
  196.1 50.0 %all-reduce.2.cloned.1.call-done = f32[1024,1280]{1,0:T(8,128)} async-done(((f32[1024,1280]{1,0:T(8,128)}), f32[1024,1280]{1,0:T(8,128)}) %all-reduce.2.cloned.1.call-update) | async-done | bytes 5242896 | tf_op jit(solution)/shard_map/psum | solution.py:65
  246.1 4.2 %multiply_reduce_fusion = f32[1024]{0:T(1024)S(1)} fusion(f32[1024,1280]{1,0:T(8,128)} %all-reduce.2.cloned.1.call-done, bf16[1024,1280]{1,0:T(8,128)(2,1)} %param.11), kind=kLoop, calls=%fused_computation.27 | loop fusion | flops 5241856 | bytes 7868416 | tf_op jit(solution)/shard_map/reduce_sum | solution.py:48
  250.3 0.6 copy-done.2
  250.9 0.8 copy-done.3
  251.7 2.3 multiply_convert_fusion
  254.0 5.2 %reshape.247 = bf16[256,5120]{1,0:T(8,128)(2,1)} reshape(bf16[1024,1280]{1,0:T(8,128)(2,1)} %multiply_convert_fusion) | data formatting | bytes 5242880 | tf_op jit(solution)/shard_map/reshape | solution.py:67
  259.3 5.0 %all-gather.3.cloned.1.call-done = bf16[5120,2048]{1,0:T(8,128)(2,1)} async-done(((bf16[160,2048]{1,0:T(8,128)(2,1)}), bf16[5120,2048]{1,0:T(8,128)(2,1)}) %all-gather.3.cloned.1.call-update) | async-done | bytes 20971536 | tf_op jit(solution)/shard_map/all_gather | solution.py:70
  264.3 10.6 %convolution_convert_fusion = bf16[256,2048]{1,0:T(8,128)(2,1)S(1)} fusion(bf16[256,5120]{1,0:T(8,128)(2,1)} %reshape.247, bf16[5120,2048]{1,0:T(8,128)(2,1)} %all-gather.3.cloned.1.call-done), kind=kOutput, calls=%fused_computation.34 | convolution fusion | flops 5369233408 | bytes 24641536 | tf_op jit(solution)/shard_map/dot_general | solution.py:68
  274.9 3.3 gather_fusion
  278.2 3.1 broadcast_select_fusion.1
  281.3 5.2 %all-to-all-start = ((bf16[32,16,2048]{2,1,0:T(8,128)(2,1)}), bf16[32,16,2048]{2,1,0:T(8,128)(2,1)S(1)}, u32[]{:S(2)}, u32[]{:S(2)}) async-start(bf16[32,16,2048]{2,1,0:T(8,128)(2,1)} %broadcast_select_fusion.1), calls=%async_computation | async-start | bytes 4194304 | tf_op jit(solution)/shard_map/all_to_all | solution.py:97
  286.6 1.2 reduce-window.16
  288.1 30.3 %all-to-all-done = bf16[32,16,2048]{2,1,0:T(8,128)(2,1)S(1)} async-done(((bf16[32,16,2048]{2,1,0:T(8,128)(2,1)}), bf16[32,16,2048]{2,1,0:T(8,128)(2,1)S(1)}, u32[]{:S(2)}, u32[]{:S(2)}) %all-to-all-start) | async-done | bytes 2097184 | tf_op jit(solution)/shard_map/all_to_all | solution.py:97
  318.4 3.3 gather_fusion.1
  321.7 3.1 fusion.24
  324.7 5.4 %psum.15 = f32[512]{0:T(512)S(1)} all-reduce(f32[512]{0:T(512)S(1)} %fusion.24), channel_id=1, replica_groups=mesh['sec'=32,'tp'=4] {'tp'}, use_global_device_ids=true, to_apply=%region_13.14 | all-reduce | flops 512 | bytes 4096 | tf_op jit(solution)/shard_map/psum | solution.py:102
  330.1 4.5 %fusion.26 = bf16[512,2048]{1,0:T(8,128)(2,1)} fusion(f32[2048]{0:T(1024)S(1)} %copy-done.6, f32[512]{0:T(512)S(1)} %add_rsqrt_fusion.1, bf16[512,2048]{1,0:T(8,128)(2,1)} %gather_fusion.1, bf16[512,2048]{1,0:T(8,128)(2,1)} %param.17, pred[512]{0:T(512)(128)(4,1)S(1)} %get-tuple-element.84), kind=kLoop, calls=%fused_computation.31 | loop fusion | flops 5242880 | bytes 6302208 | tf_op jit(solution)/shard_map/convert_element_type | solution.py:105
  (70 shorter events, 3.9 us)
Async XLA Ops:
  7.4 1.7 copy-start
  7.4 238.7 %all-reduce.2.cloned.1.call-start = ((), (), s32[]{:S(2)}) async-start(), calls=%async_computation.1 | async-start | bytes 10485760 | tf_op jit(solution)/shard_map/psum | solution.py:65
  13.6 1.3 copy-start.5
  14.8 29.0 %copy-start.4 = (bf16[320,1280]{1,0:T(8,128)(2,1)S(1)}, bf16[320,1280]{1,0:T(8,128)(2,1)}, u32[]{:S(2)}) copy-start(bf16[320,1280]{1,0:T(8,128)(2,1)} %param.14) | copy-start | bytes 2457604
  47.8 0.7 copy-start.7
  47.8 87.1 %copy-start.10 = (s32[2]{0:T(128)S(1)}, s32[2]{0:T(128)}, u32[]{:S(2)}) copy-start(s32[2]{0:T(128)} %constant.105) | copy-start | bytes 28
  47.8 87.1 %copy-start.9 = (s32[2]{0:T(128)S(1)}, s32[2]{0:T(128)}, u32[]{:S(2)}) copy-start(s32[2]{0:T(128)} %constant.108) | copy-start | bytes 28
  47.8 216.5 %all-gather.3.cloned.1.call-start = ((), (), s32[]{:S(2)}) async-start(), calls=%async_computation.2 | async-start | bytes 21626880 | tf_op jit(solution)/shard_map/all_gather | solution.py:70
  196.1 54.2 %copy-start.8 = (f32[1280]{0:T(1024)S(1)}, f32[1280]{0:T(1024)}, u32[]{:S(2)}) copy-start(f32[1280]{0:T(1024)} %param.15) | copy-start | bytes 15364
  246.1 4.8 %copy-start.2 = (f32[1024,1280]{1,0:T(8,128)S(1)}, f32[1024,1280]{1,0:T(8,128)}, u32[]{:S(2)}) copy-start(f32[1024,1280]{1,0:T(8,128)} %all-reduce.2.cloned.1.call-done) | copy-start | bytes 15728644
  246.1 5.6 %copy-start.3 = (bf16[1024,1280]{1,0:T(8,128)(2,1)S(1)}, bf16[1024,1280]{1,0:T(8,128)(2,1)}, u32[]{:S(2)}) copy-start(bf16[1024,1280]{1,0:T(8,128)(2,1)} %param.11) | copy-start | bytes 7864324
  281.3 37.1 %all-to-all-start = ((bf16[32,16,2048]{2,1,0:T(8,128)(2,1)}), bf16[32,16,2048]{2,1,0:T(8,128)(2,1)S(1)}, u32[]{:S(2)}, u32[]{:S(2)}) async-start(bf16[32,16,2048]{2,1,0:T(8,128)(2,1)} %broadcast_select_fusion.1), calls=%async_computation | async-start | bytes 4194304 | tf_op jit(solution)/shard_map/all_to_all | solution.py:97
  321.7 8.5 %copy-start.6 = (f32[2048]{0:T(1024)S(1)}, f32[2048]{0:T(1024)}, u32[]{:S(2)}) copy-start(f32[2048]{0:T(1024)} %param.19) | copy-start | bytes 24580
  330.1 4.5 %copy-start.1 = (bf16[3,1280,320]{1,2,0:T(8,128)(2,1)S(1)}, bf16[3,1280,320]{1,2,0:T(8,128)(2,1)}, u32[]{:S(2)}) copy-start(bf16[3,1280,320]{1,2,0:T(8,128)(2,1)} %param.13) | copy-start | bytes 7372804
Sparse Core Ops, SparseCore 0:
  47.9 198.0 all-reduce.1
Sparse Core Ops, SparseCore 1:
  51.3 212.9 all-gather.2
where the time goes:
time: 343 us; the launch traced here: 342 us
  blocking collectives  90 us (26%)
  waiting for transfers between devices  85.8 us (25%)
  local copies, waits for them, and re-layouts  79.8 us (23%)
  matrix products  43.7 us (13%)
  other arithmetic  21 us (6%)
  between operations  15.1 us (4%)
  starting transfers between devices  5.24 us (2%)
    all_gather x1, blocking collectives, on_device(): lax.all_gather(image_refs, 'sec', axis=0, tiled=True).reshape(sections, -1)  84.6 us
    unnamed x25, local copies, waits for them, and re-layouts  62.7 us
    psum x1, waiting for transfers between devices, on_device(): attended_terms = lax.psum(partial_terms, 'tp')  50 us
    all_to_all x1, waiting for transfers between devices, on_device(): lax.all_to_all(outgoing, 'sec', split_axis=0, concat_axis=0, tiled=True)  30.3 us
    sub x2, matrix products, one_block(): weights = jnp.exp(scores - highest)  15 us
    dot_general x1, matrix products, on_device(): jnp.dot(merged, lax.all_gather(merge_weight, 'sec', axis=0, tiled=True),...  10.6 us
    dot_general x2, matrix products, one_block(): jnp.einsum('hqk,khd->qhd', attention, value_heads, preferred_element_type...  9.67 us
  transfers between devices with their start and end apart: 3, of which 3 were waited for; matrix products, arithmetic and copies ran while one was open for 22% of the time, Pallas kernels for 0%

commit v1 on v0

v1 whole, which is shorter than its diff:
```python
import jax
import jax.numpy as jnp
from jax import lax
from jax.sharding import Mesh, PartitionSpec as P

HEAD_DIM = 80
MERGE = 4
EPSILON = 1e-06
SEC = ("z", "x", "yh")
TP = ("yl", "c")
BF = jnp.bfloat16
F32 = jnp.float32


def vision_context(patches, image_ids, qkv_weight):
    row_count = patches.shape[0]
    projected = jnp.einsum(
        "pd,cde->cpe", patches, qkv_weight, preferred_element_type=F32
    ).astype(BF)
    local_heads = projected.shape[2] // HEAD_DIM
    queries = projected[0].reshape(row_count, local_heads, HEAD_DIM)
    key_heads = projected[1].reshape(row_count, local_heads, HEAD_DIM)
    value_heads = projected[2].reshape(row_count, local_heads, HEAD_DIM)
    patch_ids = jnp.repeat(image_ids.reshape(-1), MERGE)
    block_rows = min(512, row_count)

    def one_block(block_index):
        first_row = block_index * block_rows
        query_part = lax.dynamic_slice_in_dim(queries, first_row, block_rows, 0)
        id_part = lax.dynamic_slice_in_dim(patch_ids, first_row, block_rows, 0)
        scores = jnp.einsum(
            "qhd,khd->hqk", query_part, key_heads, preferred_element_type=F32
        ) * HEAD_DIM ** (-0.5)
        same_image = id_part[:, None] == patch_ids[None, :]
        scores = jnp.where(same_image[None, :, :], scores, -1e30)
        highest = jnp.max(scores, axis=2, keepdims=True)
        weights = jnp.exp(scores - highest)
        attention = (weights / jnp.sum(weights, axis=2, keepdims=True)).astype(BF)
        context = jnp.einsum("hqk,khd->qhd", attention, value_heads, preferred_element_type=F32)
        return context.astype(BF).reshape(block_rows, local_heads * HEAD_DIM)

    contexts = lax.map(one_block, jnp.arange(row_count // block_rows))
    return contexts.reshape(row_count, local_heads * HEAD_DIM)


def swap_tp(block, k):
    return lax.ppermute(block, TP, [(i, i ^ k) for i in range(4)])


def shift_y(block, d):
    return lax.ppermute(block, ("yh", "yl"), [(i, (i + d) % 4) for i in range(4)])


def swap_core(block):
    return lax.ppermute(block, "c", [(0, 1), (1, 0)])


def on_device(
    patches,
    image_ids,
    qkv_weight,
    out_weight,
    merge_gain,
    merge_weight,
    text_rows,
    image_refs,
    llm_gain,
):
    yh = lax.axis_index("yh")
    tp = lax.axis_index(TP)
    y = lax.axis_index(("yh", "yl"))
    core = lax.axis_index("c")

    half = merge_weight.shape[1] // 2
    own = lax.dynamic_slice_in_dim(merge_weight, yh * half, half, 1)
    other = lax.dynamic_slice_in_dim(merge_weight, (1 - yh) * half, half, 1)
    arrived = lax.ppermute(other, "yh", [(0, 1), (1, 0)])
    both = jnp.concatenate(
        [jnp.where(yh == 0, own, arrived), jnp.where(yh == 0, arrived, own)], axis=0
    )
    weight = lax.all_gather(both, ("z", "x"), axis=0, tiled=True)

    out_blocks = [out_weight] + [swap_tp(out_weight, k) for k in (1, 2, 3)]

    prompt_rows = image_refs.shape[0]
    usable = image_refs >= 0
    source = jnp.where(usable, image_refs // 256, -1)
    hits = (source[:, None] == jnp.arange(32)[None, :]).astype(BF)
    before = (jnp.arange(prompt_rows)[:, None] > jnp.arange(prompt_rows)[None, :]).astype(BF)
    earlier = jnp.dot(before, hits, preferred_element_type=F32)
    arrival = jnp.sum(earlier * hits.astype(F32), axis=1).astype(jnp.int32)
    slot = jnp.where(usable, source * 16 + arrival, -1)
    pick = (slot[:, None] == jnp.arange(512)[None, :]).astype(BF)
    names = jnp.where(usable, image_refs % 256 + 1, 0).astype(BF)
    table = jnp.dot(names[None, :], pick, preferred_element_type=F32).astype(jnp.int32)
    table = jnp.broadcast_to(table.reshape(16, 1, 32), (16, 2, 32)).reshape(32, 32)
    table = lax.all_to_all(table, SEC, split_axis=0, concat_axis=0, tiled=True)

    context = vision_context(patches, image_ids, qkv_weight)
    rows = context.shape[0] // 4
    parts = [
        lax.dynamic_slice_in_dim(context, (tp ^ k) * rows, rows, 0) for k in range(4)
    ]
    parts = [parts[0]] + [swap_tp(parts[k], k) for k in (1, 2, 3)]
    terms = sum(
        jnp.dot(part, block, preferred_element_type=F32)
        for part, block in zip(parts, out_blocks)
    )
    own_patches = lax.dynamic_slice_in_dim(patches, tp * rows, rows, 0)
    attended = own_patches.astype(F32) + terms
    moment = jnp.mean(attended * attended, axis=1, keepdims=True)
    normed = (attended * lax.rsqrt(moment + EPSILON) * merge_gain).astype(BF)
    merged = normed.reshape(rows // MERGE, MERGE * normed.shape[1])

    n = merged.shape[0]
    far = jnp.concatenate([shift_y(merged[: n // 2], 2), shift_y(merged[n // 2 :], -2)], axis=0)
    ring = [merged, shift_y(merged, 1), shift_y(merged, -1), far]
    blocks = []
    ids = []
    for d, block in zip((0, 1, -1, 2), ring):
        blocks += [block, swap_core(block)]
        origin = (y - d + 4) % 4
        ids += [origin * 128 + core * 64, origin * 128 + (1 - core) * 64]
    ring_rows = jnp.concatenate(blocks, axis=0)
    row_ids = (jnp.stack(ids)[:, None] + jnp.arange(n)[None, :]).reshape(-1)

    image_rows = jnp.dot(ring_rows, weight, preferred_element_type=F32).astype(BF)
    wanted = table.reshape(32, 2, 16) - 1
    wanted = jnp.where(wanted >= 0, wanted + jnp.arange(2)[None, :, None] * 256, -1).reshape(-1)
    send = (wanted[:, None] == row_ids[None, :]).astype(BF)
    outgoing = jnp.dot(send, image_rows, preferred_element_type=F32).astype(BF)
    received = lax.all_to_all(outgoing, SEC, split_axis=0, concat_axis=0, tiled=True)
    received = received.reshape(16, 2, 32, half)
    picked = jnp.concatenate(
        [
            jnp.dot(pick, received[:, h].reshape(512, half), preferred_element_type=F32).astype(BF)
            for h in range(2)
        ],
        axis=1,
    )
    prompt = jnp.where(usable[:, None], picked, text_rows)
    widened = prompt.astype(F32)
    squares = lax.psum(jnp.sum(widened * widened, axis=1), TP)
    total_width = widened.shape[1] * 4
    inverse = lax.rsqrt(squares / total_width + EPSILON)
    return (widened * inverse[:, None] * llm_gain[None, :]).astype(BF)


def solution(mesh):
    torus = Mesh(mesh.devices.reshape(4, 4, 2, 2, 2), ("z", "x", "yh", "yl", "c"))
    return jax.shard_map(
        on_device,
        mesh=torus,
        in_specs=(
            P(SEC, None),
            P(SEC, None),
            P(None, None, TP),
            P(TP, None),
            P(),
            P(SEC, TP),
            P(SEC, TP),
            P(SEC),
            P(TP),
        ),
        out_specs=P(SEC, TP),
        check_vma=False,
    )
```

time: 343 us -> 207 us (0.60)
  local copies, waits for them, and re-layouts: 79.8 us -> 21.7 us
  blocking collectives: 90 us -> 41.5 us
  waiting for transfers between devices: 85.8 us -> 38.1 us
  starting transfers between devices: 5.24 us -> 30.6 us
  other arithmetic: 21 us -> 7.38 us
  matrix products: 43.7 us -> 52.2 us
    all_gather x1 -> x0, blocking collectives: 84.6 us -> none  [on_device(): lax.all_gather(image_refs, 'sec', axis=0, tiled=True).reshape(sections, -1)]
    unnamed x25 -> x24, local copies, waits for them, and re-layouts: 62.7 us -> 10.1 us
    psum x1 -> x0, waiting for transfers between devices: 50 us -> none  [on_device(): attended_terms = lax.psum(partial_terms, 'tp')]
    all_to_all x0 -> x1, blocking collectives: none -> 33.9 us  [on_device(): lax.all_to_all(outgoing, SEC, split_axis=0, concat_axis=0, tiled=True)]
    ppermute x0 -> x15, waiting for transfers between devices: none -> 31.7 us  [the longest x4 23.4 us: shift_y(): lax.ppermute(block, ('yh', 'yl'), [(i, (i + d) % 4) for i in range(4)])]
    all_to_all x1, waiting for transfers between devices: 30.3 us -> 6.4 us  [on_device(): table = lax.all_to_all(table, SEC, split_axis=0, concat_axis=0, tiled=True)]
    ppermute x0 -> x15, starting transfers between devices: none -> 19.6 us  [the longest x4 5.81 us: shift_y(): lax.ppermute(block, ('yh', 'yl'), [(i, (i + d) % 4) for i in range(4)])]
    dot_general x3 -> x10, matrix products: 19 us -> 27 us  [the longest x1 13.5 us: on_device(): outgoing = jnp.dot(send, image_rows, preferred_element_type=F32).astype(BF)]
  transfers between devices with their start and end apart: 3 -> 17, of which waited for: 3 -> 6; matrix products, arithmetic and copies ran while one was open for 22% -> 27% of each run, Pallas kernels for 0% -> 0%
where the time goes in v1:
time: 207 us
  matrix products  52.2 us (25%)
  blocking collectives  41.5 us (20%)
  waiting for transfers between devices  38.1 us (18%)
  starting transfers between devices  30.6 us (15%)
  local copies, waits for them, and re-layouts  21.7 us (10%)
  between operations  13.7 us (7%)
  other arithmetic  7.38 us (4%)
    all_to_all x1, blocking collectives, on_device(): lax.all_to_all(outgoing, SEC, split_axis=0, concat_axis=0, tiled=True)  33.9 us
    ppermute x4, waiting for transfers between devices, shift_y(): lax.ppermute(block, ('yh', 'yl'), [(i, (i + d) % 4) for i in range(4)])  23.4 us
    sub x2, matrix products, one_block(): weights = jnp.exp(scores - highest)  15.3 us
    dot_general x1, matrix products, on_device(): outgoing = jnp.dot(send, image_rows, preferred_element_type=F32).astype(BF)  13.5 us
    all_to_all x1, starting transfers between devices, on_device(): table = lax.all_to_all(table, SEC, split_axis=0, concat_axis=0, tiled=True)  11 us
    unnamed x24, local copies, waits for them, and re-layouts  10.1 us
    dot_general x2, matrix products, one_block(): jnp.einsum('hqk,khd->qhd', attention, value_heads, preferred_element_type...  9.97 us
    psum x1, blocking collectives, on_device(): squares = lax.psum(jnp.sum(widened * widened, axis=1), TP)  7.61 us
  transfers between devices with their start and end apart: 17, of which 6 were waited for; matrix products, arithmetic and copies ran while one was open for 27% of the time, Pallas kernels for 0%

profile of v1, /device:TPU:1, one launch (start us, length us, event | category | flops | bytes accessed | tf_op | source)
XLA Modules:
  0.0 206.6 jit_solution(4917221127937825058)
XLA Ops:
  6.5 1.1 constant_dynamic-slice_fusion
  7.7 3.8 %collective-permute-start.14 = (bf16[160,1024]{1,0:T(8,128)(2,1)S(1)}, bf16[160,1024]{1,0:T(8,128)(2,1)S(1)}, u32[]{:S(2)}, u32[]{:S(2)}) collective-permute-start(bf16[160,1024]{1,0:T(8,128)(2,1)S(1)} %constant_dynamic-slice_fusion), channel_id=1, source_target_pairs={{0,4},{4,0},{1,5},{5,1},{2,6},{6,2},{3,7},{7,3},{8,12},{12,8},{9,1... | collective-permute-start | bytes 983048 | tf_op jit(solution)/shard_map/ppermute | solution.py:77
  11.5 7.2 %collective-permute-done.14 = bf16[160,1024]{1,0:T(8,128)(2,1)S(1)} collective-permute-done((bf16[160,1024]{1,0:T(8,128)(2,1)S(1)}, bf16[160,1024]{1,0:T(8,128)(2,1)S(1)}, u32[]{:S(2)}, u32[]{:S(2)}) %collective-permute-start.14) | collective-permute-done | bytes 327712 | tf_op jit(solution)/shard_map/ppermute | solution.py:77
  20.7 1.6 collective-permute-start.1
  22.3 1.3 collective-permute-start.5
  24.7 4.5 %convert_bitcast_fusion = bf16[3,1024,320]{1,2,0:T(8,128)(2,1)S(1)} fusion(bf16[3,1280,320]{1,2,0:T(8,128)(2,1)S(1)} %copy-done, bf16[1024,1280]{1,0:T(8,128)(2,1)} %param.11), kind=kOutput, calls=%fused_computation.35 | convolution fusion | flops 2517565440 | bytes 7045120 | tf_op jit(solution)/shard_map/pd,cde->cpe/dot_general | solution.py:17
  29.1 1.3 fusion.61
  30.4 30.7 %while.11 = (s32[]{:T(128)}, bf16[2,512,320]{1,2,0:T(8,128)(2,1)}, s32[2]{0:T(128)S(1)}, s32[1024]{0:T(1024)S(1)}, bf16[1024,4,80]{0,2,1:T(8,128)(2,1)}, /*index...) while((s32[]{:T(128)}, bf16[2,512,320]{1,2,0:T(8,128)(2,1)}, ...), condition=%wide.region_4.5_spmd.clone, body=%wide.region_1.4_spmd.clone.sunk | while | flops 684360704 | bytes 25730292 | solution.py:42
  32.2 7.6 %fusion.88 = (f32[4,512]{1,0:T(4,128)S(1)}, f32[4,512,1024]{2,1,0:T(8,128)}) fusion(pred[512,1024]{1,0:T(8,128)(4,1)S(1)} %broadcast_compare_fusion.5, bf16[1024,4,80]{0,2,1:T(8,128)(2,1)} %get-tuple-element.185, bf16[1024,4,80]{0,2,1:T(8,128)(2,1)} %get-tuple-element.184, s32[]{:T(128)S(6)} %select_n.151), kind=kOutput, calls=%fused_computation.95.clone.1 | convolution fusion | flops 343933952 | bytes 9904132 | tf_op jit(solution)/shard_map/while/body/eval_jaxpr/sub | solution.py:37
  39.9 5.1 %fusion.89 = bf16[4,512,80]{1,2,0:T(8,128)(2,1)S(1)} fusion(bf16[1024,4,80]{0,2,1:T(8,128)(2,1)S(1)} %get-tuple-element.186, f32[4,512,1024]{2,1,0:T(8,128)} %get-tuple-element.154, f32[4,512]{1,0:T(4,128)S(1)} %get-tuple-element.155), kind=kOutput, calls=%fused_computation.10.clone.1 | convolution fusion | flops 339902464 | bytes 9379840 | tf_op jit(solution)/shard_map/while/body/eval_jaxpr/hqk,khd->qhd/dot_general | solution.py:39
  47.7 7.6 %fusion.88 = (f32[4,512]{1,0:T(4,128)S(1)}, f32[4,512,1024]{2,1,0:T(8,128)}) fusion(pred[512,1024]{1,0:T(8,128)(4,1)S(1)} %broadcast_compare_fusion.5, bf16[1024,4,80]{0,2,1:T(8,128)(2,1)} %get-tuple-element.185, bf16[1024,4,80]{0,2,1:T(8,128)(2,1)} %get-tuple-element.184, s32[]{:T(128)S(6)} %select_n.151), kind=kOutput, calls=%fused_computation.95.clone.1 | convolution fusion | flops 343933952 | bytes 9904132 | tf_op jit(solution)/shard_map/while/body/eval_jaxpr/sub | solution.py:37
  55.3 4.9 %fusion.89 = bf16[4,512,80]{1,2,0:T(8,128)(2,1)S(1)} fusion(bf16[1024,4,80]{0,2,1:T(8,128)(2,1)S(1)} %get-tuple-element.186, f32[4,512,1024]{2,1,0:T(8,128)} %get-tuple-element.154, f32[4,512]{1,0:T(4,128)S(1)} %get-tuple-element.155), kind=kOutput, calls=%fused_computation.10.clone.1 | convolution fusion | flops 339902464 | bytes 9379840 | tf_op jit(solution)/shard_map/while/body/eval_jaxpr/hqk,khd->qhd/dot_general | solution.py:39
  61.1 1.2 copy.12
  63.8 1.3 collective-permute-start.4
  66.4 11.0 %all-to-all-start = ((s32[32,1,32]{2,1,0:T(1,128)}), s32[32,1,32]{2,1,0:T(1,128)S(1)}, u32[]{:S(2)}, u32[]{:S(2)}) async-start(s32[32,1,32]{2,1,0:T(1,128)} %bitcast.1), calls=%async_computation | async-start | bytes 32768 | tf_op jit(solution)/shard_map/all_to_all | solution.py:97
  77.6 1.7 fusion.45
  79.6 6.4 %all-to-all-done = s32[32,1,32]{2,1,0:T(1,128)S(1)} async-done(((s32[32,1,32]{2,1,0:T(1,128)}), s32[32,1,32]{2,1,0:T(1,128)S(1)}, u32[]{:S(2)}, u32[]{:S(2)}) %all-to-all-start) | async-done | bytes 4128 | tf_op jit(solution)/shard_map/all_to_all | solution.py:97
  86.4 1.7 convolution_add_fusion.1
  88.1 1.7 fusion.63
  89.8 1.1 collective-permute-done.2
  91.0 1.8 multiply_reduce_fusion
  93.4 2.8 %collective-permute-start.6 = (bf16[64,5120]{1,0:T(8,128)(2,1)S(1)}, bf16[64,5120]{1,0:T(8,128)(2,1)}, u32[]{:S(2)}, u32[]{:S(2)}) collective-permute-start(bf16[64,5120]{1,0:T(8,128)(2,1)S(1)} %reshape.122), channel_id=1, source_target_pairs={{0,1},{1,0},{2,3},{3,2},{4,5},{5,4},{6,7},{7,6},{8,9},{9,8},{10,11... | collective-permute-start | bytes 1966088 | tf_op jit(solution)/shard_map/ppermute | solution.py:55
  96.1 2.7 %collective-permute-start.9 = (bf16[64,5120]{1,0:T(8,128)(2,1)S(1)}, bf16[64,5120]{1,0:T(8,128)(2,1)S(1)}, u32[]{:S(2)}, u32[]{:S(2)}) collective-permute-start(bf16[64,5120]{1,0:T(8,128)(2,1)S(1)} %reshape.122), channel_id=1, source_target_pairs={{0,6},{2,0},{4,2},{6,4},{1,7},{3,1},{5,3},{7,5},{8,14},{10,8},{12,... | collective-permute-start | bytes 1966088 | tf_op jit(solution)/shard_map/ppermute | solution.py:51
  99.4 3.0 %collective-permute-start.12 = (bf16[32,5120]{1,0:T(8,128)(2,1)S(1)}, bf16[32,5120]{1,0:T(8,128)(2,1)S(1)}, u32[]{:S(2)}, u32[]{:S(2)}) collective-permute-start(bf16[32,5120]{1,0:T(8,128)(2,1)S(1)} %slice.33), channel_id=1, source_target_pairs={{0,4},{2,6},{4,0},{6,2},{1,5},{3,7},{5,1},{7,3},{8,12},{10,14},{12... | collective-permute-start | bytes 983048 | tf_op jit(solution)/shard_map/ppermute | solution.py:51
  103.3 15.7 %collective-permute-done.11 = bf16[32,5120]{1,0:T(8,128)(2,1)S(1)} collective-permute-done((bf16[32,5120]{1,0:T(8,128)(2,1)S(1)}, bf16[32,5120]{1,0:T(8,128)(2,1)S(1)}, u32[]{:S(2)}, u32[]{:S(2)}) %collective-permute-start.11) | collective-permute-done | bytes 327712 | tf_op jit(solution)/shard_map/ppermute | solution.py:51
  119.0 7.0 %collective-permute-done.12 = bf16[32,5120]{1,0:T(8,128)(2,1)S(1)} collective-permute-done((bf16[32,5120]{1,0:T(8,128)(2,1)S(1)}, bf16[32,5120]{1,0:T(8,128)(2,1)S(1)}, u32[]{:S(2)}, u32[]{:S(2)}) %collective-permute-start.12) | collective-permute-done | bytes 327712 | tf_op jit(solution)/shard_map/ppermute | solution.py:51
  128.7 2.0 constant_dynamic-update-slice_fusion.7
  130.6 2.0 constant_dynamic-update-slice_fusion.6
  137.7 13.5 %fusion.33 = bf16[1024,1024]{1,0:T(8,128)(2,1)} fusion(s32[512]{0:T(512)S(1)} %add.201, s32[1024]{0:T(1024)S(1)} %add_select_fusion, bf16[512,5120]{1,0:T(8,128)(2,1)} %constant_dynamic-update-slice_fusion, bf16[5120,1024]{1,0:T(8,128)(2,1)} %all-gather.2.cloned.1.call-done), kind=kOutput, calls=%fused_computation.36 | convolution fusion | flops 6444548096 | bytes 17831936 | tf_op jit(solution)/shard_map/dot_general | solution.py:131
  151.3 33.9 %all_to_all.18 = bf16[32,32,1024]{2,1,0:T(8,128)(2,1)S(1)} all-to-all(bf16[32,32,1024]{2,1,0:T(8,128)(2,1)} %bitcast.61), channel_id=1, replica_groups=mesh['z'=4,'x'=4,'yh'=2,'yl'=2,'c'=2] {'z','x','yh'}, dimensions={0} | all-to-all | bytes 4194304 | tf_op jit(solution)/shard_map/all_to_all | solution.py:132
  188.7 7.6 %psum.7 = f32[512]{0:T(512)S(1)} all-reduce(f32[512]{0:T(512)S(1)} %fusion.24), channel_id=1, replica_groups=mesh['z'=4,'x'=4,'yh'=2,'yl'=2,'c'=2] {'yl','c'}, use_global_device_ids=true, to_apply=%region_7.8 | all-reduce | flops 512 | bytes 4096 | tf_op jit(solution)/shard_map/psum | solution.py:143
  196.4 3.4 %fusion.26 = bf16[512,2048]{1,0:T(8,128)(2,1)} fusion(f32[2048]{0:T(1024)S(1)} %copy-done.8, f32[512]{0:T(512)S(1)} %add_rsqrt_fusion, bf16[512,2048]{1,0:T(8,128)(2,1)} %param.17, bf16[512,1024]{1,0:T(8,128)(2,1)} %copy-done.3, bf16[512,1024]{1,0:T(8,128)(2,1)S(1)} %convolution_convert_fusion.2, pred[512]{0:T(512)(128)(4,1)S(1)} %get-tuple-element.84), kind=kLoop, calls=%fused_computation.25 | loop fusion | flops 9437184 | bytes 6302208 | tf_op jit(solution)/shard_map/convert_element_type | solution.py:146
  (101 shorter events, 24.2 us)
Async XLA Ops:
  6.5 18.1 %copy-start = (bf16[3,1280,320]{1,2,0:T(8,128)(2,1)S(1)}, bf16[3,1280,320]{1,2,0:T(8,128)(2,1)}, u32[]{:S(2)}) copy-start(bf16[3,1280,320]{1,2,0:T(8,128)(2,1)} %param.13) | copy-start | bytes 7372804
  6.5 131.2 %all-gather.2.cloned.1.call-start = ((), (), s32[]{:S(2)}) async-start(), calls=%async_computation.2 | async-start | bytes 11141120 | tf_op jit(solution)/shard_map/all_gather | solution.py:81
  7.7 11.0 %collective-permute-start.14 = (bf16[160,1024]{1,0:T(8,128)(2,1)S(1)}, bf16[160,1024]{1,0:T(8,128)(2,1)S(1)}, u32[]{:S(2)}, u32[]{:S(2)}) collective-permute-start(bf16[160,1024]{1,0:T(8,128)(2,1)S(1)} %constant_dynamic-slice_fusion), channel_id=1, source_target_pairs={{0,4},{4,0},{1,5},{5,1},{2,6},{6,2},{3,7},{7,3},{8,12},{12,8},{9,1... | collective-permute-start | bytes 983048 | tf_op jit(solution)/shard_map/ppermute | solution.py:77
  20.7 65.7 %collective-permute-start.1 = (bf16[320,1280]{1,0:T(8,128)(2,1)}, bf16[320,1280]{1,0:T(8,128)(2,1)}, u32[]{:S(2)}, u32[]{:S(2)}) collective-permute-start(bf16[320,1280]{1,0:T(8,128)(2,1)} %param.14), channel_id=1, source_target_pairs={{0,1},{1,0},{2,3},{3,2},{4,5},{5,4},{6,7},{7,6},{8,9},{9,8},{10,11... | collective-permute-start | bytes 2457608 | tf_op jit(solution)/shard_map/ppermute | solution.py:47
  22.3 65.8 %collective-permute-start.5 = (bf16[320,1280]{1,0:T(8,128)(2,1)}, bf16[320,1280]{1,0:T(8,128)(2,1)}, u32[]{:S(2)}, u32[]{:S(2)}) collective-permute-start(bf16[320,1280]{1,0:T(8,128)(2,1)} %param.14), channel_id=1, source_target_pairs={{0,3},{1,2},{2,1},{3,0},{4,7},{5,6},{6,5},{7,4},{8,11},{9,10},{10,... | collective-permute-start | bytes 2457608 | tf_op jit(solution)/shard_map/ppermute | solution.py:47
  23.6 67.4 %collective-permute-start.3 = (bf16[320,1280]{1,0:T(8,128)(2,1)}, bf16[320,1280]{1,0:T(8,128)(2,1)S(1)}, u32[]{:S(2)}, u32[]{:S(2)}) collective-permute-start(bf16[320,1280]{1,0:T(8,128)(2,1)} %param.14), channel_id=1, source_target_pairs={{0,2},{1,3},{2,0},{3,1},{4,6},{5,7},{6,4},{7,5},{8,10},{9,11},{10,... | collective-permute-start | bytes 2457608 | tf_op jit(solution)/shard_map/ppermute | solution.py:47
  24.7 5.8 %copy-start.6 = (s32[1,256]{1,0:T(1,128)S(1)}, s32[1,256]{1,0:T(1,128)}, u32[]{:S(2)}) copy-start(s32[1,256]{1,0:T(1,128)} %param.12) | copy-start | bytes 3076
  30.4 34.6 %copy-start.9 = (s32[512]{0:T(512)S(1)}, s32[512]{0:T(512)}, u32[]{:S(2)}) copy-start(s32[512]{0:T(512)} %param.18) | copy-start | bytes 6148
  39.9 5.1 %copy-start.4 = (bf16[2,512,320]{1,2,0:T(8,128)(2,1)S(1)}, bf16[2,512,320]{1,2,0:T(8,128)(2,1)}, u32[]{:S(2)}) copy-start(bf16[2,512,320]{1,2,0:T(8,128)(2,1)} %get-tuple-element.169) | copy-start | bytes 1966084 | tf_op jit(solution)/shard_map/while
  45.0 0.8 copy-start.5
  55.3 4.9 %copy-start.4 = (bf16[2,512,320]{1,2,0:T(8,128)(2,1)S(1)}, bf16[2,512,320]{1,2,0:T(8,128)(2,1)}, u32[]{:S(2)}) copy-start(bf16[2,512,320]{1,2,0:T(8,128)(2,1)} %get-tuple-element.169) | copy-start | bytes 1966084 | tf_op jit(solution)/shard_map/while
  60.3 0.8 copy-start.5
  63.0 23.1 %collective-permute-start = (bf16[256,320]{0,1:T(8,128)(2,1)S(1)}, bf16[256,320]{0,1:T(8,128)(2,1)S(1)}, u32[]{:S(2)}, u32[]{:S(2)}) collective-permute-start(bf16[256,320]{0,1:T(8,128)(2,1)S(1)} %get-tuple-element.98), channel_id=1, source_target_pairs={{0,1},{1,0},{2,3},{3,2},{4,5},{5,4},{6,7},{7,6},{8,9},{9,8},{10,11... | collective-permute-start | bytes 491528 | tf_op jit(solution)/shard_map/ppermute | solution.py:47
  63.8 24.3 %collective-permute-start.4 = (bf16[256,320]{0,1:T(8,128)(2,1)}, bf16[256,320]{0,1:T(8,128)(2,1)S(1)}, u32[]{:S(2)}, u32[]{:S(2)}) collective-permute-start(bf16[256,320]{0,1:T(8,128)(2,1)} %get-tuple-element.97), channel_id=1, source_target_pairs={{0,3},{1,2},{2,1},{3,0},{4,7},{5,6},{6,5},{7,4},{8,11},{9,10},{10,... | collective-permute-start | bytes 491528 | tf_op jit(solution)/shard_map/ppermute | solution.py:47
  66.4 19.6 %all-to-all-start = ((s32[32,1,32]{2,1,0:T(1,128)}), s32[32,1,32]{2,1,0:T(1,128)S(1)}, u32[]{:S(2)}, u32[]{:S(2)}) async-start(s32[32,1,32]{2,1,0:T(1,128)} %bitcast.1), calls=%async_computation | async-start | bytes 32768 | tf_op jit(solution)/shard_map/all_to_all | solution.py:97
  86.2 4.8 %collective-permute-start.2 = (bf16[256,320]{0,1:T(8,128)(2,1)S(1)}, bf16[256,320]{0,1:T(8,128)(2,1)S(1)}, u32[]{:S(2)}, u32[]{:S(2)}) collective-permute-start(bf16[256,320]{0,1:T(8,128)(2,1)S(1)} %get-tuple-element.96), channel_id=1, source_target_pairs={{0,2},{1,3},{2,0},{3,1},{4,6},{5,7},{6,4},{7,5},{8,10},{9,11},{10,... | collective-permute-start | bytes 491528 | tf_op jit(solution)/shard_map/ppermute | solution.py:47
  88.1 4.7 %copy-start.7 = (f32[1280]{0:T(1024)S(1)}, f32[1280]{0:T(1024)}, u32[]{:S(2)}) copy-start(f32[1280]{0:T(1024)} %param.15) | copy-start | bytes 15364
  93.4 35.3 %collective-permute-start.6 = (bf16[64,5120]{1,0:T(8,128)(2,1)S(1)}, bf16[64,5120]{1,0:T(8,128)(2,1)}, u32[]{:S(2)}, u32[]{:S(2)}) collective-permute-start(bf16[64,5120]{1,0:T(8,128)(2,1)S(1)} %reshape.122), channel_id=1, source_target_pairs={{0,1},{1,0},{2,3},{3,2},{4,5},{5,4},{6,7},{7,6},{8,9},{9,8},{10,11... | collective-permute-start | bytes 1966088 | tf_op jit(solution)/shard_map/ppermute | solution.py:55
  96.1 31.7 %collective-permute-start.7 = (bf16[64,5120]{1,0:T(8,128)(2,1)S(1)}, bf16[64,5120]{1,0:T(8,128)(2,1)}, u32[]{:S(2)}, u32[]{:S(2)}) collective-permute-start(bf16[64,5120]{1,0:T(8,128)(2,1)S(1)} %reshape.122), channel_id=1, source_target_pairs={{0,2},{2,4},{4,6},{6,0},{1,3},{3,5},{5,7},{7,1},{8,10},{10,12},{12... | collective-permute-start | bytes 1966088 | tf_op jit(solution)/shard_map/ppermute | solution.py:51
  96.1 32.5 %collective-permute-start.9 = (bf16[64,5120]{1,0:T(8,128)(2,1)S(1)}, bf16[64,5120]{1,0:T(8,128)(2,1)S(1)}, u32[]{:S(2)}, u32[]{:S(2)}) collective-permute-start(bf16[64,5120]{1,0:T(8,128)(2,1)S(1)} %reshape.122), channel_id=1, source_target_pairs={{0,6},{2,0},{4,2},{6,4},{1,7},{3,1},{5,3},{7,5},{8,14},{10,8},{12,... | collective-permute-start | bytes 1966088 | tf_op jit(solution)/shard_map/ppermute | solution.py:51
  99.1 19.9 %collective-permute-start.11 = (bf16[32,5120]{1,0:T(8,128)(2,1)S(1)}, bf16[32,5120]{1,0:T(8,128)(2,1)S(1)}, u32[]{:S(2)}, u32[]{:S(2)}) collective-permute-start(bf16[32,5120]{1,0:T(8,128)(2,1)S(1)} %slice.31), channel_id=1, source_target_pairs={{0,4},{2,6},{4,0},{6,2},{1,5},{3,7},{5,1},{7,3},{8,12},{10,14},{12... | collective-permute-start | bytes 983048 | tf_op jit(solution)/shard_map/ppermute | solution.py:51
  99.4 26.6 %collective-permute-start.12 = (bf16[32,5120]{1,0:T(8,128)(2,1)S(1)}, bf16[32,5120]{1,0:T(8,128)(2,1)S(1)}, u32[]{:S(2)}, u32[]{:S(2)}) collective-permute-start(bf16[32,5120]{1,0:T(8,128)(2,1)S(1)} %slice.33), channel_id=1, source_target_pairs={{0,4},{2,6},{4,0},{6,2},{1,5},{3,7},{5,1},{7,3},{8,12},{10,14},{12... | collective-permute-start | bytes 983048 | tf_op jit(solution)/shard_map/ppermute | solution.py:51
  126.1 10.7 %collective-permute-start.13 = (bf16[64,5120]{1,0:T(8,128)(2,1)S(1)}, bf16[64,5120]{1,0:T(8,128)(2,1)S(1)}, u32[]{:S(2)}, u32[]{:S(2)}) collective-permute-start(bf16[64,5120]{1,0:T(8,128)(2,1)S(1)} %pad_maximum_fusion), channel_id=1, source_target_pairs={{0,1},{1,0},{2,3},{3,2},{4,5},{5,4},{6,7},{7,6},{8,9},{9,8},{10,11... | collective-permute-start | bytes 1966088 | tf_op jit(solution)/shard_map/ppermute | solution.py:55
  127.8 4.8 %collective-permute-start.8 = (bf16[64,5120]{1,0:T(8,128)(2,1)}, bf16[64,5120]{1,0:T(8,128)(2,1)S(1)}, u32[]{:S(2)}, u32[]{:S(2)}) collective-permute-start(bf16[64,5120]{1,0:T(8,128)(2,1)} %collective-permute-done.7), channel_id=1, source_target_pairs={{0,1},{1,0},{2,3},{3,2},{4,5},{5,4},{6,7},{7,6},{8,9},{9,8},{10,11... | collective-permute-start | bytes 1966088 | tf_op jit(solution)/shard_map/ppermute | solution.py:55
  128.7 5.8 %collective-permute-start.10 = (bf16[64,5120]{1,0:T(8,128)(2,1)S(1)}, bf16[64,5120]{1,0:T(8,128)(2,1)S(1)}, u32[]{:S(2)}, u32[]{:S(2)}) collective-permute-start(bf16[64,5120]{1,0:T(8,128)(2,1)S(1)} %collective-permute-done.9), channel_id=1, source_target_pairs={{0,1},{1,0},{2,3},{3,2},{4,5},{5,4},{6,7},{7,6},{8,9},{9,8},{10,11... | collective-permute-start | bytes 1966088 | tf_op jit(solution)/shard_map/ppermute | solution.py:55
  185.2 2.7 %copy-start.2 = (bf16[512,2048]{1,0:T(8,128)(2,1)S(1)}, bf16[512,2048]{1,0:T(8,128)(2,1)}, u32[]{:S(2)}) copy-start(bf16[512,2048]{1,0:T(8,128)(2,1)} %param.17) | copy-start | bytes 6291460
  186.1 10.2 %copy-start.8 = (f32[2048]{0:T(1024)S(1)}, f32[2048]{0:T(1024)}, u32[]{:S(2)}) copy-start(f32[2048]{0:T(1024)} %param.19) | copy-start | bytes 24580
  186.9 1.0 copy-start.3
  187.9 11.9 %copy-start.1 = (bf16[3,1280,320]{1,2,0:T(8,128)(2,1)S(1)}, bf16[3,1280,320]{1,2,0:T(8,128)(2,1)}, u32[]{:S(2)}) copy-start(bf16[3,1280,320]{1,2,0:T(8,128)(2,1)} %param.13) | copy-start | bytes 7372804
Sparse Core Ops, SparseCore 0:
  20.8 83.9 all-gather.1

commit v2 on v1

--- a/solution.py
+++ b/solution.py
@@ -1,46 +1,108 @@
 import jax
 import jax.numpy as jnp
 from jax import lax
+from jax.experimental import pallas as pl
+from jax.experimental.pallas import tpu as pltpu
 from jax.sharding import Mesh, PartitionSpec as P
 
 HEAD_DIM = 80
 MERGE = 4
 EPSILON = 1e-06
+LOG2E = 1.4426950408889634
 SEC = ("z", "x", "yh")
 TP = ("yl", "c")
 BF = jnp.bfloat16
 F32 = jnp.float32
 
 
-def vision_context(patches, image_ids, qkv_weight):
-    row_count = patches.shape[0]
-    projected = jnp.einsum(
-        "pd,cde->cpe", patches, qkv_weight, preferred_element_type=F32
-    ).astype(BF)
-    local_heads = projected.shape[2] // HEAD_DIM
-    queries = projected[0].reshape(row_count, local_heads, HEAD_DIM)
-    key_heads = projected[1].reshape(row_count, local_heads, HEAD_DIM)
-    value_heads = projected[2].reshape(row_count, local_heads, HEAD_DIM)
+def attention_kernel(row_ids, column_ids, projected, context, keys, values):
+    heads = keys.shape[0]
+    row_count = projected.shape[1]
+    one = jnp.ones((row_count, 128 - HEAD_DIM), BF)
+    for head in range(heads):
+        columns = slice(head * HEAD_DIM, (head + 1) * HEAD_DIM)
+        keys[head] = projected[1, :, columns]
+        values[head] = jnp.concatenate([projected[2, :, columns], one], axis=1)
+    scale = HEAD_DIM ** (-0.5) * LOG2E
+    block = min(256, row_count)
+
+    def one_block(index, carry):
+        rows = pl.ds(pl.multiple_of(index * block, block), block)
+        same_image = row_ids[rows, :] == column_ids[...]
+        outs = []
+        for head in range(heads):
+            query = projected[0, rows, head * HEAD_DIM : (head + 1) * HEAD_DIM]
+            scores = lax.dot_general(
+                query, keys[head], (((1,), (1,)), ((), ())), preferred_element_type=F32
+            )
+            scores = jnp.where(same_image, scores, -1e30)
+            highest = jnp.max(scores, axis=1, keepdims=True)
+            weights = jnp.exp2((scores - highest) * scale).astype(BF)
+            summed = jnp.dot(weights, values[head], preferred_element_type=F32)
+            outs.append(summed[:, :HEAD_DIM] / summed[:, HEAD_DIM : HEAD_DIM + 1])
+        context[rows, :] = jnp.concatenate(outs, axis=1).astype(BF)
+        return carry
+
+    lax.fori_loop(0, row_count // block, one_block, 0)
+
+
+def vision_context(projected, image_ids):
+    row_count, width = projected.shape[1:]
+    heads = width // HEAD_DIM
     patch_ids = jnp.repeat(image_ids.reshape(-1), MERGE)
-    block_rows = min(512, row_count)
-
-    def one_block(block_index):
-        first_row = block_index * block_rows
-        query_part = lax.dynamic_slice_in_dim(queries, first_row, block_rows, 0)
-        id_part = lax.dynamic_slice_in_dim(patch_ids, first_row, block_rows, 0)
-        scores = jnp.einsum(
-            "qhd,khd->hqk", query_part, key_heads, preferred_element_type=F32
-        ) * HEAD_DIM ** (-0.5)
-        same_image = id_part[:, None] == patch_ids[None, :]
-        scores = jnp.where(same_image[None, :, :], scores, -1e30)
-        highest = jnp.max(scores, axis=2, keepdims=True)
-        weights = jnp.exp(scores - highest)
-        attention = (weights / jnp.sum(weights, axis=2, keepdims=True)).astype(BF)
-        context = jnp.einsum("hqk,khd->qhd", attention, value_heads, preferred_element_type=F32)
-        return context.astype(BF).reshape(block_rows, local_heads * HEAD_DIM)
-
-    contexts = lax.map(one_block, jnp.arange(row_count // block_rows))
-    return contexts.reshape(row_count, local_heads * HEAD_DIM)
+    return pl.pallas_call(
+        attention_kernel,
+        out_shape=jax.ShapeDtypeStruct((row_count, width), BF),
+        in_specs=[pl.BlockSpec(memory_space=pltpu.VMEM)] * 3,
+        out_specs=pl.BlockSpec(memory_space=pltpu.VMEM),
+        scratch_shapes=[
+            pltpu.VMEM((heads, row_count, HEAD_DIM), BF),
+            pltpu.VMEM((heads, row_count, 128), BF),
+        ],
+        compiler_params=pltpu.CompilerParams(vmem_limit_bytes=40 * 2**20),
+        cost_estimate=pl.CostEstimate(
+            flops=4 * heads * row_count * row_count * 256,
+            bytes_accessed=8 * row_count * width,
+            transcendentals=heads * row_count * row_count,
+        ),
+        name="vision_attention",
+    )(patch_ids[:, None], patch_ids[None, :], projected)
+
+
+def merge_kernel(*refs):
+    blocks, (weight, send, outgoing, rows) = refs[:8], refs[8:]
+    n = blocks[0].shape[0]
+
+    @pl.when(pl.program_id(0) == 0)
+    def _():
+        for k in range(8):
+            rows[k * n : (k + 1) * n, :] = blocks[k][...]
+
+    image = jnp.dot(rows[...], weight[...], preferred_element_type=F32).astype(BF)
+    outgoing[...] = jnp.dot(send[...], image, preferred_element_type=F32).astype(BF)
+
+
+def merge_and_select(blocks, weight, send, tile=256):
+    depth, columns = weight.shape
+    n = blocks[0].shape[0]
+    slots = send.shape[0]
+    whole = lambda shape: pl.BlockSpec(shape, lambda i: (0, 0), pipeline_mode=pl.Buffered(1))
+    return pl.pallas_call(
+        merge_kernel,
+        grid=(columns // tile,),
+        out_shape=jax.ShapeDtypeStruct((slots, columns), BF),
+        in_specs=[whole((n, depth))] * 8
+        + [pl.BlockSpec((depth, tile), lambda i: (0, i)), whole(send.shape)],
+        out_specs=pl.BlockSpec((slots, tile), lambda i: (0, i)),
+        scratch_shapes=[pltpu.VMEM((8 * n, depth), BF)],
+        compiler_params=pltpu.CompilerParams(vmem_limit_bytes=48 * 2**20),
+        cost_estimate=pl.CostEstimate(
+            flops=2 * 8 * n * (depth + slots) * columns,
+            bytes_accessed=2 * (8 * n * depth + depth * columns + slots * columns),
+            transcendentals=0,
+        ),
+        name="merge_rows",
+    )(*blocks, weight, send)
 
 
 def swap_tp(block, k):
@@ -75,10 +137,12 @@
     own = lax.dynamic_slice_in_dim(merge_weight, yh * half, half, 1)
     other = lax.dynamic_slice_in_dim(merge_weight, (1 - yh) * half, half, 1)
     arrived = lax.ppermute(other, "yh", [(0, 1), (1, 0)])
+    projected = jnp.einsum("pd,cde->cpe", patches, qkv_weight, preferred_element_type=F32)
+    projected = projected.astype(BF)
+    arrived, projected = lax.optimization_barrier((arrived, projected))
     both = jnp.concatenate(
         [jnp.where(yh == 0, own, arrived), jnp.where(yh == 0, arrived, own)], axis=0
     )
-    weight = lax.all_gather(both, ("z", "x"), axis=0, tiled=True)
 
     out_blocks = [out_weight] + [swap_tp(out_weight, k) for k in (1, 2, 3)]
 
@@ -94,9 +158,12 @@
     names = jnp.where(usable, image_refs % 256 + 1, 0).astype(BF)
     table = jnp.dot(names[None, :], pick, preferred_element_type=F32).astype(jnp.int32)
     table = jnp.broadcast_to(table.reshape(16, 1, 32), (16, 2, 32)).reshape(32, 32)
+    table, both, projected = lax.optimization_barrier((table, both, projected))
+    weight = lax.all_gather(both, ("z", "x"), axis=0, tiled=True)
     table = lax.all_to_all(table, SEC, split_axis=0, concat_axis=0, tiled=True)
 
-    context = vision_context(patches, image_ids, qkv_weight)
+    context = vision_context(projected, image_ids)
+    context, table, *out_blocks = lax.optimization_barrier((context, table, *out_blocks))
     rows = context.shape[0] // 4
     parts = [
         lax.dynamic_slice_in_dim(context, (tp ^ k) * rows, rows, 0) for k in range(4)
@@ -121,14 +188,12 @@
         blocks += [block, swap_core(block)]
         origin = (y - d + 4) % 4
         ids += [origin * 128 + core * 64, origin * 128 + (1 - core) * 64]
-    ring_rows = jnp.concatenate(blocks, axis=0)
     row_ids = (jnp.stack(ids)[:, None] + jnp.arange(n)[None, :]).reshape(-1)
 
-    image_rows = jnp.dot(ring_rows, weight, preferred_element_type=F32).astype(BF)
     wanted = table.reshape(32, 2, 16) - 1
     wanted = jnp.where(wanted >= 0, wanted + jnp.arange(2)[None, :, None] * 256, -1).reshape(-1)
     send = (wanted[:, None] == row_ids[None, :]).astype(BF)
-    outgoing = jnp.dot(send, image_rows, preferred_element_type=F32).astype(BF)
+    outgoing = merge_and_select(blocks, weight, send)
     received = lax.all_to_all(outgoing, SEC, split_axis=0, concat_axis=0, tiled=True)
     received = received.reshape(16, 2, 32, half)
     picked = jnp.concatenate(

time: 207 us -> 196 us (0.947)
  matrix products: 52.2 us -> 15 us
  Pallas kernels: 0 us -> 24 us
  waiting for transfers between devices: 38.1 us -> 46.2 us
  starting transfers between devices: 30.6 us -> 25.4 us
  local copies, waits for them, and re-layouts: 21.7 us -> 19.1 us
    pallas_call x0 -> x2, Pallas kernels: none -> 24 us  [the longest x1 14.2 us: merge_and_select(): pl.pallas_call(merge_kernel, grid=(columns // tile,), out_shape=jax.Shape...]
    dot_general x4 -> x1, matrix products: 28 us -> 5.65 us  [on_device(): jnp.einsum('pd,cde->cpe', patches, qkv_weight, preferred_element_type=F32)]
    sub x2 -> x0, matrix products: 15.3 us -> none  [one_block(): weights = jnp.exp(scores - highest)]
    all_to_all x1, waiting for transfers between devices: 6.4 us -> 15.8 us  [on_device(): table = lax.all_to_all(table, SEC, split_axis=0, concat_axis=0, tiled=True)]
    ppermute x1, waiting for transfers between devices: 7.16 us -> 0.01 us  [on_device(): arrived = lax.ppermute(other, 'yh', [(0, 1), (1, 0)])]
    ppermute x6, waiting for transfers between devices: 1.14 us -> 6.11 us  [swap_tp(): return lax.ppermute(block, TP, [(i, i ^ k) for i in range(4)])]
    convert_element_type x0 -> x1, local copies, waits for them, and re-layouts: none -> 4.16 us  [on_device(): projected = projected.astype(BF)]
    unnamed x24 -> x23, local copies, waits for them, and re-layouts: 10.1 us -> 6.31 us
  transfers between devices with their start and end apart: 17 -> 17, of which waited for: 6 -> 8; matrix products, arithmetic and copies ran while one was open for 27% -> 14% of each run, Pallas kernels for 0% -> 5%
where the time goes in v2:
time: 196 us; the launch traced here: 195 us
  waiting for transfers between devices  46.2 us (24%)
  blocking collectives  43 us (22%)
  starting transfers between devices  25.4 us (13%)
  Pallas kernels  24 us (12%)
  local copies, waits for them, and re-layouts  19.1 us (10%)
  matrix products  15 us (8%)
  between operations  13.6 us (7%)
  other arithmetic  8.49 us (4%)
    all_to_all x1, blocking collectives, on_device(): lax.all_to_all(outgoing, SEC, split_axis=0, concat_axis=0, tiled=True)  36.2 us
    ppermute x4, waiting for transfers between devices, shift_y(): lax.ppermute(block, ('yh', 'yl'), [(i, (i + d) % 4) for i in range(4)])  22.2 us
    all_to_all x1, waiting for transfers between devices, on_device(): table = lax.all_to_all(table, SEC, split_axis=0, concat_axis=0, tiled=True)  15.8 us
    pallas_call x1, Pallas kernels, merge_and_select(): pl.pallas_call(merge_kernel, grid=(columns // tile,), out_shape=jax.Shape...  14.2 us
    pallas_call x1, Pallas kernels, vision_context(): pl.pallas_call(attention_kernel, out_shape=jax.ShapeDtypeStruct((row_coun...  9.84 us
    all_to_all x1, starting transfers between devices, on_device(): table = lax.all_to_all(table, SEC, split_axis=0, concat_axis=0, tiled=True)  8.21 us
    dot_general x4, matrix products, on_device(): jnp.dot(part, block, preferred_element_type=F32)  7.2 us
    psum x1, blocking collectives, on_device(): squares = lax.psum(jnp.sum(widened * widened, axis=1), TP)  6.83 us
  transfers between devices with their start and end apart: 17, of which 8 were waited for; matrix products, arithmetic and copies ran while one was open for 14% of the time, Pallas kernels for 5%

profile of v2, /device:TPU:1, one launch (start us, length us, event | category | flops | bytes accessed | tf_op | source)
XLA Modules:
  0.0 194.8 jit_solution(16033301449035853043)
XLA Ops:
  6.5 1.1 constant_dynamic-slice_fusion.3
  7.7 3.8 %collective-permute-start = (bf16[160,1024]{1,0:T(8,128)(2,1)S(1)}, bf16[160,1024]{1,0:T(8,128)(2,1)}, u32[]{:S(2)}, u32[]{:S(2)}) collective-permute-start(bf16[160,1024]{1,0:T(8,128)(2,1)S(1)} %constant_dynamic-slice_fusion.3), channel_id=1, source_target_pairs={{0,4},{4,0},{1,5},{5,1},{2,6},{6,2},{3,7},{7,3},{8,12},{12,8},{9,1... | collective-permute-start | bytes 983048 | tf_op jit(solution)/shard_map/ppermute | solution.py:139
  12.5 5.6 %fusion.8 = bf16[3,320,1024]{2,1,0:T(8,128)(2,1)} fusion(bf16[3,1280,320]{1,2,0:T(8,128)(2,1)S(1)} %copy-done, bf16[1024,1280]{1,0:T(8,128)(2,1)} %param.9), kind=kOutput, calls=%fused_computation.13 | convolution fusion | flops 2517565440 | bytes 7045120 | tf_op jit(solution)/shard_map/pd,cde->cpe/dot_general | solution.py:140
  18.6 4.2 %copy.15 = bf16[3,320,1024]{1,2,0:T(8,128)(2,1)} copy(bf16[3,320,1024]{2,1,0:T(8,128)(2,1)} %fusion.8) | data formatting | bytes 3932160 | tf_op jit(solution)/shard_map/convert_element_type | solution.py:141
  22.8 1.1 broadcast_select_fusion.1
  25.9 1.2 collective-permute-start.1
  28.3 1.0 broadcast_in_dim_reshape.10.row_ids
  29.3 8.2 %all-to-all-start = ((s32[32,1,32]{2,1,0:T(1,128)}), s32[32,1,32]{2,1,0:T(1,128)S(1)}, u32[]{:S(2)}, u32[]{:S(2)}) async-start(s32[32,1,32]{2,1,0:T(1,128)} %bitcast.5), calls=%async_computation | async-start | bytes 32768 | tf_op jit(solution)/shard_map/all_to_all | solution.py:163
  37.5 1.7 copy-done.1
  39.2 1.0 copy-done.2
  40.3 9.8 %vision_attention.1 = bf16[1024,320]{1,0:T(8,128)(2,1)S(1)} custom-call(s32[1024,1]{1,0:T(8,128)S(1)} %copy-done.2, s32[1,1024]{1,0:T(1,128)S(1)} %broadcast_in_dim_reshape.9.column_ids, bf16[3,1024,320]{2,1,0:T(8,128)(2,1)S(1)} %bitcast.34), custom_call_target="tpu_custom_call" | custom-call | flops 4294967296 | bytes 2621440 | tf_op jit(solution)/shard_map/vision_attention/pallas_call | solution.py:53
  50.1 15.8 %all-to-all-done = s32[32,1,32]{2,1,0:T(1,128)S(1)} async-done(((s32[32,1,32]{2,1,0:T(1,128)}), s32[32,1,32]{2,1,0:T(1,128)S(1)}, u32[]{:S(2)}, u32[]{:S(2)}) %all-to-all-start) | async-done | bytes 4128 | tf_op jit(solution)/shard_map/all_to_all | solution.py:163
  66.8 2.2 %collective-permute-start.4 = (bf16[256,320]{1,0:T(8,128)(2,1)S(1)}, bf16[256,320]{1,0:T(8,128)(2,1)S(1)}, u32[]{:S(2)}, u32[]{:S(2)}) collective-permute-start(bf16[256,320]{1,0:T(8,128)(2,1)S(1)} %get-tuple-element.33), channel_id=1, source_target_pairs={{0,1},{1,0},{2,3},{3,2},{4,5},{5,4},{6,7},{7,6},{8,9},{9,8},{10,11... | collective-permute-start | bytes 491528 | tf_op jit(solution)/shard_map/ppermute | solution.py:109
  69.0 1.7 collective-permute-start.6
  70.7 1.1 collective-permute-done.5
  71.8 1.8 fusion.28
  73.6 5.0 %collective-permute-done.6 = bf16[256,320]{1,0:T(8,128)(2,1)S(1)} collective-permute-done((bf16[256,320]{1,0:T(8,128)(2,1)}, bf16[256,320]{1,0:T(8,128)(2,1)S(1)}, u32[]{:S(2)}, u32[]{:S(2)}) %collective-permute-start.6) | collective-permute-done | bytes 163872 | tf_op jit(solution)/shard_map/ppermute | solution.py:109
  78.6 1.7 fusion.29
  80.3 1.7 fusion.27
  82.0 2.1 %multiply_reduce_fusion = (f32[256]{0:T(256)S(1)}, f32[256,1280]{1,0:T(8,128)S(1)}) fusion(f32[256,1280]{1,0:T(8,128)S(1)} %fusion.29, f32[256,1280]{1,0:T(8,128)S(1)} %fusion.28, f32[256,1280]{1,0:T(8,128)S(1)} %fusion.27, bf16[320,1280]{1,0:T(8,128)(2,1)} %param.12, bf16[1024,320]{1,0:T(8,128)(2,1)S(1)} %vision_attention.1, s32[]{:T(128)S(6)} %select_n.86, ...), kind=kOutput, calls=%fused_computation.17 | convolution fusion | flops 212008704 | bytes 6916096 | tf_op jit(solution)/shard_map/dot_general | solution.py:173
  86.1 1.4 collective-permute-start.12
  87.8 1.5 reshape.79.refs_0_
  92.6 1.7 collective-permute-start.13
  94.3 3.0 %collective-permute-done.12 = bf16[32,5120]{1,0:T(8,128)(2,1)} collective-permute-done((bf16[32,5120]{1,0:T(8,128)(2,1)}, bf16[32,5120]{1,0:T(8,128)(2,1)}, u32[]{:S(2)}, u32[]{:S(2)}) %collective-permute-start.12) | collective-permute-done | bytes 327712 | tf_op jit(solution)/shard_map/ppermute | solution.py:113
  97.2 1.7 constant_dynamic-update-slice_fusion.1
  98.9 19.2 %collective-permute-done.13 = bf16[32,5120]{1,0:T(8,128)(2,1)S(1)} collective-permute-done((bf16[32,5120]{1,0:T(8,128)(2,1)}, bf16[32,5120]{1,0:T(8,128)(2,1)S(1)}, u32[]{:S(2)}, u32[]{:S(2)}) %collective-permute-start.13) | collective-permute-done | bytes 327712 | tf_op jit(solution)/shard_map/ppermute | solution.py:113
  120.4 1.2 compare_convert_fusion.refs_9_
  123.7 14.2 %merge_rows.1 = bf16[1024,1024]{1,0:T(8,128)(2,1)} custom-call(bf16[64,5120]{1,0:T(8,128)(2,1)S(1)} %reshape.79.refs_0_, bf16[64,5120]{1,0:T(8,128)(2,1)} %collective-permute-done.7.refs_1_, bf16[64,5120]{1,0:T(8,128)(2,1)} %collective-permute-done.8.refs_2_, bf16[64,5120]{1,0:T(8,128)(2,1)} %collective-permute-done.9.refs_3_, ...), custom_call_target="tpu_custom_call" | custom-call | flops 6442450944 | bytes 17825792 | tf_op jit(solution)/shard_map/merge_rows/pallas_call | solution.py:90
  137.9 36.2 %all_to_all.21 = bf16[32,32,1024]{2,1,0:T(8,128)(2,1)S(1)} all-to-all(bf16[32,32,1024]{2,1,0:T(8,128)(2,1)} %bitcast.36), channel_id=1, replica_groups=mesh['z'=4,'x'=4,'yh'=2,'yl'=2,'c'=2] {'z','x','yh'}, dimensions={0} | all-to-all | bytes 4194304 | tf_op jit(solution)/shard_map/all_to_all | solution.py:197
  175.9 1.0 copy-done.5
  177.8 6.8 %psum.7 = f32[512]{0:T(512)S(1)} all-reduce(f32[512]{0:T(512)S(1)} %fusion), channel_id=1, replica_groups=mesh['z'=4,'x'=4,'yh'=2,'yl'=2,'c'=2] {'yl','c'}, use_global_device_ids=true, to_apply=%region_3.4 | all-reduce | flops 512 | bytes 4096 | tf_op jit(solution)/shard_map/psum | solution.py:208
  184.6 3.4 %fusion.2 = bf16[512,2048]{1,0:T(8,128)(2,1)} fusion(f32[2048]{0:T(1024)S(1)} %copy-done.8, f32[512]{0:T(512)S(1)} %add_rsqrt_fusion, bf16[512,2048]{1,0:T(8,128)(2,1)} %param.15, bf16[512,1024]{1,0:T(8,128)(2,1)} %copy-done.5, bf16[512,1024]{1,0:T(8,128)(2,1)S(1)} %convolution_convert_fusion.1, pred[512]{0:T(512)(128)(4,1)S(1)} %get-tuple-element.28), kind=kLoop, calls=%fused_computation.4 | loop fusion | flops 9437184 | bytes 6302208 | tf_op jit(solution)/shard_map/convert_element_type | solution.py:211
  (74 shorter events, 18.0 us)
Async XLA Ops:
  6.5 5.9 %copy-start = (bf16[3,1280,320]{1,2,0:T(8,128)(2,1)S(1)}, bf16[3,1280,320]{1,2,0:T(8,128)(2,1)}, u32[]{:S(2)}) copy-start(bf16[3,1280,320]{1,2,0:T(8,128)(2,1)} %param.11) | copy-start | bytes 7372804
  6.5 117.2 %all-gather.2.cloned.1.call-start = ((), (), s32[]{:S(2)}) async-start(), calls=%async_computation.2 | async-start | bytes 11141120 | tf_op jit(solution)/shard_map/all_gather | solution.py:162
  7.7 15.1 %collective-permute-start = (bf16[160,1024]{1,0:T(8,128)(2,1)S(1)}, bf16[160,1024]{1,0:T(8,128)(2,1)}, u32[]{:S(2)}, u32[]{:S(2)}) collective-permute-start(bf16[160,1024]{1,0:T(8,128)(2,1)S(1)} %constant_dynamic-slice_fusion.3), channel_id=1, source_target_pairs={{0,4},{4,0},{1,5},{5,1},{2,6},{6,2},{3,7},{7,3},{8,12},{12,8},{9,1... | collective-permute-start | bytes 983048 | tf_op jit(solution)/shard_map/ppermute | solution.py:139
  12.5 5.7 %copy-start.9 = (s32[512]{0:T(512)S(1)}, s32[512]{0:T(512)}, u32[]{:S(2)}) copy-start(s32[512]{0:T(512)} %param.16) | copy-start | bytes 6148
  18.6 4.2 %copy-start.6 = (bf16[160,2048]{1,0:T(8,128)(2,1)S(1)}, bf16[160,2048]{1,0:T(8,128)(2,1)}, u32[]{:S(2)}) copy-start(bf16[160,2048]{1,0:T(8,128)(2,1)} %param.14) | copy-start | bytes 1966084
  22.8 5.3 %copy-start.10 = (s32[1,256]{1,0:T(1,128)S(1)}, s32[1,256]{1,0:T(1,128)}, u32[]{:S(2)}) copy-start(s32[1,256]{1,0:T(1,128)} %param.10) | copy-start | bytes 3076
  25.4 40.4 %collective-permute-start.2 = (bf16[320,1280]{1,0:T(8,128)(2,1)}, bf16[320,1280]{1,0:T(8,128)(2,1)}, u32[]{:S(2)}, u32[]{:S(2)}) collective-permute-start(bf16[320,1280]{1,0:T(8,128)(2,1)} %param.12), channel_id=1, source_target_pairs={{0,2},{1,3},{2,0},{3,1},{4,6},{5,7},{6,4},{7,5},{8,10},{9,11},{10,... | collective-permute-start | bytes 2457608 | tf_op jit(solution)/shard_map/ppermute | solution.py:109
  25.9 40.0 %collective-permute-start.1 = (bf16[320,1280]{1,0:T(8,128)(2,1)}, bf16[320,1280]{1,0:T(8,128)(2,1)}, u32[]{:S(2)}, u32[]{:S(2)}) collective-permute-start(bf16[320,1280]{1,0:T(8,128)(2,1)} %param.12), channel_id=1, source_target_pairs={{0,1},{1,0},{2,3},{3,2},{4,5},{5,4},{6,7},{7,6},{8,9},{9,8},{10,11... | collective-permute-start | bytes 2457608 | tf_op jit(solution)/shard_map/ppermute | solution.py:109
  27.2 38.7 %collective-permute-start.3 = (bf16[320,1280]{1,0:T(8,128)(2,1)}, bf16[320,1280]{1,0:T(8,128)(2,1)}, u32[]{:S(2)}, u32[]{:S(2)}) collective-permute-start(bf16[320,1280]{1,0:T(8,128)(2,1)} %param.12), channel_id=1, source_target_pairs={{0,3},{1,2},{2,1},{3,0},{4,7},{5,6},{6,5},{7,4},{8,11},{9,10},{10,... | collective-permute-start | bytes 2457608 | tf_op jit(solution)/shard_map/ppermute | solution.py:109
  29.3 36.6 %all-to-all-start = ((s32[32,1,32]{2,1,0:T(1,128)}), s32[32,1,32]{2,1,0:T(1,128)S(1)}, u32[]{:S(2)}, u32[]{:S(2)}) async-start(s32[32,1,32]{2,1,0:T(1,128)} %bitcast.5), calls=%async_computation | async-start | bytes 32768 | tf_op jit(solution)/shard_map/all_to_all | solution.py:163
  37.5 1.7 copy-start.1
  39.2 1.0 copy-start.2
  66.7 5.1 %collective-permute-start.5 = (bf16[256,320]{1,0:T(8,128)(2,1)}, bf16[256,320]{1,0:T(8,128)(2,1)}, u32[]{:S(2)}, u32[]{:S(2)}) collective-permute-start(bf16[256,320]{1,0:T(8,128)(2,1)} %get-tuple-element.35), channel_id=1, source_target_pairs={{0,2},{1,3},{2,0},{3,1},{4,6},{5,7},{6,4},{7,5},{8,10},{9,11},{10,... | collective-permute-start | bytes 491528 | tf_op jit(solution)/shard_map/ppermute | solution.py:109
  66.8 13.5 %collective-permute-start.4 = (bf16[256,320]{1,0:T(8,128)(2,1)S(1)}, bf16[256,320]{1,0:T(8,128)(2,1)S(1)}, u32[]{:S(2)}, u32[]{:S(2)}) collective-permute-start(bf16[256,320]{1,0:T(8,128)(2,1)S(1)} %get-tuple-element.33), channel_id=1, source_target_pairs={{0,1},{1,0},{2,3},{3,2},{4,5},{5,4},{6,7},{7,6},{8,9},{9,8},{10,11... | collective-permute-start | bytes 491528 | tf_op jit(solution)/shard_map/ppermute | solution.py:109
  69.0 9.6 %collective-permute-start.6 = (bf16[256,320]{1,0:T(8,128)(2,1)}, bf16[256,320]{1,0:T(8,128)(2,1)S(1)}, u32[]{:S(2)}, u32[]{:S(2)}) collective-permute-start(bf16[256,320]{1,0:T(8,128)(2,1)} %get-tuple-element.34), channel_id=1, source_target_pairs={{0,3},{1,2},{2,1},{3,0},{4,7},{5,6},{6,5},{7,4},{8,11},{9,10},{10,... | collective-permute-start | bytes 491528 | tf_op jit(solution)/shard_map/ppermute | solution.py:109
  81.9 2.1 %copy-start.7 = (f32[1280]{0:T(1024)S(1)}, f32[1280]{0:T(1024)}, u32[]{:S(2)}) copy-start(f32[1280]{0:T(1024)} %param.13) | copy-start | bytes 15364
  84.2 0.8 copy-start.4
  86.1 11.2 %collective-permute-start.12 = (bf16[32,5120]{1,0:T(8,128)(2,1)}, bf16[32,5120]{1,0:T(8,128)(2,1)}, u32[]{:S(2)}, u32[]{:S(2)}) collective-permute-start(bf16[32,5120]{1,0:T(8,128)(2,1)} %slice.19), channel_id=1, source_target_pairs={{0,4},{2,6},{4,0},{6,2},{1,5},{3,7},{5,1},{7,3},{8,12},{10,14},{12... | collective-permute-start | bytes 983048 | tf_op jit(solution)/shard_map/ppermute | solution.py:113
  89.4 30.4 %collective-permute-start.10 = (bf16[64,5120]{1,0:T(8,128)(2,1)S(1)}, bf16[64,5120]{1,0:T(8,128)(2,1)}, u32[]{:S(2)}, u32[]{:S(2)}) collective-permute-start(bf16[64,5120]{1,0:T(8,128)(2,1)S(1)} %reshape.79.refs_0_), channel_id=1, source_target_pairs={{0,6},{2,0},{4,2},{6,4},{1,7},{3,1},{5,3},{7,5},{8,14},{10,8},{12,... | collective-permute-start | bytes 1966088 | tf_op jit(solution)/shard_map/ppermute | solution.py:113
  90.2 29.6 %collective-permute-start.8 = (bf16[64,5120]{1,0:T(8,128)(2,1)S(1)}, bf16[64,5120]{1,0:T(8,128)(2,1)}, u32[]{:S(2)}, u32[]{:S(2)}) collective-permute-start(bf16[64,5120]{1,0:T(8,128)(2,1)S(1)} %reshape.79.refs_0_), channel_id=1, source_target_pairs={{0,2},{2,4},{4,6},{6,0},{1,3},{3,5},{5,7},{7,1},{8,10},{10,12},{12... | collective-permute-start | bytes 1966088 | tf_op jit(solution)/shard_map/ppermute | solution.py:113
  90.9 30.7 %collective-permute-start.7 = (bf16[64,5120]{1,0:T(8,128)(2,1)S(1)}, bf16[64,5120]{1,0:T(8,128)(2,1)}, u32[]{:S(2)}, u32[]{:S(2)}) collective-permute-start(bf16[64,5120]{1,0:T(8,128)(2,1)S(1)} %reshape.79.refs_0_), channel_id=1, source_target_pairs={{0,1},{1,0},{2,3},{3,2},{4,5},{5,4},{6,7},{7,6},{8,9},{9,8},{10,11... | collective-permute-start | bytes 1966088 | tf_op jit(solution)/shard_map/ppermute | solution.py:117
  92.6 25.6 %collective-permute-start.13 = (bf16[32,5120]{1,0:T(8,128)(2,1)}, bf16[32,5120]{1,0:T(8,128)(2,1)S(1)}, u32[]{:S(2)}, u32[]{:S(2)}) collective-permute-start(bf16[32,5120]{1,0:T(8,128)(2,1)} %slice.21), channel_id=1, source_target_pairs={{0,4},{2,6},{4,0},{6,2},{1,5},{3,7},{5,1},{7,3},{8,12},{10,14},{12... | collective-permute-start | bytes 983048 | tf_op jit(solution)/shard_map/ppermute | solution.py:113
  118.9 2.9 %collective-permute-start.14 = (bf16[64,5120]{1,0:T(8,128)(2,1)}, bf16[64,5120]{1,0:T(8,128)(2,1)}, u32[]{:S(2)}, u32[]{:S(2)}) collective-permute-start(bf16[64,5120]{1,0:T(8,128)(2,1)} %constant_dynamic-update-slice_fusion.refs_6_), channel_id=1, source_target_pairs={{0,1},{1,0},{2,3},{3,2},{4,5},{5,4},{6,7},{7,6},{8,9},{9,8},{10,11... | collective-permute-start | bytes 1966088 | tf_op jit(solution)/shard_map/ppermute | solution.py:117
  119.8 3.0 %collective-permute-start.11 = (bf16[64,5120]{1,0:T(8,128)(2,1)}, bf16[64,5120]{1,0:T(8,128)(2,1)}, u32[]{:S(2)}, u32[]{:S(2)}) collective-permute-start(bf16[64,5120]{1,0:T(8,128)(2,1)} %collective-permute-done.10.refs_4_), channel_id=1, source_target_pairs={{0,1},{1,0},{2,3},{3,2},{4,5},{5,4},{6,7},{7,6},{8,9},{9,8},{10,11... | collective-permute-start | bytes 1966088 | tf_op jit(solution)/shard_map/ppermute | solution.py:117
  119.8 3.9 %collective-permute-start.9 = (bf16[64,5120]{1,0:T(8,128)(2,1)}, bf16[64,5120]{1,0:T(8,128)(2,1)}, u32[]{:S(2)}, u32[]{:S(2)}) collective-permute-start(bf16[64,5120]{1,0:T(8,128)(2,1)} %collective-permute-done.8.refs_2_), channel_id=1, source_target_pairs={{0,1},{1,0},{2,3},{3,2},{4,5},{5,4},{6,7},{7,6},{8,9},{9,8},{10,11... | collective-permute-start | bytes 1966088 | tf_op jit(solution)/shard_map/ppermute | solution.py:117
  175.1 1.8 copy-start.3
  175.9 1.0 copy-start.5
  176.9 7.7 %copy-start.8 = (f32[2048]{0:T(1024)S(1)}, f32[2048]{0:T(1024)}, u32[]{:S(2)}) copy-start(f32[2048]{0:T(1024)} %param.17) | copy-start | bytes 24580
Sparse Core Ops, SparseCore 0:
  25.6 81.1 all-gather.1

commit v3 on v2

--- a/solution.py
+++ b/solution.py
@@ -69,36 +69,129 @@
     )(patch_ids[:, None], patch_ids[None, :], projected)
 
 
+def project_kernel(patches, weight, projected):
+    projected[0] = jnp.dot(patches[...], weight[0], preferred_element_type=F32).astype(BF)
+
+
+def project(patches, weight):
+    rows, depth = patches.shape
+    count, _, width = weight.shape
+    return pl.pallas_call(
+        project_kernel,
+        grid=(count,),
+        out_shape=jax.ShapeDtypeStruct((count, rows, width), BF),
+        in_specs=[
+            pl.BlockSpec((rows, depth), lambda i: (0, 0), pipeline_mode=pl.Buffered(1)),
+            pl.BlockSpec((1, depth, width), lambda i: (i, 0, 0)),
+        ],
+        out_specs=pl.BlockSpec((1, rows, width), lambda i: (i, 0, 0)),
+        compiler_params=pltpu.CompilerParams(vmem_limit_bytes=32 * 2**20),
+        cost_estimate=pl.CostEstimate(
+            flops=2 * rows * depth * width * count,
+            bytes_accessed=2 * (rows * depth + count * width * (depth + rows)),
+            transcendentals=0,
+        ),
+        name="project_qkv",
+    )(patches, weight)
+
+
+def norm_kernel(*refs):
+    tp, parts, outs, (patches, gain, merged, top, bottom, normed) = (
+        refs[0], refs[1:5], refs[5:9], refs[9:],
+    )
+    attended = patches[...].astype(F32)
+    for part, weight in zip(parts, outs):
+        attended += jnp.dot(part[...], weight[...], preferred_element_type=F32)
+    moment = jnp.mean(attended * attended, axis=1, keepdims=True)
+    scaled = attended * lax.rsqrt(moment + EPSILON) * gain[...]
+    count, width = merged.shape[0], scaled.shape[1]
+    for q in range(width // 128):
+        normed[q] = scaled[:, q * 128 : (q + 1) * 128]
+    for j in range(MERGE):
+        for q in range(width // 128):
+            piece = normed[q, pl.ds(j, count, stride=MERGE), :].astype(BF)
+            columns = slice(j * width + q * 128, j * width + (q + 1) * 128)
+            merged[:, columns] = piece
+            top[:, columns] = piece[: count // 2]
+            bottom[:, columns] = piece[count // 2 :]
+
+
+def project_and_norm(tp, parts, outs, patches, gain):
+    rows, depth = parts[0].shape
+    width = patches.shape[1]
+    count = rows // MERGE
+    whole = lambda shape: pl.BlockSpec(shape, lambda i, t: (0, 0))
+    return pl.pallas_call(
+        norm_kernel,
+        grid_spec=pltpu.PrefetchScalarGridSpec(
+            num_scalar_prefetch=1,
+            grid=(1,),
+            in_specs=[whole((rows, depth))] * 4
+            + [whole((depth, width))] * 4
+            + [pl.BlockSpec((rows, width), lambda i, t: (t[0], 0)), whole((1, width))],
+            out_specs=[
+                whole((count, MERGE * width)),
+                whole((count // 2, MERGE * width)),
+                whole((count // 2, MERGE * width)),
+            ],
+            scratch_shapes=[pltpu.VMEM((width // 128, rows, 128), F32)],
+        ),
+        out_shape=[
+            jax.ShapeDtypeStruct((count, MERGE * width), BF),
+            jax.ShapeDtypeStruct((count // 2, MERGE * width), BF),
+            jax.ShapeDtypeStruct((count // 2, MERGE * width), BF),
+        ],
+        compiler_params=pltpu.CompilerParams(vmem_limit_bytes=32 * 2**20),
+        cost_estimate=pl.CostEstimate(
+            flops=8 * rows * depth * width,
+            bytes_accessed=8 * depth * (rows + width) + 4 * rows * width,
+            transcendentals=rows,
+        ),
+        name="project_and_norm",
+    )(tp.reshape(1).astype(jnp.int32), *parts, *outs, patches, gain[None, :])
+
+
 def merge_kernel(*refs):
-    blocks, (weight, send, outgoing, rows) = refs[:8], refs[8:]
-    n = blocks[0].shape[0]
-
-    @pl.when(pl.program_id(0) == 0)
+    blocks, (weight, send, outgoing, rows, total) = refs[:-5], refs[-5:]
+    step = pl.program_id(0)
+    first = 0
+    for block in blocks:
+        rows[first : first + block.shape[0], :] = block[...]
+        first += block.shape[0]
+    term = jnp.dot(rows[...], weight[...], preferred_element_type=F32)
+
+    @pl.when(step == 0)
     def _():
-        for k in range(8):
-            rows[k * n : (k + 1) * n, :] = blocks[k][...]
-
-    image = jnp.dot(rows[...], weight[...], preferred_element_type=F32).astype(BF)
-    outgoing[...] = jnp.dot(send[...], image, preferred_element_type=F32).astype(BF)
-
-
-def merge_and_select(blocks, weight, send, tile=256):
+        total[...] = term
+
+    @pl.when(step > 0)
+    def _():
+        total[...] += term
+
+    @pl.when(step == pl.num_programs(0) - 1)
+    def _():
+        image = total[...].astype(BF)
+        outgoing[...] = jnp.dot(send[...], image, preferred_element_type=F32).astype(BF)
+
+
+def merge_and_select(blocks, weight, send, tile=1280):
     depth, columns = weight.shape
-    n = blocks[0].shape[0]
-    slots = send.shape[0]
-    whole = lambda shape: pl.BlockSpec(shape, lambda i: (0, 0), pipeline_mode=pl.Buffered(1))
+    slots, count = send.shape
     return pl.pallas_call(
         merge_kernel,
-        grid=(columns // tile,),
+        grid=(depth // tile,),
         out_shape=jax.ShapeDtypeStruct((slots, columns), BF),
-        in_specs=[whole((n, depth))] * 8
-        + [pl.BlockSpec((depth, tile), lambda i: (0, i)), whole(send.shape)],
-        out_specs=pl.BlockSpec((slots, tile), lambda i: (0, i)),
-        scratch_shapes=[pltpu.VMEM((8 * n, depth), BF)],
+        in_specs=[pl.BlockSpec((b.shape[0], tile), lambda i: (0, i)) for b in blocks]
+        + [
+            pl.BlockSpec((tile, columns), lambda i: (i, 0)),
+            pl.BlockSpec((slots, count), lambda i: (0, 0), pipeline_mode=pl.Buffered(1)),
+        ],
+        out_specs=pl.BlockSpec((slots, columns), lambda i: (0, 0)),
+        scratch_shapes=[pltpu.VMEM((count, tile), BF), pltpu.VMEM((count, columns), F32)],
         compiler_params=pltpu.CompilerParams(vmem_limit_bytes=48 * 2**20),
         cost_estimate=pl.CostEstimate(
-            flops=2 * 8 * n * (depth + slots) * columns,
-            bytes_accessed=2 * (8 * n * depth + depth * columns + slots * columns),
+            flops=2 * count * (depth + slots) * columns,
+            bytes_accessed=2 * (count * depth + depth * columns + slots * columns),
             transcendentals=0,
         ),
         name="merge_rows",
@@ -137,8 +230,7 @@
     own = lax.dynamic_slice_in_dim(merge_weight, yh * half, half, 1)
     other = lax.dynamic_slice_in_dim(merge_weight, (1 - yh) * half, half, 1)
     arrived = lax.ppermute(other, "yh", [(0, 1), (1, 0)])
-    projected = jnp.einsum("pd,cde->cpe", patches, qkv_weight, preferred_element_type=F32)
-    projected = projected.astype(BF)
+    projected = project(patches, qkv_weight)
     arrived, projected = lax.optimization_barrier((arrived, projected))
     both = jnp.concatenate(
         [jnp.where(yh == 0, own, arrived), jnp.where(yh == 0, arrived, own)], axis=0
@@ -158,37 +250,33 @@
     names = jnp.where(usable, image_refs % 256 + 1, 0).astype(BF)
     table = jnp.dot(names[None, :], pick, preferred_element_type=F32).astype(jnp.int32)
     table = jnp.broadcast_to(table.reshape(16, 1, 32), (16, 2, 32)).reshape(32, 32)
-    table, both, projected = lax.optimization_barrier((table, both, projected))
+    both, projected = lax.optimization_barrier((both, projected))
     weight = lax.all_gather(both, ("z", "x"), axis=0, tiled=True)
-    table = lax.all_to_all(table, SEC, split_axis=0, concat_axis=0, tiled=True)
 
     context = vision_context(projected, image_ids)
-    context, table, *out_blocks = lax.optimization_barrier((context, table, *out_blocks))
     rows = context.shape[0] // 4
     parts = [
         lax.dynamic_slice_in_dim(context, (tp ^ k) * rows, rows, 0) for k in range(4)
     ]
     parts = [parts[0]] + [swap_tp(parts[k], k) for k in (1, 2, 3)]
-    terms = sum(
-        jnp.dot(part, block, preferred_element_type=F32)
-        for part, block in zip(parts, out_blocks)
-    )
-    own_patches = lax.dynamic_slice_in_dim(patches, tp * rows, rows, 0)
-    attended = own_patches.astype(F32) + terms
-    moment = jnp.mean(attended * attended, axis=1, keepdims=True)
-    normed = (attended * lax.rsqrt(moment + EPSILON) * merge_gain).astype(BF)
-    merged = normed.reshape(rows // MERGE, MERGE * normed.shape[1])
-
-    n = merged.shape[0]
-    far = jnp.concatenate([shift_y(merged[: n // 2], 2), shift_y(merged[n // 2 :], -2)], axis=0)
-    ring = [merged, shift_y(merged, 1), shift_y(merged, -1), far]
+    merged, top, bottom = project_and_norm(tp, parts, out_blocks, patches, merge_gain)
+    table, merged, top, bottom = lax.optimization_barrier((table, merged, top, bottom))
+    table = lax.all_to_all(table, SEC, split_axis=0, concat_axis=0, tiled=True)
+
+    ring = [
+        (0, 0, merged),
+        (1, 0, shift_y(merged, 1)),
+        (-1, 0, shift_y(merged, -1)),
+        (2, 0, shift_y(top, 2)),
+        (2, top.shape[0], shift_y(bottom, -2)),
+    ]
     blocks = []
     ids = []
-    for d, block in zip((0, 1, -1, 2), ring):
+    for d, first, block in ring:
         blocks += [block, swap_core(block)]
-        origin = (y - d + 4) % 4
-        ids += [origin * 128 + core * 64, origin * 128 + (1 - core) * 64]
-    row_ids = (jnp.stack(ids)[:, None] + jnp.arange(n)[None, :]).reshape(-1)
+        origin = (y - d + 4) % 4 * 128 + first
+        ids += [origin + c * 64 + jnp.arange(block.shape[0]) for c in (core, 1 - core)]
+    row_ids = jnp.concatenate(ids)
 
     wanted = table.reshape(32, 2, 16) - 1
     wanted = jnp.where(wanted >= 0, wanted + jnp.arange(2)[None, :, None] * 256, -1).reshape(-1)

time: 196 us -> 191 us (0.974)
  waiting for transfers between devices: 46.2 us -> 27 us
  starting transfers between devices: 25.4 us -> 42.8 us
  matrix products: 15 us -> 2.13 us
  Pallas kernels: 24 us -> 30.8 us
  local copies, waits for them, and re-layouts: 19.1 us -> 22.7 us
    ppermute x4, waiting for transfers between devices: 22.2 us -> 1.51 us  [shift_y(): lax.ppermute(block, ('yh', 'yl'), [(i, (i + d) % 4) for i in range(4)])]
    ppermute x4 -> x5, starting transfers between devices: 2.08 us -> 21.7 us  [swap_core(): return lax.ppermute(block, 'c', [(0, 1), (1, 0)])]
    ppermute x6, waiting for transfers between devices: 6.11 us -> 25.5 us  [swap_tp(): return lax.ppermute(block, TP, [(i, i ^ k) for i in range(4)])]
    all_to_all x1, waiting for transfers between devices: 15.8 us -> 0.01 us  [on_device(): table = lax.all_to_all(table, SEC, split_axis=0, concat_axis=0, tiled=True)]
    dot_general x5 -> x0, matrix products: 12.8 us -> none  [the longest x4 7.2 us: on_device(): jnp.dot(part, block, preferred_element_type=F32)]
    unnamed x23 -> x45, local copies, waits for them, and re-layouts: 6.31 us -> 18.4 us
    pallas_call x1 -> x3, Pallas kernels: 14.2 us -> 20.9 us  [the longest x1 11.8 us: merge_and_select(): pl.pallas_call(merge_kernel, grid=(depth // tile,), out_shape=jax.ShapeDt...]
    convert_element_type x1 -> x0, local copies, waits for them, and re-layouts: 4.16 us -> none  [on_device(): projected = projected.astype(BF)]
  transfers between devices with their start and end apart: 17 -> 18, of which waited for: 8 -> 5; matrix products, arithmetic and copies ran while one was open for 14% -> 5% of each run, Pallas kernels for 5% -> 10%
where the time goes in v3:
time: 191 us; the launch traced here: 190 us
  blocking collectives  43.7 us (23%)
  starting transfers between devices  42.8 us (22%)
  Pallas kernels  30.8 us (16%)
  waiting for transfers between devices  27 us (14%)
  local copies, waits for them, and re-layouts  22.7 us (12%)
  between operations  13.6 us (7%)
  other arithmetic  7.35 us (4%)
  matrix products  2.13 us (1%)
    all_to_all x1, blocking collectives, on_device(): lax.all_to_all(outgoing, SEC, split_axis=0, concat_axis=0, tiled=True)  36.9 us
    ppermute x6, waiting for transfers between devices, swap_tp(): return lax.ppermute(block, TP, [(i, i ^ k) for i in range(4)])  25.5 us
    ppermute x5, starting transfers between devices, swap_core(): return lax.ppermute(block, 'c', [(0, 1), (1, 0)])  21.7 us
    unnamed x45, local copies, waits for them, and re-layouts  18.4 us
    pallas_call x1, Pallas kernels, merge_and_select(): pl.pallas_call(merge_kernel, grid=(depth // tile,), out_shape=jax.ShapeDt...  11.8 us
    pallas_call x1, Pallas kernels, vision_context(): pl.pallas_call(attention_kernel, out_shape=jax.ShapeDtypeStruct((row_coun...  9.84 us
    all_to_all x1, starting transfers between devices, on_device(): table = lax.all_to_all(table, SEC, split_axis=0, concat_axis=0, tiled=True)  8.15 us
    psum x1, blocking collectives, on_device(): squares = lax.psum(jnp.sum(widened * widened, axis=1), TP)  6.79 us
  transfers between devices with their start and end apart: 18, of which 5 were waited for; matrix products, arithmetic and copies ran while one was open for 5% of the time, Pallas kernels for 10%

profile of v3, /device:TPU:1, one launch (start us, length us, event | category | flops | bytes accessed | tf_op | source)
XLA Modules:
  0.0 190.2 jit_solution(266249124407098017)
XLA Ops:
  6.5 1.0 constant_dynamic-slice_fusion.4
  7.5 3.8 %collective-permute-start = (bf16[160,1024]{1,0:T(8,128)(2,1)S(1)}, bf16[160,1024]{1,0:T(8,128)(2,1)}, u32[]{:S(2)}, u32[]{:S(2)}) collective-permute-start(bf16[160,1024]{1,0:T(8,128)(2,1)S(1)} %constant_dynamic-slice_fusion.4), channel_id=1, source_target_pairs={{0,4},{4,0},{1,5},{5,1},{2,6},{6,2},{3,7},{7,3},{8,12},{12,8},{9,1... | collective-permute-start | bytes 983048 | tf_op jit(solution)/shard_map/ppermute | solution.py:232
  11.4 4.0 %copy.13.weight = bf16[3,1280,320]{2,1,0:T(8,128)(2,1)S(1)} copy(bf16[3,1280,320]{1,2,0:T(8,128)(2,1)} %param.11) | data formatting | bytes 4915200 | tf_op args[2]
  15.4 1.7 copy-done
  17.1 4.6 %project_qkv.1.projected = bf16[3,1024,320]{2,1,0:T(8,128)(2,1)S(1)} custom-call(bf16[1024,1280]{1,0:T(8,128)(2,1)S(1)} %copy-done, bf16[3,1280,320]{2,1,0:T(8,128)(2,1)S(1)} %copy.13.weight), custom_call_target="tpu_custom_call" | custom-call | flops 2516582400 | bytes 7045120 | tf_op jit(solution)/shard_map/project_qkv/pallas_call | solution.py:79
  21.7 1.5 copy-done.13
  23.3 1.2 broadcast_select_fusion.1
  25.9 1.2 collective-permute-start.4
  27.1 1.0 collective-permute-start.6
  28.3 1.0 broadcast_in_dim_reshape.9.row_ids
  29.6 1.0 copy-done.4
  30.6 1.7 copy-done.14
  32.3 9.8 %vision_attention.1 = bf16[1024,320]{1,0:T(8,128)(2,1)S(1)} custom-call(s32[1024,1]{1,0:T(8,128)S(1)} %copy-done.4, s32[1,1024]{1,0:T(1,128)S(1)} %broadcast_in_dim_reshape.8.column_ids, bf16[3,1024,320]{2,1,0:T(8,128)(2,1)S(1)} %copy-done.14), custom_call_target="tpu_custom_call" | custom-call | flops 4294967296 | bytes 2621440 | tf_op jit(solution)/shard_map/vision_attention/pallas_call | solution.py:53
  43.8 1.1 collective-permute-start.2
  45.0 24.1 %collective-permute-done.3.refs_4_ = bf16[256,320]{1,0:T(8,128)(2,1)S(1)} collective-permute-done((bf16[256,320]{1,0:T(8,128)(2,1)S(1)}, bf16[256,320]{1,0:T(8,128)(2,1)S(1)}, u32[]{:S(2)}, u32[]{:S(2)}) %collective-permute-start.3) | collective-permute-done | bytes 163872 | tf_op jit(solution)/shard_map/ppermute | solution.py:202
  70.3 1.2 collective-permute-done.1.refs_2_
  73.4 4.5 %project_and_norm.1 = (bf16[64,5120]{1,0:T(8,128)(2,1)}, bf16[32,5120]{1,0:T(8,128)(2,1)S(1)}, bf16[32,5120]{1,0:T(8,128)(2,1)S(1)}) custom-call(s32[1]{0:T(128)} %bitcast.2.refs_0_, bf16[256,320]{1,0:T(8,128)(2,1)S(1)} %copy-done.3, bf16[256,320]{1,0:T(8,128)(2,1)} %collective-permute-done.1.refs_2_, bf16[256,320]{1,0:T(8,128)(2,1)} %collective-permute-done.2.refs_3_, ...), custom_call_target="tpu_custom_call" | custom-call | flops 838860800 | bytes 5242880 | tf_op jit(solution)/shard_map/project_and_norm/pallas_call | solution.py:124
  82.4 2.2 %collective-permute-start.14 = (bf16[32,5120]{1,0:T(8,128)(2,1)}, bf16[32,5120]{1,0:T(8,128)(2,1)}, u32[]{:S(2)}, u32[]{:S(2)}) collective-permute-start(bf16[32,5120]{1,0:T(8,128)(2,1)} %copy-done.7), channel_id=1, source_target_pairs={{0,4},{2,6},{4,0},{6,2},{1,5},{3,7},{5,1},{7,3},{8,12},{10,14},{12... | collective-permute-start | bytes 983048 | tf_op jit(solution)/shard_map/ppermute | solution.py:206
  84.6 1.8 collective-permute-start.7
  86.4 8.2 %all-to-all-start = ((s32[32,1,32]{2,1,0:T(1,128)}), s32[32,1,32]{2,1,0:T(1,128)S(1)}, u32[]{:S(2)}, u32[]{:S(2)}) async-start(s32[32,1,32]{2,1,0:T(1,128)} %bitcast.4), calls=%async_computation | async-start | bytes 32768 | tf_op jit(solution)/shard_map/all_to_all | solution.py:264
  94.5 1.4 collective-permute-done.10.refs_4_
  95.9 2.6 %collective-permute-start.11 = (bf16[64,5120]{1,0:T(8,128)(2,1)S(1)}, bf16[64,5120]{1,0:T(8,128)(2,1)S(1)}, u32[]{:S(2)}, u32[]{:S(2)}) collective-permute-start(bf16[64,5120]{1,0:T(8,128)(2,1)S(1)} %collective-permute-done.10.refs_4_), channel_id=1, source_target_pairs={{0,1},{1,0},{2,3},{3,2},{4,5},{5,4},{6,7},{7,6},{8,9},{9,8},{10,11... | collective-permute-start | bytes 1966088 | tf_op jit(solution)/shard_map/ppermute | solution.py:210
  98.6 15.0 %collective-permute-start.9 = (bf16[64,5120]{1,0:T(8,128)(2,1)S(1)}, bf16[64,5120]{1,0:T(8,128)(2,1)S(1)}, u32[]{:S(2)}, u32[]{:S(2)}) collective-permute-start(bf16[64,5120]{1,0:T(8,128)(2,1)S(1)} %collective-permute-done.8.refs_2_), channel_id=1, source_target_pairs={{0,1},{1,0},{2,3},{3,2},{4,5},{5,4},{6,7},{7,6},{8,9},{9,8},{10,11... | collective-permute-start | bytes 1966088 | tf_op jit(solution)/shard_map/ppermute | solution.py:210
  114.1 1.9 %collective-permute-start.13 = (bf16[32,5120]{1,0:T(8,128)(2,1)}, bf16[32,5120]{1,0:T(8,128)(2,1)S(1)}, u32[]{:S(2)}, u32[]{:S(2)}) collective-permute-start(bf16[32,5120]{1,0:T(8,128)(2,1)} %collective-permute-done.12.refs_6_), channel_id=1, source_target_pairs={{0,1},{1,0},{2,3},{3,2},{4,5},{5,4},{6,7},{7,6},{8,9},{9,8},{10,11... | collective-permute-start | bytes 983048 | tf_op jit(solution)/shard_map/ppermute | solution.py:210
  116.3 1.2 compare_convert_fusion.refs_11_
  119.0 1.0 copy-done.10
  120.0 1.0 copy-done.12
  121.0 11.8 %merge_rows.1 = bf16[1024,1024]{1,0:T(8,128)(2,1)} custom-call(bf16[64,5120]{1,0:T(8,128)(2,1)} %get-tuple-element.22.refs_0_, bf16[64,5120]{1,0:T(8,128)(2,1)S(1)} %collective-permute-done.7.refs_1_, bf16[64,5120]{1,0:T(8,128)(2,1)S(1)} %collective-permute-done.8.refs_2_, bf16[64,5120]{1,0:T(8,128)(2,1)S(1)} %collective-permute-done.9.refs_3_, ...), custom_call_target="tpu_custom_call" | custom-call | flops 6442450944 | bytes 17825792 | tf_op jit(solution)/shard_map/merge_rows/pallas_call | solution.py:180
  132.8 36.9 %all_to_all.18 = bf16[32,32,1024]{2,1,0:T(8,128)(2,1)S(1)} all-to-all(bf16[32,32,1024]{2,1,0:T(8,128)(2,1)} %bitcast.13), channel_id=1, replica_groups=mesh['z'=4,'x'=4,'yh'=2,'yl'=2,'c'=2] {'z','x','yh'}, dimensions={0} | all-to-all | bytes 4194304 | tf_op jit(solution)/shard_map/all_to_all | solution.py:285
  171.6 1.0 copy-done.16
  173.4 6.8 %psum.7 = f32[512]{0:T(512)S(1)} all-reduce(f32[512]{0:T(512)S(1)} %fusion), channel_id=1, replica_groups=mesh['z'=4,'x'=4,'yh'=2,'yl'=2,'c'=2] {'yl','c'}, use_global_device_ids=true, to_apply=%region_2.3 | all-reduce | flops 512 | bytes 4096 | tf_op jit(solution)/shard_map/psum | solution.py:296
  180.2 3.1 %fusion.2 = bf16[512,2048]{1,0:T(8,128)(2,1)} fusion(f32[2048]{0:T(1024)S(1)} %copy-done.18, f32[512]{0:T(512)S(1)} %add_rsqrt_fusion, bf16[512,2048]{1,0:T(8,128)(2,1)S(1)} %copy-done.15, bf16[512,1024]{1,0:T(8,128)(2,1)} %copy-done.16, bf16[512,1024]{1,0:T(8,128)(2,1)S(1)} %convolution_convert_fusion.1, pred[512]{0:T(512)(128)(4,1)S(1)} %get-tuple-element.28), kind=kLoop, calls=%fused_computation.4 | loop fusion | flops 9437184 | bytes 6302208 | tf_op jit(solution)/shard_map/convert_element_type | solution.py:299
  (91 shorter events, 16.1 us)
Async XLA Ops:
  6.5 112.5 %all-gather.2.cloned.1.call-start = ((), (), s32[]{:S(2)}) async-start(), calls=%async_computation.2 | async-start | bytes 11141120 | tf_op jit(solution)/shard_map/all_gather | solution.py:254
  7.5 15.7 %collective-permute-start = (bf16[160,1024]{1,0:T(8,128)(2,1)S(1)}, bf16[160,1024]{1,0:T(8,128)(2,1)}, u32[]{:S(2)}, u32[]{:S(2)}) collective-permute-start(bf16[160,1024]{1,0:T(8,128)(2,1)S(1)} %constant_dynamic-slice_fusion.4), channel_id=1, source_target_pairs={{0,4},{4,0},{1,5},{5,1},{2,6},{6,2},{3,7},{7,3},{8,12},{12,8},{9,1... | collective-permute-start | bytes 983048 | tf_op jit(solution)/shard_map/ppermute | solution.py:232
  15.4 1.7 copy-start
  17.1 6.1 %copy-start.17 = (bf16[160,2048]{1,0:T(8,128)(2,1)S(1)}, bf16[160,2048]{1,0:T(8,128)(2,1)}, u32[]{:S(2)}) copy-start(bf16[160,2048]{1,0:T(8,128)(2,1)} %param.14) | copy-start | bytes 1966084
  21.7 1.5 copy-start.13
  23.2 2.1 %copy-start.2 = (bf16[320,1280]{1,0:T(8,128)(2,1)S(1)}, bf16[320,1280]{1,0:T(8,128)(2,1)}, u32[]{:S(2)}) copy-start(bf16[320,1280]{1,0:T(8,128)(2,1)} %refs_5_.1) | copy-start | bytes 2457604
  23.2 4.8 %copy-start.21 = (s32[1,256]{1,0:T(1,128)S(1)}, s32[1,256]{1,0:T(1,128)}, u32[]{:S(2)}) copy-start(s32[1,256]{1,0:T(1,128)} %param.10) | copy-start | bytes 3076
  23.2 6.0 %copy-start.19 = (s32[512]{0:T(512)S(1)}, s32[512]{0:T(512)}, u32[]{:S(2)}) copy-start(s32[512]{0:T(512)} %param.16) | copy-start | bytes 6148
  25.4 46.1 %collective-permute-start.5 = (bf16[320,1280]{1,0:T(8,128)(2,1)S(1)}, bf16[320,1280]{1,0:T(8,128)(2,1)}, u32[]{:S(2)}, u32[]{:S(2)}) collective-permute-start(bf16[320,1280]{1,0:T(8,128)(2,1)S(1)} %copy-done.2), channel_id=1, source_target_pairs={{0,2},{1,3},{2,0},{3,1},{4,6},{5,7},{6,4},{7,5},{8,10},{9,11},{10,... | collective-permute-start | bytes 2457608 | tf_op jit(solution)/shard_map/ppermute | solution.py:202
  25.9 45.7 %collective-permute-start.4 = (bf16[320,1280]{1,0:T(8,128)(2,1)S(1)}, bf16[320,1280]{1,0:T(8,128)(2,1)}, u32[]{:S(2)}, u32[]{:S(2)}) collective-permute-start(bf16[320,1280]{1,0:T(8,128)(2,1)S(1)} %copy-done.2), channel_id=1, source_target_pairs={{0,1},{1,0},{2,3},{3,2},{4,5},{5,4},{6,7},{7,6},{8,9},{9,8},{10,11... | collective-permute-start | bytes 2457608 | tf_op jit(solution)/shard_map/ppermute | solution.py:202
  27.1 44.4 %collective-permute-start.6 = (bf16[320,1280]{1,0:T(8,128)(2,1)S(1)}, bf16[320,1280]{1,0:T(8,128)(2,1)}, u32[]{:S(2)}, u32[]{:S(2)}) collective-permute-start(bf16[320,1280]{1,0:T(8,128)(2,1)S(1)} %copy-done.2), channel_id=1, source_target_pairs={{0,3},{1,2},{2,1},{3,0},{4,7},{5,6},{6,5},{7,4},{8,11},{9,10},{10,... | collective-permute-start | bytes 2457608 | tf_op jit(solution)/shard_map/ppermute | solution.py:202
  29.6 1.0 copy-start.4
  30.6 1.7 copy-start.14
  32.3 37.8 %copy-start.20 = (f32[1280]{0:T(1024)S(1)}, f32[1280]{0:T(1024)}, u32[]{:S(2)}) copy-start(f32[1280]{0:T(1024)} %param.13) | copy-start | bytes 15364
  32.3 39.3 %copy-start.1 = (bf16[1024,1280]{1,0:T(8,128)(2,1)S(1)}, bf16[1024,1280]{1,0:T(8,128)(2,1)}, u32[]{:S(2)}) copy-start(bf16[1024,1280]{1,0:T(8,128)(2,1)} %refs_9_.1) | copy-start | bytes 7864324
  43.0 26.1 %collective-permute-start.3 = (bf16[256,320]{1,0:T(8,128)(2,1)S(1)}, bf16[256,320]{1,0:T(8,128)(2,1)S(1)}, u32[]{:S(2)}, u32[]{:S(2)}) collective-permute-start(bf16[256,320]{1,0:T(8,128)(2,1)S(1)} %get-tuple-element.33), channel_id=1, source_target_pairs={{0,3},{1,2},{2,1},{3,0},{4,7},{5,6},{6,5},{7,4},{8,11},{9,10},{10,... | collective-permute-start | bytes 491528 | tf_op jit(solution)/shard_map/ppermute | solution.py:202
  43.8 26.5 %collective-permute-start.2 = (bf16[256,320]{1,0:T(8,128)(2,1)}, bf16[256,320]{1,0:T(8,128)(2,1)}, u32[]{:S(2)}, u32[]{:S(2)}) collective-permute-start(bf16[256,320]{1,0:T(8,128)(2,1)} %get-tuple-element.34), channel_id=1, source_target_pairs={{0,2},{1,3},{2,0},{3,1},{4,6},{5,7},{6,4},{7,5},{8,10},{9,11},{10,... | collective-permute-start | bytes 491528 | tf_op jit(solution)/shard_map/ppermute | solution.py:202
  69.7 1.8 collective-permute-start.1
  80.0 15.9 %collective-permute-start.10 = (bf16[64,5120]{1,0:T(8,128)(2,1)}, bf16[64,5120]{1,0:T(8,128)(2,1)S(1)}, u32[]{:S(2)}, u32[]{:S(2)}) collective-permute-start(bf16[64,5120]{1,0:T(8,128)(2,1)} %get-tuple-element.22.refs_0_), channel_id=1, source_target_pairs={{0,6},{2,0},{4,2},{6,4},{1,7},{3,1},{5,3},{7,5},{8,14},{10,8},{12,... | collective-permute-start | bytes 1966088 | tf_op jit(solution)/shard_map/ppermute | solution.py:206
  80.9 17.8 %collective-permute-start.8 = (bf16[64,5120]{1,0:T(8,128)(2,1)}, bf16[64,5120]{1,0:T(8,128)(2,1)S(1)}, u32[]{:S(2)}, u32[]{:S(2)}) collective-permute-start(bf16[64,5120]{1,0:T(8,128)(2,1)} %get-tuple-element.22.refs_0_), channel_id=1, source_target_pairs={{0,2},{2,4},{4,6},{6,0},{1,3},{3,5},{5,7},{7,1},{8,10},{10,12},{12... | collective-permute-start | bytes 1966088 | tf_op jit(solution)/shard_map/ppermute | solution.py:206
  81.5 32.6 %collective-permute-start.12 = (bf16[32,5120]{1,0:T(8,128)(2,1)}, bf16[32,5120]{1,0:T(8,128)(2,1)}, u32[]{:S(2)}, u32[]{:S(2)}) collective-permute-start(bf16[32,5120]{1,0:T(8,128)(2,1)} %copy-done.8), channel_id=1, source_target_pairs={{0,4},{2,6},{4,0},{6,2},{1,5},{3,7},{5,1},{7,3},{8,12},{10,14},{12... | collective-permute-start | bytes 983048 | tf_op jit(solution)/shard_map/ppermute | solution.py:206
  82.4 33.7 %collective-permute-start.14 = (bf16[32,5120]{1,0:T(8,128)(2,1)}, bf16[32,5120]{1,0:T(8,128)(2,1)}, u32[]{:S(2)}, u32[]{:S(2)}) collective-permute-start(bf16[32,5120]{1,0:T(8,128)(2,1)} %copy-done.7), channel_id=1, source_target_pairs={{0,4},{2,6},{4,0},{6,2},{1,5},{3,7},{5,1},{7,3},{8,12},{10,14},{12... | collective-permute-start | bytes 983048 | tf_op jit(solution)/shard_map/ppermute | solution.py:206
  84.6 34.4 %collective-permute-start.7 = (bf16[64,5120]{1,0:T(8,128)(2,1)}, bf16[64,5120]{1,0:T(8,128)(2,1)S(1)}, u32[]{:S(2)}, u32[]{:S(2)}) collective-permute-start(bf16[64,5120]{1,0:T(8,128)(2,1)} %get-tuple-element.22.refs_0_), channel_id=1, source_target_pairs={{0,1},{1,0},{2,3},{3,2},{4,5},{5,4},{6,7},{7,6},{8,9},{9,8},{10,11... | collective-permute-start | bytes 1966088 | tf_op jit(solution)/shard_map/ppermute | solution.py:210
  86.4 27.6 %all-to-all-start = ((s32[32,1,32]{2,1,0:T(1,128)}), s32[32,1,32]{2,1,0:T(1,128)S(1)}, u32[]{:S(2)}, u32[]{:S(2)}) async-start(s32[32,1,32]{2,1,0:T(1,128)} %bitcast.4), calls=%async_computation | async-start | bytes 32768 | tf_op jit(solution)/shard_map/all_to_all | solution.py:264
  95.9 23.1 %collective-permute-start.11 = (bf16[64,5120]{1,0:T(8,128)(2,1)S(1)}, bf16[64,5120]{1,0:T(8,128)(2,1)S(1)}, u32[]{:S(2)}, u32[]{:S(2)}) collective-permute-start(bf16[64,5120]{1,0:T(8,128)(2,1)S(1)} %collective-permute-done.10.refs_4_), channel_id=1, source_target_pairs={{0,1},{1,0},{2,3},{3,2},{4,5},{5,4},{6,7},{7,6},{8,9},{9,8},{10,11... | collective-permute-start | bytes 1966088 | tf_op jit(solution)/shard_map/ppermute | solution.py:210
  98.6 20.3 %collective-permute-start.9 = (bf16[64,5120]{1,0:T(8,128)(2,1)S(1)}, bf16[64,5120]{1,0:T(8,128)(2,1)S(1)}, u32[]{:S(2)}, u32[]{:S(2)}) collective-permute-start(bf16[64,5120]{1,0:T(8,128)(2,1)S(1)} %collective-permute-done.8.refs_2_), channel_id=1, source_target_pairs={{0,1},{1,0},{2,3},{3,2},{4,5},{5,4},{6,7},{7,6},{8,9},{9,8},{10,11... | collective-permute-start | bytes 1966088 | tf_op jit(solution)/shard_map/ppermute | solution.py:210
  114.1 3.4 %collective-permute-start.13 = (bf16[32,5120]{1,0:T(8,128)(2,1)}, bf16[32,5120]{1,0:T(8,128)(2,1)S(1)}, u32[]{:S(2)}, u32[]{:S(2)}) collective-permute-start(bf16[32,5120]{1,0:T(8,128)(2,1)} %collective-permute-done.12.refs_6_), channel_id=1, source_target_pairs={{0,1},{1,0},{2,3},{3,2},{4,5},{5,4},{6,7},{7,6},{8,9},{9,8},{10,11... | collective-permute-start | bytes 983048 | tf_op jit(solution)/shard_map/ppermute | solution.py:210
  116.0 2.2 %collective-permute-start.15 = (bf16[32,5120]{1,0:T(8,128)(2,1)}, bf16[32,5120]{1,0:T(8,128)(2,1)S(1)}, u32[]{:S(2)}, u32[]{:S(2)}) collective-permute-start(bf16[32,5120]{1,0:T(8,128)(2,1)} %collective-permute-done.14.refs_8_), channel_id=1, source_target_pairs={{0,1},{1,0},{2,3},{3,2},{4,5},{5,4},{6,7},{7,6},{8,9},{9,8},{10,11... | collective-permute-start | bytes 983048 | tf_op jit(solution)/shard_map/ppermute | solution.py:210
  119.0 1.0 copy-start.10
  170.8 1.8 copy-start.15
  171.6 1.0 copy-start.16
  172.6 7.6 %copy-start.18 = (f32[2048]{0:T(1024)S(1)}, f32[2048]{0:T(1024)}, u32[]{:S(2)}) copy-start(f32[2048]{0:T(1024)} %param.17) | copy-start | bytes 24580
  (8 other events, 6.4 us)
Sparse Core Ops, SparseCore 0:
  25.5 81.1 all-gather.1

commit v4 on v3

--- a/solution.py
+++ b/solution.py
@@ -1,3 +1,5 @@
+import functools
+
 import jax
 import jax.numpy as jnp
 from jax import lax
@@ -59,7 +61,7 @@
             pltpu.VMEM((heads, row_count, HEAD_DIM), BF),
             pltpu.VMEM((heads, row_count, 128), BF),
         ],
-        compiler_params=pltpu.CompilerParams(vmem_limit_bytes=40 * 2**20),
+        compiler_params=pltpu.CompilerParams(vmem_limit_bytes=24 * 2**20),
         cost_estimate=pl.CostEstimate(
             flops=4 * heads * row_count * row_count * 256,
             bytes_accessed=8 * row_count * width,
@@ -70,22 +72,24 @@
 
 
 def project_kernel(patches, weight, projected):
-    projected[0] = jnp.dot(patches[...], weight[0], preferred_element_type=F32).astype(BF)
+    projected[0] = lax.dot_general(
+        patches[...], weight[0], (((1,), (1,)), ((), ())), preferred_element_type=F32
+    ).astype(BF)
 
 
 def project(patches, weight):
     rows, depth = patches.shape
-    count, _, width = weight.shape
+    count, width, _ = weight.shape
     return pl.pallas_call(
         project_kernel,
         grid=(count,),
         out_shape=jax.ShapeDtypeStruct((count, rows, width), BF),
         in_specs=[
             pl.BlockSpec((rows, depth), lambda i: (0, 0), pipeline_mode=pl.Buffered(1)),
-            pl.BlockSpec((1, depth, width), lambda i: (i, 0, 0)),
+            pl.BlockSpec((1, width, depth), lambda i: (i, 0, 0)),
         ],
         out_specs=pl.BlockSpec((1, rows, width), lambda i: (i, 0, 0)),
-        compiler_params=pltpu.CompilerParams(vmem_limit_bytes=32 * 2**20),
+        compiler_params=pltpu.CompilerParams(vmem_limit_bytes=14 * 2**20),
         cost_estimate=pl.CostEstimate(
             flops=2 * rows * depth * width * count,
             bytes_accessed=2 * (rows * depth + count * width * (depth + rows)),
@@ -141,7 +145,7 @@
             jax.ShapeDtypeStruct((count // 2, MERGE * width), BF),
             jax.ShapeDtypeStruct((count // 2, MERGE * width), BF),
         ],
-        compiler_params=pltpu.CompilerParams(vmem_limit_bytes=32 * 2**20),
+        compiler_params=pltpu.CompilerParams(vmem_limit_bytes=24 * 2**20),
         cost_estimate=pl.CostEstimate(
             flops=8 * rows * depth * width,
             bytes_accessed=8 * depth * (rows + width) + 4 * rows * width,
@@ -188,7 +192,7 @@
         ],
         out_specs=pl.BlockSpec((slots, columns), lambda i: (0, 0)),
         scratch_shapes=[pltpu.VMEM((count, tile), BF), pltpu.VMEM((count, columns), F32)],
-        compiler_params=pltpu.CompilerParams(vmem_limit_bytes=48 * 2**20),
+        compiler_params=pltpu.CompilerParams(vmem_limit_bytes=32 * 2**20),
         cost_estimate=pl.CostEstimate(
             flops=2 * count * (depth + slots) * columns,
             bytes_accessed=2 * (count * depth + depth * columns + slots * columns),
@@ -196,6 +200,130 @@
         ),
         name="merge_rows",
     )(*blocks, weight, send)
+
+
+def pick_kernel(received, pick, usable, text, prompt, squares):
+    arrived = received[...].reshape(pick.shape[1], received.shape[-1])
+    picked = jnp.dot(pick[...], arrived, preferred_element_type=F32)
+    value = jnp.where(usable[...] > 0, picked, text[...].astype(F32))
+    prompt[...] = value.astype(BF)
+    total = jnp.sum(value * value, axis=1, keepdims=True)
+
+    @pl.when(pl.program_id(0) == 0)
+    def _():
+        squares[...] = total
+
+    @pl.when(pl.program_id(0) > 0)
+    def _():
+        squares[...] += total
+
+
+def pick_rows(received, pick, usable, text, offset):
+    planes, halves, rows, part = received.shape
+    count, slots = pick.shape
+    return pl.pallas_call(
+        pick_kernel,
+        grid=(halves,),
+        out_shape=[
+            jax.ShapeDtypeStruct((count, halves * part), BF),
+            jax.ShapeDtypeStruct((count, 1), F32),
+        ],
+        in_specs=[
+            pl.BlockSpec((planes, 1, rows, part), lambda h: (0, h, 0, 0)),
+            pl.BlockSpec((count, slots), lambda h: (0, 0), pipeline_mode=pl.Buffered(1)),
+            pl.BlockSpec((count, 1), lambda h: (0, 0), pipeline_mode=pl.Buffered(1)),
+            pl.BlockSpec((count, part), lambda h: (0, 2 * h + offset)),
+        ],
+        out_specs=[
+            pl.BlockSpec((count, part), lambda h: (0, h)),
+            pl.BlockSpec((count, 1), lambda h: (0, 0)),
+        ],
+        compiler_params=pltpu.CompilerParams(vmem_limit_bytes=14 * 2**20),
+        cost_estimate=pl.CostEstimate(
+            flops=2 * count * slots * halves * part,
+            bytes_accessed=6 * count * halves * part,
+            transcendentals=0,
+        ),
+        name="pick_rows",
+    )(received, pick, usable, text)
+
+
+def finish_kernel(early, late, squares, gain, out, *, width):
+    inverse = lax.rsqrt(squares[...] / width + EPSILON)
+
+    @pl.when(pl.program_id(0) % 2 == 0)
+    def _():
+        out[...] = (early[...].astype(F32) * inverse * gain[...]).astype(BF)
+
+    @pl.when(pl.program_id(0) % 2 == 1)
+    def _():
+        out[...] = (late[...].astype(F32) * inverse * gain[...]).astype(BF)
+
+
+def finish(early, late, squares, gain):
+    count, width = early.shape
+    part = width // 2
+    return pl.pallas_call(
+        functools.partial(finish_kernel, width=8 * width),
+        grid=(4,),
+        out_shape=jax.ShapeDtypeStruct((count, 2 * width), BF),
+        in_specs=[
+            pl.BlockSpec((count, part), lambda j: (0, j // 2)),
+            pl.BlockSpec((count, part), lambda j: (0, j // 2)),
+            pl.BlockSpec((count, 1), lambda j: (0, 0)),
+            pl.BlockSpec((1, part), lambda j: (0, j)),
+        ],
+        out_specs=pl.BlockSpec((count, part), lambda j: (0, j)),
+        compiler_params=pltpu.CompilerParams(vmem_limit_bytes=14 * 2**20),
+        cost_estimate=pl.CostEstimate(
+            flops=6 * count * width, bytes_accessed=8 * count * width, transcendentals=count
+        ),
+        name="finish",
+    )(early, late, squares, gain[None, :])
+
+
+def arrange_kernel(*refs):
+    places, pieces, (whole, sems) = refs[0], refs[1:-2], refs[-2:]
+    rows = whole.shape[0] // places.shape[0]
+    copies = []
+    for piece in pieces:
+        for first in range(0, piece.shape[0], rows):
+            index = len(copies)
+            place = pl.multiple_of(places[index] * rows, rows)
+            copy = pltpu.make_async_copy(
+                piece.at[pl.ds(first, rows)], whole.at[pl.ds(place, rows)], sems.at[index]
+            )
+            copy.start()
+            copies.append(copy)
+    for copy in copies:
+        copy.wait()
+
+
+def arrange(places, pieces):
+    rows = sum(piece.shape[0] for piece in pieces)
+    columns = pieces[0].shape[1]
+    return pl.pallas_call(
+        arrange_kernel,
+        out_shape=jax.ShapeDtypeStruct((rows, columns), BF),
+        in_specs=[pl.BlockSpec(memory_space=pltpu.SMEM)]
+        + [pl.BlockSpec(memory_space=pl.ANY)] * len(pieces),
+        out_specs=pl.BlockSpec(memory_space=pl.ANY),
+        scratch_shapes=[pltpu.SemaphoreType.DMA((places.shape[0],))],
+        cost_estimate=pl.CostEstimate(
+            flops=0, bytes_accessed=4 * rows * columns, transcendentals=0
+        ),
+        name="arrange_weight",
+    )(places, *pieces)
+
+
+def shift(block, axis, d):
+    return lax.ppermute(block, axis, [(i, (i + d) % 4) for i in range(4)])
+
+
+def ring(block, axis):
+    n = block.shape[0] // 2
+    before, after = shift(block, axis, 1), shift(block, axis, -1)
+    return [block, before, after, shift(before[:n], axis, 1), shift(after[n:], axis, -1)]
 
 
 def swap_tp(block, k):
@@ -227,16 +355,37 @@
     core = lax.axis_index("c")
 
     half = merge_weight.shape[1] // 2
+    part = half // 2
     own = lax.dynamic_slice_in_dim(merge_weight, yh * half, half, 1)
     other = lax.dynamic_slice_in_dim(merge_weight, (1 - yh) * half, half, 1)
-    arrived = lax.ppermute(other, "yh", [(0, 1), (1, 0)])
-    projected = project(patches, qkv_weight)
-    arrived, projected = lax.optimization_barrier((arrived, projected))
-    both = jnp.concatenate(
-        [jnp.where(yh == 0, own, arrived), jnp.where(yh == 0, arrived, own)], axis=0
-    )
-
-    out_blocks = [out_weight] + [swap_tp(out_weight, k) for k in (1, 2, 3)]
+    swap = lambda block: lax.ppermute(block, "yh", [(0, 1), (1, 0)])
+    arrived = swap(other[:, :part])
+    first_own = own[:, part:]
+    first_other = swap(other[:, part:])
+    is_own = (jnp.arange(2) == yh)[:, None, None]
+    both = jnp.where(is_own, own[None, :, :part], arrived[None]).reshape(-1, part)
+    weight = lax.all_gather(both, ("z", "x"), axis=0, tiled=True)
+    own_z = ring(first_own, "z")
+    other_x = ring(first_other, "x")
+    own_zx = ring(jnp.concatenate(own_z, axis=0), "x")
+    other_xz = ring(jnp.concatenate(other_x, axis=0), "z")
+    near = jnp.array([0, -1, 1, 2])
+    z_of = (lax.axis_index("z") + near) % 4
+    x_of = (lax.axis_index("x") + near) % 4
+    places = jnp.concatenate(
+        [
+            ((z_of[None, :] * 4 + x_of[:, None]) * 2 + yh).reshape(-1),
+            ((z_of[:, None] * 4 + x_of[None, :]) * 2 + 1 - yh).reshape(-1),
+        ]
+    ).astype(jnp.int32)
+    first_weight = arrange(places, own_zx + other_xz)
+
+    out_weight, arrived = lax.optimization_barrier((out_weight, arrived))
+    out_far = lax.ppermute(out_weight, "yl", [(0, 1), (1, 0)])
+    out_blocks = [out_weight, swap_core(out_weight), out_far, swap_core(out_far)]
+
+    projected = project(patches, jnp.swapaxes(qkv_weight, 1, 2))
+    projected, both = lax.optimization_barrier((projected, both))
 
     prompt_rows = image_refs.shape[0]
     usable = image_refs >= 0
@@ -250,9 +399,6 @@
     names = jnp.where(usable, image_refs % 256 + 1, 0).astype(BF)
     table = jnp.dot(names[None, :], pick, preferred_element_type=F32).astype(jnp.int32)
     table = jnp.broadcast_to(table.reshape(16, 1, 32), (16, 2, 32)).reshape(32, 32)
-    both, projected = lax.optimization_barrier((both, projected))
-    weight = lax.all_gather(both, ("z", "x"), axis=0, tiled=True)
-
     context = vision_context(projected, image_ids)
     rows = context.shape[0] // 4
     parts = [
@@ -263,7 +409,7 @@
     table, merged, top, bottom = lax.optimization_barrier((table, merged, top, bottom))
     table = lax.all_to_all(table, SEC, split_axis=0, concat_axis=0, tiled=True)
 
-    ring = [
+    near_rows = [
         (0, 0, merged),
         (1, 0, shift_y(merged, 1)),
         (-1, 0, shift_y(merged, -1)),
@@ -272,7 +418,7 @@
     ]
     blocks = []
     ids = []
-    for d, first, block in ring:
+    for d, first, block in near_rows:
         blocks += [block, swap_core(block)]
         origin = (y - d + 4) % 4 * 128 + first
         ids += [origin + c * 64 + jnp.arange(block.shape[0]) for c in (core, 1 - core)]
@@ -281,22 +427,19 @@
     wanted = table.reshape(32, 2, 16) - 1
     wanted = jnp.where(wanted >= 0, wanted + jnp.arange(2)[None, :, None] * 256, -1).reshape(-1)
     send = (wanted[:, None] == row_ids[None, :]).astype(BF)
-    outgoing = merge_and_select(blocks, weight, send)
-    received = lax.all_to_all(outgoing, SEC, split_axis=0, concat_axis=0, tiled=True)
-    received = received.reshape(16, 2, 32, half)
-    picked = jnp.concatenate(
-        [
-            jnp.dot(pick, received[:, h].reshape(512, half), preferred_element_type=F32).astype(BF)
-            for h in range(2)
-        ],
-        axis=1,
-    )
-    prompt = jnp.where(usable[:, None], picked, text_rows)
-    widened = prompt.astype(F32)
-    squares = lax.psum(jnp.sum(widened * widened, axis=1), TP)
-    total_width = widened.shape[1] * 4
-    inverse = lax.rsqrt(squares / total_width + EPSILON)
-    return (widened * inverse[:, None] * llm_gain[None, :]).astype(BF)
+
+    def route(weight):
+        outgoing = merge_and_select(blocks, weight, send)
+        received = lax.all_to_all(outgoing, SEC, split_axis=0, concat_axis=0, tiled=True)
+        return received.reshape(16, 2, 32, -1)
+
+    usable = usable.astype(jnp.int32)[:, None]
+    late, late_squares = pick_rows(route(first_weight), pick, usable, text_rows, 1)
+    early, early_squares = pick_rows(route(weight), pick, usable, text_rows, 0)
+    squares = early_squares + late_squares
+    flat = squares.reshape(4, -1)
+    total = flat + swap_tp(flat, 1) + swap_tp(flat, 2) + swap_tp(flat, 3)
+    return finish(early, late, total.reshape(squares.shape), llm_gain)
 
 
 def solution(mesh):

time: 191 us -> 391 us (2.05)
  Pallas kernels: 30.8 us -> 198 us
  blocking collectives: 43.7 us -> 0 us
  starting transfers between devices: 42.8 us -> 72.8 us
  waiting for transfers between devices: 27 us -> 54.8 us
  local copies, waits for them, and re-layouts: 22.7 us -> 47 us
  other arithmetic: 7.35 us -> 2.76 us
    pallas_call x0 -> x4, Pallas kernels: none -> 167 us  [the longest x1 161 us: arrange(): pl.pallas_call(arrange_kernel, out_shape=jax.ShapeDtypeStruct((rows, colu...]
    all_to_all x1 -> x0, blocking collectives: 36.9 us -> none  [on_device(): lax.all_to_all(outgoing, SEC, split_axis=0, concat_axis=0, tiled=True)]
    ppermute x1 -> x19, waiting for transfers between devices: 0.01 us -> 28.7 us  [the longest x16 25.2 us: shift(): return lax.ppermute(block, axis, [(i, (i + d) % 4) for i in range(4)])]
    ppermute x1 -> x19, starting transfers between devices: 3.82 us -> 27.1 us  [the longest x16 20.1 us: shift(): return lax.ppermute(block, axis, [(i, (i + d) % 4) for i in range(4)])]
    ppermute x6, waiting for transfers between devices: 25.5 us -> 5.35 us  [swap_tp(): return lax.ppermute(block, TP, [(i, i ^ k) for i in range(4)])]
    all_to_all x0 -> x2, waiting for transfers between devices: none -> 19.1 us  [route(): lax.all_to_all(outgoing, SEC, split_axis=0, concat_axis=0, tiled=True)]
    unnamed x45 -> x95, local copies, waits for them, and re-layouts: 18.4 us -> 35.6 us
    all_to_all x0 -> x2, starting transfers between devices: none -> 9 us  [route(): lax.all_to_all(outgoing, SEC, split_axis=0, concat_axis=0, tiled=True)]
  transfers between devices with their start and end apart: 18 -> 40, of which waited for: 5 -> 12; matrix products, arithmetic and copies ran while one was open for 5% -> 5% of each run, Pallas kernels for 10% -> 50%
where the time goes in v4:
time: 391 us; the launch traced here: 390 us
  Pallas kernels  198 us (51%)
  starting transfers between devices  72.8 us (19%)
  waiting for transfers between devices  54.8 us (14%)
  local copies, waits for them, and re-layouts  47 us (12%)
  between operations  14 us (4%)
    pallas_call x1, Pallas kernels, arrange(): pl.pallas_call(arrange_kernel, out_shape=jax.ShapeDtypeStruct((rows, colu...  161 us
    unnamed x95, local copies, waits for them, and re-layouts  35.6 us
    ppermute x16, waiting for transfers between devices, shift(): return lax.ppermute(block, axis, [(i, (i + d) % 4) for i in range(4)])  25.2 us
    ppermute x16, starting transfers between devices, shift(): return lax.ppermute(block, axis, [(i, (i + d) % 4) for i in range(4)])  20.1 us
    all_to_all x2, waiting for transfers between devices, route(): lax.all_to_all(outgoing, SEC, split_axis=0, concat_axis=0, tiled=True)  19.1 us
    ppermute x7, starting transfers between devices, swap_core(): return lax.ppermute(block, 'c', [(0, 1), (1, 0)])  17.7 us
    pallas_call x2, Pallas kernels, merge_and_select(): pl.pallas_call(merge_kernel, grid=(depth // tile,), out_shape=jax.ShapeDt...  13.7 us
    ppermute x6, starting transfers between devices, swap_tp(): return lax.ppermute(block, TP, [(i, i ^ k) for i in range(4)])  13.6 us
  transfers between devices with their start and end apart: 40, of which 12 were waited for; matrix products, arithmetic and copies ran while one was open for 5% of the time, Pallas kernels for 50%

profile of v4, /device:TPU:1, one launch (start us, length us, event | category | flops | bytes accessed | tf_op | source)
XLA Modules:
  0.0 389.7 jit_solution(10990228902363023900)
XLA Ops:
  6.5 2.1 constant_dynamic-slice_fusion.6
  8.7 3.7 collective-permute-start
  12.6 3.5 collective-permute-done
  18.6 2.2 collective-permute-start.17
  20.8 2.9 collective-permute-start.24
  26.2 4.6 %project_qkv.1.projected = bf16[3,1024,320]{2,1,0:T(8,128)(2,1)S(1)} custom-call(bf16[1024,1280]{1,0:T(8,128)(2,1)S(1)} %copy-done.9, bf16[3,320,1280]{2,1,0:T(8,128)(2,1)S(1)} %bitcast.22), custom_call_target="tpu_custom_call" | custom-call | flops 2516582400 | bytes 7045120 | tf_op jit(solution)/shard_map/project_qkv/pallas_call | solution.py:83
  35.3 2.7 collective-permute-start.19
  40.1 9.8 %vision_attention.1 = bf16[1024,320]{1,0:T(8,128)(2,1)S(1)} custom-call(s32[1024,1]{1,0:T(8,128)S(1)} %broadcast_in_dim_reshape.9.row_ids, s32[1,1024]{1,0:T(1,128)S(1)} %broadcast_in_dim_reshape.8.column_ids, bf16[3,1024,320]{2,1,0:T(8,128)(2,1)S(1)} %copy-done.31), custom_call_target="tpu_custom_call" | custom-call | flops 4294967296 | bytes 2621440 | tf_op jit(solution)/shard_map/vision_attention/pallas_call | solution.py:55
  56.3 3.8 collective-permute-start.1
  62.8 3.6 collective-permute-start.4
  72.0 19.7 %collective-permute-done.27 = bf16[80,512]{1,0:T(8,128)(2,1)S(1)} collective-permute-done((bf16[80,512]{1,0:T(8,128)(2,1)S(1)}, bf16[80,512]{1,0:T(8,128)(2,1)S(1)}, u32[]{:S(2)}, u32[]{:S(2)}) %collective-permute-start.27) | collective-permute-done | bytes 81952 | tf_op jit(solution)/shard_map/ppermute | solution.py:320
  91.7 4.5 %collective-permute-start.3 = (bf16[256,320]{1,0:T(8,128)(2,1)S(1)}, bf16[256,320]{1,0:T(8,128)(2,1)S(1)}, u32[]{:S(2)}, u32[]{:S(2)}) collective-permute-start(bf16[256,320]{1,0:T(8,128)(2,1)S(1)} %get-tuple-element.35), channel_id=1, source_target_pairs={{0,3},{1,2},{2,1},{3,0},{4,7},{5,6},{6,5},{7,4},{8,11},{9,10},{10,... | collective-permute-start | bytes 491528 | tf_op jit(solution)/shard_map/ppermute | solution.py:330
  98.1 3.8 collective-permute-done.3.refs_4_
  102.6 2.7 collective-permute-start.30
  113.3 2.6 project_and_norm.1
  123.9 2.7 collective-permute-start.32
  127.9 3.2 collective-permute-done.31.refs_9_
  131.9 3.9 %all-to-all-start = ((s32[32,1,32]{2,1,0:T(1,128)}), s32[32,1,32]{2,1,0:T(1,128)S(1)}, u32[]{:S(2)}, u32[]{:S(2)}) async-start(s32[32,1,32]{2,1,0:T(1,128)} %bitcast.7), calls=%async_computation | async-start | bytes 32768 | tf_op jit(solution)/shard_map/all_to_all | solution.py:410
  135.8 3.6 collective-permute-start.7
  139.6 9.7 %collective-permute-start.9 = (bf16[64,5120]{1,0:T(8,128)(2,1)S(1)}, bf16[64,5120]{1,0:T(8,128)(2,1)}, u32[]{:S(2)}, u32[]{:S(2)}) collective-permute-start(bf16[64,5120]{1,0:T(8,128)(2,1)S(1)} %collective-permute-done.8.refs_2_), channel_id=1, source_target_pairs={{0,1},{1,0},{2,3},{3,2},{4,5},{5,4},{6,7},{7,6},{8,9},{9,8},{10,11... | collective-permute-start | bytes 1966088 | tf_op jit(solution)/shard_map/ppermute | solution.py:338
  150.1 160.9 %arrange_weight.1.refs_10_ = bf16[5120,512]{1,0:T(8,128)(2,1)} custom-call(s32[32]{0:T(128)} %pad_add_fusion.refs_0_, bf16[640,512]{1,0:T(8,128)(2,1)} %constant_dynamic-update-slice_fusion.refs_1_, bf16[640,512]{1,0:T(8,128)(2,1)} %collective-permute-done.20.refs_2_, bf16[640,512]{1,0:T(8,128)(2,1)} %collective-permute-done.21.refs_3_, ...), custom_call_target="tpu_custom_call" | custom-call | bytes 10485760 | tf_op jit(solution)/shard_map/arrange_weight/pallas_call | solution.py:305
  313.6 2.6 copy-done
  316.1 6.8 %merge_rows.3 = bf16[1024,512]{1,0:T(8,128)(2,1)} custom-call(bf16[64,5120]{1,0:T(8,128)(2,1)S(1)} %get-tuple-element.23.refs_0_, bf16[64,5120]{1,0:T(8,128)(2,1)} %collective-permute-done.7.refs_1_, bf16[64,5120]{1,0:T(8,128)(2,1)S(1)} %collective-permute-done.8.refs_2_, bf16[64,5120]{1,0:T(8,128)(2,1)} %collective-permute-done.9.refs_3_, ...), custom_call_target="tpu_custom_call" | custom-call | flops 3221225472 | bytes 11534336 | tf_op jit(solution)/shard_map/merge_rows/pallas_call | solution.py:184
  323.0 4.3 %all-to-all-start.2 = ((bf16[32,32,512]{2,1,0:T(8,128)(2,1)}), bf16[32,32,512]{2,1,0:T(8,128)(2,1)S(1)}, u32[]{:S(2)}, u32[]{:S(2)}) async-start(bf16[32,32,512]{2,1,0:T(8,128)(2,1)} %bitcast.11), calls=%async_computation.2 | async-start | bytes 2097152 | tf_op jit(solution)/shard_map/all_to_all | solution.py:433
  327.3 2.5 copy-done.2
  333.9 6.8 %merge_rows.2 = bf16[1024,512]{1,0:T(8,128)(2,1)} custom-call(bf16[64,5120]{1,0:T(8,128)(2,1)S(1)} %get-tuple-element.23.refs_0_, bf16[64,5120]{1,0:T(8,128)(2,1)} %collective-permute-done.7.refs_1_, bf16[64,5120]{1,0:T(8,128)(2,1)S(1)} %copy-done.8, bf16[64,5120]{1,0:T(8,128)(2,1)} %collective-permute-done.9.refs_3_, bf16[64,5120]{1,0:T(8,128)(2,1)S(1)} %copy-done.6, ...), custom_call_target="tpu_custom_call" | custom-call | flops 3221225472 | bytes 11534336 | tf_op jit(solution)/shard_map/merge_rows/pallas_call | solution.py:184
  340.8 5.2 %all-to-all-done.2 = bf16[32,32,512]{2,1,0:T(8,128)(2,1)S(1)} async-done(((bf16[32,32,512]{2,1,0:T(8,128)(2,1)}), bf16[32,32,512]{2,1,0:T(8,128)(2,1)S(1)}, u32[]{:S(2)}, u32[]{:S(2)}) %all-to-all-start.2) | async-done | bytes 1048608 | tf_op jit(solution)/shard_map/all_to_all | solution.py:433
  346.0 4.7 %all-to-all-start.1 = ((bf16[32,32,512]{2,1,0:T(8,128)(2,1)}), bf16[32,32,512]{2,1,0:T(8,128)(2,1)}, u32[]{:S(2)}, u32[]{:S(2)}) async-start(bf16[32,32,512]{2,1,0:T(8,128)(2,1)} %bitcast.8), calls=%async_computation.1 | async-start | bytes 2097152 | tf_op jit(solution)/shard_map/all_to_all | solution.py:433
  354.7 13.9 %all-to-all-done.1 = bf16[32,32,512]{2,1,0:T(8,128)(2,1)} async-done(((bf16[32,32,512]{2,1,0:T(8,128)(2,1)}), bf16[32,32,512]{2,1,0:T(8,128)(2,1)}, u32[]{:S(2)}, u32[]{:S(2)}) %all-to-all-start.1) | async-done | bytes 1048608 | tf_op jit(solution)/shard_map/all_to_all | solution.py:433
  368.6 2.3 pick_rows.2
  372.0 2.5 collective-permute-start.33
  380.4 2.5 finish.1
  (205 shorter events, 65.2 us)
Async XLA Ops:
  6.5 320.8 %all-gather.2.cloned.1.call-start = ((), (), s32[]{:S(2)}) async-start(), calls=%async_computation.3 | async-start | bytes 5570560 | tf_op jit(solution)/shard_map/all_gather | solution.py:367
  16.9 17.4 %collective-permute-start.16 = (bf16[160,512]{1,0:T(8,128)(2,1)}, bf16[160,512]{1,0:T(8,128)(2,1)S(1)}, u32[]{:S(2)}, u32[]{:S(2)}) collective-permute-start(bf16[160,512]{1,0:T(8,128)(2,1)} %get-tuple-element.43), channel_id=1, source_target_pairs={{0,32},{32,64},{64,96},{96,0},{1,33},{33,65},{65,97},{97,1},{2,34}... | collective-permute-start | bytes 491528 | tf_op jit(solution)/shard_map/ppermute | solution.py:320
  18.6 15.8 %collective-permute-start.17 = (bf16[160,512]{1,0:T(8,128)(2,1)}, bf16[160,512]{1,0:T(8,128)(2,1)}, u32[]{:S(2)}, u32[]{:S(2)}) collective-permute-start(bf16[160,512]{1,0:T(8,128)(2,1)} %get-tuple-element.43), channel_id=1, source_target_pairs={{0,96},{32,0},{64,32},{96,64},{1,97},{33,1},{65,33},{97,65},{2,98}... | collective-permute-start | bytes 491528 | tf_op jit(solution)/shard_map/ppermute | solution.py:320
  20.8 29.1 %collective-permute-start.24 = (bf16[160,512]{1,0:T(8,128)(2,1)}, bf16[160,512]{1,0:T(8,128)(2,1)}, u32[]{:S(2)}, u32[]{:S(2)}) collective-permute-start(bf16[160,512]{1,0:T(8,128)(2,1)} %get-tuple-element.39), channel_id=1, source_target_pairs={{0,4},{4,0},{1,5},{5,1},{2,6},{6,2},{3,7},{7,3},{8,12},{12,8},{9,1... | collective-permute-start | bytes 491528 | tf_op jit(solution)/shard_map/ppermute | solution.py:361
  34.3 20.6 %collective-permute-start.18 = (bf16[80,512]{1,0:T(8,128)(2,1)S(1)}, bf16[80,512]{1,0:T(8,128)(2,1)S(1)}, u32[]{:S(2)}, u32[]{:S(2)}) collective-permute-start(bf16[80,512]{1,0:T(8,128)(2,1)S(1)} %slice.48), channel_id=1, source_target_pairs={{0,32},{32,64},{64,96},{96,0},{1,33},{33,65},{65,97},{97,1},{2,34}... | collective-permute-start | bytes 245768 | tf_op jit(solution)/shard_map/ppermute | solution.py:320
  35.3 20.3 %collective-permute-start.19 = (bf16[80,512]{1,0:T(8,128)(2,1)S(1)}, bf16[80,512]{1,0:T(8,128)(2,1)S(1)}, u32[]{:S(2)}, u32[]{:S(2)}) collective-permute-start(bf16[80,512]{1,0:T(8,128)(2,1)S(1)} %slice.49), channel_id=1, source_target_pairs={{0,96},{32,0},{64,32},{96,64},{1,97},{33,1},{65,33},{97,65},{2,98}... | collective-permute-start | bytes 245768 | tf_op jit(solution)/shard_map/ppermute | solution.py:320
  38.0 28.5 %collective-permute-start.5 = (bf16[320,1280]{1,0:T(8,128)(2,1)S(1)}, bf16[320,1280]{1,0:T(8,128)(2,1)S(1)}, u32[]{:S(2)}, u32[]{:S(2)}) collective-permute-start(bf16[320,1280]{1,0:T(8,128)(2,1)S(1)} %copy-done.19), channel_id=1, source_target_pairs={{0,2},{2,0},{1,3},{3,1},{4,6},{6,4},{5,7},{7,5},{8,10},{10,8},{9,1... | collective-permute-start | bytes 2457608 | tf_op jit(solution)/shard_map/ppermute | solution.py:384
  49.9 10.3 %collective-permute-start.25 = (bf16[160,512]{1,0:T(8,128)(2,1)}, bf16[160,512]{1,0:T(8,128)(2,1)S(1)}, u32[]{:S(2)}, u32[]{:S(2)}) collective-permute-start(bf16[160,512]{1,0:T(8,128)(2,1)} %collective-permute-done.24), channel_id=1, source_target_pairs={{0,8},{8,16},{16,24},{24,0},{1,9},{9,17},{17,25},{25,1},{2,10},{10... | collective-permute-start | bytes 491528 | tf_op jit(solution)/shard_map/ppermute | solution.py:320
  51.2 11.6 %collective-permute-start.26 = (bf16[160,512]{1,0:T(8,128)(2,1)}, bf16[160,512]{1,0:T(8,128)(2,1)S(1)}, u32[]{:S(2)}, u32[]{:S(2)}) collective-permute-start(bf16[160,512]{1,0:T(8,128)(2,1)} %collective-permute-done.24), channel_id=1, source_target_pairs={{0,24},{8,0},{16,8},{24,16},{1,25},{9,1},{17,9},{25,17},{2,26},{10... | collective-permute-start | bytes 491528 | tf_op jit(solution)/shard_map/ppermute | solution.py:320
  56.3 46.3 %collective-permute-start.20 = (bf16[640,512]{1,0:T(8,128)(2,1)}, bf16[640,512]{1,0:T(8,128)(2,1)}, u32[]{:S(2)}, u32[]{:S(2)}) collective-permute-start(bf16[640,512]{1,0:T(8,128)(2,1)} %constant_dynamic-update-slice_fusion.refs_1_), channel_id=1, source_target_pairs={{0,8},{8,16},{16,24},{24,0},{1,9},{9,17},{17,25},{25,1},{2,10},{10... | collective-permute-start | bytes 1966088 | tf_op jit(solution)/shard_map/ppermute | solution.py:320
  56.3 10.9 %collective-permute-start.1 = (bf16[256,320]{1,0:T(8,128)(2,1)S(1)}, bf16[256,320]{1,0:T(8,128)(2,1)S(1)}, u32[]{:S(2)}, u32[]{:S(2)}) collective-permute-start(bf16[256,320]{1,0:T(8,128)(2,1)S(1)} %get-tuple-element.37), channel_id=1, source_target_pairs={{0,1},{1,0},{2,3},{3,2},{4,5},{5,4},{6,7},{7,6},{8,9},{9,8},{10,11... | collective-permute-start | bytes 491528 | tf_op jit(solution)/shard_map/ppermute | solution.py:330
  60.2 8.5 %collective-permute-start.2 = (bf16[256,320]{1,0:T(8,128)(2,1)S(1)}, bf16[256,320]{1,0:T(8,128)(2,1)S(1)}, u32[]{:S(2)}, u32[]{:S(2)}) collective-permute-start(bf16[256,320]{1,0:T(8,128)(2,1)S(1)} %get-tuple-element.36), channel_id=1, source_target_pairs={{0,2},{1,3},{2,0},{3,1},{4,6},{5,7},{6,4},{7,5},{8,10},{9,11},{10,... | collective-permute-start | bytes 491528 | tf_op jit(solution)/shard_map/ppermute | solution.py:330
  62.8 43.8 %collective-permute-start.4 = (bf16[320,1280]{1,0:T(8,128)(2,1)S(1)}, bf16[320,1280]{1,0:T(8,128)(2,1)S(1)}, u32[]{:S(2)}, u32[]{:S(2)}) collective-permute-start(bf16[320,1280]{1,0:T(8,128)(2,1)S(1)} %copy-done.19), channel_id=1, source_target_pairs={{0,1},{1,0},{2,3},{3,2},{4,5},{5,4},{6,7},{7,6},{8,9},{9,8},{10,11... | collective-permute-start | bytes 2457608 | tf_op jit(solution)/shard_map/ppermute | solution.py:338
  66.5 40.3 %collective-permute-start.6 = (bf16[320,1280]{1,0:T(8,128)(2,1)S(1)}, bf16[320,1280]{1,0:T(8,128)(2,1)S(1)}, u32[]{:S(2)}, u32[]{:S(2)}) collective-permute-start(bf16[320,1280]{1,0:T(8,128)(2,1)S(1)} %collective-permute-done.5.refs_7_), channel_id=1, source_target_pairs={{0,1},{1,0},{2,3},{3,2},{4,5},{5,4},{6,7},{7,6},{8,9},{9,8},{10,11... | collective-permute-start | bytes 2457608 | tf_op jit(solution)/shard_map/ppermute | solution.py:338
  67.9 23.7 %collective-permute-start.27 = (bf16[80,512]{1,0:T(8,128)(2,1)S(1)}, bf16[80,512]{1,0:T(8,128)(2,1)S(1)}, u32[]{:S(2)}, u32[]{:S(2)}) collective-permute-start(bf16[80,512]{1,0:T(8,128)(2,1)S(1)} %slice.52), channel_id=1, source_target_pairs={{0,8},{8,16},{16,24},{24,0},{1,9},{9,17},{17,25},{25,1},{2,10},{10... | collective-permute-start | bytes 245768 | tf_op jit(solution)/shard_map/ppermute | solution.py:320
  69.4 26.8 %collective-permute-start.28 = (bf16[80,512]{1,0:T(8,128)(2,1)S(1)}, bf16[80,512]{1,0:T(8,128)(2,1)S(1)}, u32[]{:S(2)}, u32[]{:S(2)}) collective-permute-start(bf16[80,512]{1,0:T(8,128)(2,1)S(1)} %slice.53), channel_id=1, source_target_pairs={{0,24},{8,0},{16,8},{24,16},{1,25},{9,1},{17,9},{25,17},{2,26},{10... | collective-permute-start | bytes 245768 | tf_op jit(solution)/shard_map/ppermute | solution.py:320
  91.7 10.2 %collective-permute-start.3 = (bf16[256,320]{1,0:T(8,128)(2,1)S(1)}, bf16[256,320]{1,0:T(8,128)(2,1)S(1)}, u32[]{:S(2)}, u32[]{:S(2)}) collective-permute-start(bf16[256,320]{1,0:T(8,128)(2,1)S(1)} %get-tuple-element.35), channel_id=1, source_target_pairs={{0,3},{1,2},{2,1},{3,0},{4,7},{5,6},{6,5},{7,4},{8,11},{9,10},{10,... | collective-permute-start | bytes 491528 | tf_op jit(solution)/shard_map/ppermute | solution.py:330
  96.1 20.6 %collective-permute-start.21 = (bf16[640,512]{1,0:T(8,128)(2,1)}, bf16[640,512]{1,0:T(8,128)(2,1)}, u32[]{:S(2)}, u32[]{:S(2)}) collective-permute-start(bf16[640,512]{1,0:T(8,128)(2,1)} %constant_dynamic-update-slice_fusion.refs_1_), channel_id=1, source_target_pairs={{0,24},{8,0},{16,8},{24,16},{1,25},{9,1},{17,9},{25,17},{2,26},{10... | collective-permute-start | bytes 1966088 | tf_op jit(solution)/shard_map/ppermute | solution.py:320
  102.5 17.4 %collective-permute-start.29 = (bf16[640,512]{1,0:T(8,128)(2,1)}, bf16[640,512]{1,0:T(8,128)(2,1)}, u32[]{:S(2)}, u32[]{:S(2)}) collective-permute-start(bf16[640,512]{1,0:T(8,128)(2,1)} %constant_dynamic-update-slice_fusion.5.refs_6_), channel_id=1, source_target_pairs={{0,32},{32,64},{64,96},{96,0},{1,33},{33,65},{65,97},{97,1},{2,34}... | collective-permute-start | bytes 1966088 | tf_op jit(solution)/shard_map/ppermute | solution.py:320
  102.6 20.2 %collective-permute-start.30 = (bf16[640,512]{1,0:T(8,128)(2,1)}, bf16[640,512]{1,0:T(8,128)(2,1)}, u32[]{:S(2)}, u32[]{:S(2)}) collective-permute-start(bf16[640,512]{1,0:T(8,128)(2,1)} %constant_dynamic-update-slice_fusion.5.refs_6_), channel_id=1, source_target_pairs={{0,96},{32,0},{64,32},{96,64},{1,97},{33,1},{65,33},{97,65},{2,98}... | collective-permute-start | bytes 1966088 | tf_op jit(solution)/shard_map/ppermute | solution.py:320
  106.7 17.2 %collective-permute-start.22 = (bf16[320,512]{1,0:T(8,128)(2,1)S(1)}, bf16[320,512]{1,0:T(8,128)(2,1)S(1)}, u32[]{:S(2)}, u32[]{:S(2)}) collective-permute-start(bf16[320,512]{1,0:T(8,128)(2,1)S(1)} %slice.50), channel_id=1, source_target_pairs={{0,8},{8,16},{16,24},{24,0},{1,9},{9,17},{17,25},{25,1},{2,10},{10... | collective-permute-start | bytes 983048 | tf_op jit(solution)/shard_map/ppermute | solution.py:320
  116.6 22.9 %collective-permute-start.10 = (bf16[64,5120]{1,0:T(8,128)(2,1)S(1)}, bf16[64,5120]{1,0:T(8,128)(2,1)S(1)}, u32[]{:S(2)}, u32[]{:S(2)}) collective-permute-start(bf16[64,5120]{1,0:T(8,128)(2,1)S(1)} %get-tuple-element.23.refs_0_), channel_id=1, source_target_pairs={{0,6},{2,0},{4,2},{6,4},{1,7},{3,1},{5,3},{7,5},{8,14},{10,8},{12,... | collective-permute-start | bytes 1966088 | tf_op jit(solution)/shard_map/ppermute | solution.py:334
  116.7 22.9 %collective-permute-start.8 = (bf16[64,5120]{1,0:T(8,128)(2,1)S(1)}, bf16[64,5120]{1,0:T(8,128)(2,1)S(1)}, u32[]{:S(2)}, u32[]{:S(2)}) collective-permute-start(bf16[64,5120]{1,0:T(8,128)(2,1)S(1)} %get-tuple-element.23.refs_0_), channel_id=1, source_target_pairs={{0,2},{2,4},{4,6},{6,0},{1,3},{3,5},{5,7},{7,1},{8,10},{10,12},{12... | collective-permute-start | bytes 1966088 | tf_op jit(solution)/shard_map/ppermute | solution.py:334
  123.9 12.0 %collective-permute-start.32 = (bf16[320,512]{1,0:T(8,128)(2,1)S(1)}, bf16[320,512]{1,0:T(8,128)(2,1)}, u32[]{:S(2)}, u32[]{:S(2)}) collective-permute-start(bf16[320,512]{1,0:T(8,128)(2,1)S(1)} %slice.55), channel_id=1, source_target_pairs={{0,96},{32,0},{64,32},{96,64},{1,97},{33,1},{65,33},{97,65},{2,98}... | collective-permute-start | bytes 983048 | tf_op jit(solution)/shard_map/ppermute | solution.py:320
  127.9 183.2 %collective-permute-start.12 = (bf16[32,5120]{1,0:T(8,128)(2,1)}, bf16[32,5120]{1,0:T(8,128)(2,1)S(1)}, u32[]{:S(2)}, u32[]{:S(2)}) collective-permute-start(bf16[32,5120]{1,0:T(8,128)(2,1)} %get-tuple-element.24), channel_id=1, source_target_pairs={{0,4},{2,6},{4,0},{6,2},{1,5},{3,7},{5,1},{7,3},{8,12},{10,14},{12... | collective-permute-start | bytes 983048 | tf_op jit(solution)/shard_map/ppermute | solution.py:334
  131.2 180.1 %collective-permute-start.14 = (bf16[32,5120]{1,0:T(8,128)(2,1)}, bf16[32,5120]{1,0:T(8,128)(2,1)}, u32[]{:S(2)}, u32[]{:S(2)}) collective-permute-start(bf16[32,5120]{1,0:T(8,128)(2,1)} %get-tuple-element.25), channel_id=1, source_target_pairs={{0,4},{2,6},{4,0},{6,2},{1,5},{3,7},{5,1},{7,3},{8,12},{10,14},{12... | collective-permute-start | bytes 983048 | tf_op jit(solution)/shard_map/ppermute | solution.py:334
  131.9 179.1 %all-to-all-start = ((s32[32,1,32]{2,1,0:T(1,128)}), s32[32,1,32]{2,1,0:T(1,128)S(1)}, u32[]{:S(2)}, u32[]{:S(2)}) async-start(s32[32,1,32]{2,1,0:T(1,128)} %bitcast.7), calls=%async_computation | async-start | bytes 32768 | tf_op jit(solution)/shard_map/all_to_all | solution.py:410
  135.8 177.7 %collective-permute-start.7 = (bf16[64,5120]{1,0:T(8,128)(2,1)S(1)}, bf16[64,5120]{1,0:T(8,128)(2,1)}, u32[]{:S(2)}, u32[]{:S(2)}) collective-permute-start(bf16[64,5120]{1,0:T(8,128)(2,1)S(1)} %get-tuple-element.23.refs_0_), channel_id=1, source_target_pairs={{0,1},{1,0},{2,3},{3,2},{4,5},{5,4},{6,7},{7,6},{8,9},{9,8},{10,11... | collective-permute-start | bytes 1966088 | tf_op jit(solution)/shard_map/ppermute | solution.py:338
  139.5 174.0 %collective-permute-start.11 = (bf16[64,5120]{1,0:T(8,128)(2,1)S(1)}, bf16[64,5120]{1,0:T(8,128)(2,1)}, u32[]{:S(2)}, u32[]{:S(2)}) collective-permute-start(bf16[64,5120]{1,0:T(8,128)(2,1)S(1)} %collective-permute-done.10.refs_4_), channel_id=1, source_target_pairs={{0,1},{1,0},{2,3},{3,2},{4,5},{5,4},{6,7},{7,6},{8,9},{9,8},{10,11... | collective-permute-start | bytes 1966088 | tf_op jit(solution)/shard_map/ppermute | solution.py:338
  139.6 173.9 %collective-permute-start.9 = (bf16[64,5120]{1,0:T(8,128)(2,1)S(1)}, bf16[64,5120]{1,0:T(8,128)(2,1)}, u32[]{:S(2)}, u32[]{:S(2)}) collective-permute-start(bf16[64,5120]{1,0:T(8,128)(2,1)S(1)} %collective-permute-done.8.refs_2_), channel_id=1, source_target_pairs={{0,1},{1,0},{2,3},{3,2},{4,5},{5,4},{6,7},{7,6},{8,9},{9,8},{10,11... | collective-permute-start | bytes 1966088 | tf_op jit(solution)/shard_map/ppermute | solution.py:338
  323.0 23.1 %all-to-all-start.2 = ((bf16[32,32,512]{2,1,0:T(8,128)(2,1)}), bf16[32,32,512]{2,1,0:T(8,128)(2,1)S(1)}, u32[]{:S(2)}, u32[]{:S(2)}) async-start(bf16[32,32,512]{2,1,0:T(8,128)(2,1)} %bitcast.11), calls=%async_computation.2 | async-start | bytes 2097152 | tf_op jit(solution)/shard_map/all_to_all | solution.py:433
  346.0 22.5 %all-to-all-start.1 = ((bf16[32,32,512]{2,1,0:T(8,128)(2,1)}), bf16[32,32,512]{2,1,0:T(8,128)(2,1)}, u32[]{:S(2)}, u32[]{:S(2)}) async-start(bf16[32,32,512]{2,1,0:T(8,128)(2,1)} %bitcast.8), calls=%async_computation.1 | async-start | bytes 2097152 | tf_op jit(solution)/shard_map/all_to_all | solution.py:433
  (52 other events, 648.2 us)
Sparse Core Ops, SparseCore 0:
  17.0 78.3 all-gather.1

commit v5 on v3

v5 whole, which is shorter than its diff:
```python
import functools

import jax
import jax.numpy as jnp
from jax import lax
from jax.experimental import pallas as pl
from jax.experimental.pallas import tpu as pltpu
from jax.sharding import Mesh, PartitionSpec as P

HEAD_DIM = 80
MERGE = 4
EPSILON = 1e-06
LOG2E = 1.4426950408889634
SEC = ("z", "x", "yh")
TP = ("yl", "c")
BF = jnp.bfloat16
FIRST = 256
F32 = jnp.float32


def attention_kernel(row_ids, column_ids, patches, weight, context, queries, keys, values):
    heads = keys.shape[0]
    row_count = patches.shape[0]
    block = min(256, row_count)
    one = jnp.ones((block, 128 - HEAD_DIM), BF)

    def project(index, carry):
        rows = pl.ds(pl.multiple_of(index * block, block), block)
        query, key, value = (
            lax.dot_general(
                patches[rows, :], weight[c], (((1,), (1,)), ((), ())), preferred_element_type=F32
            ).astype(BF)
            for c in range(3)
        )
        for head in range(heads):
            columns = slice(head * HEAD_DIM, (head + 1) * HEAD_DIM)
            queries[head, rows, :] = query[:, columns]
            keys[head, rows, :] = key[:, columns]
            values[head, rows, :] = jnp.concatenate([value[:, columns], one], axis=1)
        return carry

    lax.fori_loop(0, row_count // block, project, 0)
    scale = HEAD_DIM ** (-0.5) * LOG2E

    def one_block(index, carry):
        rows = pl.ds(pl.multiple_of(index * block, block), block)
        same_image = row_ids[rows, :] == column_ids[...]
        outs = []
        for head in range(heads):
            scores = lax.dot_general(
                queries[head, rows, :],
                keys[head],
                (((1,), (1,)), ((), ())),
                preferred_element_type=F32,
            )
            scores = jnp.where(same_image, scores, -1e30)
            highest = jnp.max(scores, axis=1, keepdims=True)
            weights = jnp.exp2((scores - highest) * scale).astype(BF)
            summed = jnp.dot(weights, values[head], preferred_element_type=F32)
            outs.append(summed[:, :HEAD_DIM] / summed[:, HEAD_DIM : HEAD_DIM + 1])
        context[rows, :] = jnp.concatenate(outs, axis=1).astype(BF)
        return carry

    lax.fori_loop(0, row_count // block, one_block, 0)


def vision_context(patches, weight, image_ids):
    row_count, depth = patches.shape
    width = weight.shape[1]
    heads = width // HEAD_DIM
    patch_ids = jnp.repeat(image_ids.reshape(-1), MERGE)
    return pl.pallas_call(
        attention_kernel,
        out_shape=jax.ShapeDtypeStruct((row_count, width), BF),
        in_specs=[pl.BlockSpec(memory_space=pltpu.VMEM)] * 4,
        out_specs=pl.BlockSpec(memory_space=pltpu.VMEM),
        scratch_shapes=[
            pltpu.VMEM((heads, row_count, HEAD_DIM), BF),
            pltpu.VMEM((heads, row_count, HEAD_DIM), BF),
            pltpu.VMEM((heads, row_count, 128), BF),
        ],
        compiler_params=pltpu.CompilerParams(vmem_limit_bytes=20 * 2**20),
        cost_estimate=pl.CostEstimate(
            flops=4 * heads * row_count * row_count * 256 + 6 * row_count * depth * width,
            bytes_accessed=2 * (row_count + 3 * width) * depth,
            transcendentals=heads * row_count * row_count,
        ),
        name="vision_attention",
    )(patch_ids[:, None], patch_ids[None, :], patches, weight)


def norm_kernel(*refs):
    tp, parts, outs, (patches, gain, merged, top, bottom, normed) = (
        refs[0], refs[1:5], refs[5:9], refs[9:],
    )
    attended = patches[...].astype(F32)
    for part, weight in zip(parts, outs):
        attended += jnp.dot(part[...], weight[...], preferred_element_type=F32)
    moment = jnp.mean(attended * attended, axis=1, keepdims=True)
    scaled = attended * lax.rsqrt(moment + EPSILON) * gain[...]
    count, width = merged.shape[0], scaled.shape[1]
    for q in range(width // 128):
        normed[q] = scaled[:, q * 128 : (q + 1) * 128]
    for j in range(MERGE):
        for q in range(width // 128):
            piece = normed[q, pl.ds(j, count, stride=MERGE), :].astype(BF)
            columns = slice(j * width + q * 128, j * width + (q + 1) * 128)
            merged[:, columns] = piece
            top[:, columns] = piece[: count // 2]
            bottom[:, columns] = piece[count // 2 :]


def project_and_norm(tp, parts, outs, patches, gain):
    rows, depth = parts[0].shape
    width = patches.shape[1]
    count = rows // MERGE
    whole = lambda shape: pl.BlockSpec(shape, lambda i, t: (0, 0))
    return pl.pallas_call(
        norm_kernel,
        grid_spec=pltpu.PrefetchScalarGridSpec(
            num_scalar_prefetch=1,
            grid=(1,),
            in_specs=[whole((rows, depth))] * 4
            + [whole((depth, width))] * 4
            + [pl.BlockSpec((rows, width), lambda i, t: (t[0], 0)), whole((1, width))],
            out_specs=[
                whole((count, MERGE * width)),
                whole((count // 2, MERGE * width)),
                whole((count // 2, MERGE * width)),
            ],
            scratch_shapes=[pltpu.VMEM((width // 128, rows, 128), F32)],
        ),
        out_shape=[
            jax.ShapeDtypeStruct((count, MERGE * width), BF),
            jax.ShapeDtypeStruct((count // 2, MERGE * width), BF),
            jax.ShapeDtypeStruct((count // 2, MERGE * width), BF),
        ],
        compiler_params=pltpu.CompilerParams(vmem_limit_bytes=18 * 2**20),
        cost_estimate=pl.CostEstimate(
            flops=8 * rows * depth * width,
            bytes_accessed=8 * depth * (rows + width) + 4 * rows * width,
            transcendentals=rows,
        ),
        name="project_and_norm",
    )(tp.reshape(1).astype(jnp.int32), *parts, *outs, patches, gain[None, :])


def first_merge_kernel(*refs):
    places, blocks, pieces, (send, outgoing, rows, whole) = (
        refs[0], refs[1:-9], refs[-9:-4], refs[-4:],
    )
    first = 0
    for block in blocks:
        rows[first : first + block.shape[0], :] = block[...]
        first += block.shape[0]
    unit = whole.shape[0] // places.shape[0]
    index = 0
    for piece in pieces:
        for first in range(0, piece.shape[0], unit):
            place = pl.multiple_of(places[index] * unit, unit)
            whole[pl.ds(place, unit), :] = piece[first : first + unit, :]
            index += 1
    depth = rows.shape[1]
    tile = depth // 4

    def step(k, total):
        first = pl.multiple_of(k * tile, tile)
        return total + jnp.dot(
            rows[:, pl.ds(first, tile)], whole[pl.ds(first, tile), :], preferred_element_type=F32
        )

    total = lax.fori_loop(0, 4, step, jnp.zeros((rows.shape[0], whole.shape[1]), F32))
    outgoing[...] = jnp.dot(
        send[...], total.astype(BF), preferred_element_type=F32
    ).astype(BF)


def first_merge(places, blocks, pieces, send):
    slots, count = send.shape
    depth, columns = blocks[0].shape[1], pieces[0].shape[1]
    vmem = pl.BlockSpec(memory_space=pltpu.VMEM)
    return pl.pallas_call(
        first_merge_kernel,
        out_shape=[
            jax.ShapeDtypeStruct((slots, columns), BF),
            jax.ShapeDtypeStruct((count, depth), BF),
        ],
        in_specs=[pl.BlockSpec(memory_space=pltpu.SMEM)]
        + [vmem] * (len(blocks) + len(pieces) + 1),
        out_specs=[vmem, vmem],
        scratch_shapes=[pltpu.VMEM((depth, columns), BF)],
        compiler_params=pltpu.CompilerParams(vmem_limit_bytes=20 * 2**20),
        cost_estimate=pl.CostEstimate(
            flops=2 * count * (depth + slots) * columns,
            bytes_accessed=2 * (count * depth + depth * columns + slots * columns),
            transcendentals=0,
        ),
        name="merge_first",
    )(places, *blocks, *pieces, send)


def merge_kernel(rows, weight, send, outgoing, total):
    step = pl.program_id(0)
    term = jnp.dot(rows[...], weight[...], preferred_element_type=F32)

    @pl.when(step == 0)
    def _():
        total[...] = term

    @pl.when(step > 0)
    def _():
        total[...] += term

    @pl.when(step == pl.num_programs(0) - 1)
    def _():
        image = total[...].astype(BF)
        outgoing[...] = jnp.dot(send[...], image, preferred_element_type=F32).astype(BF)


def merge_and_select(rows, weight, send, tile=1280):
    depth, columns = weight.shape
    slots, count = send.shape
    return pl.pallas_call(
        merge_kernel,
        grid=(depth // tile,),
        out_shape=jax.ShapeDtypeStruct((slots, columns), BF),
        in_specs=[
            pl.BlockSpec((count, tile), lambda i: (0, i)),
            pl.BlockSpec((tile, columns), lambda i: (i, 0)),
            pl.BlockSpec((slots, count), lambda i: (0, 0), pipeline_mode=pl.Buffered(1)),
        ],
        out_specs=pl.BlockSpec((slots, columns), lambda i: (0, 0)),
        scratch_shapes=[pltpu.VMEM((count, columns), F32)],
        compiler_params=pltpu.CompilerParams(vmem_limit_bytes=24 * 2**20),
        cost_estimate=pl.CostEstimate(
            flops=2 * count * (depth + slots) * columns,
            bytes_accessed=2 * (count * depth + depth * columns + slots * columns),
            transcendentals=0,
        ),
        name="merge_rows",
    )(rows, weight, send)


def pick_kernel(received, pick, usable, text, prompt, squares, *, first):
    arrived = received[...].reshape(pick.shape[1], received.shape[-1])
    picked = jnp.dot(pick[...], arrived, preferred_element_type=F32)
    own = text[:, first : first + picked.shape[1]].astype(F32)
    value = jnp.where(usable[...] > 0, picked, own)
    prompt[...] = value.astype(BF)
    total = jnp.sum(value * value, axis=1, keepdims=True)

    @pl.when(pl.program_id(0) == 0)
    def _():
        squares[...] = total

    @pl.when(pl.program_id(0) > 0)
    def _():
        squares[...] += total


def pick_rows(received, pick, usable, text, first):
    planes, halves, rows, part = received.shape
    count, slots = pick.shape
    half = text.shape[1] // halves
    return pl.pallas_call(
        functools.partial(pick_kernel, first=first),
        grid=(halves,),
        out_shape=[
            jax.ShapeDtypeStruct((count, halves * part), BF),
            jax.ShapeDtypeStruct((count, 1), F32),
        ],
        in_specs=[
            pl.BlockSpec((planes, 1, rows, part), lambda h: (0, h, 0, 0)),
            pl.BlockSpec((count, slots), lambda h: (0, 0), pipeline_mode=pl.Buffered(1)),
            pl.BlockSpec((count, 1), lambda h: (0, 0), pipeline_mode=pl.Buffered(1)),
            pl.BlockSpec((count, half), lambda h: (0, h)),
        ],
        out_specs=[
            pl.BlockSpec((count, part), lambda h: (0, h)),
            pl.BlockSpec((count, 1), lambda h: (0, 0)),
        ],
        compiler_params=pltpu.CompilerParams(vmem_limit_bytes=16 * 2**20),
        cost_estimate=pl.CostEstimate(
            flops=2 * count * slots * halves * part,
            bytes_accessed=6 * count * halves * part,
            transcendentals=0,
        ),
        name="pick_rows",
    )(received, pick, usable, text)


def finish_kernel(first, second, squares, gain, out, *, width):
    inverse = lax.rsqrt(squares[...] / width + EPSILON)
    part = first.shape[1]
    out[:, :part] = (first[...].astype(F32) * inverse * gain[:, :part]).astype(BF)
    out[:, part:] = (second[...].astype(F32) * inverse * gain[:, part:]).astype(BF)


def finish(first, second, squares, gain):
    count = first.shape[0]
    parts = first.shape[1] // 2, second.shape[1] // 2
    half = sum(parts)
    return pl.pallas_call(
        functools.partial(finish_kernel, width=8 * half),
        grid=(2,),
        out_shape=jax.ShapeDtypeStruct((count, 2 * half), BF),
        in_specs=[
            pl.BlockSpec((count, parts[0]), lambda h: (0, h)),
            pl.BlockSpec((count, parts[1]), lambda h: (0, h)),
            pl.BlockSpec((count, 1), lambda h: (0, 0)),
            pl.BlockSpec((1, half), lambda h: (0, h)),
        ],
        out_specs=pl.BlockSpec((count, half), lambda h: (0, h)),
        compiler_params=pltpu.CompilerParams(vmem_limit_bytes=14 * 2**20),
        cost_estimate=pl.CostEstimate(
            flops=6 * count * half, bytes_accessed=8 * count * half, transcendentals=count
        ),
        name="finish",
    )(first, second, squares, gain[None, :])


def shift(block, axis, d):
    return lax.ppermute(block, axis, [(i, (i + d) % 4) for i in range(4)])


def ring_near(block, axis):
    return [shift(block, axis, 1), shift(block, axis, -1)]


def ring_far(before, after, axis):
    n = before.shape[0] // 2
    return [shift(before[:n], axis, 1), shift(after[n:], axis, -1)]


def swap_tp(block, k):
    return lax.ppermute(block, TP, [(i, i ^ k) for i in range(4)])


def shift_y(block, d):
    return lax.ppermute(block, ("yh", "yl"), [(i, (i + d) % 4) for i in range(4)])


def swap_core(block):
    return lax.ppermute(block, "c", [(0, 1), (1, 0)])


def on_device(
    patches,
    image_ids,
    qkv_weight,
    out_weight,
    merge_gain,
    merge_weight,
    text_rows,
    image_refs,
    llm_gain,
):
    yh = lax.axis_index("yh")
    tp = lax.axis_index(TP)
    y = lax.axis_index(("yh", "yl"))
    core = lax.axis_index("c")

    half = merge_weight.shape[1] // 2
    own = lax.dynamic_slice_in_dim(merge_weight, yh * half, half, 1)
    other = lax.dynamic_slice_in_dim(merge_weight, (1 - yh) * half, half, 1)
    swap = lambda block: lax.ppermute(block, "yh", [(0, 1), (1, 0)])
    arrived = [swap(other[:, FIRST:]), swap(other[:, :FIRST])]

    prompt_rows = image_refs.shape[0]
    usable = image_refs >= 0
    source = jnp.where(usable, image_refs // 256, -1)
    hits = (source[:, None] == jnp.arange(32)[None, :]).astype(BF)
    before = (jnp.arange(prompt_rows)[:, None] > jnp.arange(prompt_rows)[None, :]).astype(BF)
    earlier = jnp.dot(before, hits, preferred_element_type=F32)
    arrival = jnp.sum(earlier * hits.astype(F32), axis=1).astype(jnp.int32)
    slot = jnp.where(usable, source * 16 + arrival, -1)
    pick = (slot[:, None] == jnp.arange(512)[None, :]).astype(BF)
    names = jnp.where(usable, image_refs % 256 + 1, 0).astype(BF)
    table = jnp.dot(names[None, :], pick, preferred_element_type=F32).astype(jnp.int32)
    table = jnp.broadcast_to(table.reshape(16, 1, 32), (16, 2, 32)).reshape(32, 32)
    usable = usable.astype(jnp.int32)[:, None]

    arrived, table, pick, usable, out_weight = lax.optimization_barrier(
        (arrived, table, pick, usable, out_weight)
    )
    is_own = (jnp.arange(2) == yh)[:, None, None]
    second = jnp.where(is_own, own[None, :, FIRST:], arrived[0][None]).reshape(-1, half - FIRST)
    first = jnp.where(is_own, own[None, :, :FIRST], arrived[1][None]).reshape(-1, FIRST)
    second_weight = lax.all_gather(second, ("z", "x"), axis=0, tiled=True)
    near_z = ring_near(first, "z")

    out_far = lax.ppermute(out_weight, "yl", [(0, 1), (1, 0)])
    out_blocks = [out_weight, swap_core(out_weight), out_far, swap_core(out_far)]

    patches, first, second = lax.optimization_barrier((patches, first, second))
    context = vision_context(patches, jnp.swapaxes(qkv_weight, 1, 2), image_ids)
    context, near_z = lax.optimization_barrier((context, near_z))
    far_z = ring_far(*near_z, "z")
    rows = context.shape[0] // 4
    parts = [
        lax.dynamic_slice_in_dim(context, (tp ^ k) * rows, rows, 0) for k in range(4)
    ]
    parts = [parts[0]] + [swap_tp(parts[k], k) for k in (1, 2, 3)]
    parts, far_z = lax.optimization_barrier((parts, far_z))
    all_z = jnp.concatenate([first] + near_z + far_z, axis=0)
    near_x = ring_near(all_z, "x")
    merged, top, bottom = project_and_norm(tp, parts, out_blocks, patches, merge_gain)

    table, merged, top, bottom = lax.optimization_barrier((table, merged, top, bottom))
    near_rows = [
        (0, 0, merged),
        (1, 0, shift_y(merged, 1)),
        (-1, 0, shift_y(merged, -1)),
        (2, 0, shift_y(top, 2)),
        (2, top.shape[0], shift_y(bottom, -2)),
    ]
    table = lax.all_to_all(table, SEC, split_axis=0, concat_axis=0, tiled=True)
    far_x = ring_far(*near_x, "x")
    near = jnp.array([0, -1, 1, 2])
    z_of = (lax.axis_index("z") + near) % 4
    x_of = (lax.axis_index("x") + near) % 4
    places = (z_of[None, :] * 4 + x_of[:, None]).reshape(-1).astype(jnp.int32)
    blocks = []
    ids = []
    for d, offset, block in near_rows:
        blocks += [block, swap_core(block)]
        origin = (y - d + 4) % 4 * 128 + offset
        ids += [origin + c * 64 + jnp.arange(block.shape[0]) for c in (core, 1 - core)]
    row_ids = jnp.concatenate(ids)

    wanted = table.reshape(32, 2, 16) - 1
    wanted = jnp.where(wanted >= 0, wanted + jnp.arange(2)[None, :, None] * 256, -1).reshape(-1)
    send = (wanted[:, None] == row_ids[None, :]).astype(BF)

    def route(outgoing, offset):
        received = lax.all_to_all(outgoing, SEC, split_axis=0, concat_axis=0, tiled=True)
        received = received.reshape(16, 2, 32, -1)
        return pick_rows(received, pick, usable, text_rows, offset)

    outgoing, all_rows = first_merge(places, blocks, [all_z] + near_x + far_x, send)
    first_prompt, first_squares = route(outgoing, 0)
    outgoing = merge_and_select(all_rows, second_weight, send)
    second_prompt, second_squares = route(outgoing, FIRST)
    squares = first_squares + second_squares
    flat = squares.reshape(4, -1)
    total = flat + swap_tp(flat, 1) + swap_tp(flat, 2) + swap_tp(flat, 3)
    return finish(first_prompt, second_prompt, total.reshape(squares.shape), llm_gain)


def solution(mesh):
    torus = Mesh(mesh.devices.reshape(4, 4, 2, 2, 2), ("z", "x", "yh", "yl", "c"))
    return jax.shard_map(
        on_device,
        mesh=torus,
        in_specs=(
            P(SEC, None),
            P(SEC, None),
            P(None, None, TP),
            P(TP, None),
            P(),
            P(SEC, TP),
            P(SEC, TP),
            P(SEC),
            P(TP),
        ),
        out_specs=P(SEC, TP),
        check_vma=False,
    )
```

time: 191 us -> 213 us (1.12)
  waiting for transfers between devices: 27 us -> 75.6 us
  blocking collectives: 43.7 us -> 0 us
  starting transfers between devices: 42.8 us -> 55.4 us
  Pallas kernels: 30.8 us -> 37.3 us
  other arithmetic: 7.35 us -> 4.88 us
    all_to_all x1 -> x0, blocking collectives: 36.9 us -> none  [on_device(): lax.all_to_all(outgoing, SEC, split_axis=0, concat_axis=0, tiled=True)]
    ppermute x1 -> x11, waiting for transfers between devices: 0.01 us -> 36.1 us  [the longest x8 32.4 us: shift(): return lax.ppermute(block, axis, [(i, (i + d) % 4) for i in range(4)])]
    all_to_all x0 -> x2, waiting for transfers between devices: none -> 21.1 us  [route(): lax.all_to_all(outgoing, SEC, split_axis=0, concat_axis=0, tiled=True)]
    ppermute x5 -> x7, starting transfers between devices: 21.7 us -> 5.97 us  [swap_core(): return lax.ppermute(block, 'c', [(0, 1), (1, 0)])]
    ppermute x6, waiting for transfers between devices: 25.5 us -> 10.6 us  [swap_tp(): return lax.ppermute(block, TP, [(i, i ^ k) for i in range(4)])]
    ppermute x1 -> x11, starting transfers between devices: 3.82 us -> 17.7 us  [the longest x8 12.3 us: shift(): return lax.ppermute(block, axis, [(i, (i + d) % 4) for i in range(4)])]
    all_to_all x0 -> x2, starting transfers between devices: none -> 13.4 us  [route(): lax.all_to_all(outgoing, SEC, split_axis=0, concat_axis=0, tiled=True)]
    pallas_call x1 -> x4, Pallas kernels: 4.58 us -> 11.8 us  [the longest x1 6.23 us: first_merge(): pl.pallas_call(first_merge_kernel, out_shape=[jax.ShapeDtypeStruct((slots...]
  transfers between devices with their start and end apart: 18 -> 32, of which waited for: 5 -> 12; matrix products, arithmetic and copies ran while one was open for 5% -> 3% of each run, Pallas kernels for 10% -> 15%
where the time goes in v5:
time: 213 us; the launch traced here: 212 us
  waiting for transfers between devices  75.6 us (35%)
  starting transfers between devices  55.4 us (26%)
  Pallas kernels  37.3 us (18%)
  local copies, waits for them, and re-layouts  24.5 us (12%)
  between operations  13.8 us (6%)
  other arithmetic  4.88 us (2%)
    ppermute x8, waiting for transfers between devices, shift(): return lax.ppermute(block, axis, [(i, (i + d) % 4) for i in range(4)])  32.4 us
    all_to_all x2, waiting for transfers between devices, route(): lax.all_to_all(outgoing, SEC, split_axis=0, concat_axis=0, tiled=True)  21.1 us
    unnamed x44, local copies, waits for them, and re-layouts  19.7 us
    pallas_call x1, Pallas kernels, vision_context(): pl.pallas_call(attention_kernel, out_shape=jax.ShapeDtypeStruct((row_coun...  14 us
    all_to_all x2, starting transfers between devices, route(): lax.all_to_all(outgoing, SEC, split_axis=0, concat_axis=0, tiled=True)  13.4 us
    ppermute x8, starting transfers between devices, shift(): return lax.ppermute(block, axis, [(i, (i + d) % 4) for i in range(4)])  12.3 us
    ppermute x6, waiting for transfers between devices, swap_tp(): return lax.ppermute(block, TP, [(i, i ^ k) for i in range(4)])  10.6 us
    ppermute x4, starting transfers between devices, shift_y(): lax.ppermute(block, ('yh', 'yl'), [(i, (i + d) % 4) for i in range(4)])  7.91 us
  transfers between devices with their start and end apart: 32, of which 12 were waited for; matrix products, arithmetic and copies ran while one was open for 3% of the time, Pallas kernels for 15%

profile of v5, /device:TPU:1, one launch (start us, length us, event | category | flops | bytes accessed | tf_op | source)
XLA Modules:
  0.0 212.2 jit_solution(6829292406389843547)
XLA Ops:
  7.6 3.8 %collective-permute-start = (bf16[160,768]{1,0:T(8,128)(2,1)S(1)}, bf16[160,768]{1,0:T(8,128)(2,1)S(1)}, u32[]{:S(2)}, u32[]{:S(2)}) collective-permute-start(bf16[160,768]{1,0:T(8,128)(2,1)S(1)} %get-tuple-element.72), channel_id=1, source_target_pairs={{0,4},{4,0},{1,5},{5,1},{2,6},{6,2},{3,7},{7,3},{8,12},{12,8},{9,1... | collective-permute-start | bytes 737288 | tf_op jit(solution)/shard_map/ppermute | solution.py:366
  15.0 3.7 %collective-permute-done.1 = bf16[160,256]{1,0:T(8,128)(2,1)S(1)} collective-permute-done((bf16[160,256]{1,0:T(8,128)(2,1)S(1)}, bf16[160,256]{1,0:T(8,128)(2,1)S(1)}, u32[]{:S(2)}, u32[]{:S(2)}) %collective-permute-start.1) | collective-permute-done | bytes 81952 | tf_op jit(solution)/shard_map/ppermute | solution.py:366
  23.9 2.2 %collective-permute-start.3 = (bf16[320,256]{1,0:T(8,128)(2,1)S(1)}, bf16[320,256]{1,0:T(8,128)(2,1)S(1)}, u32[]{:S(2)}, u32[]{:S(2)}) collective-permute-start(bf16[320,256]{1,0:T(8,128)(2,1)S(1)} %bitcast_select_fusion.1), channel_id=1, source_target_pairs={{0,96},{32,0},{64,32},{96,64},{1,97},{33,1},{65,33},{97,65},{2,98}... | collective-permute-start | bytes 491528 | tf_op jit(solution)/shard_map/ppermute | solution.py:323
  26.1 2.1 collective-permute-start.9
  28.2 1.7 copy-done.1
  31.6 14.0 %vision_attention.1 = bf16[1024,320]{1,0:T(8,128)(2,1)S(1)} custom-call(s32[1024,1]{1,0:T(8,128)S(1)} %broadcast_in_dim_reshape.9.row_ids, s32[1,1024]{1,0:T(1,128)S(1)} %broadcast_in_dim_reshape.8.column_ids, bf16[1024,1280]{1,0:T(8,128)(2,1)S(1)} %copy-done.1, bf16[3,320,1280]{2,1,0:T(8,128)(2,1)S(1)} %bitcast.27), custom_call_target="tpu_custom_call" | custom-call | flops 6811549696 | bytes 5079040 | tf_op jit(solution)/shard_map/vision_attention/pallas_call | solution.py:72
  45.8 2.7 %collective-permute-start.8 = (bf16[160,256]{1,0:T(8,128)(2,1)S(1)}, bf16[160,256]{1,0:T(8,128)(2,1)S(1)}, u32[]{:S(2)}, u32[]{:S(2)}) collective-permute-start(bf16[160,256]{1,0:T(8,128)(2,1)S(1)} %slice.29), channel_id=1, source_target_pairs={{0,96},{32,0},{64,32},{96,64},{1,97},{33,1},{65,33},{97,65},{2,98}... | collective-permute-start | bytes 245768 | tf_op jit(solution)/shard_map/ppermute | solution.py:323
  49.2 1.9 collective-permute-done.7
  53.6 3.2 %collective-permute-done.5.refs_3_ = bf16[256,320]{1,0:T(8,128)(2,1)S(1)} collective-permute-done((bf16[256,320]{1,0:T(8,128)(2,1)S(1)}, bf16[256,320]{1,0:T(8,128)(2,1)S(1)}, u32[]{:S(2)}, u32[]{:S(2)}) %collective-permute-start.5) | collective-permute-done | bytes 163872 | tf_op jit(solution)/shard_map/ppermute | solution.py:336
  56.8 5.6 %collective-permute-done.6.refs_4_ = bf16[256,320]{1,0:T(8,128)(2,1)S(1)} collective-permute-done((bf16[256,320]{1,0:T(8,128)(2,1)S(1)}, bf16[256,320]{1,0:T(8,128)(2,1)S(1)}, u32[]{:S(2)}, u32[]{:S(2)}) %collective-permute-start.6) | collective-permute-done | bytes 163872 | tf_op jit(solution)/shard_map/ppermute | solution.py:336
  66.8 1.8 copy-done.2
  68.6 4.8 %project_and_norm.1 = (bf16[64,5120]{1,0:T(8,128)(2,1)}, bf16[32,5120]{1,0:T(8,128)(2,1)}, bf16[32,5120]{1,0:T(8,128)(2,1)}) custom-call(s32[1]{0:T(128)} %bitcast.3.refs_0_, bf16[256,320]{1,0:T(8,128)(2,1)S(1)} %get-tuple-element.42.refs_1_, bf16[256,320]{1,0:T(8,128)(2,1)S(1)} %collective-permute-done.4.refs_2_, ...), custom_call_target="tpu_custom_call" | custom-call | flops 838860800 | bytes 5242880 | tf_op jit(solution)/shard_map/project_and_norm/pallas_call | solution.py:118
  74.2 1.9 collective-permute-start.15
  76.1 18.2 %collective-permute-done.21.refs_12_ = bf16[1280,256]{1,0:T(8,128)(2,1)S(1)} collective-permute-done((bf16[1280,256]{1,0:T(8,128)(2,1)S(1)}, bf16[1280,256]{1,0:T(8,128)(2,1)S(1)}, u32[]{:S(2)}, u32[]{:S(2)}) %collective-permute-start.21) | collective-permute-done | bytes 655392 | tf_op jit(solution)/shard_map/ppermute | solution.py:323
  94.5 2.9 %collective-permute-start.24 = (bf16[640,256]{1,0:T(8,128)(2,1)S(1)}, bf16[640,256]{1,0:T(8,128)(2,1)S(1)}, u32[]{:S(2)}, u32[]{:S(2)}) collective-permute-start(bf16[640,256]{1,0:T(8,128)(2,1)S(1)} %slice.33), channel_id=1, source_target_pairs={{0,24},{8,0},{16,8},{24,16},{1,25},{9,1},{17,9},{25,17},{2,26},{10... | collective-permute-start | bytes 983048 | tf_op jit(solution)/shard_map/ppermute | solution.py:323
  97.5 2.6 %collective-permute-start.17 = (bf16[32,5120]{1,0:T(8,128)(2,1)}, bf16[32,5120]{1,0:T(8,128)(2,1)}, u32[]{:S(2)}, u32[]{:S(2)}) collective-permute-start(bf16[32,5120]{1,0:T(8,128)(2,1)} %get-tuple-element.51), channel_id=1, source_target_pairs={{0,4},{2,6},{4,0},{6,2},{1,5},{3,7},{5,1},{7,3},{8,12},{10,14},{12... | collective-permute-start | bytes 983048 | tf_op jit(solution)/shard_map/ppermute | solution.py:340
  100.1 12.3 %collective-permute-done.23.refs_14_ = bf16[640,256]{1,0:T(8,128)(2,1)S(1)} collective-permute-done((bf16[640,256]{1,0:T(8,128)(2,1)S(1)}, bf16[640,256]{1,0:T(8,128)(2,1)S(1)}, u32[]{:S(2)}, u32[]{:S(2)}) %collective-permute-start.23) | collective-permute-done | bytes 327712 | tf_op jit(solution)/shard_map/ppermute | solution.py:323
  112.4 2.6 %collective-permute-start.19 = (bf16[32,5120]{1,0:T(8,128)(2,1)}, bf16[32,5120]{1,0:T(8,128)(2,1)}, u32[]{:S(2)}, u32[]{:S(2)}) collective-permute-start(bf16[32,5120]{1,0:T(8,128)(2,1)} %get-tuple-element.52), channel_id=1, source_target_pairs={{0,4},{2,6},{4,0},{6,2},{1,5},{3,7},{5,1},{7,3},{8,12},{10,14},{12... | collective-permute-start | bytes 983048 | tf_op jit(solution)/shard_map/ppermute | solution.py:340
  115.0 3.8 %all-to-all-start = ((s32[32,1,32]{2,1,0:T(1,128)}), s32[32,1,32]{2,1,0:T(1,128)S(1)}, u32[]{:S(2)}, u32[]{:S(2)}) async-start(s32[32,1,32]{2,1,0:T(1,128)} %bitcast.10), calls=%async_computation | async-start | bytes 32768 | tf_op jit(solution)/shard_map/all_to_all | solution.py:417
  121.3 6.2 %all-to-all-done = s32[32,1,32]{2,1,0:T(1,128)S(1)} async-done(((s32[32,1,32]{2,1,0:T(1,128)}), s32[32,1,32]{2,1,0:T(1,128)S(1)}, u32[]{:S(2)}, u32[]{:S(2)}) %all-to-all-start) | async-done | bytes 4128 | tf_op jit(solution)/shard_map/all_to_all | solution.py:417
  127.6 1.8 collective-permute-start.18
  132.5 6.2 %merge_first.1 = (bf16[1024,256]{1,0:T(8,128)(2,1)}, bf16[512,5120]{1,0:T(8,128)(2,1)S(1)}) custom-call(s32[16]{0:T(128)S(1)} %add.249.refs_0_, bf16[64,5120]{1,0:T(8,128)(2,1)} %get-tuple-element.50.refs_1_, bf16[64,5120]{1,0:T(8,128)(2,1)} %collective-permute-done.12.refs_2_, bf16[64,5120]{1,0:T(8,128)(2,1)} %collective-permute-done.13.refs_3_, ...), custom_call_target="tpu_custom_call" | custom-call | flops 1610612736 | bytes 8388608 | tf_op jit(solution)/shard_map/merge_first/pallas_call | solution.py:182
  138.7 2.4 %copy-done.14 = bf16[512,5120]{1,0:T(8,128)(2,1)} copy-done((bf16[512,5120]{1,0:T(8,128)(2,1)}, bf16[512,5120]{1,0:T(8,128)(2,1)S(1)}, u32[]{:S(2)}) %copy-start.14) | copy-done | bytes 5242904
  141.1 3.9 %all-to-all-start.1 = ((bf16[32,32,256]{2,1,0:T(8,128)(2,1)}), bf16[32,32,256]{2,1,0:T(8,128)(2,1)S(1)}, u32[]{:S(2)}, u32[]{:S(2)}) async-start(bf16[32,32,256]{2,1,0:T(8,128)(2,1)} %bitcast.11), calls=%async_computation.1 | async-start | bytes 1048576 | tf_op jit(solution)/shard_map/all_to_all | solution.py:436
  145.0 3.2 %copy-done.13 = bf16[5120,768]{1,0:T(8,128)(2,1)S(1)} copy-done((bf16[5120,768]{1,0:T(8,128)(2,1)S(1)}, bf16[5120,768]{1,0:T(8,128)(2,1)}, u32[]{:S(2)}) %copy-start.13) | copy-done | bytes 7864344
  148.2 2.5 %copy-done.15 = bf16[512,5120]{1,0:T(8,128)(2,1)S(1)} copy-done((bf16[512,5120]{1,0:T(8,128)(2,1)S(1)}, bf16[512,5120]{1,0:T(8,128)(2,1)}, u32[]{:S(2)}) %copy-start.15) | copy-done | bytes 5242904
  150.7 6.6 %merge_rows.1 = bf16[1024,768]{1,0:T(8,128)(2,1)S(1)} custom-call(bf16[512,5120]{1,0:T(8,128)(2,1)S(1)} %copy-done.15, bf16[5120,768]{1,0:T(8,128)(2,1)S(1)} %copy-done.13, bf16[1024,512]{1,0:T(8,128)(2,1)S(1)} %compare_convert_fusion.refs_16_.send), custom_call_target="tpu_custom_call" | custom-call | flops 4831838208 | bytes 14680064 | tf_op jit(solution)/shard_map/merge_rows/pallas_call | solution.py:223
  158.5 9.5 %all-to-all-start.2 = ((bf16[32,32,768]{2,1,0:T(8,128)(2,1)}), bf16[32,32,768]{2,1,0:T(8,128)(2,1)}, u32[]{:S(2)}, u32[]{:S(2)}) async-start(bf16[32,32,768]{2,1,0:T(8,128)(2,1)} %bitcast.25), calls=%async_computation.2 | async-start | bytes 3145728 | tf_op jit(solution)/shard_map/all_to_all | solution.py:436
  170.8 21.1 %all-to-all-done.2 = bf16[32,32,768]{2,1,0:T(8,128)(2,1)} async-done(((bf16[32,32,768]{2,1,0:T(8,128)(2,1)}), bf16[32,32,768]{2,1,0:T(8,128)(2,1)}, u32[]{:S(2)}, u32[]{:S(2)}) %all-to-all-start.2) | async-done | bytes 1572896 | tf_op jit(solution)/shard_map/all_to_all | solution.py:436
  191.8 2.8 %pick_rows.3 = (bf16[512,1536]{1,0:T(8,128)(2,1)S(1)}, f32[512,1]{1,0:T(8,128)S(1)}) custom-call(bf16[16,2,32,768]{3,2,1,0:T(8,128)(2,1)} %bitcast.14.received, bf16[512,512]{1,0:T(8,128)(2,1)S(1)} %fusion.1.pick, s32[512,1]{1,0:T(8,128)S(1)} %copy.16.usable, bf16[512,2048]{1,0:T(8,128)(2,1)S(1)} %copy-done), custom_call_target="tpu_custom_call" | custom-call | flops 805306368 | bytes 4718592 | tf_op jit(solution)/shard_map/pick_rows/pallas_call | solution.py:265
  195.9 2.5 %collective-permute-start.25 = (f32[4,128]{1,0:T(4,128)S(1)}, f32[4,128]{1,0:T(4,128)S(1)}, u32[]{:S(2)}, u32[]{:S(2)}) collective-permute-start(f32[4,128]{1,0:T(4,128)S(1)} %bitcast.28), channel_id=1, source_target_pairs={{0,1},{1,0},{2,3},{3,2},{4,5},{5,4},{6,7},{7,6},{8,9},{9,8},{10,11... | collective-permute-start | bytes 6152 | tf_op jit(solution)/shard_map/ppermute | solution.py:336
  203.5 1.8 finish.1
  (131 shorter events, 36.1 us)
Async XLA Ops:
  6.5 138.4 %all-gather.2.cloned.1.call-start = ((), (), s32[]{:S(2)}) async-start(), calls=%async_computation.3 | async-start | bytes 8355840 | tf_op jit(solution)/shard_map/all_gather | solution.py:389
  7.6 11.0 %collective-permute-start = (bf16[160,768]{1,0:T(8,128)(2,1)S(1)}, bf16[160,768]{1,0:T(8,128)(2,1)S(1)}, u32[]{:S(2)}, u32[]{:S(2)}) collective-permute-start(bf16[160,768]{1,0:T(8,128)(2,1)S(1)} %get-tuple-element.72), channel_id=1, source_target_pairs={{0,4},{4,0},{1,5},{5,1},{2,6},{6,2},{3,7},{7,3},{8,12},{12,8},{9,1... | collective-permute-start | bytes 737288 | tf_op jit(solution)/shard_map/ppermute | solution.py:366
  12.4 6.2 %collective-permute-start.1 = (bf16[160,256]{1,0:T(8,128)(2,1)S(1)}, bf16[160,256]{1,0:T(8,128)(2,1)S(1)}, u32[]{:S(2)}, u32[]{:S(2)}) collective-permute-start(bf16[160,256]{1,0:T(8,128)(2,1)S(1)} %get-tuple-element.74), channel_id=1, source_target_pairs={{0,4},{4,0},{1,5},{5,1},{2,6},{6,2},{3,7},{7,3},{8,12},{12,8},{9,1... | collective-permute-start | bytes 245768 | tf_op jit(solution)/shard_map/ppermute | solution.py:366
  20.2 28.3 %collective-permute-start.10 = (bf16[320,1280]{1,0:T(8,128)(2,1)}, bf16[320,1280]{1,0:T(8,128)(2,1)}, u32[]{:S(2)}, u32[]{:S(2)}) collective-permute-start(bf16[320,1280]{1,0:T(8,128)(2,1)} %refs_5_), channel_id=1, source_target_pairs={{0,2},{2,0},{1,3},{3,1},{4,6},{6,4},{5,7},{7,5},{8,10},{10,8},{9,1... | collective-permute-start | bytes 2457608 | tf_op jit(solution)/shard_map/ppermute | solution.py:392
  22.2 23.5 %collective-permute-start.2 = (bf16[320,256]{1,0:T(8,128)(2,1)S(1)}, bf16[320,256]{1,0:T(8,128)(2,1)S(1)}, u32[]{:S(2)}, u32[]{:S(2)}) collective-permute-start(bf16[320,256]{1,0:T(8,128)(2,1)S(1)} %bitcast_select_fusion.1), channel_id=1, source_target_pairs={{0,32},{32,64},{64,96},{96,0},{1,33},{33,65},{65,97},{97,1},{2,34}... | collective-permute-start | bytes 491528 | tf_op jit(solution)/shard_map/ppermute | solution.py:323
  23.9 21.8 %collective-permute-start.3 = (bf16[320,256]{1,0:T(8,128)(2,1)S(1)}, bf16[320,256]{1,0:T(8,128)(2,1)S(1)}, u32[]{:S(2)}, u32[]{:S(2)}) collective-permute-start(bf16[320,256]{1,0:T(8,128)(2,1)S(1)} %bitcast_select_fusion.1), channel_id=1, source_target_pairs={{0,96},{32,0},{64,32},{96,64},{1,97},{33,1},{65,33},{97,65},{2,98}... | collective-permute-start | bytes 491528 | tf_op jit(solution)/shard_map/ppermute | solution.py:323
  26.1 40.8 %collective-permute-start.9 = (bf16[320,1280]{1,0:T(8,128)(2,1)}, bf16[320,1280]{1,0:T(8,128)(2,1)}, u32[]{:S(2)}, u32[]{:S(2)}) collective-permute-start(bf16[320,1280]{1,0:T(8,128)(2,1)} %refs_5_), channel_id=1, source_target_pairs={{0,1},{1,0},{2,3},{3,2},{4,5},{5,4},{6,7},{7,6},{8,9},{9,8},{10,11... | collective-permute-start | bytes 2457608 | tf_op jit(solution)/shard_map/ppermute | solution.py:344
  45.8 5.4 %collective-permute-start.7 = (bf16[160,256]{1,0:T(8,128)(2,1)S(1)}, bf16[160,256]{1,0:T(8,128)(2,1)S(1)}, u32[]{:S(2)}, u32[]{:S(2)}) collective-permute-start(bf16[160,256]{1,0:T(8,128)(2,1)S(1)} %slice.28), channel_id=1, source_target_pairs={{0,32},{32,64},{64,96},{96,0},{1,33},{33,65},{65,97},{97,1},{2,34}... | collective-permute-start | bytes 245768 | tf_op jit(solution)/shard_map/ppermute | solution.py:323
  45.8 6.0 %collective-permute-start.8 = (bf16[160,256]{1,0:T(8,128)(2,1)S(1)}, bf16[160,256]{1,0:T(8,128)(2,1)S(1)}, u32[]{:S(2)}, u32[]{:S(2)}) collective-permute-start(bf16[160,256]{1,0:T(8,128)(2,1)S(1)} %slice.29), channel_id=1, source_target_pairs={{0,96},{32,0},{64,32},{96,64},{1,97},{33,1},{65,33},{97,65},{2,98}... | collective-permute-start | bytes 245768 | tf_op jit(solution)/shard_map/ppermute | solution.py:323
  48.5 18.3 %collective-permute-start.11 = (bf16[320,1280]{1,0:T(8,128)(2,1)}, bf16[320,1280]{1,0:T(8,128)(2,1)}, u32[]{:S(2)}, u32[]{:S(2)}) collective-permute-start(bf16[320,1280]{1,0:T(8,128)(2,1)} %collective-permute-done.10.refs_7_), channel_id=1, source_target_pairs={{0,1},{1,0},{2,3},{3,2},{4,5},{5,4},{6,7},{7,6},{8,9},{9,8},{10,11... | collective-permute-start | bytes 2457608 | tf_op jit(solution)/shard_map/ppermute | solution.py:344
  49.2 4.4 %collective-permute-start.4 = (bf16[256,320]{1,0:T(8,128)(2,1)S(1)}, bf16[256,320]{1,0:T(8,128)(2,1)S(1)}, u32[]{:S(2)}, u32[]{:S(2)}) collective-permute-start(bf16[256,320]{1,0:T(8,128)(2,1)S(1)} %get-tuple-element.69), channel_id=1, source_target_pairs={{0,1},{1,0},{2,3},{3,2},{4,5},{5,4},{6,7},{7,6},{8,9},{9,8},{10,11... | collective-permute-start | bytes 491528 | tf_op jit(solution)/shard_map/ppermute | solution.py:336
  51.1 5.6 %collective-permute-start.5 = (bf16[256,320]{1,0:T(8,128)(2,1)S(1)}, bf16[256,320]{1,0:T(8,128)(2,1)S(1)}, u32[]{:S(2)}, u32[]{:S(2)}) collective-permute-start(bf16[256,320]{1,0:T(8,128)(2,1)S(1)} %get-tuple-element.68), channel_id=1, source_target_pairs={{0,2},{1,3},{2,0},{3,1},{4,6},{5,7},{6,4},{7,5},{8,10},{9,11},{10,... | collective-permute-start | bytes 491528 | tf_op jit(solution)/shard_map/ppermute | solution.py:336
  51.9 10.5 %collective-permute-start.6 = (bf16[256,320]{1,0:T(8,128)(2,1)S(1)}, bf16[256,320]{1,0:T(8,128)(2,1)S(1)}, u32[]{:S(2)}, u32[]{:S(2)}) collective-permute-start(bf16[256,320]{1,0:T(8,128)(2,1)S(1)} %get-tuple-element.67), channel_id=1, source_target_pairs={{0,3},{1,2},{2,1},{3,0},{4,7},{5,6},{6,5},{7,4},{8,11},{9,10},{10,... | collective-permute-start | bytes 491528 | tf_op jit(solution)/shard_map/ppermute | solution.py:336
  62.4 32.0 %collective-permute-start.21 = (bf16[1280,256]{1,0:T(8,128)(2,1)S(1)}, bf16[1280,256]{1,0:T(8,128)(2,1)S(1)}, u32[]{:S(2)}, u32[]{:S(2)}) collective-permute-start(bf16[1280,256]{1,0:T(8,128)(2,1)S(1)} %constant_dynamic-update-slice_fusion.refs_11_), channel_id=1, source_target_pairs={{0,8},{8,16},{16,24},{24,0},{1,9},{9,17},{17,25},{25,1},{2,10},{10... | collective-permute-start | bytes 1966088 | tf_op jit(solution)/shard_map/ppermute | solution.py:323
  63.6 30.8 %collective-permute-start.22 = (bf16[1280,256]{1,0:T(8,128)(2,1)S(1)}, bf16[1280,256]{1,0:T(8,128)(2,1)S(1)}, u32[]{:S(2)}, u32[]{:S(2)}) collective-permute-start(bf16[1280,256]{1,0:T(8,128)(2,1)S(1)} %constant_dynamic-update-slice_fusion.refs_11_), channel_id=1, source_target_pairs={{0,24},{8,0},{16,8},{24,16},{1,25},{9,1},{17,9},{25,17},{2,26},{10... | collective-permute-start | bytes 1966088 | tf_op jit(solution)/shard_map/ppermute | solution.py:323
  73.4 46.3 %collective-permute-start.13 = (bf16[64,5120]{1,0:T(8,128)(2,1)}, bf16[64,5120]{1,0:T(8,128)(2,1)}, u32[]{:S(2)}, u32[]{:S(2)}) collective-permute-start(bf16[64,5120]{1,0:T(8,128)(2,1)} %get-tuple-element.50.refs_1_), channel_id=1, source_target_pairs={{0,2},{2,4},{4,6},{6,0},{1,3},{3,5},{5,7},{7,1},{8,10},{10,12},{12... | collective-permute-start | bytes 1966088 | tf_op jit(solution)/shard_map/ppermute | solution.py:340
  74.2 45.6 %collective-permute-start.15 = (bf16[64,5120]{1,0:T(8,128)(2,1)}, bf16[64,5120]{1,0:T(8,128)(2,1)}, u32[]{:S(2)}, u32[]{:S(2)}) collective-permute-start(bf16[64,5120]{1,0:T(8,128)(2,1)} %get-tuple-element.50.refs_1_), channel_id=1, source_target_pairs={{0,6},{2,0},{4,2},{6,4},{1,7},{3,1},{5,3},{7,5},{8,14},{10,8},{12,... | collective-permute-start | bytes 1966088 | tf_op jit(solution)/shard_map/ppermute | solution.py:340
  94.4 18.0 %collective-permute-start.23 = (bf16[640,256]{1,0:T(8,128)(2,1)S(1)}, bf16[640,256]{1,0:T(8,128)(2,1)S(1)}, u32[]{:S(2)}, u32[]{:S(2)}) collective-permute-start(bf16[640,256]{1,0:T(8,128)(2,1)S(1)} %slice.32), channel_id=1, source_target_pairs={{0,8},{8,16},{16,24},{24,0},{1,9},{9,17},{17,25},{25,1},{2,10},{10... | collective-permute-start | bytes 983048 | tf_op jit(solution)/shard_map/ppermute | solution.py:323
  94.5 24.4 %collective-permute-start.24 = (bf16[640,256]{1,0:T(8,128)(2,1)S(1)}, bf16[640,256]{1,0:T(8,128)(2,1)S(1)}, u32[]{:S(2)}, u32[]{:S(2)}) collective-permute-start(bf16[640,256]{1,0:T(8,128)(2,1)S(1)} %slice.33), channel_id=1, source_target_pairs={{0,24},{8,0},{16,8},{24,16},{1,25},{9,1},{17,9},{25,17},{2,26},{10... | collective-permute-start | bytes 983048 | tf_op jit(solution)/shard_map/ppermute | solution.py:323
  97.5 30.1 %collective-permute-start.17 = (bf16[32,5120]{1,0:T(8,128)(2,1)}, bf16[32,5120]{1,0:T(8,128)(2,1)}, u32[]{:S(2)}, u32[]{:S(2)}) collective-permute-start(bf16[32,5120]{1,0:T(8,128)(2,1)} %get-tuple-element.51), channel_id=1, source_target_pairs={{0,4},{2,6},{4,0},{6,2},{1,5},{3,7},{5,1},{7,3},{8,12},{10,14},{12... | collective-permute-start | bytes 983048 | tf_op jit(solution)/shard_map/ppermute | solution.py:340
  112.4 17.0 %collective-permute-start.19 = (bf16[32,5120]{1,0:T(8,128)(2,1)}, bf16[32,5120]{1,0:T(8,128)(2,1)}, u32[]{:S(2)}, u32[]{:S(2)}) collective-permute-start(bf16[32,5120]{1,0:T(8,128)(2,1)} %get-tuple-element.52), channel_id=1, source_target_pairs={{0,4},{2,6},{4,0},{6,2},{1,5},{3,7},{5,1},{7,3},{8,12},{10,14},{12... | collective-permute-start | bytes 983048 | tf_op jit(solution)/shard_map/ppermute | solution.py:340
  115.0 12.4 %all-to-all-start = ((s32[32,1,32]{2,1,0:T(1,128)}), s32[32,1,32]{2,1,0:T(1,128)S(1)}, u32[]{:S(2)}, u32[]{:S(2)}) async-start(s32[32,1,32]{2,1,0:T(1,128)} %bitcast.10), calls=%async_computation | async-start | bytes 32768 | tf_op jit(solution)/shard_map/all_to_all | solution.py:417
  118.9 12.5 %collective-permute-start.12 = (bf16[64,5120]{1,0:T(8,128)(2,1)}, bf16[64,5120]{1,0:T(8,128)(2,1)}, u32[]{:S(2)}, u32[]{:S(2)}) collective-permute-start(bf16[64,5120]{1,0:T(8,128)(2,1)} %get-tuple-element.50.refs_1_), channel_id=1, source_target_pairs={{0,1},{1,0},{2,3},{3,2},{4,5},{5,4},{6,7},{7,6},{8,9},{9,8},{10,11... | collective-permute-start | bytes 1966088 | tf_op jit(solution)/shard_map/ppermute | solution.py:344
  119.8 11.6 %collective-permute-start.14 = (bf16[64,5120]{1,0:T(8,128)(2,1)}, bf16[64,5120]{1,0:T(8,128)(2,1)}, u32[]{:S(2)}, u32[]{:S(2)}) collective-permute-start(bf16[64,5120]{1,0:T(8,128)(2,1)} %collective-permute-done.13.refs_3_), channel_id=1, source_target_pairs={{0,1},{1,0},{2,3},{3,2},{4,5},{5,4},{6,7},{7,6},{8,9},{9,8},{10,11... | collective-permute-start | bytes 1966088 | tf_op jit(solution)/shard_map/ppermute | solution.py:344
  119.9 11.5 %collective-permute-start.16 = (bf16[64,5120]{1,0:T(8,128)(2,1)}, bf16[64,5120]{1,0:T(8,128)(2,1)}, u32[]{:S(2)}, u32[]{:S(2)}) collective-permute-start(bf16[64,5120]{1,0:T(8,128)(2,1)} %collective-permute-done.15.refs_5_), channel_id=1, source_target_pairs={{0,1},{1,0},{2,3},{3,2},{4,5},{5,4},{6,7},{7,6},{8,9},{9,8},{10,11... | collective-permute-start | bytes 1966088 | tf_op jit(solution)/shard_map/ppermute | solution.py:344
  127.6 3.3 %collective-permute-start.18 = (bf16[32,5120]{1,0:T(8,128)(2,1)}, bf16[32,5120]{1,0:T(8,128)(2,1)S(1)}, u32[]{:S(2)}, u32[]{:S(2)}) collective-permute-start(bf16[32,5120]{1,0:T(8,128)(2,1)} %collective-permute-done.17.refs_7_), channel_id=1, source_target_pairs={{0,1},{1,0},{2,3},{3,2},{4,5},{5,4},{6,7},{7,6},{8,9},{9,8},{10,11... | collective-permute-start | bytes 983048 | tf_op jit(solution)/shard_map/ppermute | solution.py:344
  129.4 1.9 collective-permute-start.20
  141.1 17.4 %all-to-all-start.1 = ((bf16[32,32,256]{2,1,0:T(8,128)(2,1)}), bf16[32,32,256]{2,1,0:T(8,128)(2,1)S(1)}, u32[]{:S(2)}, u32[]{:S(2)}) async-start(bf16[32,32,256]{2,1,0:T(8,128)(2,1)} %bitcast.11), calls=%async_computation.1 | async-start | bytes 1048576 | tf_op jit(solution)/shard_map/all_to_all | solution.py:436
  158.5 33.3 %all-to-all-start.2 = ((bf16[32,32,768]{2,1,0:T(8,128)(2,1)}), bf16[32,32,768]{2,1,0:T(8,128)(2,1)}, u32[]{:S(2)}, u32[]{:S(2)}) async-start(bf16[32,32,768]{2,1,0:T(8,128)(2,1)} %bitcast.25), calls=%async_computation.2 | async-start | bytes 3145728 | tf_op jit(solution)/shard_map/all_to_all | solution.py:436
  195.9 4.2 %collective-permute-start.25 = (f32[4,128]{1,0:T(4,128)S(1)}, f32[4,128]{1,0:T(4,128)S(1)}, u32[]{:S(2)}, u32[]{:S(2)}) collective-permute-start(f32[4,128]{1,0:T(4,128)S(1)} %bitcast.28), channel_id=1, source_target_pairs={{0,1},{1,0},{2,3},{3,2},{4,5},{5,4},{6,7},{7,6},{8,9},{9,8},{10,11... | collective-permute-start | bytes 6152 | tf_op jit(solution)/shard_map/ppermute | solution.py:336
  198.4 2.5 %collective-permute-start.26 = (f32[4,128]{1,0:T(4,128)S(1)}, f32[4,128]{1,0:T(4,128)S(1)}, u32[]{:S(2)}, u32[]{:S(2)}) collective-permute-start(f32[4,128]{1,0:T(4,128)S(1)} %bitcast.29), channel_id=1, source_target_pairs={{0,2},{1,3},{2,0},{3,1},{4,6},{5,7},{6,4},{7,5},{8,10},{9,11},{10,... | collective-permute-start | bytes 6152 | tf_op jit(solution)/shard_map/ppermute | solution.py:336
  198.9 3.0 %collective-permute-start.27 = (f32[4,128]{1,0:T(4,128)S(1)}, f32[4,128]{1,0:T(4,128)S(1)}, u32[]{:S(2)}, u32[]{:S(2)}) collective-permute-start(f32[4,128]{1,0:T(4,128)S(1)} %bitcast.30), channel_id=1, source_target_pairs={{0,3},{1,2},{2,1},{3,0},{4,7},{5,6},{6,5},{7,4},{8,11},{9,10},{10,... | collective-permute-start | bytes 6152 | tf_op jit(solution)/shard_map/ppermute | solution.py:336
  (20 other events, 107.4 us)
Sparse Core Ops, SparseCore 0:
  20.4 92.6 all-gather.1

commit v6 on v5

--- a/solution.py
+++ b/solution.py
@@ -14,7 +14,6 @@
 SEC = ("z", "x", "yh")
 TP = ("yl", "c")
 BF = jnp.bfloat16
-FIRST = 256
 F32 = jnp.float32
 
 
@@ -145,107 +144,57 @@
     )(tp.reshape(1).astype(jnp.int32), *parts, *outs, patches, gain[None, :])
 
 
-def first_merge_kernel(*refs):
-    places, blocks, pieces, (send, outgoing, rows, whole) = (
-        refs[0], refs[1:-9], refs[-9:-4], refs[-4:],
-    )
+def merge_kernel(*refs):
+    blocks, (weight, send, outgoing, rows, total) = refs[:-5], refs[-5:]
+    step = pl.program_id(0)
     first = 0
     for block in blocks:
         rows[first : first + block.shape[0], :] = block[...]
         first += block.shape[0]
-    unit = whole.shape[0] // places.shape[0]
-    index = 0
-    for piece in pieces:
-        for first in range(0, piece.shape[0], unit):
-            place = pl.multiple_of(places[index] * unit, unit)
-            whole[pl.ds(place, unit), :] = piece[first : first + unit, :]
-            index += 1
-    depth = rows.shape[1]
-    tile = depth // 4
-
-    def step(k, total):
-        first = pl.multiple_of(k * tile, tile)
-        return total + jnp.dot(
-            rows[:, pl.ds(first, tile)], whole[pl.ds(first, tile), :], preferred_element_type=F32
-        )
-
-    total = lax.fori_loop(0, 4, step, jnp.zeros((rows.shape[0], whole.shape[1]), F32))
-    outgoing[...] = jnp.dot(
-        send[...], total.astype(BF), preferred_element_type=F32
-    ).astype(BF)
-
-
-def first_merge(places, blocks, pieces, send):
+    term = jnp.dot(rows[...], weight[...], preferred_element_type=F32)
+
+    @pl.when(step == 0)
+    def _():
+        total[...] = term
+
+    @pl.when(step > 0)
+    def _():
+        total[...] += term
+
+    @pl.when(step == pl.num_programs(0) - 1)
+    def _():
+        image = total[...].astype(BF)
+        outgoing[...] = jnp.dot(send[...], image, preferred_element_type=F32).astype(BF)
+
+
+def merge_and_select(blocks, weight, send, tile=640):
+    depth, columns = weight.shape
     slots, count = send.shape
-    depth, columns = blocks[0].shape[1], pieces[0].shape[1]
-    vmem = pl.BlockSpec(memory_space=pltpu.VMEM)
-    return pl.pallas_call(
-        first_merge_kernel,
-        out_shape=[
-            jax.ShapeDtypeStruct((slots, columns), BF),
-            jax.ShapeDtypeStruct((count, depth), BF),
-        ],
-        in_specs=[pl.BlockSpec(memory_space=pltpu.SMEM)]
-        + [vmem] * (len(blocks) + len(pieces) + 1),
-        out_specs=[vmem, vmem],
-        scratch_shapes=[pltpu.VMEM((depth, columns), BF)],
-        compiler_params=pltpu.CompilerParams(vmem_limit_bytes=20 * 2**20),
+    return pl.pallas_call(
+        merge_kernel,
+        grid=(depth // tile,),
+        out_shape=jax.ShapeDtypeStruct((slots, columns), BF),
+        in_specs=[pl.BlockSpec((b.shape[0], tile), lambda i: (0, i)) for b in blocks]
+        + [
+            pl.BlockSpec((tile, columns), lambda i: (i, 0)),
+            pl.BlockSpec((slots, count), lambda i: (0, 0), pipeline_mode=pl.Buffered(1)),
+        ],
+        out_specs=pl.BlockSpec((slots, columns), lambda i: (0, 0)),
+        scratch_shapes=[pltpu.VMEM((count, tile), BF), pltpu.VMEM((count, columns), F32)],
+        compiler_params=pltpu.CompilerParams(vmem_limit_bytes=24 * 2**20),
         cost_estimate=pl.CostEstimate(
             flops=2 * count * (depth + slots) * columns,
             bytes_accessed=2 * (count * depth + depth * columns + slots * columns),
             transcendentals=0,
         ),
-        name="merge_first",
-    )(places, *blocks, *pieces, send)
-
-
-def merge_kernel(rows, weight, send, outgoing, total):
-    step = pl.program_id(0)
-    term = jnp.dot(rows[...], weight[...], preferred_element_type=F32)
-
-    @pl.when(step == 0)
-    def _():
-        total[...] = term
-
-    @pl.when(step > 0)
-    def _():
-        total[...] += term
-
-    @pl.when(step == pl.num_programs(0) - 1)
-    def _():
-        image = total[...].astype(BF)
-        outgoing[...] = jnp.dot(send[...], image, preferred_element_type=F32).astype(BF)
-
-
-def merge_and_select(rows, weight, send, tile=1280):
-    depth, columns = weight.shape
-    slots, count = send.shape
-    return pl.pallas_call(
-        merge_kernel,
-        grid=(depth // tile,),
-        out_shape=jax.ShapeDtypeStruct((slots, columns), BF),
-        in_specs=[
-            pl.BlockSpec((count, tile), lambda i: (0, i)),
-            pl.BlockSpec((tile, columns), lambda i: (i, 0)),
-            pl.BlockSpec((slots, count), lambda i: (0, 0), pipeline_mode=pl.Buffered(1)),
-        ],
-        out_specs=pl.BlockSpec((slots, columns), lambda i: (0, 0)),
-        scratch_shapes=[pltpu.VMEM((count, columns), F32)],
-        compiler_params=pltpu.CompilerParams(vmem_limit_bytes=24 * 2**20),
-        cost_estimate=pl.CostEstimate(
-            flops=2 * count * (depth + slots) * columns,
-            bytes_accessed=2 * (count * depth + depth * columns + slots * columns),
-            transcendentals=0,
-        ),
         name="merge_rows",
-    )(rows, weight, send)
-
-
-def pick_kernel(received, pick, usable, text, prompt, squares, *, first):
+    )(*blocks, weight, send)
+
+
+def pick_kernel(received, pick, usable, text, prompt, squares):
     arrived = received[...].reshape(pick.shape[1], received.shape[-1])
     picked = jnp.dot(pick[...], arrived, preferred_element_type=F32)
-    own = text[:, first : first + picked.shape[1]].astype(F32)
-    value = jnp.where(usable[...] > 0, picked, own)
+    value = jnp.where(usable[...] > 0, picked, text[...].astype(F32))
     prompt[...] = value.astype(BF)
     total = jnp.sum(value * value, axis=1, keepdims=True)
 
@@ -258,12 +207,11 @@
         squares[...] += total
 
 
-def pick_rows(received, pick, usable, text, first):
+def pick_rows(received, pick, usable, text):
     planes, halves, rows, part = received.shape
     count, slots = pick.shape
-    half = text.shape[1] // halves
-    return pl.pallas_call(
-        functools.partial(pick_kernel, first=first),
+    return pl.pallas_call(
+        pick_kernel,
         grid=(halves,),
         out_shape=[
             jax.ShapeDtypeStruct((count, halves * part), BF),
@@ -273,7 +221,7 @@
             pl.BlockSpec((planes, 1, rows, part), lambda h: (0, h, 0, 0)),
             pl.BlockSpec((count, slots), lambda h: (0, 0), pipeline_mode=pl.Buffered(1)),
             pl.BlockSpec((count, 1), lambda h: (0, 0), pipeline_mode=pl.Buffered(1)),
-            pl.BlockSpec((count, half), lambda h: (0, h)),
+            pl.BlockSpec((count, part), lambda h: (0, h)),
         ],
         out_specs=[
             pl.BlockSpec((count, part), lambda h: (0, h)),
@@ -289,47 +237,30 @@
     )(received, pick, usable, text)
 
 
-def finish_kernel(first, second, squares, gain, out, *, width):
+def finish_kernel(prompt, squares, gain, out, *, width):
     inverse = lax.rsqrt(squares[...] / width + EPSILON)
-    part = first.shape[1]
-    out[:, :part] = (first[...].astype(F32) * inverse * gain[:, :part]).astype(BF)
-    out[:, part:] = (second[...].astype(F32) * inverse * gain[:, part:]).astype(BF)
-
-
-def finish(first, second, squares, gain):
-    count = first.shape[0]
-    parts = first.shape[1] // 2, second.shape[1] // 2
-    half = sum(parts)
-    return pl.pallas_call(
-        functools.partial(finish_kernel, width=8 * half),
-        grid=(2,),
-        out_shape=jax.ShapeDtypeStruct((count, 2 * half), BF),
+    out[...] = (prompt[...].astype(F32) * inverse * gain[...]).astype(BF)
+
+
+def finish(prompt, squares, gain):
+    count, width = prompt.shape
+    part = width // 4
+    return pl.pallas_call(
+        functools.partial(finish_kernel, width=4 * width),
+        grid=(4,),
+        out_shape=jax.ShapeDtypeStruct((count, width), BF),
         in_specs=[
-            pl.BlockSpec((count, parts[0]), lambda h: (0, h)),
-            pl.BlockSpec((count, parts[1]), lambda h: (0, h)),
+            pl.BlockSpec((count, part), lambda h: (0, h)),
             pl.BlockSpec((count, 1), lambda h: (0, 0)),
-            pl.BlockSpec((1, half), lambda h: (0, h)),
-        ],
-        out_specs=pl.BlockSpec((count, half), lambda h: (0, h)),
-        compiler_params=pltpu.CompilerParams(vmem_limit_bytes=14 * 2**20),
-        cost_estimate=pl.CostEstimate(
-            flops=6 * count * half, bytes_accessed=8 * count * half, transcendentals=count
+            pl.BlockSpec((1, part), lambda h: (0, h)),
+        ],
+        out_specs=pl.BlockSpec((count, part), lambda h: (0, h)),
+        compiler_params=pltpu.CompilerParams(vmem_limit_bytes=10 * 2**20),
+        cost_estimate=pl.CostEstimate(
+            flops=3 * count * width, bytes_accessed=4 * count * width, transcendentals=count
         ),
         name="finish",
-    )(first, second, squares, gain[None, :])
-
-
-def shift(block, axis, d):
-    return lax.ppermute(block, axis, [(i, (i + d) % 4) for i in range(4)])
-
-
-def ring_near(block, axis):
-    return [shift(block, axis, 1), shift(block, axis, -1)]
-
-
-def ring_far(before, after, axis):
-    n = before.shape[0] // 2
-    return [shift(before[:n], axis, 1), shift(after[n:], axis, -1)]
+    )(prompt, squares, gain[None, :])
 
 
 def swap_tp(block, k):
@@ -363,8 +294,7 @@
     half = merge_weight.shape[1] // 2
     own = lax.dynamic_slice_in_dim(merge_weight, yh * half, half, 1)
     other = lax.dynamic_slice_in_dim(merge_weight, (1 - yh) * half, half, 1)
-    swap = lambda block: lax.ppermute(block, "yh", [(0, 1), (1, 0)])
-    arrived = [swap(other[:, FIRST:]), swap(other[:, :FIRST])]
+    arrived = lax.ppermute(other, "yh", [(0, 1), (1, 0)])
 
     prompt_rows = image_refs.shape[0]
     usable = image_refs >= 0
@@ -384,26 +314,19 @@
         (arrived, table, pick, usable, out_weight)
     )
     is_own = (jnp.arange(2) == yh)[:, None, None]
-    second = jnp.where(is_own, own[None, :, FIRST:], arrived[0][None]).reshape(-1, half - FIRST)
-    first = jnp.where(is_own, own[None, :, :FIRST], arrived[1][None]).reshape(-1, FIRST)
-    second_weight = lax.all_gather(second, ("z", "x"), axis=0, tiled=True)
-    near_z = ring_near(first, "z")
+    both = jnp.where(is_own, own[None], arrived[None]).reshape(-1, half)
+    weight = lax.all_gather(both, ("z", "x"), axis=0, tiled=True)
 
     out_far = lax.ppermute(out_weight, "yl", [(0, 1), (1, 0)])
     out_blocks = [out_weight, swap_core(out_weight), out_far, swap_core(out_far)]
 
-    patches, first, second = lax.optimization_barrier((patches, first, second))
+    patches, both = lax.optimization_barrier((patches, both))
     context = vision_context(patches, jnp.swapaxes(qkv_weight, 1, 2), image_ids)
-    context, near_z = lax.optimization_barrier((context, near_z))
-    far_z = ring_far(*near_z, "z")
     rows = context.shape[0] // 4
     parts = [
         lax.dynamic_slice_in_dim(context, (tp ^ k) * rows, rows, 0) for k in range(4)
     ]
     parts = [parts[0]] + [swap_tp(parts[k], k) for k in (1, 2, 3)]
-    parts, far_z = lax.optimization_barrier((parts, far_z))
-    all_z = jnp.concatenate([first] + near_z + far_z, axis=0)
-    near_x = ring_near(all_z, "x")
     merged, top, bottom = project_and_norm(tp, parts, out_blocks, patches, merge_gain)
 
     table, merged, top, bottom = lax.optimization_barrier((table, merged, top, bottom))
@@ -415,11 +338,6 @@
         (2, top.shape[0], shift_y(bottom, -2)),
     ]
     table = lax.all_to_all(table, SEC, split_axis=0, concat_axis=0, tiled=True)
-    far_x = ring_far(*near_x, "x")
-    near = jnp.array([0, -1, 1, 2])
-    z_of = (lax.axis_index("z") + near) % 4
-    x_of = (lax.axis_index("x") + near) % 4
-    places = (z_of[None, :] * 4 + x_of[:, None]).reshape(-1).astype(jnp.int32)
     blocks = []
     ids = []
     for d, offset, block in near_rows:
@@ -432,19 +350,13 @@
     wanted = jnp.where(wanted >= 0, wanted + jnp.arange(2)[None, :, None] * 256, -1).reshape(-1)
     send = (wanted[:, None] == row_ids[None, :]).astype(BF)
 
-    def route(outgoing, offset):
-        received = lax.all_to_all(outgoing, SEC, split_axis=0, concat_axis=0, tiled=True)
-        received = received.reshape(16, 2, 32, -1)
-        return pick_rows(received, pick, usable, text_rows, offset)
-
-    outgoing, all_rows = first_merge(places, blocks, [all_z] + near_x + far_x, send)
-    first_prompt, first_squares = route(outgoing, 0)
-    outgoing = merge_and_select(all_rows, second_weight, send)
-    second_prompt, second_squares = route(outgoing, FIRST)
-    squares = first_squares + second_squares
+    outgoing = merge_and_select(blocks, weight, send)
+    received = lax.all_to_all(outgoing, SEC, split_axis=0, concat_axis=0, tiled=True)
+    received = received.reshape(16, 2, 32, half)
+    prompt, squares = pick_rows(received, pick, usable, text_rows)
     flat = squares.reshape(4, -1)
     total = flat + swap_tp(flat, 1) + swap_tp(flat, 2) + swap_tp(flat, 3)
-    return finish(first_prompt, second_prompt, total.reshape(squares.shape), llm_gain)
+    return finish(prompt, total.reshape(squares.shape), llm_gain)
 
 
 def solution(mesh):

time: 213 us -> 196 us (0.920)
  starting transfers between devices: 55.4 us -> 38.9 us
  waiting for transfers between devices: 75.6 us -> 82.7 us
  local copies, waits for them, and re-layouts: 24.5 us -> 20.6 us
  Pallas kernels: 37.3 us -> 34.6 us
    ppermute x10 -> x1, waiting for transfers between devices: 36.1 us -> 5.02 us  [on_device(): arrived = lax.ppermute(other, 'yh', [(0, 1), (1, 0)])]
    ppermute x4, waiting for transfers between devices: 0.01 us -> 19.3 us  [shift_y(): lax.ppermute(block, ('yh', 'yl'), [(i, (i + d) % 4) for i in range(4)])]
    ppermute x1, waiting for transfers between devices: 0.01 us -> 14.1 us  [on_device(): out_far = lax.ppermute(out_weight, 'yl', [(0, 1), (1, 0)])]
    ppermute x10 -> x1, starting transfers between devices: 16.3 us -> 3.74 us  [on_device(): arrived = lax.ppermute(other, 'yh', [(0, 1), (1, 0)])]
    all_to_all x2 -> x1, waiting for transfers between devices: 21.1 us -> 30.6 us  [on_device(): lax.all_to_all(outgoing, SEC, split_axis=0, concat_axis=0, tiled=True)]
    pallas_call x4 -> x2, Pallas kernels: 11.8 us -> 4.51 us  [the longest x1 2.32 us: finish(): pl.pallas_call(functools.partial(finish_kernel, width=4 * width), grid=(4...]
    all_to_all x2 -> x1, starting transfers between devices: 13.4 us -> 6.23 us  [on_device(): lax.all_to_all(outgoing, SEC, split_axis=0, concat_axis=0, tiled=True)]
    all_to_all x1, starting transfers between devices: 3.85 us -> 9.54 us  [on_device(): table = lax.all_to_all(table, SEC, split_axis=0, concat_axis=0, tiled=True)]
  transfers between devices with their start and end apart: 32 -> 22, of which waited for: 12 -> 11; matrix products, arithmetic and copies ran while one was open for 3% -> 2% of each run, Pallas kernels for 15% -> 9%
where the time goes in v6:
time: 196 us; the launch traced here: 195 us
  waiting for transfers between devices  82.7 us (42%)
  starting transfers between devices  38.9 us (20%)
  Pallas kernels  34.6 us (18%)
  local copies, waits for them, and re-layouts  20.6 us (11%)
  between operations  13.6 us (7%)
  other arithmetic  3.97 us (2%)
    all_to_all x1, waiting for transfers between devices, on_device(): lax.all_to_all(outgoing, SEC, split_axis=0, concat_axis=0, tiled=True)  30.6 us
    ppermute x4, waiting for transfers between devices, shift_y(): lax.ppermute(block, ('yh', 'yl'), [(i, (i + d) % 4) for i in range(4)])  19.3 us
    unnamed x32, local copies, waits for them, and re-layouts  16 us
    ppermute x1, waiting for transfers between devices, on_device(): out_far = lax.ppermute(out_weight, 'yl', [(0, 1), (1, 0)])  14.1 us
    pallas_call x1, Pallas kernels, vision_context(): pl.pallas_call(attention_kernel, out_shape=jax.ShapeDtypeStruct((row_coun...  14 us
    pallas_call x1, Pallas kernels, merge_and_select(): pl.pallas_call(merge_kernel, grid=(depth // tile,), out_shape=jax.ShapeDt...  12.1 us
    ppermute x6, waiting for transfers between devices, swap_tp(): return lax.ppermute(block, TP, [(i, i ^ k) for i in range(4)])  11.4 us
    all_to_all x1, starting transfers between devices, on_device(): table = lax.all_to_all(table, SEC, split_axis=0, concat_axis=0, tiled=True)  9.54 us
  transfers between devices with their start and end apart: 22, of which 11 were waited for; matrix products, arithmetic and copies ran while one was open for 2% of the time, Pallas kernels for 9%

profile of v6, /device:TPU:1, one launch (start us, length us, event | category | flops | bytes accessed | tf_op | source)
XLA Modules:
  0.0 195.0 jit_solution(2731349642881196584)
XLA Ops:
  6.5 1.9 constant_dynamic-slice_fusion.4
  8.4 3.7 %collective-permute-start = (bf16[160,1024]{1,0:T(8,128)(2,1)}, bf16[160,1024]{1,0:T(8,128)(2,1)}, u32[]{:S(2)}, u32[]{:S(2)}) collective-permute-start(bf16[160,1024]{1,0:T(8,128)(2,1)} %get-tuple-element.42), channel_id=1, source_target_pairs={{0,4},{4,0},{1,5},{5,1},{2,6},{6,2},{3,7},{7,3},{8,12},{12,8},{9,1... | collective-permute-start | bytes 983048 | tf_op jit(solution)/shard_map/ppermute | solution.py:297
  14.6 5.0 %collective-permute-done = bf16[160,1024]{1,0:T(8,128)(2,1)} collective-permute-done((bf16[160,1024]{1,0:T(8,128)(2,1)}, bf16[160,1024]{1,0:T(8,128)(2,1)}, u32[]{:S(2)}, u32[]{:S(2)}) %collective-permute-start) | collective-permute-done | bytes 327712 | tf_op jit(solution)/shard_map/ppermute | solution.py:297
  20.2 2.0 %bitcast_select_fusion = bf16[320,1024]{1,0:T(8,128)(2,1)} fusion(pred[320]{0:T(512)(128)(4,1)S(1)} %broadcast_in_dim.78, bf16[160,1024]{1,0:T(8,128)(2,1)} %collective-permute-done, bf16[160,1024]{1,0:T(8,128)(2,1)S(1)} %get-tuple-element.41), kind=kLoop, calls=%fused_computation.7 | loop fusion | flops 327680 | bytes 1311040 | tf_op jit(solution)/shard_map/jit(_where)/select_n | solution.py:317
  22.2 1.4 collective-permute-start.5
  24.8 1.9 collective-permute-start.4
  26.7 14.1 %collective-permute-done.5.refs_7_ = bf16[320,1280]{1,0:T(8,128)(2,1)} collective-permute-done((bf16[320,1280]{1,0:T(8,128)(2,1)}, bf16[320,1280]{1,0:T(8,128)(2,1)}, u32[]{:S(2)}, u32[]{:S(2)}) %collective-permute-start.5) | collective-permute-done | bytes 819232 | tf_op jit(solution)/shard_map/ppermute | solution.py:320
  40.8 2.4 %collective-permute-start.6 = (bf16[320,1280]{1,0:T(8,128)(2,1)}, bf16[320,1280]{1,0:T(8,128)(2,1)S(1)}, u32[]{:S(2)}, u32[]{:S(2)}) collective-permute-start(bf16[320,1280]{1,0:T(8,128)(2,1)} %collective-permute-done.5.refs_7_), channel_id=1, source_target_pairs={{0,1},{1,0},{2,3},{3,2},{4,5},{5,4},{6,7},{7,6},{8,9},{9,8},{10,11... | collective-permute-start | bytes 2457608 | tf_op jit(solution)/shard_map/ppermute | solution.py:275
  44.3 1.7 copy-done.9
  46.0 14.0 %vision_attention.1 = bf16[1024,320]{1,0:T(8,128)(2,1)S(1)} custom-call(s32[1024,1]{1,0:T(8,128)S(1)} %copy-done.6, s32[1,1024]{1,0:T(1,128)S(1)} %broadcast_in_dim_reshape.8.column_ids, bf16[1024,1280]{1,0:T(8,128)(2,1)S(1)} %copy-done, bf16[3,320,1280]{2,1,0:T(8,128)(2,1)S(1)} %bitcast.21), custom_call_target="tpu_custom_call" | custom-call | flops 6811549696 | bytes 5079040 | tf_op jit(solution)/shard_map/vision_attention/pallas_call | solution.py:71
  60.3 1.4 collective-permute-start.2
  62.4 4.1 %collective-permute-done.2.refs_3_ = bf16[256,320]{1,0:T(8,128)(2,1)S(1)} collective-permute-done((bf16[256,320]{1,0:T(8,128)(2,1)S(1)}, bf16[256,320]{1,0:T(8,128)(2,1)S(1)}, u32[]{:S(2)}, u32[]{:S(2)}) %collective-permute-start.2) | collective-permute-done | bytes 163872 | tf_op jit(solution)/shard_map/ppermute | solution.py:267
  66.5 5.1 %collective-permute-done.3.refs_4_ = bf16[256,320]{1,0:T(8,128)(2,1)S(1)} collective-permute-done((bf16[256,320]{1,0:T(8,128)(2,1)S(1)}, bf16[256,320]{1,0:T(8,128)(2,1)S(1)}, u32[]{:S(2)}, u32[]{:S(2)}) %collective-permute-start.3) | collective-permute-done | bytes 163872 | tf_op jit(solution)/shard_map/ppermute | solution.py:267
  71.6 4.0 %project_and_norm.1 = (bf16[64,5120]{1,0:T(8,128)(2,1)}, bf16[32,5120]{1,0:T(8,128)(2,1)}, bf16[32,5120]{1,0:T(8,128)(2,1)}) custom-call(s32[1]{0:T(128)} %bitcast.3.refs_0_, bf16[256,320]{1,0:T(8,128)(2,1)S(1)} %get-tuple-element.40.refs_1_, bf16[256,320]{1,0:T(8,128)(2,1)S(1)} %collective-permute-done.1.refs_2_, ...), custom_call_target="tpu_custom_call" | custom-call | flops 838860800 | bytes 5242880 | tf_op jit(solution)/shard_map/project_and_norm/pallas_call | solution.py:117
  75.6 2.7 %collective-permute-start.10 = (bf16[64,5120]{1,0:T(8,128)(2,1)}, bf16[64,5120]{1,0:T(8,128)(2,1)S(1)}, u32[]{:S(2)}, u32[]{:S(2)}) collective-permute-start(bf16[64,5120]{1,0:T(8,128)(2,1)} %get-tuple-element.27.refs_0_), channel_id=1, source_target_pairs={{0,6},{2,0},{4,2},{6,4},{1,7},{3,1},{5,3},{7,5},{8,14},{10,8},{12,... | collective-permute-start | bytes 1966088 | tf_op jit(solution)/shard_map/ppermute | solution.py:271
  78.4 1.7 collective-permute-start.12
  80.1 1.3 collective-permute-start.14
  81.7 9.5 %all-to-all-start = ((s32[32,1,32]{2,1,0:T(1,128)}), s32[32,1,32]{2,1,0:T(1,128)S(1)}, u32[]{:S(2)}, u32[]{:S(2)}) async-start(s32[32,1,32]{2,1,0:T(1,128)} %bitcast.8), calls=%async_computation | async-start | bytes 32768 | tf_op jit(solution)/shard_map/all_to_all | solution.py:340
  91.2 16.1 %collective-permute-done.10.refs_4_ = bf16[64,5120]{1,0:T(8,128)(2,1)S(1)} collective-permute-done((bf16[64,5120]{1,0:T(8,128)(2,1)}, bf16[64,5120]{1,0:T(8,128)(2,1)S(1)}, u32[]{:S(2)}, u32[]{:S(2)}) %collective-permute-start.10) | collective-permute-done | bytes 655392 | tf_op jit(solution)/shard_map/ppermute | solution.py:271
  107.4 3.2 %collective-permute-done.8.refs_2_ = bf16[64,5120]{1,0:T(8,128)(2,1)S(1)} collective-permute-done((bf16[64,5120]{1,0:T(8,128)(2,1)}, bf16[64,5120]{1,0:T(8,128)(2,1)S(1)}, u32[]{:S(2)}, u32[]{:S(2)}) %collective-permute-start.8) | collective-permute-done | bytes 655392 | tf_op jit(solution)/shard_map/ppermute | solution.py:271
  116.7 4.0 %copy-done.8 = bf16[5120,1024]{1,0:T(8,128)(2,1)S(1)} copy-done((bf16[5120,1024]{1,0:T(8,128)(2,1)S(1)}, bf16[5120,1024]{1,0:T(8,128)(2,1)}, u32[]{:S(2)}) %copy-start.8) | copy-done | bytes 10485784
  122.6 12.1 %merge_rows.1 = bf16[1024,1024]{1,0:T(8,128)(2,1)S(1)} custom-call(bf16[64,5120]{1,0:T(8,128)(2,1)} %get-tuple-element.27.refs_0_, bf16[64,5120]{1,0:T(8,128)(2,1)S(1)} %collective-permute-done.7.refs_1_, bf16[64,5120]{1,0:T(8,128)(2,1)S(1)} %collective-permute-done.8.refs_2_, bf16[64,5120]{1,0:T(8,128)(2,1)} %collective-permute-done.9.refs_3_, ...), custom_call_target="tpu_custom_call" | custom-call | flops 6442450944 | bytes 17825792 | tf_op jit(solution)/shard_map/merge_rows/pallas_call | solution.py:173
  134.7 1.3 copy-done.4
  136.0 6.2 %all-to-all-start.1 = ((bf16[32,32,1024]{2,1,0:T(8,128)(2,1)}), bf16[32,32,1024]{2,1,0:T(8,128)(2,1)S(1)}, u32[]{:S(2)}, u32[]{:S(2)}) async-start(bf16[32,32,1024]{2,1,0:T(8,128)(2,1)} %bitcast.19), calls=%async_computation.1 | async-start | bytes 4194304 | tf_op jit(solution)/shard_map/all_to_all | solution.py:354
  142.4 30.6 %all-to-all-done.1 = bf16[32,32,1024]{2,1,0:T(8,128)(2,1)S(1)} async-done(((bf16[32,32,1024]{2,1,0:T(8,128)(2,1)}), bf16[32,32,1024]{2,1,0:T(8,128)(2,1)S(1)}, u32[]{:S(2)}, u32[]{:S(2)}) %all-to-all-start.1) | async-done | bytes 2097184 | tf_op jit(solution)/shard_map/all_to_all | solution.py:354
  173.0 1.6 copy-done.1
  174.6 2.2 %pick_rows.1 = (bf16[512,2048]{1,0:T(8,128)(2,1)S(1)}, f32[512,1]{1,0:T(8,128)S(1)}) custom-call(bf16[16,2,32,1024]{3,2,1,0:T(8,128)(2,1)S(1)} %bitcast.18, bf16[512,512]{1,0:T(8,128)(2,1)S(1)} %fusion.1.pick, s32[512,1]{1,0:T(8,128)S(1)} %copy.14.usable, bf16[512,2048]{1,0:T(8,128)(2,1)S(1)} %copy-done.1), custom_call_target="tpu_custom_call" | custom-call | flops 1073741824 | bytes 6291456 | tf_op jit(solution)/shard_map/pick_rows/pallas_call | solution.py:213
  176.8 1.3 copy-done.2
  178.3 1.8 collective-permute-start.16
  182.6 1.5 collective-permute-done.18
  184.3 1.6 copy-done.3
  185.9 2.3 %finish.1 = bf16[512,2048]{1,0:T(8,128)(2,1)} custom-call(bf16[512,2048]{1,0:T(8,128)(2,1)S(1)} %copy-done.3, f32[512,1]{1,0:T(8,128)S(1)} %copy.15.squares, f32[1,2048]{1,0:T(1,128)S(1)} %bitcast.20), custom_call_target="tpu_custom_call" | custom-call | flops 3145728 | bytes 4194304 | tf_op jit(solution)/shard_map/finish/pallas_call | solution.py:248
  (87 shorter events, 17.5 us)
Async XLA Ops:
  6.5 110.1 %all-gather.2.cloned.1.call-start = ((), (), s32[]{:S(2)}) async-start(), calls=%async_computation.2 | async-start | bytes 11141120 | tf_op jit(solution)/shard_map/all_gather | solution.py:318
  6.5 17.0 %copy-start.15 = (s32[1,256]{1,0:T(1,128)S(1)}, s32[1,256]{1,0:T(1,128)}, u32[]{:S(2)}) copy-start(s32[1,256]{1,0:T(1,128)} %param.10) | copy-start | bytes 3076
  8.4 34.8 %copy-start = (bf16[1024,1280]{1,0:T(8,128)(2,1)S(1)}, bf16[1024,1280]{1,0:T(8,128)(2,1)}, u32[]{:S(2)}) copy-start(bf16[1024,1280]{1,0:T(8,128)(2,1)} %refs_9_) | copy-start | bytes 7864324
  8.4 11.2 %collective-permute-start = (bf16[160,1024]{1,0:T(8,128)(2,1)}, bf16[160,1024]{1,0:T(8,128)(2,1)}, u32[]{:S(2)}, u32[]{:S(2)}) collective-permute-start(bf16[160,1024]{1,0:T(8,128)(2,1)} %get-tuple-element.42), channel_id=1, source_target_pairs={{0,4},{4,0},{1,5},{5,1},{2,6},{6,2},{3,7},{7,3},{8,12},{12,8},{9,1... | collective-permute-start | bytes 983048 | tf_op jit(solution)/shard_map/ppermute | solution.py:297
  22.2 18.6 %collective-permute-start.5 = (bf16[320,1280]{1,0:T(8,128)(2,1)}, bf16[320,1280]{1,0:T(8,128)(2,1)}, u32[]{:S(2)}, u32[]{:S(2)}) collective-permute-start(bf16[320,1280]{1,0:T(8,128)(2,1)} %refs_5_), channel_id=1, source_target_pairs={{0,2},{2,0},{1,3},{3,1},{4,6},{6,4},{5,7},{7,5},{8,10},{10,8},{9,1... | collective-permute-start | bytes 2457608 | tf_op jit(solution)/shard_map/ppermute | solution.py:320
  24.8 46.8 %collective-permute-start.4 = (bf16[320,1280]{1,0:T(8,128)(2,1)}, bf16[320,1280]{1,0:T(8,128)(2,1)S(1)}, u32[]{:S(2)}, u32[]{:S(2)}) collective-permute-start(bf16[320,1280]{1,0:T(8,128)(2,1)} %refs_5_), channel_id=1, source_target_pairs={{0,1},{1,0},{2,3},{3,2},{4,5},{5,4},{6,7},{7,6},{8,9},{9,8},{10,11... | collective-permute-start | bytes 2457608 | tf_op jit(solution)/shard_map/ppermute | solution.py:275
  40.8 30.8 %collective-permute-start.6 = (bf16[320,1280]{1,0:T(8,128)(2,1)}, bf16[320,1280]{1,0:T(8,128)(2,1)S(1)}, u32[]{:S(2)}, u32[]{:S(2)}) collective-permute-start(bf16[320,1280]{1,0:T(8,128)(2,1)} %collective-permute-done.5.refs_7_), channel_id=1, source_target_pairs={{0,1},{1,0},{2,3},{3,2},{4,5},{5,4},{6,7},{7,6},{8,9},{9,8},{10,11... | collective-permute-start | bytes 2457608 | tf_op jit(solution)/shard_map/ppermute | solution.py:275
  44.3 1.7 copy-start.9
  46.0 16.4 %copy-start.14 = (f32[1280]{0:T(1024)S(1)}, f32[1280]{0:T(1024)}, u32[]{:S(2)}) copy-start(f32[1280]{0:T(1024)} %param.13) | copy-start | bytes 15364
  60.1 11.5 %copy-start.5 = (bf16[320,1280]{1,0:T(8,128)(2,1)S(1)}, bf16[320,1280]{1,0:T(8,128)(2,1)}, u32[]{:S(2)}) copy-start(bf16[320,1280]{1,0:T(8,128)(2,1)} %refs_5_) | copy-start | bytes 2457604
  60.2 2.2 %collective-permute-start.1 = (bf16[256,320]{1,0:T(8,128)(2,1)S(1)}, bf16[256,320]{1,0:T(8,128)(2,1)S(1)}, u32[]{:S(2)}, u32[]{:S(2)}) collective-permute-start(bf16[256,320]{1,0:T(8,128)(2,1)S(1)} %get-tuple-element.39), channel_id=1, source_target_pairs={{0,1},{1,0},{2,3},{3,2},{4,5},{5,4},{6,7},{7,6},{8,9},{9,8},{10,11... | collective-permute-start | bytes 491528 | tf_op jit(solution)/shard_map/ppermute | solution.py:267
  60.3 6.2 %collective-permute-start.2 = (bf16[256,320]{1,0:T(8,128)(2,1)S(1)}, bf16[256,320]{1,0:T(8,128)(2,1)S(1)}, u32[]{:S(2)}, u32[]{:S(2)}) collective-permute-start(bf16[256,320]{1,0:T(8,128)(2,1)S(1)} %get-tuple-element.38), channel_id=1, source_target_pairs={{0,2},{1,3},{2,0},{3,1},{4,6},{5,7},{6,4},{7,5},{8,10},{9,11},{10,... | collective-permute-start | bytes 491528 | tf_op jit(solution)/shard_map/ppermute | solution.py:267
  61.7 9.9 %collective-permute-start.3 = (bf16[256,320]{1,0:T(8,128)(2,1)S(1)}, bf16[256,320]{1,0:T(8,128)(2,1)S(1)}, u32[]{:S(2)}, u32[]{:S(2)}) collective-permute-start(bf16[256,320]{1,0:T(8,128)(2,1)S(1)} %get-tuple-element.37), channel_id=1, source_target_pairs={{0,3},{1,2},{2,1},{3,0},{4,7},{5,6},{6,5},{7,4},{8,11},{9,10},{10,... | collective-permute-start | bytes 491528 | tf_op jit(solution)/shard_map/ppermute | solution.py:267
  75.6 31.7 %collective-permute-start.10 = (bf16[64,5120]{1,0:T(8,128)(2,1)}, bf16[64,5120]{1,0:T(8,128)(2,1)S(1)}, u32[]{:S(2)}, u32[]{:S(2)}) collective-permute-start(bf16[64,5120]{1,0:T(8,128)(2,1)} %get-tuple-element.27.refs_0_), channel_id=1, source_target_pairs={{0,6},{2,0},{4,2},{6,4},{1,7},{3,1},{5,3},{7,5},{8,14},{10,8},{12,... | collective-permute-start | bytes 1966088 | tf_op jit(solution)/shard_map/ppermute | solution.py:271
  78.4 32.3 %collective-permute-start.8 = (bf16[64,5120]{1,0:T(8,128)(2,1)}, bf16[64,5120]{1,0:T(8,128)(2,1)S(1)}, u32[]{:S(2)}, u32[]{:S(2)}) collective-permute-start(bf16[64,5120]{1,0:T(8,128)(2,1)} %get-tuple-element.27.refs_0_), channel_id=1, source_target_pairs={{0,2},{2,4},{4,6},{6,0},{1,3},{3,5},{5,7},{7,1},{8,10},{10,12},{12... | collective-permute-start | bytes 1966088 | tf_op jit(solution)/shard_map/ppermute | solution.py:271
  78.4 34.5 %collective-permute-start.12 = (bf16[32,5120]{1,0:T(8,128)(2,1)}, bf16[32,5120]{1,0:T(8,128)(2,1)}, u32[]{:S(2)}, u32[]{:S(2)}) collective-permute-start(bf16[32,5120]{1,0:T(8,128)(2,1)} %get-tuple-element.28), channel_id=1, source_target_pairs={{0,4},{2,6},{4,0},{6,2},{1,5},{3,7},{5,1},{7,3},{8,12},{10,14},{12... | collective-permute-start | bytes 983048 | tf_op jit(solution)/shard_map/ppermute | solution.py:271
  80.1 33.7 %collective-permute-start.14 = (bf16[32,5120]{1,0:T(8,128)(2,1)}, bf16[32,5120]{1,0:T(8,128)(2,1)}, u32[]{:S(2)}, u32[]{:S(2)}) collective-permute-start(bf16[32,5120]{1,0:T(8,128)(2,1)} %get-tuple-element.29), channel_id=1, source_target_pairs={{0,4},{2,6},{4,0},{6,2},{1,5},{3,7},{5,1},{7,3},{8,12},{10,14},{12... | collective-permute-start | bytes 983048 | tf_op jit(solution)/shard_map/ppermute | solution.py:271
  81.5 35.2 %collective-permute-start.7 = (bf16[64,5120]{1,0:T(8,128)(2,1)}, bf16[64,5120]{1,0:T(8,128)(2,1)S(1)}, u32[]{:S(2)}, u32[]{:S(2)}) collective-permute-start(bf16[64,5120]{1,0:T(8,128)(2,1)} %get-tuple-element.27.refs_0_), channel_id=1, source_target_pairs={{0,1},{1,0},{2,3},{3,2},{4,5},{5,4},{6,7},{7,6},{8,9},{9,8},{10,11... | collective-permute-start | bytes 1966088 | tf_op jit(solution)/shard_map/ppermute | solution.py:275
  81.7 31.0 %all-to-all-start = ((s32[32,1,32]{2,1,0:T(1,128)}), s32[32,1,32]{2,1,0:T(1,128)S(1)}, u32[]{:S(2)}, u32[]{:S(2)}) async-start(s32[32,1,32]{2,1,0:T(1,128)} %bitcast.8), calls=%async_computation | async-start | bytes 32768 | tf_op jit(solution)/shard_map/all_to_all | solution.py:340
  107.3 9.4 %collective-permute-start.11 = (bf16[64,5120]{1,0:T(8,128)(2,1)S(1)}, bf16[64,5120]{1,0:T(8,128)(2,1)}, u32[]{:S(2)}, u32[]{:S(2)}) collective-permute-start(bf16[64,5120]{1,0:T(8,128)(2,1)S(1)} %collective-permute-done.10.refs_4_), channel_id=1, source_target_pairs={{0,1},{1,0},{2,3},{3,2},{4,5},{5,4},{6,7},{7,6},{8,9},{9,8},{10,11... | collective-permute-start | bytes 1966088 | tf_op jit(solution)/shard_map/ppermute | solution.py:275
  110.6 6.0 %collective-permute-start.9 = (bf16[64,5120]{1,0:T(8,128)(2,1)S(1)}, bf16[64,5120]{1,0:T(8,128)(2,1)}, u32[]{:S(2)}, u32[]{:S(2)}) collective-permute-start(bf16[64,5120]{1,0:T(8,128)(2,1)S(1)} %collective-permute-done.8.refs_2_), channel_id=1, source_target_pairs={{0,1},{1,0},{2,3},{3,2},{4,5},{5,4},{6,7},{7,6},{8,9},{9,8},{10,11... | collective-permute-start | bytes 1966088 | tf_op jit(solution)/shard_map/ppermute | solution.py:275
  112.8 2.4 %collective-permute-start.13 = (bf16[32,5120]{1,0:T(8,128)(2,1)}, bf16[32,5120]{1,0:T(8,128)(2,1)S(1)}, u32[]{:S(2)}, u32[]{:S(2)}) collective-permute-start(bf16[32,5120]{1,0:T(8,128)(2,1)} %collective-permute-done.12.refs_6_), channel_id=1, source_target_pairs={{0,1},{1,0},{2,3},{3,2},{4,5},{5,4},{6,7},{7,6},{8,9},{9,8},{10,11... | collective-permute-start | bytes 983048 | tf_op jit(solution)/shard_map/ppermute | solution.py:275
  113.8 2.2 %collective-permute-start.15 = (bf16[32,5120]{1,0:T(8,128)(2,1)}, bf16[32,5120]{1,0:T(8,128)(2,1)S(1)}, u32[]{:S(2)}, u32[]{:S(2)}) collective-permute-start(bf16[32,5120]{1,0:T(8,128)(2,1)} %collective-permute-done.14.refs_8_), channel_id=1, source_target_pairs={{0,1},{1,0},{2,3},{3,2},{4,5},{5,4},{6,7},{7,6},{8,9},{9,8},{10,11... | collective-permute-start | bytes 983048 | tf_op jit(solution)/shard_map/ppermute | solution.py:275
  116.7 4.0 %copy-start.8 = (bf16[5120,1024]{1,0:T(8,128)(2,1)S(1)}, bf16[5120,1024]{1,0:T(8,128)(2,1)}, u32[]{:S(2)}) copy-start(bf16[5120,1024]{1,0:T(8,128)(2,1)} %all-gather.2.cloned.1.call-done.refs_10_) | copy-start | bytes 31457284
  134.7 1.3 copy-start.4
  136.0 37.0 %all-to-all-start.1 = ((bf16[32,32,1024]{2,1,0:T(8,128)(2,1)}), bf16[32,32,1024]{2,1,0:T(8,128)(2,1)S(1)}, u32[]{:S(2)}, u32[]{:S(2)}) async-start(bf16[32,32,1024]{2,1,0:T(8,128)(2,1)} %bitcast.19), calls=%async_computation.1 | async-start | bytes 4194304 | tf_op jit(solution)/shard_map/all_to_all | solution.py:354
  173.0 1.6 copy-start.1
  174.6 9.6 %copy-start.7 = (f32[2048]{0:T(1024)S(1)}, f32[2048]{0:T(1024)}, u32[]{:S(2)}) copy-start(f32[2048]{0:T(1024)} %param.17) | copy-start | bytes 24580
  178.3 3.6 %collective-permute-start.16 = (f32[4,128]{1,0:T(4,128)S(1)}, f32[4,128]{1,0:T(4,128)S(1)}, u32[]{:S(2)}, u32[]{:S(2)}) collective-permute-start(f32[4,128]{1,0:T(4,128)S(1)} %bitcast.22), channel_id=1, source_target_pairs={{0,1},{1,0},{2,3},{3,2},{4,5},{5,4},{6,7},{7,6},{8,9},{9,8},{10,11... | collective-permute-start | bytes 6152 | tf_op jit(solution)/shard_map/ppermute | solution.py:267
  180.1 2.5 %collective-permute-start.17 = (f32[4,128]{1,0:T(4,128)S(1)}, f32[4,128]{1,0:T(4,128)S(1)}, u32[]{:S(2)}, u32[]{:S(2)}) collective-permute-start(f32[4,128]{1,0:T(4,128)S(1)} %bitcast.23), channel_id=1, source_target_pairs={{0,2},{1,3},{2,0},{3,1},{4,6},{5,7},{6,4},{7,5},{8,10},{9,11},{10,... | collective-permute-start | bytes 6152 | tf_op jit(solution)/shard_map/ppermute | solution.py:267
  181.1 3.0 %collective-permute-start.18 = (f32[4,128]{1,0:T(4,128)S(1)}, f32[4,128]{1,0:T(4,128)S(1)}, u32[]{:S(2)}, u32[]{:S(2)}) collective-permute-start(f32[4,128]{1,0:T(4,128)S(1)} %bitcast.24), channel_id=1, source_target_pairs={{0,3},{1,2},{2,1},{3,0},{4,7},{5,6},{6,5},{7,4},{8,11},{9,10},{10,... | collective-permute-start | bytes 6152 | tf_op jit(solution)/shard_map/ppermute | solution.py:267
  184.3 1.6 copy-start.3
  (6 other events, 5.7 us)
Sparse Core Ops, SparseCore 0:
  22.3 83.9 all-gather.1

commit v7 on v6

--- a/solution.py
+++ b/solution.py
@@ -17,40 +17,53 @@
 F32 = jnp.float32
 
 
-def attention_kernel(row_ids, column_ids, patches, weight, context, queries, keys, values):
+def project_kernel(patches, weight, projected):
+    projected[0] = lax.dot_general(
+        patches[...], weight[0], (((1,), (1,)), ((), ())), preferred_element_type=F32
+    ).astype(BF)
+
+
+def project(patches, weight):
+    rows, depth = patches.shape
+    count, width, _ = weight.shape
+    return pl.pallas_call(
+        project_kernel,
+        grid=(count,),
+        out_shape=jax.ShapeDtypeStruct((count, rows, width), BF),
+        in_specs=[
+            pl.BlockSpec((rows, depth), lambda i: (0, 0), pipeline_mode=pl.Buffered(1)),
+            pl.BlockSpec((1, width, depth), lambda i: (i, 0, 0)),
+        ],
+        out_specs=pl.BlockSpec((1, rows, width), lambda i: (i, 0, 0)),
+        compiler_params=pltpu.CompilerParams(vmem_limit_bytes=14 * 2**20),
+        cost_estimate=pl.CostEstimate(
+            flops=2 * rows * depth * width * count,
+            bytes_accessed=2 * (rows * depth + count * width * (depth + rows)),
+            transcendentals=0,
+        ),
+        name="project_qkv",
+    )(patches, weight)
+
+
+def attention_kernel(row_ids, column_ids, projected, context, keys, values):
     heads = keys.shape[0]
-    row_count = patches.shape[0]
+    row_count = projected.shape[1]
+    one = jnp.ones((row_count, 128 - HEAD_DIM), BF)
+    for head in range(heads):
+        columns = slice(head * HEAD_DIM, (head + 1) * HEAD_DIM)
+        keys[head] = projected[1, :, columns]
+        values[head] = jnp.concatenate([projected[2, :, columns], one], axis=1)
+    scale = HEAD_DIM ** (-0.5) * LOG2E
     block = min(256, row_count)
-    one = jnp.ones((block, 128 - HEAD_DIM), BF)
-
-    def project(index, carry):
-        rows = pl.ds(pl.multiple_of(index * block, block), block)
-        query, key, value = (
-            lax.dot_general(
-                patches[rows, :], weight[c], (((1,), (1,)), ((), ())), preferred_element_type=F32
-            ).astype(BF)
-            for c in range(3)
-        )
-        for head in range(heads):
-            columns = slice(head * HEAD_DIM, (head + 1) * HEAD_DIM)
-            queries[head, rows, :] = query[:, columns]
-            keys[head, rows, :] = key[:, columns]
-            values[head, rows, :] = jnp.concatenate([value[:, columns], one], axis=1)
-        return carry
-
-    lax.fori_loop(0, row_count // block, project, 0)
-    scale = HEAD_DIM ** (-0.5) * LOG2E
 
     def one_block(index, carry):
         rows = pl.ds(pl.multiple_of(index * block, block), block)
         same_image = row_ids[rows, :] == column_ids[...]
         outs = []
         for head in range(heads):
+            query = projected[0, rows, head * HEAD_DIM : (head + 1) * HEAD_DIM]
             scores = lax.dot_general(
-                queries[head, rows, :],
-                keys[head],
-                (((1,), (1,)), ((), ())),
-                preferred_element_type=F32,
+                query, keys[head], (((1,), (1,)), ((), ())), preferred_element_type=F32
             )
             scores = jnp.where(same_image, scores, -1e30)
             highest = jnp.max(scores, axis=1, keepdims=True)
@@ -63,29 +76,26 @@
     lax.fori_loop(0, row_count // block, one_block, 0)
 
 
-def vision_context(patches, weight, image_ids):
-    row_count, depth = patches.shape
-    width = weight.shape[1]
+def vision_context(projected, patch_ids):
+    row_count, width = projected.shape[1:]
     heads = width // HEAD_DIM
-    patch_ids = jnp.repeat(image_ids.reshape(-1), MERGE)
     return pl.pallas_call(
         attention_kernel,
         out_shape=jax.ShapeDtypeStruct((row_count, width), BF),
-        in_specs=[pl.BlockSpec(memory_space=pltpu.VMEM)] * 4,
+        in_specs=[pl.BlockSpec(memory_space=pltpu.VMEM)] * 3,
         out_specs=pl.BlockSpec(memory_space=pltpu.VMEM),
         scratch_shapes=[
             pltpu.VMEM((heads, row_count, HEAD_DIM), BF),
-            pltpu.VMEM((heads, row_count, HEAD_DIM), BF),
             pltpu.VMEM((heads, row_count, 128), BF),
         ],
         compiler_params=pltpu.CompilerParams(vmem_limit_bytes=20 * 2**20),
         cost_estimate=pl.CostEstimate(
-            flops=4 * heads * row_count * row_count * 256 + 6 * row_count * depth * width,
-            bytes_accessed=2 * (row_count + 3 * width) * depth,
+            flops=4 * heads * row_count * row_count * 256,
+            bytes_accessed=8 * row_count * width,
             transcendentals=heads * row_count * row_count,
         ),
         name="vision_attention",
-    )(patch_ids[:, None], patch_ids[None, :], patches, weight)
+    )(patch_ids[:, None], patch_ids[None, :], projected)
 
 
 def norm_kernel(*refs):
@@ -144,51 +154,29 @@
     )(tp.reshape(1).astype(jnp.int32), *parts, *outs, patches, gain[None, :])
 
 
-def merge_kernel(*refs):
-    blocks, (weight, send, outgoing, rows, total) = refs[:-5], refs[-5:]
-    step = pl.program_id(0)
+def stack_kernel(*refs):
     first = 0
-    for block in blocks:
-        rows[first : first + block.shape[0], :] = block[...]
+    for block in refs[:-1]:
+        refs[-1][first : first + block.shape[0], :] = block[...]
         first += block.shape[0]
-    term = jnp.dot(rows[...], weight[...], preferred_element_type=F32)
-
-    @pl.when(step == 0)
-    def _():
-        total[...] = term
-
-    @pl.when(step > 0)
-    def _():
-        total[...] += term
-
-    @pl.when(step == pl.num_programs(0) - 1)
-    def _():
-        image = total[...].astype(BF)
-        outgoing[...] = jnp.dot(send[...], image, preferred_element_type=F32).astype(BF)
-
-
-def merge_and_select(blocks, weight, send, tile=640):
-    depth, columns = weight.shape
-    slots, count = send.shape
-    return pl.pallas_call(
-        merge_kernel,
+
+
+def stack_rows(blocks):
+    count = sum(block.shape[0] for block in blocks)
+    depth = blocks[0].shape[1]
+    tile = depth // 4
+    return pl.pallas_call(
+        stack_kernel,
         grid=(depth // tile,),
-        out_shape=jax.ShapeDtypeStruct((slots, columns), BF),
-        in_specs=[pl.BlockSpec((b.shape[0], tile), lambda i: (0, i)) for b in blocks]
-        + [
-            pl.BlockSpec((tile, columns), lambda i: (i, 0)),
-            pl.BlockSpec((slots, count), lambda i: (0, 0), pipeline_mode=pl.Buffered(1)),
-        ],
-        out_specs=pl.BlockSpec((slots, columns), lambda i: (0, 0)),
-        scratch_shapes=[pltpu.VMEM((count, tile), BF), pltpu.VMEM((count, columns), F32)],
-        compiler_params=pltpu.CompilerParams(vmem_limit_bytes=24 * 2**20),
-        cost_estimate=pl.CostEstimate(
-            flops=2 * count * (depth + slots) * columns,
-            bytes_accessed=2 * (count * depth + depth * columns + slots * columns),
-            transcendentals=0,
-        ),
-        name="merge_rows",
-    )(*blocks, weight, send)
+        out_shape=jax.ShapeDtypeStruct((count, depth), BF),
+        in_specs=[pl.BlockSpec((b.shape[0], tile), lambda i: (0, i)) for b in blocks],
+        out_specs=pl.BlockSpec((count, tile), lambda i: (0, i)),
+        compiler_params=pltpu.CompilerParams(vmem_limit_bytes=10 * 2**20),
+        cost_estimate=pl.CostEstimate(
+            flops=0, bytes_accessed=4 * count * depth, transcendentals=0
+        ),
+        name="stack_rows",
+    )(*blocks)
 
 
 def pick_kernel(received, pick, usable, text, prompt, squares):
@@ -227,7 +215,7 @@
             pl.BlockSpec((count, part), lambda h: (0, h)),
             pl.BlockSpec((count, 1), lambda h: (0, 0)),
         ],
-        compiler_params=pltpu.CompilerParams(vmem_limit_bytes=16 * 2**20),
+        compiler_params=pltpu.CompilerParams(vmem_limit_bytes=56 * 2**20),
         cost_estimate=pl.CostEstimate(
             flops=2 * count * slots * halves * part,
             bytes_accessed=6 * count * halves * part,
@@ -255,7 +243,7 @@
             pl.BlockSpec((1, part), lambda h: (0, h)),
         ],
         out_specs=pl.BlockSpec((count, part), lambda h: (0, h)),
-        compiler_params=pltpu.CompilerParams(vmem_limit_bytes=10 * 2**20),
+        compiler_params=pltpu.CompilerParams(vmem_limit_bytes=56 * 2**20),
         cost_estimate=pl.CostEstimate(
             flops=3 * count * width, bytes_accessed=4 * count * width, transcendentals=count
         ),
@@ -310,18 +298,21 @@
     table = jnp.broadcast_to(table.reshape(16, 1, 32), (16, 2, 32)).reshape(32, 32)
     usable = usable.astype(jnp.int32)[:, None]
 
-    arrived, table, pick, usable, out_weight = lax.optimization_barrier(
-        (arrived, table, pick, usable, out_weight)
+    projected = project(patches, jnp.swapaxes(qkv_weight, 1, 2))
+    arrived, table, pick, usable, out_weight, projected = lax.optimization_barrier(
+        (arrived, table, pick, usable, out_weight, projected)
     )
     is_own = (jnp.arange(2) == yh)[:, None, None]
     both = jnp.where(is_own, own[None], arrived[None]).reshape(-1, half)
     weight = lax.all_gather(both, ("z", "x"), axis=0, tiled=True)
 
     out_far = lax.ppermute(out_weight, "yl", [(0, 1), (1, 0)])
+
+    patch_ids = jnp.repeat(image_ids.reshape(-1), MERGE)
+    patch_ids, both = lax.optimization_barrier((patch_ids, both))
+    context = vision_context(projected, patch_ids)
+    context, out_far = lax.optimization_barrier((context, out_far))
     out_blocks = [out_weight, swap_core(out_weight), out_far, swap_core(out_far)]
-
-    patches, both = lax.optimization_barrier((patches, both))
-    context = vision_context(patches, jnp.swapaxes(qkv_weight, 1, 2), image_ids)
     rows = context.shape[0] // 4
     parts = [
         lax.dynamic_slice_in_dim(context, (tp ^ k) * rows, rows, 0) for k in range(4)
@@ -350,7 +341,8 @@
     wanted = jnp.where(wanted >= 0, wanted + jnp.arange(2)[None, :, None] * 256, -1).reshape(-1)
     send = (wanted[:, None] == row_ids[None, :]).astype(BF)
 
-    outgoing = merge_and_select(blocks, weight, send)
+    image_rows = jnp.dot(stack_rows(blocks), weight, preferred_element_type=F32).astype(BF)
+    outgoing = jnp.dot(send, image_rows, preferred_element_type=F32).astype(BF)
     received = lax.all_to_all(outgoing, SEC, split_axis=0, concat_axis=0, tiled=True)
     received = received.reshape(16, 2, 32, half)
     prompt, squares = pick_rows(received, pick, usable, text_rows)

time: 196 us -> 193 us (0.985)
  matrix products: 0.61 us -> 14.1 us
  waiting for transfers between devices: 82.7 us -> 75.8 us
  starting transfers between devices: 38.9 us -> 34 us
  Pallas kernels: 34.6 us -> 30.6 us
    dot_general x0 -> x1, matrix products: none -> 13.5 us  [on_device(): outgoing = jnp.dot(send, image_rows, preferred_element_type=F32).astype(BF)]
    ppermute x1, waiting for transfers between devices: 14.1 us -> 2.44 us  [on_device(): out_far = lax.ppermute(out_weight, 'yl', [(0, 1), (1, 0)])]
    ppermute x4, waiting for transfers between devices: 19.3 us -> 26.8 us  [shift_y(): lax.ppermute(block, ('yh', 'yl'), [(i, (i + d) % 4) for i in range(4)])]
    all_to_all x1, waiting for transfers between devices: 1.3 us -> 7.67 us  [on_device(): table = lax.all_to_all(table, SEC, split_axis=0, concat_axis=0, tiled=True)]
    ppermute x1, waiting for transfers between devices: 5.02 us -> 0.01 us  [on_device(): arrived = lax.ppermute(other, 'yh', [(0, 1), (1, 0)])]
    pallas_call x1 -> x2, Pallas kernels: 12.1 us -> 7.51 us  [the longest x1 4.63 us: project(): pl.pallas_call(project_kernel, grid=(count,), out_shape=jax.ShapeDtypeStr...]
    pallas_call x1, Pallas kernels: 14 us -> 9.91 us  [vision_context(): pl.pallas_call(attention_kernel, out_shape=jax.ShapeDtypeStruct((row_coun...]
    pallas_call x1, Pallas kernels: 2.19 us -> 4.65 us  [pick_rows(): pl.pallas_call(pick_kernel, grid=(halves,), out_shape=[jax.ShapeDtypeStru...]
  transfers between devices with their start and end apart: 22 -> 22, of which waited for: 11 -> 9; matrix products, arithmetic and copies ran while one was open for 2% -> 4% of each run, Pallas kernels for 9% -> 11%
where the time goes in v7:
time: 193 us
  waiting for transfers between devices  75.8 us (39%)
  starting transfers between devices  34 us (18%)
  Pallas kernels  30.6 us (16%)
  local copies, waits for them, and re-layouts  20.1 us (10%)
  matrix products  14.1 us (7%)
  between operations  13.6 us (7%)
  other arithmetic  4.54 us (2%)
    all_to_all x1, waiting for transfers between devices, on_device(): lax.all_to_all(outgoing, SEC, split_axis=0, concat_axis=0, tiled=True)  28.5 us
    ppermute x4, waiting for transfers between devices, shift_y(): lax.ppermute(block, ('yh', 'yl'), [(i, (i + d) % 4) for i in range(4)])  26.8 us
    unnamed x28, local copies, waits for them, and re-layouts  13.6 us
    dot_general x1, matrix products, on_device(): outgoing = jnp.dot(send, image_rows, preferred_element_type=F32).astype(BF)  13.5 us
    ppermute x6, waiting for transfers between devices, swap_tp(): return lax.ppermute(block, TP, [(i, i ^ k) for i in range(4)])  10.3 us
    pallas_call x1, Pallas kernels, vision_context(): pl.pallas_call(attention_kernel, out_shape=jax.ShapeDtypeStruct((row_coun...  9.91 us
    all_to_all x1, starting transfers between devices, on_device(): table = lax.all_to_all(table, SEC, split_axis=0, concat_axis=0, tiled=True)  7.87 us
    all_to_all x1, waiting for transfers between devices, on_device(): table = lax.all_to_all(table, SEC, split_axis=0, concat_axis=0, tiled=True)  7.67 us
  transfers between devices with their start and end apart: 22, of which 9 were waited for; matrix products, arithmetic and copies ran while one was open for 4% of the time, Pallas kernels for 11%

profile of v7, /device:TPU:1, one launch (start us, length us, event | category | flops | bytes accessed | tf_op | source)
XLA Modules:
  0.0 192.8 jit_solution(5786201741395720398)
XLA Ops:
  6.5 1.1 constant_dynamic-slice_fusion.4
  7.7 3.8 %collective-permute-start = (bf16[160,1024]{1,0:T(8,128)(2,1)S(1)}, bf16[160,1024]{1,0:T(8,128)(2,1)S(1)}, u32[]{:S(2)}, u32[]{:S(2)}) collective-permute-start(bf16[160,1024]{1,0:T(8,128)(2,1)S(1)} %get-tuple-element.48), channel_id=1, source_target_pairs={{0,4},{4,0},{1,5},{5,1},{2,6},{6,2},{3,7},{7,3},{8,12},{12,8},{9,1... | collective-permute-start | bytes 983048 | tf_op jit(solution)/shard_map/ppermute | solution.py:285
  13.6 1.7 copy-done.1
  15.3 1.7 copy-done.6
  17.0 4.6 %project_qkv.1.projected = bf16[3,1024,320]{2,1,0:T(8,128)(2,1)S(1)} custom-call(bf16[1024,1280]{1,0:T(8,128)(2,1)S(1)} %copy-done.1, bf16[3,320,1280]{2,1,0:T(8,128)(2,1)S(1)} %bitcast.24), custom_call_target="tpu_custom_call" | custom-call | flops 2516582400 | bytes 7045120 | tf_op jit(solution)/shard_map/project_qkv/pallas_call | solution.py:29
  21.7 1.5 copy-done.9
  26.7 1.3 collective-permute-start.5
  30.0 1.7 copy-done.10
  31.7 9.9 %vision_attention.1 = bf16[1024,320]{1,0:T(8,128)(2,1)S(1)} custom-call(s32[1024,1]{1,0:T(8,128)S(1)} %copy-done.5, s32[1,1024]{1,0:T(1,128)S(1)} %bitcast.23, bf16[3,1024,320]{2,1,0:T(8,128)(2,1)S(1)} %copy-done.10), custom_call_target="tpu_custom_call" | custom-call | flops 4294967296 | bytes 2621440 | tf_op jit(solution)/shard_map/vision_attention/pallas_call | solution.py:82
  42.5 2.4 %collective-permute-done.1.refs_7_ = bf16[320,1280]{1,0:T(8,128)(2,1)} collective-permute-done((bf16[320,1280]{1,0:T(8,128)(2,1)S(1)}, bf16[320,1280]{1,0:T(8,128)(2,1)}, u32[]{:S(2)}, u32[]{:S(2)}) %collective-permute-start.1) | collective-permute-done | bytes 819232 | tf_op jit(solution)/shard_map/ppermute | solution.py:309
  44.9 1.9 collective-permute-start.6
  46.8 1.3 constant_dynamic-slice_fusion
  48.7 1.7 collective-permute-start.4
  50.4 4.0 %collective-permute-done.3.refs_3_ = bf16[256,320]{1,0:T(8,128)(2,1)S(1)} collective-permute-done((bf16[256,320]{1,0:T(8,128)(2,1)S(1)}, bf16[256,320]{1,0:T(8,128)(2,1)S(1)}, u32[]{:S(2)}, u32[]{:S(2)}) %collective-permute-start.3) | collective-permute-done | bytes 163872 | tf_op jit(solution)/shard_map/ppermute | solution.py:255
  54.4 4.8 %collective-permute-done.4.refs_4_ = bf16[256,320]{1,0:T(8,128)(2,1)S(1)} collective-permute-done((bf16[256,320]{1,0:T(8,128)(2,1)S(1)}, bf16[256,320]{1,0:T(8,128)(2,1)S(1)}, u32[]{:S(2)}, u32[]{:S(2)}) %collective-permute-start.4) | collective-permute-done | bytes 163872 | tf_op jit(solution)/shard_map/ppermute | solution.py:255
  59.1 4.4 %project_and_norm.1 = (bf16[64,5120]{1,0:T(8,128)(2,1)}, bf16[32,5120]{1,0:T(8,128)(2,1)S(1)}, bf16[32,5120]{1,0:T(8,128)(2,1)S(1)}) custom-call(s32[1]{0:T(128)} %bitcast.4.refs_0_, bf16[256,320]{1,0:T(8,128)(2,1)S(1)} %get-tuple-element.46.refs_1_, bf16[256,320]{1,0:T(8,128)(2,1)S(1)} %collective-permute-done.2.refs_2_, ...), custom_call_target="tpu_custom_call" | custom-call | flops 838860800 | bytes 5242880 | tf_op jit(solution)/shard_map/project_and_norm/pallas_call | solution.py:127
  67.5 2.4 %collective-permute-start.14 = (bf16[32,5120]{1,0:T(8,128)(2,1)}, bf16[32,5120]{1,0:T(8,128)(2,1)}, u32[]{:S(2)}, u32[]{:S(2)}) collective-permute-start(bf16[32,5120]{1,0:T(8,128)(2,1)} %copy-done.7), channel_id=1, source_target_pairs={{0,4},{2,6},{4,0},{6,2},{1,5},{3,7},{5,1},{7,3},{8,12},{10,14},{12... | collective-permute-start | bytes 983048 | tf_op jit(solution)/shard_map/ppermute | solution.py:259
  69.9 11.8 %collective-permute-done.10.refs_4_ = bf16[64,5120]{1,0:T(8,128)(2,1)S(1)} collective-permute-done((bf16[64,5120]{1,0:T(8,128)(2,1)}, bf16[64,5120]{1,0:T(8,128)(2,1)S(1)}, u32[]{:S(2)}, u32[]{:S(2)}) %collective-permute-start.10) | collective-permute-done | bytes 655392 | tf_op jit(solution)/shard_map/ppermute | solution.py:259
  82.6 15.0 %collective-permute-done.8.refs_2_ = bf16[64,5120]{1,0:T(8,128)(2,1)S(1)} collective-permute-done((bf16[64,5120]{1,0:T(8,128)(2,1)}, bf16[64,5120]{1,0:T(8,128)(2,1)S(1)}, u32[]{:S(2)}, u32[]{:S(2)}) %collective-permute-start.8) | collective-permute-done | bytes 655392 | tf_op jit(solution)/shard_map/ppermute | solution.py:259
  98.4 7.9 %all-to-all-start = ((s32[32,1,32]{2,1,0:T(1,128)}), s32[32,1,32]{2,1,0:T(1,128)S(1)}, u32[]{:S(2)}, u32[]{:S(2)}) async-start(s32[32,1,32]{2,1,0:T(1,128)} %bitcast.10), calls=%async_computation | async-start | bytes 32768 | tf_op jit(solution)/shard_map/all_to_all | solution.py:331
  107.2 7.7 %all-to-all-done = s32[32,1,32]{2,1,0:T(1,128)S(1)} async-done(((s32[32,1,32]{2,1,0:T(1,128)}), s32[32,1,32]{2,1,0:T(1,128)S(1)}, u32[]{:S(2)}, u32[]{:S(2)}) %all-to-all-start) | async-done | bytes 4128 | tf_op jit(solution)/shard_map/all_to_all | solution.py:331
  115.0 2.9 %stack_rows.1 = bf16[512,5120]{1,0:T(8,128)(2,1)S(1)} custom-call(bf16[64,5120]{1,0:T(8,128)(2,1)} %get-tuple-element.34.refs_0_, bf16[64,5120]{1,0:T(8,128)(2,1)S(1)} %collective-permute-done.7.refs_1_, bf16[64,5120]{1,0:T(8,128)(2,1)S(1)} %collective-permute-done.8.refs_2_, bf16[64,5120]{1,0:T(8,128)(2,1)S(1)} %collective-permute-done.9.refs_3_, ...), custom_call_target="tpu_custom_call" | custom-call | bytes 10485760 | tf_op jit(solution)/shard_map/stack_rows/pallas_call | solution.py:168
  117.9 2.3 %copy-done = bf16[512,5120]{1,0:T(8,128)(2,1)} copy-done((bf16[512,5120]{1,0:T(8,128)(2,1)}, bf16[512,5120]{1,0:T(8,128)(2,1)S(1)}, u32[]{:S(2)}) %copy-start) | copy-done | bytes 5242904
  120.2 13.5 %fusion.2 = bf16[1024,1024]{1,0:T(8,128)(2,1)} fusion(s32[512]{0:T(512)S(1)} %concatenate.3, s32[1024]{0:T(1024)S(1)} %add_select_fusion, bf16[512,5120]{1,0:T(8,128)(2,1)} %copy-done, bf16[5120,1024]{1,0:T(8,128)(2,1)} %all-gather.2.cloned.1.call-done), kind=kOutput, calls=%fused_computation.2 | convolution fusion | flops 6444548096 | bytes 17831936 | tf_op jit(solution)/shard_map/dot_general | solution.py:345
  133.7 4.0 %all-to-all-start.1 = ((bf16[32,32,1024]{2,1,0:T(8,128)(2,1)}), bf16[32,32,1024]{2,1,0:T(8,128)(2,1)S(1)}, u32[]{:S(2)}, u32[]{:S(2)}) async-start(bf16[32,32,1024]{2,1,0:T(8,128)(2,1)} %bitcast.26), calls=%async_computation.1 | async-start | bytes 4194304 | tf_op jit(solution)/shard_map/all_to_all | solution.py:346
  138.6 28.5 %all-to-all-done.1 = bf16[32,32,1024]{2,1,0:T(8,128)(2,1)S(1)} async-done(((bf16[32,32,1024]{2,1,0:T(8,128)(2,1)}), bf16[32,32,1024]{2,1,0:T(8,128)(2,1)S(1)}, u32[]{:S(2)}, u32[]{:S(2)}) %all-to-all-start.1) | async-done | bytes 2097184 | tf_op jit(solution)/shard_map/all_to_all | solution.py:346
  167.1 1.3 copy-done.11
  168.4 4.7 %pick_rows.1 = (bf16[512,2048]{1,0:T(8,128)(2,1)}, f32[512,1]{1,0:T(8,128)}) custom-call(bf16[16,2,32,1024]{3,2,1,0:T(8,128)(2,1)} %bitcast.25, bf16[512,512]{1,0:T(8,128)(2,1)} %fusion.7.pick, s32[512,1]{1,0:T(8,128)} %copy.14.usable, bf16[512,2048]{1,0:T(8,128)(2,1)} %text.1), custom_call_target="tpu_custom_call" | custom-call | flops 1073741824 | bytes 6291456 | tf_op jit(solution)/shard_map/pick_rows/pallas_call | solution.py:201
  173.0 1.1 reduce.1
  174.1 3.5 %collective-permute-start.16 = (f32[4,128]{1,0:T(4,128)S(1)}, f32[4,128]{1,0:T(4,128)S(1)}, u32[]{:S(2)}, u32[]{:S(2)}) collective-permute-start(f32[4,128]{1,0:T(4,128)S(1)} %bitcast.28), channel_id=1, source_target_pairs={{0,1},{1,0},{2,3},{3,2},{4,5},{5,4},{6,7},{7,6},{8,9},{9,8},{10,11... | collective-permute-start | bytes 6152 | tf_op jit(solution)/shard_map/ppermute | solution.py:255
  177.6 1.7 collective-permute-start.18
  181.8 4.2 %finish.1 = bf16[512,2048]{1,0:T(8,128)(2,1)} custom-call(bf16[512,2048]{1,0:T(8,128)(2,1)} %get-tuple-element.39.prompt, f32[512,1]{1,0:T(8,128)} %copy.15.squares, f32[1,2048]{1,0:T(1,128)} %bitcast.27), custom_call_target="tpu_custom_call" | custom-call | flops 3145728 | bytes 4194304 | tf_op jit(solution)/shard_map/finish/pallas_call | solution.py:236
  (84 shorter events, 19.1 us)
Async XLA Ops:
  6.5 113.7 %all-gather.2.cloned.1.call-start = ((), (), s32[]{:S(2)}) async-start(), calls=%async_computation.2 | async-start | bytes 11141120 | tf_op jit(solution)/shard_map/all_gather | solution.py:307
  7.7 16.7 %collective-permute-start = (bf16[160,1024]{1,0:T(8,128)(2,1)S(1)}, bf16[160,1024]{1,0:T(8,128)(2,1)S(1)}, u32[]{:S(2)}, u32[]{:S(2)}) collective-permute-start(bf16[160,1024]{1,0:T(8,128)(2,1)S(1)} %get-tuple-element.48), channel_id=1, source_target_pairs={{0,4},{4,0},{1,5},{5,1},{2,6},{6,2},{3,7},{7,3},{8,12},{12,8},{9,1... | collective-permute-start | bytes 983048 | tf_op jit(solution)/shard_map/ppermute | solution.py:285
  13.6 1.7 copy-start.1
  15.3 1.7 copy-start.6
  17.0 8.9 %copy-start.3 = (bf16[320,1280]{1,0:T(8,128)(2,1)S(1)}, bf16[320,1280]{1,0:T(8,128)(2,1)}, u32[]{:S(2)}) copy-start(bf16[320,1280]{1,0:T(8,128)(2,1)} %refs_5_) | copy-start | bytes 2457604
  17.0 9.4 %copy-start.13 = (s32[1,256]{1,0:T(1,128)S(1)}, s32[1,256]{1,0:T(1,128)}, u32[]{:S(2)}) copy-start(s32[1,256]{1,0:T(1,128)} %param.10) | copy-start | bytes 3076
  21.7 1.5 copy-start.9
  26.0 19.0 %collective-permute-start.1 = (bf16[320,1280]{1,0:T(8,128)(2,1)S(1)}, bf16[320,1280]{1,0:T(8,128)(2,1)}, u32[]{:S(2)}, u32[]{:S(2)}) collective-permute-start(bf16[320,1280]{1,0:T(8,128)(2,1)S(1)} %copy-done.3), channel_id=1, source_target_pairs={{0,2},{2,0},{1,3},{3,1},{4,6},{6,4},{5,7},{7,5},{8,10},{10,8},{9,1... | collective-permute-start | bytes 2457608 | tf_op jit(solution)/shard_map/ppermute | solution.py:309
  26.7 23.7 %collective-permute-start.5 = (bf16[320,1280]{1,0:T(8,128)(2,1)S(1)}, bf16[320,1280]{1,0:T(8,128)(2,1)}, u32[]{:S(2)}, u32[]{:S(2)}) collective-permute-start(bf16[320,1280]{1,0:T(8,128)(2,1)S(1)} %copy-done.3), channel_id=1, source_target_pairs={{0,1},{1,0},{2,3},{3,2},{4,5},{5,4},{6,7},{7,6},{8,9},{9,8},{10,11... | collective-permute-start | bytes 2457608 | tf_op jit(solution)/shard_map/ppermute | solution.py:263
  30.0 1.7 copy-start.10
  31.7 18.6 %copy-start.12 = (f32[1280]{0:T(1024)S(1)}, f32[1280]{0:T(1024)}, u32[]{:S(2)}) copy-start(f32[1280]{0:T(1024)} %param.13) | copy-start | bytes 15364
  31.7 27.4 %copy-start.2 = (bf16[1024,1280]{1,0:T(8,128)(2,1)S(1)}, bf16[1024,1280]{1,0:T(8,128)(2,1)}, u32[]{:S(2)}) copy-start(bf16[1024,1280]{1,0:T(8,128)(2,1)} %refs_9_.1) | copy-start | bytes 7864324
  44.9 14.2 %collective-permute-start.6 = (bf16[320,1280]{1,0:T(8,128)(2,1)}, bf16[320,1280]{1,0:T(8,128)(2,1)}, u32[]{:S(2)}, u32[]{:S(2)}) collective-permute-start(bf16[320,1280]{1,0:T(8,128)(2,1)} %collective-permute-done.1.refs_7_), channel_id=1, source_target_pairs={{0,1},{1,0},{2,3},{3,2},{4,5},{5,4},{6,7},{7,6},{8,9},{9,8},{10,11... | collective-permute-start | bytes 2457608 | tf_op jit(solution)/shard_map/ppermute | solution.py:263
  48.1 2.2 %collective-permute-start.2 = (bf16[256,320]{1,0:T(8,128)(2,1)S(1)}, bf16[256,320]{1,0:T(8,128)(2,1)S(1)}, u32[]{:S(2)}, u32[]{:S(2)}) collective-permute-start(bf16[256,320]{1,0:T(8,128)(2,1)S(1)} %get-tuple-element.45), channel_id=1, source_target_pairs={{0,1},{1,0},{2,3},{3,2},{4,5},{5,4},{6,7},{7,6},{8,9},{9,8},{10,11... | collective-permute-start | bytes 491528 | tf_op jit(solution)/shard_map/ppermute | solution.py:255
  48.2 6.1 %collective-permute-start.3 = (bf16[256,320]{1,0:T(8,128)(2,1)S(1)}, bf16[256,320]{1,0:T(8,128)(2,1)S(1)}, u32[]{:S(2)}, u32[]{:S(2)}) collective-permute-start(bf16[256,320]{1,0:T(8,128)(2,1)S(1)} %get-tuple-element.44), channel_id=1, source_target_pairs={{0,2},{1,3},{2,0},{3,1},{4,6},{5,7},{6,4},{7,5},{8,10},{9,11},{10,... | collective-permute-start | bytes 491528 | tf_op jit(solution)/shard_map/ppermute | solution.py:255
  48.7 10.5 %collective-permute-start.4 = (bf16[256,320]{1,0:T(8,128)(2,1)S(1)}, bf16[256,320]{1,0:T(8,128)(2,1)S(1)}, u32[]{:S(2)}, u32[]{:S(2)}) collective-permute-start(bf16[256,320]{1,0:T(8,128)(2,1)S(1)} %get-tuple-element.43), channel_id=1, source_target_pairs={{0,3},{1,2},{2,1},{3,0},{4,7},{5,6},{6,5},{7,4},{8,11},{9,10},{10,... | collective-permute-start | bytes 491528 | tf_op jit(solution)/shard_map/ppermute | solution.py:255
  64.9 16.8 %collective-permute-start.10 = (bf16[64,5120]{1,0:T(8,128)(2,1)}, bf16[64,5120]{1,0:T(8,128)(2,1)S(1)}, u32[]{:S(2)}, u32[]{:S(2)}) collective-permute-start(bf16[64,5120]{1,0:T(8,128)(2,1)} %get-tuple-element.34.refs_0_), channel_id=1, source_target_pairs={{0,6},{2,0},{4,2},{6,4},{1,7},{3,1},{5,3},{7,5},{8,14},{10,8},{12,... | collective-permute-start | bytes 1966088 | tf_op jit(solution)/shard_map/ppermute | solution.py:259
  65.7 31.9 %collective-permute-start.8 = (bf16[64,5120]{1,0:T(8,128)(2,1)}, bf16[64,5120]{1,0:T(8,128)(2,1)S(1)}, u32[]{:S(2)}, u32[]{:S(2)}) collective-permute-start(bf16[64,5120]{1,0:T(8,128)(2,1)} %get-tuple-element.34.refs_0_), channel_id=1, source_target_pairs={{0,2},{2,4},{4,6},{6,0},{1,3},{3,5},{5,7},{7,1},{8,10},{10,12},{12... | collective-permute-start | bytes 1966088 | tf_op jit(solution)/shard_map/ppermute | solution.py:259
  66.4 48.6 %collective-permute-start.7 = (bf16[64,5120]{1,0:T(8,128)(2,1)}, bf16[64,5120]{1,0:T(8,128)(2,1)S(1)}, u32[]{:S(2)}, u32[]{:S(2)}) collective-permute-start(bf16[64,5120]{1,0:T(8,128)(2,1)} %get-tuple-element.34.refs_0_), channel_id=1, source_target_pairs={{0,1},{1,0},{2,3},{3,2},{4,5},{5,4},{6,7},{7,6},{8,9},{9,8},{10,11... | collective-permute-start | bytes 1966088 | tf_op jit(solution)/shard_map/ppermute | solution.py:263
  66.9 39.6 %collective-permute-start.12 = (bf16[32,5120]{1,0:T(8,128)(2,1)}, bf16[32,5120]{1,0:T(8,128)(2,1)}, u32[]{:S(2)}, u32[]{:S(2)}) collective-permute-start(bf16[32,5120]{1,0:T(8,128)(2,1)} %copy-done.8), channel_id=1, source_target_pairs={{0,4},{2,6},{4,0},{6,2},{1,5},{3,7},{5,1},{7,3},{8,12},{10,14},{12... | collective-permute-start | bytes 983048 | tf_op jit(solution)/shard_map/ppermute | solution.py:259
  67.5 39.4 %collective-permute-start.14 = (bf16[32,5120]{1,0:T(8,128)(2,1)}, bf16[32,5120]{1,0:T(8,128)(2,1)}, u32[]{:S(2)}, u32[]{:S(2)}) collective-permute-start(bf16[32,5120]{1,0:T(8,128)(2,1)} %copy-done.7), channel_id=1, source_target_pairs={{0,4},{2,6},{4,0},{6,2},{1,5},{3,7},{5,1},{7,3},{8,12},{10,14},{12... | collective-permute-start | bytes 983048 | tf_op jit(solution)/shard_map/ppermute | solution.py:259
  81.7 33.3 %collective-permute-start.11 = (bf16[64,5120]{1,0:T(8,128)(2,1)S(1)}, bf16[64,5120]{1,0:T(8,128)(2,1)S(1)}, u32[]{:S(2)}, u32[]{:S(2)}) collective-permute-start(bf16[64,5120]{1,0:T(8,128)(2,1)S(1)} %collective-permute-done.10.refs_4_), channel_id=1, source_target_pairs={{0,1},{1,0},{2,3},{3,2},{4,5},{5,4},{6,7},{7,6},{8,9},{9,8},{10,11... | collective-permute-start | bytes 1966088 | tf_op jit(solution)/shard_map/ppermute | solution.py:263
  97.6 17.4 %collective-permute-start.9 = (bf16[64,5120]{1,0:T(8,128)(2,1)S(1)}, bf16[64,5120]{1,0:T(8,128)(2,1)S(1)}, u32[]{:S(2)}, u32[]{:S(2)}) collective-permute-start(bf16[64,5120]{1,0:T(8,128)(2,1)S(1)} %collective-permute-done.8.refs_2_), channel_id=1, source_target_pairs={{0,1},{1,0},{2,3},{3,2},{4,5},{5,4},{6,7},{7,6},{8,9},{9,8},{10,11... | collective-permute-start | bytes 1966088 | tf_op jit(solution)/shard_map/ppermute | solution.py:263
  98.4 16.5 %all-to-all-start = ((s32[32,1,32]{2,1,0:T(1,128)}), s32[32,1,32]{2,1,0:T(1,128)S(1)}, u32[]{:S(2)}, u32[]{:S(2)}) async-start(s32[32,1,32]{2,1,0:T(1,128)} %bitcast.10), calls=%async_computation | async-start | bytes 32768 | tf_op jit(solution)/shard_map/all_to_all | solution.py:331
  106.5 8.4 %collective-permute-start.13 = (bf16[32,5120]{1,0:T(8,128)(2,1)}, bf16[32,5120]{1,0:T(8,128)(2,1)}, u32[]{:S(2)}, u32[]{:S(2)}) collective-permute-start(bf16[32,5120]{1,0:T(8,128)(2,1)} %collective-permute-done.12.refs_6_), channel_id=1, source_target_pairs={{0,1},{1,0},{2,3},{3,2},{4,5},{5,4},{6,7},{7,6},{8,9},{9,8},{10,11... | collective-permute-start | bytes 983048 | tf_op jit(solution)/shard_map/ppermute | solution.py:263
  106.9 8.1 %collective-permute-start.15 = (bf16[32,5120]{1,0:T(8,128)(2,1)}, bf16[32,5120]{1,0:T(8,128)(2,1)}, u32[]{:S(2)}, u32[]{:S(2)}) collective-permute-start(bf16[32,5120]{1,0:T(8,128)(2,1)} %collective-permute-done.14.refs_8_), channel_id=1, source_target_pairs={{0,1},{1,0},{2,3},{3,2},{4,5},{5,4},{6,7},{7,6},{8,9},{9,8},{10,11... | collective-permute-start | bytes 983048 | tf_op jit(solution)/shard_map/ppermute | solution.py:263
  117.9 2.3 %copy-start = (bf16[512,5120]{1,0:T(8,128)(2,1)}, bf16[512,5120]{1,0:T(8,128)(2,1)S(1)}, u32[]{:S(2)}) copy-start(bf16[512,5120]{1,0:T(8,128)(2,1)S(1)} %stack_rows.1) | copy-start | bytes 15728644
  133.7 33.3 %all-to-all-start.1 = ((bf16[32,32,1024]{2,1,0:T(8,128)(2,1)}), bf16[32,32,1024]{2,1,0:T(8,128)(2,1)S(1)}, u32[]{:S(2)}, u32[]{:S(2)}) async-start(bf16[32,32,1024]{2,1,0:T(8,128)(2,1)} %bitcast.26), calls=%async_computation.1 | async-start | bytes 4194304 | tf_op jit(solution)/shard_map/all_to_all | solution.py:346
  167.1 1.3 copy-start.11
  174.1 5.2 %collective-permute-start.16 = (f32[4,128]{1,0:T(4,128)S(1)}, f32[4,128]{1,0:T(4,128)S(1)}, u32[]{:S(2)}, u32[]{:S(2)}) collective-permute-start(f32[4,128]{1,0:T(4,128)S(1)} %bitcast.28), channel_id=1, source_target_pairs={{0,1},{1,0},{2,3},{3,2},{4,5},{5,4},{6,7},{7,6},{8,9},{9,8},{10,11... | collective-permute-start | bytes 6152 | tf_op jit(solution)/shard_map/ppermute | solution.py:255
  177.6 2.5 %collective-permute-start.17 = (f32[4,128]{1,0:T(4,128)S(1)}, f32[4,128]{1,0:T(4,128)S(1)}, u32[]{:S(2)}, u32[]{:S(2)}) collective-permute-start(f32[4,128]{1,0:T(4,128)S(1)} %bitcast.29), channel_id=1, source_target_pairs={{0,2},{1,3},{2,0},{3,1},{4,6},{5,7},{6,4},{7,5},{8,10},{9,11},{10,... | collective-permute-start | bytes 6152 | tf_op jit(solution)/shard_map/ppermute | solution.py:255
  177.6 3.3 %collective-permute-start.18 = (f32[4,128]{1,0:T(4,128)S(1)}, f32[4,128]{1,0:T(4,128)S(1)}, u32[]{:S(2)}, u32[]{:S(2)}) collective-permute-start(f32[4,128]{1,0:T(4,128)S(1)} %bitcast.30), channel_id=1, source_target_pairs={{0,3},{1,2},{2,1},{3,0},{4,7},{5,6},{6,5},{7,4},{8,11},{9,10},{10,... | collective-permute-start | bytes 6152 | tf_op jit(solution)/shard_map/ppermute | solution.py:255
  (4 other events, 3.4 us)
Sparse Core Ops, SparseCore 0:
  26.1 81.0 all-gather.1

commit v8 on v7

--- a/solution.py
+++ b/solution.py
@@ -179,20 +179,108 @@
     )(*blocks)
 
 
-def pick_kernel(received, pick, usable, text, prompt, squares):
+def square_sums(block):
+    value = block.astype(F32)
+    return jnp.sum(value * value, axis=1, keepdims=True)
+
+
+def diagonal():
+    shape = (128, 128)
+    return lax.broadcasted_iota(jnp.int32, shape, 0) == lax.broadcasted_iota(jnp.int32, shape, 1)
+
+
+def to_lanes(column, out):
+    eye = diagonal()
+    for q in range(out.shape[0]):
+        part = jnp.where(eye, column[q * 128 : (q + 1) * 128], 0.0)
+        out[q : q + 1, :] = jnp.sum(part, axis=0, keepdims=True)
+
+
+def to_column(lanes):
+    eye = diagonal()
+    return jnp.concatenate(
+        [
+            jnp.sum(jnp.where(eye, lanes[q : q + 1], 0.0), axis=1, keepdims=True)
+            for q in range(lanes.shape[0])
+        ],
+        axis=0,
+    )
+
+
+def text_kernel(text, usable, squares):
+    squares[...] = jnp.where(usable[...] > 0, 0.0, square_sums(text[...]))
+
+
+def text_squares(text, usable):
+    count, width = text.shape
+    return pl.pallas_call(
+        text_kernel,
+        grid=(4,),
+        out_shape=jax.ShapeDtypeStruct((count, 1), F32),
+        in_specs=[
+            pl.BlockSpec((count // 4, width), lambda i: (i, 0)),
+            pl.BlockSpec((count // 4, 1), lambda i: (i, 0)),
+        ],
+        out_specs=pl.BlockSpec((count // 4, 1), lambda i: (i, 0)),
+        compiler_params=pltpu.CompilerParams(vmem_limit_bytes=10 * 2**20),
+        cost_estimate=pl.CostEstimate(
+            flops=2 * count * width, bytes_accessed=2 * count * width, transcendentals=0
+        ),
+        name="text_squares",
+    )(text, usable)
+
+
+def squares_kernel(received, pick, from_text, squares, total):
+    arrived = received[...].reshape(pick.shape[1], received.shape[-1])
+    step = pl.program_id(0)
+
+    @pl.when(step == 0)
+    def _():
+        total[...] = square_sums(arrived)
+
+    @pl.when(step > 0)
+    def _():
+        total[...] += square_sums(arrived)
+
+    @pl.when(step == pl.num_programs(0) - 1)
+    def _():
+        rest = jnp.broadcast_to(total[...], (total.shape[0], 128))
+        chosen = jnp.broadcast_to(from_text[...], (pick.shape[0], 128))
+        for _ in range(3):
+            part = rest.astype(BF)
+            chosen += jnp.dot(pick[...], part, preferred_element_type=F32)
+            rest = rest - part.astype(F32)
+        to_lanes(chosen[:, :1], squares)
+
+
+def slot_squares(received, pick, from_text):
+    planes, halves, rows, part = received.shape
+    count, slots = pick.shape
+    return pl.pallas_call(
+        squares_kernel,
+        grid=(halves,),
+        out_shape=jax.ShapeDtypeStruct((count // 128, 128), F32),
+        in_specs=[
+            pl.BlockSpec((planes, 1, rows, part), lambda h: (0, h, 0, 0)),
+            pl.BlockSpec((count, slots), lambda h: (0, 0), pipeline_mode=pl.Buffered(1)),
+            pl.BlockSpec((count, 1), lambda h: (0, 0), pipeline_mode=pl.Buffered(1)),
+        ],
+        out_specs=pl.BlockSpec((count // 128, 128), lambda h: (0, 0)),
+        scratch_shapes=[pltpu.VMEM((slots, 1), F32)],
+        compiler_params=pltpu.CompilerParams(vmem_limit_bytes=14 * 2**20),
+        cost_estimate=pl.CostEstimate(
+            flops=2 * slots * halves * part,
+            bytes_accessed=2 * slots * halves * part,
+            transcendentals=0,
+        ),
+        name="slot_squares",
+    )(received, pick, from_text)
+
+
+def pick_kernel(received, pick, usable, text, prompt):
     arrived = received[...].reshape(pick.shape[1], received.shape[-1])
     picked = jnp.dot(pick[...], arrived, preferred_element_type=F32)
-    value = jnp.where(usable[...] > 0, picked, text[...].astype(F32))
-    prompt[...] = value.astype(BF)
-    total = jnp.sum(value * value, axis=1, keepdims=True)
-
-    @pl.when(pl.program_id(0) == 0)
-    def _():
-        squares[...] = total
-
-    @pl.when(pl.program_id(0) > 0)
-    def _():
-        squares[...] += total
+    prompt[...] = jnp.where(usable[...] > 0, picked, text[...].astype(F32)).astype(BF)
 
 
 def pick_rows(received, pick, usable, text):
@@ -201,21 +289,15 @@
     return pl.pallas_call(
         pick_kernel,
         grid=(halves,),
-        out_shape=[
-            jax.ShapeDtypeStruct((count, halves * part), BF),
-            jax.ShapeDtypeStruct((count, 1), F32),
-        ],
+        out_shape=jax.ShapeDtypeStruct((count, halves * part), BF),
         in_specs=[
             pl.BlockSpec((planes, 1, rows, part), lambda h: (0, h, 0, 0)),
             pl.BlockSpec((count, slots), lambda h: (0, 0), pipeline_mode=pl.Buffered(1)),
             pl.BlockSpec((count, 1), lambda h: (0, 0), pipeline_mode=pl.Buffered(1)),
             pl.BlockSpec((count, part), lambda h: (0, h)),
         ],
-        out_specs=[
-            pl.BlockSpec((count, part), lambda h: (0, h)),
-            pl.BlockSpec((count, 1), lambda h: (0, 0)),
-        ],
-        compiler_params=pltpu.CompilerParams(vmem_limit_bytes=56 * 2**20),
+        out_specs=pl.BlockSpec((count, part), lambda h: (0, h)),
+        compiler_params=pltpu.CompilerParams(vmem_limit_bytes=14 * 2**20),
         cost_estimate=pl.CostEstimate(
             flops=2 * count * slots * halves * part,
             bytes_accessed=6 * count * halves * part,
@@ -225,30 +307,34 @@
     )(received, pick, usable, text)
 
 
-def finish_kernel(prompt, squares, gain, out, *, width):
-    inverse = lax.rsqrt(squares[...] / width + EPSILON)
-    out[...] = (prompt[...].astype(F32) * inverse * gain[...]).astype(BF)
+def finish_kernel(prompt, own, core, far, both, gain, out, inverse, *, width):
+    @pl.when(pl.program_id(0) == 0)
+    def _():
+        total = to_column(own[...] + core[...] + far[...] + both[...])
+        inverse[...] = lax.rsqrt(total / width + EPSILON)
+
+    out[...] = (prompt[...].astype(F32) * inverse[...] * gain[...]).astype(BF)
 
 
 def finish(prompt, squares, gain):
     count, width = prompt.shape
     part = width // 4
+    small = pl.BlockSpec((count // 128, 128), lambda h: (0, 0))
     return pl.pallas_call(
         functools.partial(finish_kernel, width=4 * width),
         grid=(4,),
         out_shape=jax.ShapeDtypeStruct((count, width), BF),
-        in_specs=[
-            pl.BlockSpec((count, part), lambda h: (0, h)),
-            pl.BlockSpec((count, 1), lambda h: (0, 0)),
-            pl.BlockSpec((1, part), lambda h: (0, h)),
-        ],
+        in_specs=[pl.BlockSpec((count, part), lambda h: (0, h))]
+        + [small] * 4
+        + [pl.BlockSpec((1, part), lambda h: (0, h))],
         out_specs=pl.BlockSpec((count, part), lambda h: (0, h)),
-        compiler_params=pltpu.CompilerParams(vmem_limit_bytes=56 * 2**20),
+        scratch_shapes=[pltpu.VMEM((count, 1), F32)],
+        compiler_params=pltpu.CompilerParams(vmem_limit_bytes=10 * 2**20),
         cost_estimate=pl.CostEstimate(
             flops=3 * count * width, bytes_accessed=4 * count * width, transcendentals=count
         ),
         name="finish",
-    )(prompt, squares, gain[None, :])
+    )(prompt, *squares, gain[None, :])
 
 
 def swap_tp(block, k):
@@ -298,9 +384,8 @@
     table = jnp.broadcast_to(table.reshape(16, 1, 32), (16, 2, 32)).reshape(32, 32)
     usable = usable.astype(jnp.int32)[:, None]
 
-    projected = project(patches, jnp.swapaxes(qkv_weight, 1, 2))
-    arrived, table, pick, usable, out_weight, projected = lax.optimization_barrier(
-        (arrived, table, pick, usable, out_weight, projected)
+    arrived, table, pick, usable, out_weight = lax.optimization_barrier(
+        (arrived, table, pick, usable, out_weight)
     )
     is_own = (jnp.arange(2) == yh)[:, None, None]
     both = jnp.where(is_own, own[None], arrived[None]).reshape(-1, half)
@@ -309,26 +394,30 @@
     out_far = lax.ppermute(out_weight, "yl", [(0, 1), (1, 0)])
 
     patch_ids = jnp.repeat(image_ids.reshape(-1), MERGE)
-    patch_ids, both = lax.optimization_barrier((patch_ids, both))
+    patch_ids, patches, both = lax.optimization_barrier((patch_ids, patches, both))
+    projected = project(patches, jnp.swapaxes(qkv_weight, 1, 2))
     context = vision_context(projected, patch_ids)
-    context, out_far = lax.optimization_barrier((context, out_far))
-    out_blocks = [out_weight, swap_core(out_weight), out_far, swap_core(out_far)]
     rows = context.shape[0] // 4
     parts = [
         lax.dynamic_slice_in_dim(context, (tp ^ k) * rows, rows, 0) for k in range(4)
     ]
     parts = [parts[0]] + [swap_tp(parts[k], k) for k in (1, 2, 3)]
+    parts[2], out_far = lax.optimization_barrier((parts[2], out_far))
+    out_blocks = [out_weight, swap_core(out_weight), out_far, swap_core(out_far)]
     merged, top, bottom = project_and_norm(tp, parts, out_blocks, patches, merge_gain)
 
     table, merged, top, bottom = lax.optimization_barrier((table, merged, top, bottom))
+    after, before = shift_y(merged, 1), shift_y(merged, -1)
+    far = [shift_y(top, 2), shift_y(bottom, -2)]
+    table = lax.all_to_all(table, SEC, split_axis=0, concat_axis=0, tiled=True)
+    after, before, table = lax.optimization_barrier((after, before, table))
     near_rows = [
         (0, 0, merged),
-        (1, 0, shift_y(merged, 1)),
-        (-1, 0, shift_y(merged, -1)),
-        (2, 0, shift_y(top, 2)),
-        (2, top.shape[0], shift_y(bottom, -2)),
+        (1, 0, after),
+        (-1, 0, before),
+        (2, 0, far[0]),
+        (2, top.shape[0], far[1]),
     ]
-    table = lax.all_to_all(table, SEC, split_axis=0, concat_axis=0, tiled=True)
     blocks = []
     ids = []
     for d, offset, block in near_rows:
@@ -342,13 +431,13 @@
     send = (wanted[:, None] == row_ids[None, :]).astype(BF)
 
     image_rows = jnp.dot(stack_rows(blocks), weight, preferred_element_type=F32).astype(BF)
+    image_rows, send = lax.optimization_barrier((image_rows, send))
     outgoing = jnp.dot(send, image_rows, preferred_element_type=F32).astype(BF)
     received = lax.all_to_all(outgoing, SEC, split_axis=0, concat_axis=0, tiled=True)
     received = received.reshape(16, 2, 32, half)
-    prompt, squares = pick_rows(received, pick, usable, text_rows)
-    flat = squares.reshape(4, -1)
-    total = flat + swap_tp(flat, 1) + swap_tp(flat, 2) + swap_tp(flat, 3)
-    return finish(prompt, total.reshape(squares.shape), llm_gain)
+    squares = slot_squares(received, pick, text_squares(text_rows, usable))
+    squares = [squares] + [swap_tp(squares, k) for k in (1, 2, 3)]
+    return finish(pick_rows(received, pick, usable, text_rows), squares, llm_gain)
 
 
 def solution(mesh):

time: 193 us -> 174 us (0.902)
  waiting for transfers between devices: 75.8 us -> 59.8 us
  starting transfers between devices: 34 us -> 41.5 us
  local copies, waits for them, and re-layouts: 20.1 us -> 12.8 us
    ppermute x4, waiting for transfers between devices: 26.8 us -> 12.7 us  [shift_y(): lax.ppermute(block, ('yh', 'yl'), [(i, (i + d) % 4) for i in range(4)])]
    dot_general x1, matrix products: 13.5 us -> 2.6 us  [on_device(): outgoing = jnp.dot(send, image_rows, preferred_element_type=F32).astype(BF)]
    dot_general x0 -> x1, matrix products: none -> 9.89 us  [on_device(): jnp.dot(stack_rows(blocks), weight, preferred_element_type=F32).astype(BF)]
    ppermute x7, starting transfers between devices: 5.97 us -> 11.6 us  [swap_core(): return lax.ppermute(block, 'c', [(0, 1), (1, 0)])]
    all_to_all x1, waiting for transfers between devices: 7.67 us -> 2.21 us  [on_device(): table = lax.all_to_all(table, SEC, split_axis=0, concat_axis=0, tiled=True)]
    ppermute x1, waiting for transfers between devices: 0.01 us -> 4.71 us  [on_device(): arrived = lax.ppermute(other, 'yh', [(0, 1), (1, 0)])]
    unnamed x28 -> x22, local copies, waits for them, and re-layouts: 13.6 us -> 9.05 us
    ppermute x6, starting transfers between devices: 7.41 us -> 4.62 us  [swap_tp(): return lax.ppermute(block, TP, [(i, i ^ k) for i in range(4)])]
  transfers between devices with their start and end apart: 22 -> 22, of which waited for: 9 -> 11; matrix products, arithmetic and copies ran while one was open for 4% -> 3% of each run, Pallas kernels for 11% -> 14%
where the time goes in v8:
time: 174 us; the launch traced here: 173 us
  waiting for transfers between devices  59.8 us (34%)
  starting transfers between devices  41.5 us (24%)
  Pallas kernels  28.8 us (17%)
  between operations  13.7 us (8%)
  matrix products  13.1 us (8%)
  local copies, waits for them, and re-layouts  12.8 us (7%)
  other arithmetic  3.8 us (2%)
    all_to_all x1, waiting for transfers between devices, on_device(): lax.all_to_all(outgoing, SEC, split_axis=0, concat_axis=0, tiled=True)  28.2 us
    ppermute x4, waiting for transfers between devices, shift_y(): lax.ppermute(block, ('yh', 'yl'), [(i, (i + d) % 4) for i in range(4)])  12.7 us
    ppermute x7, starting transfers between devices, swap_core(): return lax.ppermute(block, 'c', [(0, 1), (1, 0)])  11.6 us
    ppermute x6, waiting for transfers between devices, swap_tp(): return lax.ppermute(block, TP, [(i, i ^ k) for i in range(4)])  10.6 us
    pallas_call x1, Pallas kernels, vision_context(): pl.pallas_call(attention_kernel, out_shape=jax.ShapeDtypeStruct((row_coun...  9.9 us
    dot_general x1, matrix products, on_device(): jnp.dot(stack_rows(blocks), weight, preferred_element_type=F32).astype(BF)  9.89 us
    all_to_all x1, starting transfers between devices, on_device(): table = lax.all_to_all(table, SEC, split_axis=0, concat_axis=0, tiled=True)  9.07 us
    unnamed x22, local copies, waits for them, and re-layouts  9.05 us
  transfers between devices with their start and end apart: 22, of which 11 were waited for; matrix products, arithmetic and copies ran while one was open for 3% of the time, Pallas kernels for 14%

profile of v8, /device:TPU:1, one launch (start us, length us, event | category | flops | bytes accessed | tf_op | source)
XLA Modules:
  0.0 173.5 jit_solution(10442757572874620268)
XLA Ops:
  7.7 3.8 %collective-permute-start = (bf16[160,1024]{1,0:T(8,128)(2,1)S(1)}, bf16[160,1024]{1,0:T(8,128)(2,1)S(1)}, u32[]{:S(2)}, u32[]{:S(2)}) collective-permute-start(bf16[160,1024]{1,0:T(8,128)(2,1)S(1)} %get-tuple-element.54), channel_id=1, source_target_pairs={{0,4},{4,0},{1,5},{5,1},{2,6},{6,2},{3,7},{7,3},{8,12},{12,8},{9,1... | collective-permute-start | bytes 983048 | tf_op jit(solution)/shard_map/ppermute | solution.py:371
  14.0 4.7 %collective-permute-done = bf16[160,1024]{1,0:T(8,128)(2,1)S(1)} collective-permute-done((bf16[160,1024]{1,0:T(8,128)(2,1)S(1)}, bf16[160,1024]{1,0:T(8,128)(2,1)S(1)}, u32[]{:S(2)}, u32[]{:S(2)}) %collective-permute-start) | collective-permute-done | bytes 327712 | tf_op jit(solution)/shard_map/ppermute | solution.py:371
  22.2 1.7 %copy-done.3 = bf16[1024,1280]{1,0:T(8,128)(2,1)S(1)} copy-done((bf16[1024,1280]{1,0:T(8,128)(2,1)S(1)}, bf16[1024,1280]{1,0:T(8,128)(2,1)}, u32[]{:S(2)}) %copy-start.3) | copy-done | bytes 2621464
  24.0 1.7 copy-done.7
  25.7 4.6 %project_qkv.1.projected = bf16[3,1024,320]{2,1,0:T(8,128)(2,1)S(1)} custom-call(bf16[1024,1280]{1,0:T(8,128)(2,1)S(1)} %copy-done.3, bf16[3,320,1280]{2,1,0:T(8,128)(2,1)S(1)} %bitcast.27), custom_call_target="tpu_custom_call" | custom-call | flops 2516582400 | bytes 7045120 | tf_op jit(solution)/shard_map/project_qkv/pallas_call | solution.py:29
  30.3 9.9 %vision_attention.1 = bf16[1024,320]{1,0:T(8,128)(2,1)S(1)} custom-call(s32[1024,1]{1,0:T(8,128)S(1)} %copy.13.row_ids, s32[1,1024]{1,0:T(1,128)S(1)} %bitcast.25, bf16[3,1024,320]{2,1,0:T(8,128)(2,1)S(1)} %project_qkv.1.projected), custom_call_target="tpu_custom_call" | custom-call | flops 4294967296 | bytes 2621440 | tf_op jit(solution)/shard_map/vision_attention/pallas_call | solution.py:82
  41.2 2.1 %collective-permute-start.5 = (bf16[320,1280]{1,0:T(8,128)(2,1)S(1)}, bf16[320,1280]{1,0:T(8,128)(2,1)S(1)}, u32[]{:S(2)}, u32[]{:S(2)}) collective-permute-start(bf16[320,1280]{1,0:T(8,128)(2,1)S(1)} %copy-done.5), channel_id=1, source_target_pairs={{0,1},{1,0},{2,3},{3,2},{4,5},{5,4},{6,7},{7,6},{8,9},{9,8},{10,11... | collective-permute-start | bytes 2457608 | tf_op jit(solution)/shard_map/ppermute | solution.py:349
  43.3 2.7 %collective-permute-done.2.refs_3_ = bf16[256,320]{1,0:T(8,128)(2,1)S(1)} collective-permute-done((bf16[256,320]{1,0:T(8,128)(2,1)S(1)}, bf16[256,320]{1,0:T(8,128)(2,1)S(1)}, u32[]{:S(2)}, u32[]{:S(2)}) %collective-permute-start.2) | collective-permute-done | bytes 163872 | tf_op jit(solution)/shard_map/ppermute | solution.py:341
  46.0 2.6 %collective-permute-start.6 = (bf16[320,1280]{1,0:T(8,128)(2,1)S(1)}, bf16[320,1280]{1,0:T(8,128)(2,1)}, u32[]{:S(2)}, u32[]{:S(2)}) collective-permute-start(bf16[320,1280]{1,0:T(8,128)(2,1)S(1)} %collective-permute-done.3.refs_7_), channel_id=1, source_target_pairs={{0,1},{1,0},{2,3},{3,2},{4,5},{5,4},{6,7},{7,6},{8,9},{9,8},{10,11... | collective-permute-start | bytes 2457608 | tf_op jit(solution)/shard_map/ppermute | solution.py:349
  49.1 1.9 %collective-permute-done.1.refs_2_ = bf16[256,320]{1,0:T(8,128)(2,1)} collective-permute-done((bf16[256,320]{1,0:T(8,128)(2,1)}, bf16[256,320]{1,0:T(8,128)(2,1)}, u32[]{:S(2)}, u32[]{:S(2)}) %collective-permute-start.1) | collective-permute-done | bytes 163872 | tf_op jit(solution)/shard_map/ppermute | solution.py:341
  51.0 5.0 %collective-permute-done.4.refs_4_ = bf16[256,320]{1,0:T(8,128)(2,1)} collective-permute-done((bf16[256,320]{1,0:T(8,128)(2,1)}, bf16[256,320]{1,0:T(8,128)(2,1)}, u32[]{:S(2)}, u32[]{:S(2)}) %collective-permute-start.4) | collective-permute-done | bytes 163872 | tf_op jit(solution)/shard_map/ppermute | solution.py:341
  56.0 1.7 %copy-done.4 = bf16[1024,1280]{1,0:T(8,128)(2,1)S(1)} copy-done((bf16[1024,1280]{1,0:T(8,128)(2,1)S(1)}, bf16[1024,1280]{1,0:T(8,128)(2,1)}, u32[]{:S(2)}) %copy-start.4) | copy-done | bytes 2621464
  57.8 4.5 %project_and_norm.1 = (bf16[64,5120]{1,0:T(8,128)(2,1)}, bf16[32,5120]{1,0:T(8,128)(2,1)}, bf16[32,5120]{1,0:T(8,128)(2,1)}) custom-call(s32[1]{0:T(128)} %bitcast.3.refs_0_, bf16[256,320]{1,0:T(8,128)(2,1)S(1)} %get-tuple-element.52.refs_1_, bf16[256,320]{1,0:T(8,128)(2,1)} %collective-permute-done.1.refs_2_, ...), custom_call_target="tpu_custom_call" | custom-call | flops 838860800 | bytes 5242880 | tf_op jit(solution)/shard_map/project_and_norm/pallas_call | solution.py:127
  62.3 2.7 %collective-permute-start.9 = (bf16[64,5120]{1,0:T(8,128)(2,1)}, bf16[64,5120]{1,0:T(8,128)(2,1)S(1)}, u32[]{:S(2)}, u32[]{:S(2)}) collective-permute-start(bf16[64,5120]{1,0:T(8,128)(2,1)} %get-tuple-element.36.refs_0_), channel_id=1, source_target_pairs={{0,6},{2,0},{4,2},{6,4},{1,7},{3,1},{5,3},{7,5},{8,14},{10,8},{12,... | collective-permute-start | bytes 1966088 | tf_op jit(solution)/shard_map/ppermute | solution.py:345
  66.1 1.9 %collective-permute-start.14 = (bf16[32,5120]{1,0:T(8,128)(2,1)}, bf16[32,5120]{1,0:T(8,128)(2,1)}, u32[]{:S(2)}, u32[]{:S(2)}) collective-permute-start(bf16[32,5120]{1,0:T(8,128)(2,1)} %get-tuple-element.41), channel_id=1, source_target_pairs={{0,4},{2,6},{4,0},{6,2},{1,5},{3,7},{5,1},{7,3},{8,12},{10,14},{12... | collective-permute-start | bytes 983048 | tf_op jit(solution)/shard_map/ppermute | solution.py:345
  68.0 9.1 %all-to-all-start = ((s32[32,1,32]{2,1,0:T(1,128)}), s32[32,1,32]{2,1,0:T(1,128)S(1)}, u32[]{:S(2)}, u32[]{:S(2)}) async-start(s32[32,1,32]{2,1,0:T(1,128)} %bitcast.10), calls=%async_computation | async-start | bytes 32768 | tf_op jit(solution)/shard_map/all_to_all | solution.py:412
  77.4 1.8 %collective-permute-start.7 = (bf16[64,5120]{1,0:T(8,128)(2,1)}, bf16[64,5120]{1,0:T(8,128)(2,1)S(1)}, u32[]{:S(2)}, u32[]{:S(2)}) collective-permute-start(bf16[64,5120]{1,0:T(8,128)(2,1)} %get-tuple-element.36.refs_0_), channel_id=1, source_target_pairs={{0,1},{1,0},{2,3},{3,2},{4,5},{5,4},{6,7},{7,6},{8,9},{9,8},{10,11... | collective-permute-start | bytes 1966088 | tf_op jit(solution)/shard_map/ppermute | solution.py:349
  79.2 7.7 %collective-permute-done.12.refs_6_ = bf16[32,5120]{1,0:T(8,128)(2,1)} collective-permute-done((bf16[32,5120]{1,0:T(8,128)(2,1)}, bf16[32,5120]{1,0:T(8,128)(2,1)}, u32[]{:S(2)}, u32[]{:S(2)}) %collective-permute-start.12) | collective-permute-done | bytes 327712 | tf_op jit(solution)/shard_map/ppermute | solution.py:345
  87.0 2.1 %collective-permute-start.13 = (bf16[32,5120]{1,0:T(8,128)(2,1)}, bf16[32,5120]{1,0:T(8,128)(2,1)}, u32[]{:S(2)}, u32[]{:S(2)}) collective-permute-start(bf16[32,5120]{1,0:T(8,128)(2,1)} %collective-permute-done.12.refs_6_), channel_id=1, source_target_pairs={{0,1},{1,0},{2,3},{3,2},{4,5},{5,4},{6,7},{7,6},{8,9},{9,8},{10,11... | collective-permute-start | bytes 983048 | tf_op jit(solution)/shard_map/ppermute | solution.py:349
  89.0 5.0 %collective-permute-done.14.refs_8_ = bf16[32,5120]{1,0:T(8,128)(2,1)} collective-permute-done((bf16[32,5120]{1,0:T(8,128)(2,1)}, bf16[32,5120]{1,0:T(8,128)(2,1)}, u32[]{:S(2)}, u32[]{:S(2)}) %collective-permute-start.14) | collective-permute-done | bytes 327712 | tf_op jit(solution)/shard_map/ppermute | solution.py:345
  95.2 2.2 %all-to-all-done = s32[32,1,32]{2,1,0:T(1,128)S(1)} async-done(((s32[32,1,32]{2,1,0:T(1,128)}), s32[32,1,32]{2,1,0:T(1,128)S(1)}, u32[]{:S(2)}, u32[]{:S(2)}) %all-to-all-start) | async-done | bytes 4128 | tf_op jit(solution)/shard_map/all_to_all | solution.py:412
  101.8 3.0 %stack_rows.1 = bf16[512,5120]{1,0:T(8,128)(2,1)S(1)} custom-call(bf16[64,5120]{1,0:T(8,128)(2,1)} %get-tuple-element.36.refs_0_, bf16[64,5120]{1,0:T(8,128)(2,1)S(1)} %collective-permute-done.7.refs_1_, bf16[64,5120]{1,0:T(8,128)(2,1)S(1)} %collective-permute-done.8.refs_2_, bf16[64,5120]{1,0:T(8,128)(2,1)S(1)} %collective-permute-done.10.refs_3_, ...), custom_call_target="tpu_custom_call" | custom-call | bytes 10485760 | tf_op jit(solution)/shard_map/stack_rows/pallas_call | solution.py:168
  104.8 2.3 %copy-done.2 = bf16[512,5120]{1,0:T(8,128)(2,1)} copy-done((bf16[512,5120]{1,0:T(8,128)(2,1)}, bf16[512,5120]{1,0:T(8,128)(2,1)S(1)}, u32[]{:S(2)}) %copy-start.2) | copy-done | bytes 5242904
  107.1 9.9 %convolution_convert_fusion.1 = bf16[512,1024]{1,0:T(8,128)(2,1)S(1)} fusion(bf16[512,5120]{1,0:T(8,128)(2,1)} %copy-done.2, bf16[5120,1024]{1,0:T(8,128)(2,1)} %all-gather.2.cloned.1.call-done), kind=kOutput, calls=%fused_computation.2 | convolution fusion | flops 5369233408 | bytes 16777216 | tf_op jit(solution)/shard_map/dot_general | solution.py:433
  117.0 2.6 %convolution_convert_fusion = bf16[1024,1024]{1,0:T(8,128)(2,1)} fusion(bf16[1024,512]{1,0:T(8,128)(2,1)S(1)} %copy-done.8, bf16[512,1024]{1,0:T(8,128)(2,1)S(1)} %convolution_convert_fusion.1), kind=kOutput, calls=%fused_computation.1 | convolution fusion | flops 1074790400 | bytes 4194304 | tf_op jit(solution)/shard_map/dot_general | solution.py:435
  119.6 5.3 %all-to-all-start.1 = ((bf16[32,32,1024]{2,1,0:T(8,128)(2,1)}), bf16[32,32,1024]{2,1,0:T(8,128)(2,1)S(1)}, u32[]{:S(2)}, u32[]{:S(2)}) async-start(bf16[32,32,1024]{2,1,0:T(8,128)(2,1)} %bitcast.28), calls=%async_computation.1 | async-start | bytes 4194304 | tf_op jit(solution)/shard_map/all_to_all | solution.py:436
  127.4 28.2 %all-to-all-done.1 = bf16[32,32,1024]{2,1,0:T(8,128)(2,1)S(1)} async-done(((bf16[32,32,1024]{2,1,0:T(8,128)(2,1)}), bf16[32,32,1024]{2,1,0:T(8,128)(2,1)S(1)}, u32[]{:S(2)}, u32[]{:S(2)}) %all-to-all-start.1) | async-done | bytes 2097184 | tf_op jit(solution)/shard_map/all_to_all | solution.py:436
  155.6 1.6 slot_squares.1.own
  157.3 1.9 %collective-permute-start.16 = (f32[4,128]{1,0:T(4,128)S(1)}, f32[4,128]{1,0:T(4,128)S(1)}, u32[]{:S(2)}, u32[]{:S(2)}) collective-permute-start(f32[4,128]{1,0:T(4,128)S(1)} %slot_squares.1.own), channel_id=1, source_target_pairs={{0,1},{1,0},{2,3},{3,2},{4,5},{5,4},{6,7},{7,6},{8,9},{9,8},{10,11... | collective-permute-start | bytes 6152 | tf_op jit(solution)/shard_map/ppermute | solution.py:341
  159.2 2.0 %collective-permute-start.17 = (f32[4,128]{1,0:T(4,128)S(1)}, f32[4,128]{1,0:T(4,128)S(1)}, u32[]{:S(2)}, u32[]{:S(2)}) collective-permute-start(f32[4,128]{1,0:T(4,128)S(1)} %slot_squares.1.own), channel_id=1, source_target_pairs={{0,2},{1,3},{2,0},{3,1},{4,6},{5,7},{6,4},{7,5},{8,10},{9,11},{10,... | collective-permute-start | bytes 6152 | tf_op jit(solution)/shard_map/ppermute | solution.py:341
  161.2 1.9 %pick_rows.1.prompt = bf16[512,2048]{1,0:T(8,128)(2,1)S(1)} custom-call(bf16[16,2,32,1024]{3,2,1,0:T(8,128)(2,1)S(1)} %bitcast.23, bf16[512,512]{1,0:T(8,128)(2,1)S(1)} %fusion.1.pick, s32[512,1]{1,0:T(8,128)S(1)} %copy.14.usable, bf16[512,2048]{1,0:T(8,128)(2,1)S(1)} %copy-done.1), custom_call_target="tpu_custom_call" | custom-call | flops 1073741824 | bytes 6291456 | tf_op jit(solution)/shard_map/pick_rows/pallas_call | solution.py:289
  164.2 2.5 %finish.1 = bf16[512,2048]{1,0:T(8,128)(2,1)} custom-call(bf16[512,2048]{1,0:T(8,128)(2,1)S(1)} %pick_rows.1.prompt, f32[4,128]{1,0:T(4,128)S(1)} %slot_squares.1.own, f32[4,128]{1,0:T(4,128)S(1)} %collective-permute-done.16.core, f32[4,128]{1,0:T(4,128)S(1)} %collective-permute-done.17.far, f32[4,128]{1,0:T(4,128)S(1)} %collective-permute-done.18.both, ...), custom_call_target="tpu_custom_call" | custom-call | flops 3145728 | bytes 4194304 | tf_op jit(solution)/shard_map/finish/pallas_call | solution.py:323
  (79 shorter events, 19.2 us)
Async XLA Ops:
  6.5 13.8 %copy-start.10 = (s32[1,256]{1,0:T(1,128)S(1)}, s32[1,256]{1,0:T(1,128)}, u32[]{:S(2)}) copy-start(s32[1,256]{1,0:T(1,128)} %param.10) | copy-start | bytes 3076
  6.5 100.5 %all-gather.2.cloned.1.call-start = ((), (), s32[]{:S(2)}) async-start(), calls=%async_computation.2 | async-start | bytes 11141120 | tf_op jit(solution)/shard_map/all_gather | solution.py:392
  6.5 14.3 %copy-start.5 = (bf16[320,1280]{1,0:T(8,128)(2,1)S(1)}, bf16[320,1280]{1,0:T(8,128)(2,1)}, u32[]{:S(2)}) copy-start(bf16[320,1280]{1,0:T(8,128)(2,1)} %refs_5_) | copy-start | bytes 2457604
  7.7 11.0 %collective-permute-start = (bf16[160,1024]{1,0:T(8,128)(2,1)S(1)}, bf16[160,1024]{1,0:T(8,128)(2,1)S(1)}, u32[]{:S(2)}, u32[]{:S(2)}) collective-permute-start(bf16[160,1024]{1,0:T(8,128)(2,1)S(1)} %get-tuple-element.54), channel_id=1, source_target_pairs={{0,4},{4,0},{1,5},{5,1},{2,6},{6,2},{3,7},{7,3},{8,12},{12,8},{9,1... | collective-permute-start | bytes 983048 | tf_op jit(solution)/shard_map/ppermute | solution.py:371
  20.9 25.1 %collective-permute-start.3 = (bf16[320,1280]{1,0:T(8,128)(2,1)S(1)}, bf16[320,1280]{1,0:T(8,128)(2,1)S(1)}, u32[]{:S(2)}, u32[]{:S(2)}) collective-permute-start(bf16[320,1280]{1,0:T(8,128)(2,1)S(1)} %copy-done.5), channel_id=1, source_target_pairs={{0,2},{2,0},{1,3},{3,1},{4,6},{6,4},{5,7},{7,5},{8,10},{10,8},{9,1... | collective-permute-start | bytes 2457608 | tf_op jit(solution)/shard_map/ppermute | solution.py:394
  22.2 1.7 %copy-start.3 = (bf16[1024,1280]{1,0:T(8,128)(2,1)S(1)}, bf16[1024,1280]{1,0:T(8,128)(2,1)}, u32[]{:S(2)}) copy-start(bf16[1024,1280]{1,0:T(8,128)(2,1)} %refs_9_) | copy-start | bytes 7864324
  24.0 1.7 copy-start.7
  30.3 18.8 %copy-start.9 = (f32[1280]{0:T(1024)S(1)}, f32[1280]{0:T(1024)}, u32[]{:S(2)}) copy-start(f32[1280]{0:T(1024)} %param.13) | copy-start | bytes 15364
  41.1 4.9 %collective-permute-start.2 = (bf16[256,320]{1,0:T(8,128)(2,1)S(1)}, bf16[256,320]{1,0:T(8,128)(2,1)S(1)}, u32[]{:S(2)}, u32[]{:S(2)}) collective-permute-start(bf16[256,320]{1,0:T(8,128)(2,1)S(1)} %get-tuple-element.50), channel_id=1, source_target_pairs={{0,2},{1,3},{2,0},{3,1},{4,6},{5,7},{6,4},{7,5},{8,10},{9,11},{10,... | collective-permute-start | bytes 491528 | tf_op jit(solution)/shard_map/ppermute | solution.py:341
  41.2 14.8 %collective-permute-start.5 = (bf16[320,1280]{1,0:T(8,128)(2,1)S(1)}, bf16[320,1280]{1,0:T(8,128)(2,1)S(1)}, u32[]{:S(2)}, u32[]{:S(2)}) collective-permute-start(bf16[320,1280]{1,0:T(8,128)(2,1)S(1)} %copy-done.5), channel_id=1, source_target_pairs={{0,1},{1,0},{2,3},{3,2},{4,5},{5,4},{6,7},{7,6},{8,9},{9,8},{10,11... | collective-permute-start | bytes 2457608 | tf_op jit(solution)/shard_map/ppermute | solution.py:349
  46.0 10.0 %collective-permute-start.6 = (bf16[320,1280]{1,0:T(8,128)(2,1)S(1)}, bf16[320,1280]{1,0:T(8,128)(2,1)}, u32[]{:S(2)}, u32[]{:S(2)}) collective-permute-start(bf16[320,1280]{1,0:T(8,128)(2,1)S(1)} %collective-permute-done.3.refs_7_), channel_id=1, source_target_pairs={{0,1},{1,0},{2,3},{3,2},{4,5},{5,4},{6,7},{7,6},{8,9},{9,8},{10,11... | collective-permute-start | bytes 2457608 | tf_op jit(solution)/shard_map/ppermute | solution.py:349
  48.6 2.4 %collective-permute-start.1 = (bf16[256,320]{1,0:T(8,128)(2,1)}, bf16[256,320]{1,0:T(8,128)(2,1)}, u32[]{:S(2)}, u32[]{:S(2)}) collective-permute-start(bf16[256,320]{1,0:T(8,128)(2,1)} %get-tuple-element.51), channel_id=1, source_target_pairs={{0,1},{1,0},{2,3},{3,2},{4,5},{5,4},{6,7},{7,6},{8,9},{9,8},{10,11... | collective-permute-start | bytes 491528 | tf_op jit(solution)/shard_map/ppermute | solution.py:341
  48.6 7.4 %collective-permute-start.4 = (bf16[256,320]{1,0:T(8,128)(2,1)}, bf16[256,320]{1,0:T(8,128)(2,1)}, u32[]{:S(2)}, u32[]{:S(2)}) collective-permute-start(bf16[256,320]{1,0:T(8,128)(2,1)} %get-tuple-element.49), channel_id=1, source_target_pairs={{0,3},{1,2},{2,1},{3,0},{4,7},{5,6},{6,5},{7,4},{8,11},{9,10},{10,... | collective-permute-start | bytes 491528 | tf_op jit(solution)/shard_map/ppermute | solution.py:341
  56.0 1.7 %copy-start.4 = (bf16[1024,1280]{1,0:T(8,128)(2,1)S(1)}, bf16[1024,1280]{1,0:T(8,128)(2,1)}, u32[]{:S(2)}) copy-start(bf16[1024,1280]{1,0:T(8,128)(2,1)} %refs_9_) | copy-start | bytes 7864324
  62.3 35.1 %collective-permute-start.8 = (bf16[64,5120]{1,0:T(8,128)(2,1)}, bf16[64,5120]{1,0:T(8,128)(2,1)S(1)}, u32[]{:S(2)}, u32[]{:S(2)}) collective-permute-start(bf16[64,5120]{1,0:T(8,128)(2,1)} %get-tuple-element.36.refs_0_), channel_id=1, source_target_pairs={{0,2},{2,4},{4,6},{6,0},{1,3},{3,5},{5,7},{7,1},{8,10},{10,12},{12... | collective-permute-start | bytes 1966088 | tf_op jit(solution)/shard_map/ppermute | solution.py:345
  62.3 35.1 %collective-permute-start.9 = (bf16[64,5120]{1,0:T(8,128)(2,1)}, bf16[64,5120]{1,0:T(8,128)(2,1)S(1)}, u32[]{:S(2)}, u32[]{:S(2)}) collective-permute-start(bf16[64,5120]{1,0:T(8,128)(2,1)} %get-tuple-element.36.refs_0_), channel_id=1, source_target_pairs={{0,6},{2,0},{4,2},{6,4},{1,7},{3,1},{5,3},{7,5},{8,14},{10,8},{12,... | collective-permute-start | bytes 1966088 | tf_op jit(solution)/shard_map/ppermute | solution.py:345
  65.0 22.0 %collective-permute-start.12 = (bf16[32,5120]{1,0:T(8,128)(2,1)}, bf16[32,5120]{1,0:T(8,128)(2,1)}, u32[]{:S(2)}, u32[]{:S(2)}) collective-permute-start(bf16[32,5120]{1,0:T(8,128)(2,1)} %get-tuple-element.40), channel_id=1, source_target_pairs={{0,4},{2,6},{4,0},{6,2},{1,5},{3,7},{5,1},{7,3},{8,12},{10,14},{12... | collective-permute-start | bytes 983048 | tf_op jit(solution)/shard_map/ppermute | solution.py:345
  66.1 27.8 %collective-permute-start.14 = (bf16[32,5120]{1,0:T(8,128)(2,1)}, bf16[32,5120]{1,0:T(8,128)(2,1)}, u32[]{:S(2)}, u32[]{:S(2)}) collective-permute-start(bf16[32,5120]{1,0:T(8,128)(2,1)} %get-tuple-element.41), channel_id=1, source_target_pairs={{0,4},{2,6},{4,0},{6,2},{1,5},{3,7},{5,1},{7,3},{8,12},{10,14},{12... | collective-permute-start | bytes 983048 | tf_op jit(solution)/shard_map/ppermute | solution.py:345
  68.0 29.4 %all-to-all-start = ((s32[32,1,32]{2,1,0:T(1,128)}), s32[32,1,32]{2,1,0:T(1,128)S(1)}, u32[]{:S(2)}, u32[]{:S(2)}) async-start(s32[32,1,32]{2,1,0:T(1,128)} %bitcast.10), calls=%async_computation | async-start | bytes 32768 | tf_op jit(solution)/shard_map/all_to_all | solution.py:412
  77.4 23.2 %collective-permute-start.7 = (bf16[64,5120]{1,0:T(8,128)(2,1)}, bf16[64,5120]{1,0:T(8,128)(2,1)S(1)}, u32[]{:S(2)}, u32[]{:S(2)}) collective-permute-start(bf16[64,5120]{1,0:T(8,128)(2,1)} %get-tuple-element.36.refs_0_), channel_id=1, source_target_pairs={{0,1},{1,0},{2,3},{3,2},{4,5},{5,4},{6,7},{7,6},{8,9},{9,8},{10,11... | collective-permute-start | bytes 1966088 | tf_op jit(solution)/shard_map/ppermute | solution.py:349
  87.0 13.6 %collective-permute-start.13 = (bf16[32,5120]{1,0:T(8,128)(2,1)}, bf16[32,5120]{1,0:T(8,128)(2,1)}, u32[]{:S(2)}, u32[]{:S(2)}) collective-permute-start(bf16[32,5120]{1,0:T(8,128)(2,1)} %collective-permute-done.12.refs_6_), channel_id=1, source_target_pairs={{0,1},{1,0},{2,3},{3,2},{4,5},{5,4},{6,7},{7,6},{8,9},{9,8},{10,11... | collective-permute-start | bytes 983048 | tf_op jit(solution)/shard_map/ppermute | solution.py:349
  94.0 6.6 %collective-permute-start.15 = (bf16[32,5120]{1,0:T(8,128)(2,1)}, bf16[32,5120]{1,0:T(8,128)(2,1)}, u32[]{:S(2)}, u32[]{:S(2)}) collective-permute-start(bf16[32,5120]{1,0:T(8,128)(2,1)} %collective-permute-done.14.refs_8_), channel_id=1, source_target_pairs={{0,1},{1,0},{2,3},{3,2},{4,5},{5,4},{6,7},{7,6},{8,9},{9,8},{10,11... | collective-permute-start | bytes 983048 | tf_op jit(solution)/shard_map/ppermute | solution.py:349
  97.4 3.3 %collective-permute-start.10 = (bf16[64,5120]{1,0:T(8,128)(2,1)S(1)}, bf16[64,5120]{1,0:T(8,128)(2,1)S(1)}, u32[]{:S(2)}, u32[]{:S(2)}) collective-permute-start(bf16[64,5120]{1,0:T(8,128)(2,1)S(1)} %collective-permute-done.8.refs_2_), channel_id=1, source_target_pairs={{0,1},{1,0},{2,3},{3,2},{4,5},{5,4},{6,7},{7,6},{8,9},{9,8},{10,11... | collective-permute-start | bytes 1966088 | tf_op jit(solution)/shard_map/ppermute | solution.py:349
  99.0 2.8 %collective-permute-start.11 = (bf16[64,5120]{1,0:T(8,128)(2,1)S(1)}, bf16[64,5120]{1,0:T(8,128)(2,1)}, u32[]{:S(2)}, u32[]{:S(2)}) collective-permute-start(bf16[64,5120]{1,0:T(8,128)(2,1)S(1)} %collective-permute-done.9.refs_4_), channel_id=1, source_target_pairs={{0,1},{1,0},{2,3},{3,2},{4,5},{5,4},{6,7},{7,6},{8,9},{9,8},{10,11... | collective-permute-start | bytes 1966088 | tf_op jit(solution)/shard_map/ppermute | solution.py:349
  104.8 2.3 %copy-start.2 = (bf16[512,5120]{1,0:T(8,128)(2,1)}, bf16[512,5120]{1,0:T(8,128)(2,1)S(1)}, u32[]{:S(2)}) copy-start(bf16[512,5120]{1,0:T(8,128)(2,1)S(1)} %stack_rows.1) | copy-start | bytes 15728644
  107.1 9.9 %copy-start.8 = (bf16[1024,512]{1,0:T(8,128)(2,1)S(1)}, bf16[1024,512]{1,0:T(8,128)(2,1)}, u32[]{:S(2)}) copy-start(bf16[1024,512]{1,0:T(8,128)(2,1)} %compare_convert_fusion) | copy-start | bytes 3145732
  119.6 36.1 %all-to-all-start.1 = ((bf16[32,32,1024]{2,1,0:T(8,128)(2,1)}), bf16[32,32,1024]{2,1,0:T(8,128)(2,1)S(1)}, u32[]{:S(2)}, u32[]{:S(2)}) async-start(bf16[32,32,1024]{2,1,0:T(8,128)(2,1)} %bitcast.28), calls=%async_computation.1 | async-start | bytes 4194304 | tf_op jit(solution)/shard_map/all_to_all | solution.py:436
  155.6 5.6 %copy-start.1 = (bf16[512,2048]{1,0:T(8,128)(2,1)S(1)}, bf16[512,2048]{1,0:T(8,128)(2,1)}, u32[]{:S(2)}) copy-start(bf16[512,2048]{1,0:T(8,128)(2,1)} %text.3) | copy-start | bytes 6291460
  157.3 6.9 %copy-start.6 = (f32[2048]{0:T(1024)S(1)}, f32[2048]{0:T(1024)}, u32[]{:S(2)}) copy-start(f32[2048]{0:T(1024)} %param.17) | copy-start | bytes 24580
  157.3 5.9 %collective-permute-start.16 = (f32[4,128]{1,0:T(4,128)S(1)}, f32[4,128]{1,0:T(4,128)S(1)}, u32[]{:S(2)}, u32[]{:S(2)}) collective-permute-start(f32[4,128]{1,0:T(4,128)S(1)} %slot_squares.1.own), channel_id=1, source_target_pairs={{0,1},{1,0},{2,3},{3,2},{4,5},{5,4},{6,7},{7,6},{8,9},{9,8},{10,11... | collective-permute-start | bytes 6152 | tf_op jit(solution)/shard_map/ppermute | solution.py:341
  159.2 4.0 %collective-permute-start.17 = (f32[4,128]{1,0:T(4,128)S(1)}, f32[4,128]{1,0:T(4,128)S(1)}, u32[]{:S(2)}, u32[]{:S(2)}) collective-permute-start(f32[4,128]{1,0:T(4,128)S(1)} %slot_squares.1.own), channel_id=1, source_target_pairs={{0,2},{1,3},{2,0},{3,1},{4,6},{5,7},{6,4},{7,5},{8,10},{9,11},{10,... | collective-permute-start | bytes 6152 | tf_op jit(solution)/shard_map/ppermute | solution.py:341
  161.1 3.0 %collective-permute-start.18 = (f32[4,128]{1,0:T(4,128)S(1)}, f32[4,128]{1,0:T(4,128)S(1)}, u32[]{:S(2)}, u32[]{:S(2)}) collective-permute-start(f32[4,128]{1,0:T(4,128)S(1)} %slot_squares.1.own), channel_id=1, source_target_pairs={{0,3},{1,2},{2,1},{3,0},{4,7},{5,6},{6,5},{7,4},{8,11},{9,10},{10,... | collective-permute-start | bytes 6152 | tf_op jit(solution)/shard_map/ppermute | solution.py:341
  (1 other events, 1.6 us)
Sparse Core Ops, SparseCore 0:
  20.5 83.9 all-gather.1

commit v9 on v8

--- a/solution.py
+++ b/solution.py
@@ -99,12 +99,13 @@
 
 
 def norm_kernel(*refs):
-    tp, parts, outs, (patches, gain, merged, top, bottom, normed) = (
-        refs[0], refs[1:5], refs[5:9], refs[9:],
-    )
+    parts, outs, (patches, gain, merged, normed) = refs[1:5], refs[5:11], refs[11:]
+    outs = [outs[0][...], outs[1][...]] + [
+        jnp.concatenate([outs[k][...], outs[k + 1][...]], axis=0) for k in (2, 4)
+    ]
     attended = patches[...].astype(F32)
     for part, weight in zip(parts, outs):
-        attended += jnp.dot(part[...], weight[...], preferred_element_type=F32)
+        attended += jnp.dot(part[...], weight, preferred_element_type=F32)
     moment = jnp.mean(attended * attended, axis=1, keepdims=True)
     scaled = attended * lax.rsqrt(moment + EPSILON) * gain[...]
     count, width = merged.shape[0], scaled.shape[1]
@@ -115,8 +116,6 @@
             piece = normed[q, pl.ds(j, count, stride=MERGE), :].astype(BF)
             columns = slice(j * width + q * 128, j * width + (q + 1) * 128)
             merged[:, columns] = piece
-            top[:, columns] = piece[: count // 2]
-            bottom[:, columns] = piece[count // 2 :]
 
 
 def project_and_norm(tp, parts, outs, patches, gain):
@@ -130,20 +129,12 @@
             num_scalar_prefetch=1,
             grid=(1,),
             in_specs=[whole((rows, depth))] * 4
-            + [whole((depth, width))] * 4
+            + [whole(out.shape) for out in outs]
             + [pl.BlockSpec((rows, width), lambda i, t: (t[0], 0)), whole((1, width))],
-            out_specs=[
-                whole((count, MERGE * width)),
-                whole((count // 2, MERGE * width)),
-                whole((count // 2, MERGE * width)),
-            ],
+            out_specs=whole((count, MERGE * width)),
             scratch_shapes=[pltpu.VMEM((width // 128, rows, 128), F32)],
         ),
-        out_shape=[
-            jax.ShapeDtypeStruct((count, MERGE * width), BF),
-            jax.ShapeDtypeStruct((count // 2, MERGE * width), BF),
-            jax.ShapeDtypeStruct((count // 2, MERGE * width), BF),
-        ],
+        out_shape=jax.ShapeDtypeStruct((count, MERGE * width), BF),
         compiler_params=pltpu.CompilerParams(vmem_limit_bytes=18 * 2**20),
         cost_estimate=pl.CostEstimate(
             flops=8 * rows * depth * width,
@@ -168,7 +159,7 @@
     return pl.pallas_call(
         stack_kernel,
         grid=(depth // tile,),
-        out_shape=jax.ShapeDtypeStruct((count, depth), BF),
+        out_shape=pltpu.HBM((count, depth), BF),
         in_specs=[pl.BlockSpec((b.shape[0], tile), lambda i: (0, i)) for b in blocks],
         out_specs=pl.BlockSpec((count, tile), lambda i: (0, i)),
         compiler_params=pltpu.CompilerParams(vmem_limit_bytes=10 * 2**20),
@@ -391,24 +382,26 @@
     both = jnp.where(is_own, own[None], arrived[None]).reshape(-1, half)
     weight = lax.all_gather(both, ("z", "x"), axis=0, tiled=True)
 
-    out_far = lax.ppermute(out_weight, "yl", [(0, 1), (1, 0)])
+    middle = out_weight.shape[0] // 2
+    out_far = [shift_y(out_weight[:middle], 1), shift_y(out_weight[middle:], -1)]
 
     patch_ids = jnp.repeat(image_ids.reshape(-1), MERGE)
     patch_ids, patches, both = lax.optimization_barrier((patch_ids, patches, both))
     projected = project(patches, jnp.swapaxes(qkv_weight, 1, 2))
     context = vision_context(projected, patch_ids)
+    context, *out_far = lax.optimization_barrier((context, *out_far))
     rows = context.shape[0] // 4
     parts = [
         lax.dynamic_slice_in_dim(context, (tp ^ k) * rows, rows, 0) for k in range(4)
     ]
     parts = [parts[0]] + [swap_tp(parts[k], k) for k in (1, 2, 3)]
-    parts[2], out_far = lax.optimization_barrier((parts[2], out_far))
-    out_blocks = [out_weight, swap_core(out_weight), out_far, swap_core(out_far)]
-    merged, top, bottom = project_and_norm(tp, parts, out_blocks, patches, merge_gain)
-
-    table, merged, top, bottom = lax.optimization_barrier((table, merged, top, bottom))
+    out_blocks = [out_weight, swap_core(out_weight)] + out_far + [swap_core(b) for b in out_far]
+    merged = project_and_norm(tp, parts, out_blocks, patches, merge_gain)
+
+    table, merged = lax.optimization_barrier((table, merged))
     after, before = shift_y(merged, 1), shift_y(merged, -1)
-    far = [shift_y(top, 2), shift_y(bottom, -2)]
+    count = merged.shape[0] // 2
+    far = [shift_y(after[:count], 1), shift_y(before[count:], -1)]
     table = lax.all_to_all(table, SEC, split_axis=0, concat_axis=0, tiled=True)
     after, before, table = lax.optimization_barrier((after, before, table))
     near_rows = [
@@ -416,7 +409,7 @@
         (1, 0, after),
         (-1, 0, before),
         (2, 0, far[0]),
-        (2, top.shape[0], far[1]),
+        (2, count, far[1]),
     ]
     blocks = []
     ids = []

time: 174 us -> 173 us (level)
  starting transfers between devices: 41.5 us -> 38.3 us
  local copies, waits for them, and re-layouts: 12.8 us -> 14.8 us
    ppermute x7 -> x8, starting transfers between devices: 11.6 us -> 5.23 us  [swap_core(): return lax.ppermute(block, 'c', [(0, 1), (1, 0)])]
    all_gather x1, waiting for transfers between devices: 0.01 us -> 4.04 us  [on_device(): weight = lax.all_gather(both, ('z', 'x'), axis=0, tiled=True)]
    ppermute x4 -> x6, starting transfers between devices: 5.73 us -> 8.33 us  [shift_y(): lax.ppermute(block, ('yh', 'yl'), [(i, (i + d) % 4) for i in range(4)])]
    all_to_all x1, starting transfers between devices: 5.32 us -> 7.71 us  [on_device(): lax.all_to_all(outgoing, SEC, split_axis=0, concat_axis=0, tiled=True)]
    ppermute x4 -> x6, waiting for transfers between devices: 12.7 us -> 10.3 us  [shift_y(): lax.ppermute(block, ('yh', 'yl'), [(i, (i + d) % 4) for i in range(4)])]
    all_to_all x1, waiting for transfers between devices: 2.21 us -> 0.01 us  [on_device(): table = lax.all_to_all(table, SEC, split_axis=0, concat_axis=0, tiled=True)]
    unnamed x22 -> x26, local copies, waits for them, and re-layouts: 9.05 us -> 9.26 us
  transfers between devices with their start and end apart: 22 -> 24, of which waited for: 11 -> 10; matrix products, arithmetic and copies ran while one was open for 3% -> 5% of each run, Pallas kernels for 14% -> 14%
where the time goes in v9:
time: 173 us; the launch traced here: 172 us
  waiting for transfers between devices  58.5 us (34%)
  starting transfers between devices  38.3 us (22%)
  Pallas kernels  28.7 us (17%)
  local copies, waits for them, and re-layouts  14.8 us (9%)
  between operations  13.7 us (8%)
  matrix products  13 us (8%)
  other arithmetic  4.93 us (3%)
    all_to_all x1, waiting for transfers between devices, on_device(): lax.all_to_all(outgoing, SEC, split_axis=0, concat_axis=0, tiled=True)  27.9 us
    ppermute x6, waiting for transfers between devices, swap_tp(): return lax.ppermute(block, TP, [(i, i ^ k) for i in range(4)])  10.7 us
    ppermute x6, waiting for transfers between devices, shift_y(): lax.ppermute(block, ('yh', 'yl'), [(i, (i + d) % 4) for i in range(4)])  10.3 us
    pallas_call x1, Pallas kernels, vision_context(): pl.pallas_call(attention_kernel, out_shape=jax.ShapeDtypeStruct((row_coun...  9.88 us
    dot_general x1, matrix products, on_device(): jnp.dot(stack_rows(blocks), weight, preferred_element_type=F32).astype(BF)  9.82 us
    unnamed x26, local copies, waits for them, and re-layouts  9.26 us
    ppermute x6, starting transfers between devices, shift_y(): lax.ppermute(block, ('yh', 'yl'), [(i, (i + d) % 4) for i in range(4)])  8.33 us
    all_to_all x1, starting transfers between devices, on_device(): table = lax.all_to_all(table, SEC, split_axis=0, concat_axis=0, tiled=True)  8.18 us
  transfers between devices with their start and end apart: 24, of which 10 were waited for; matrix products, arithmetic and copies ran while one was open for 5% of the time, Pallas kernels for 14%

profile of v9, /device:TPU:1, one launch (start us, length us, event | category | flops | bytes accessed | tf_op | source)
XLA Modules:
  0.0 172.0 jit_solution(16034902260264764540)
XLA Ops:
  7.7 3.8 %collective-permute-start = (bf16[160,1024]{1,0:T(8,128)(2,1)S(1)}, bf16[160,1024]{1,0:T(8,128)(2,1)S(1)}, u32[]{:S(2)}, u32[]{:S(2)}) collective-permute-start(bf16[160,1024]{1,0:T(8,128)(2,1)S(1)} %get-tuple-element.48), channel_id=1, source_target_pairs={{0,4},{4,0},{1,5},{5,1},{2,6},{6,2},{3,7},{7,3},{8,12},{12,8},{9,1... | collective-permute-start | bytes 983048 | tf_op jit(solution)/shard_map/ppermute | solution.py:362
  14.0 4.7 %collective-permute-done = bf16[160,1024]{1,0:T(8,128)(2,1)S(1)} collective-permute-done((bf16[160,1024]{1,0:T(8,128)(2,1)S(1)}, bf16[160,1024]{1,0:T(8,128)(2,1)S(1)}, u32[]{:S(2)}, u32[]{:S(2)}) %collective-permute-start) | collective-permute-done | bytes 327712 | tf_op jit(solution)/shard_map/ppermute | solution.py:362
  20.6 1.6 collective-permute-start.6
  23.2 1.3 collective-permute-start.1
  24.5 1.4 collective-permute-start.2
  25.9 1.7 %copy-done.3 = bf16[1024,1280]{1,0:T(8,128)(2,1)S(1)} copy-done((bf16[1024,1280]{1,0:T(8,128)(2,1)S(1)}, bf16[1024,1280]{1,0:T(8,128)(2,1)}, u32[]{:S(2)}) %copy-start.3) | copy-done | bytes 2621464
  27.7 1.7 copy-done.7
  29.4 4.6 %project_qkv.1.projected = bf16[3,1024,320]{2,1,0:T(8,128)(2,1)S(1)} custom-call(bf16[1024,1280]{1,0:T(8,128)(2,1)S(1)} %copy-done.3, bf16[3,320,1280]{2,1,0:T(8,128)(2,1)S(1)} %bitcast.27), custom_call_target="tpu_custom_call" | custom-call | flops 2516582400 | bytes 7045120 | tf_op jit(solution)/shard_map/project_qkv/pallas_call | solution.py:29
  34.0 1.5 copy-done.8
  37.6 1.7 copy-done.9
  39.3 9.9 %vision_attention.1 = bf16[1024,320]{1,0:T(8,128)(2,1)S(1)} custom-call(s32[1024,1]{1,0:T(8,128)S(1)} %copy-done.5, s32[1,1024]{1,0:T(1,128)S(1)} %bitcast.25, bf16[3,1024,320]{2,1,0:T(8,128)(2,1)S(1)} %copy-done.9), custom_call_target="tpu_custom_call" | custom-call | flops 4294967296 | bytes 2621440 | tf_op jit(solution)/shard_map/vision_attention/pallas_call | solution.py:82
  50.5 1.4 collective-permute-done.3.refs_2_
  52.4 4.5 %collective-permute-done.4.refs_3_ = bf16[256,320]{1,0:T(8,128)(2,1)S(1)} collective-permute-done((bf16[256,320]{1,0:T(8,128)(2,1)S(1)}, bf16[256,320]{1,0:T(8,128)(2,1)S(1)}, u32[]{:S(2)}, u32[]{:S(2)}) %collective-permute-start.4) | collective-permute-done | bytes 163872 | tf_op jit(solution)/shard_map/ppermute | solution.py:332
  56.8 4.8 %collective-permute-done.5.refs_4_ = bf16[256,320]{1,0:T(8,128)(2,1)S(1)} collective-permute-done((bf16[256,320]{1,0:T(8,128)(2,1)S(1)}, bf16[256,320]{1,0:T(8,128)(2,1)S(1)}, u32[]{:S(2)}, u32[]{:S(2)}) %collective-permute-start.5) | collective-permute-done | bytes 163872 | tf_op jit(solution)/shard_map/ppermute | solution.py:332
  61.7 2.8 %project_and_norm.1.refs_0_ = bf16[64,5120]{1,0:T(8,128)(2,1)S(1)} custom-call(s32[1]{0:T(128)} %bitcast.3.refs_0_, bf16[256,320]{1,0:T(8,128)(2,1)S(1)} %get-tuple-element.46.refs_1_, bf16[256,320]{1,0:T(8,128)(2,1)S(1)} %collective-permute-done.3.refs_2_, bf16[256,320]{1,0:T(8,128)(2,1)S(1)} %collective-permute-done.4.refs_3_, ...), custom_call_target="tpu_custom_call" | custom-call | flops 838860800 | bytes 5242880 | tf_op jit(solution)/shard_map/project_and_norm/pallas_call | solution.py:126
  64.6 2.7 %collective-permute-start.11 = (bf16[64,5120]{1,0:T(8,128)(2,1)S(1)}, bf16[64,5120]{1,0:T(8,128)(2,1)S(1)}, u32[]{:S(2)}, u32[]{:S(2)}) collective-permute-start(bf16[64,5120]{1,0:T(8,128)(2,1)S(1)} %project_and_norm.1.refs_0_), channel_id=1, source_target_pairs={{0,6},{2,0},{4,2},{6,4},{1,7},{3,1},{5,3},{7,5},{8,14},{10,8},{12,... | collective-permute-start | bytes 1966088 | tf_op jit(solution)/shard_map/ppermute | solution.py:336
  68.4 8.2 %all-to-all-start = ((s32[32,1,32]{2,1,0:T(1,128)}), s32[32,1,32]{2,1,0:T(1,128)S(1)}, u32[]{:S(2)}, u32[]{:S(2)}) async-start(s32[32,1,32]{2,1,0:T(1,128)} %bitcast.10), calls=%async_computation | async-start | bytes 32768 | tf_op jit(solution)/shard_map/all_to_all | solution.py:405
  76.6 5.8 %collective-permute-done.10.refs_2_ = bf16[64,5120]{1,0:T(8,128)(2,1)S(1)} collective-permute-done((bf16[64,5120]{1,0:T(8,128)(2,1)S(1)}, bf16[64,5120]{1,0:T(8,128)(2,1)S(1)}, u32[]{:S(2)}, u32[]{:S(2)}) %collective-permute-start.10) | collective-permute-done | bytes 655392 | tf_op jit(solution)/shard_map/ppermute | solution.py:336
  82.6 2.7 %collective-permute-start.16 = (bf16[32,5120]{1,0:T(8,128)(2,1)S(1)}, bf16[32,5120]{1,0:T(8,128)(2,1)}, u32[]{:S(2)}, u32[]{:S(2)}) collective-permute-start(bf16[32,5120]{1,0:T(8,128)(2,1)S(1)} %slice.17), channel_id=1, source_target_pairs={{0,6},{2,0},{4,2},{6,4},{1,7},{3,1},{5,3},{7,5},{8,14},{10,8},{12,... | collective-permute-start | bytes 983048 | tf_op jit(solution)/shard_map/ppermute | solution.py:336
  88.0 4.5 %collective-permute-done.14.refs_6_ = bf16[32,5120]{1,0:T(8,128)(2,1)S(1)} collective-permute-done((bf16[32,5120]{1,0:T(8,128)(2,1)S(1)}, bf16[32,5120]{1,0:T(8,128)(2,1)S(1)}, u32[]{:S(2)}, u32[]{:S(2)}) %collective-permute-start.14) | collective-permute-done | bytes 327712 | tf_op jit(solution)/shard_map/ppermute | solution.py:336
  95.8 4.6 %stack_rows.1 = bf16[512,5120]{1,0:T(8,128)(2,1)} custom-call(bf16[64,5120]{1,0:T(8,128)(2,1)S(1)} %project_and_norm.1.refs_0_, bf16[64,5120]{1,0:T(8,128)(2,1)} %collective-permute-done.9.refs_1_, bf16[64,5120]{1,0:T(8,128)(2,1)S(1)} %collective-permute-done.10.refs_2_, bf16[64,5120]{1,0:T(8,128)(2,1)} %collective-permute-done.12.refs_3_, ...), custom_call_target="tpu_custom_call" | custom-call | bytes 10485760 | tf_op jit(solution)/shard_map/stack_rows/pallas_call | solution.py:159
  100.4 4.0 %all-gather.2.cloned.1.call-done = bf16[5120,1024]{1,0:T(8,128)(2,1)} async-done(((bf16[320,1024]{1,0:T(8,128)(2,1)}), bf16[5120,1024]{1,0:T(8,128)(2,1)}) %all-gather.2.cloned.1.call-update) | async-done | bytes 10485776 | tf_op jit(solution)/shard_map/all_gather | solution.py:383
  104.5 9.8 %convolution_convert_fusion.1 = bf16[512,1024]{1,0:T(8,128)(2,1)S(1)} fusion(bf16[512,5120]{1,0:T(8,128)(2,1)} %stack_rows.1, bf16[5120,1024]{1,0:T(8,128)(2,1)} %all-gather.2.cloned.1.call-done), kind=kOutput, calls=%fused_computation.2 | convolution fusion | flops 5369233408 | bytes 16777216 | tf_op jit(solution)/shard_map/dot_general | solution.py:426
  114.3 2.6 %convolution_convert_fusion = bf16[1024,1024]{1,0:T(8,128)(2,1)} fusion(bf16[1024,512]{1,0:T(8,128)(2,1)S(1)} %copy-done.10, bf16[512,1024]{1,0:T(8,128)(2,1)S(1)} %convolution_convert_fusion.1), kind=kOutput, calls=%fused_computation.1 | convolution fusion | flops 1074790400 | bytes 4194304 | tf_op jit(solution)/shard_map/dot_general | solution.py:428
  116.9 7.7 %all-to-all-start.1 = ((bf16[32,32,1024]{2,1,0:T(8,128)(2,1)}), bf16[32,32,1024]{2,1,0:T(8,128)(2,1)S(1)}, u32[]{:S(2)}, u32[]{:S(2)}) async-start(bf16[32,32,1024]{2,1,0:T(8,128)(2,1)} %bitcast.28), calls=%async_computation.1 | async-start | bytes 4194304 | tf_op jit(solution)/shard_map/all_to_all | solution.py:429
  124.8 1.6 copy-done
  127.1 27.9 %all-to-all-done.1 = bf16[32,32,1024]{2,1,0:T(8,128)(2,1)S(1)} async-done(((bf16[32,32,1024]{2,1,0:T(8,128)(2,1)}), bf16[32,32,1024]{2,1,0:T(8,128)(2,1)S(1)}, u32[]{:S(2)}, u32[]{:S(2)}) %all-to-all-start.1) | async-done | bytes 2097184 | tf_op jit(solution)/shard_map/all_to_all | solution.py:429
  155.1 1.6 slot_squares.1.own
  156.7 2.3 %collective-permute-start.18 = (f32[4,128]{1,0:T(4,128)S(1)}, f32[4,128]{1,0:T(4,128)S(1)}, u32[]{:S(2)}, u32[]{:S(2)}) collective-permute-start(f32[4,128]{1,0:T(4,128)S(1)} %slot_squares.1.own), channel_id=1, source_target_pairs={{0,1},{1,0},{2,3},{3,2},{4,5},{5,4},{6,7},{7,6},{8,9},{9,8},{10,11... | collective-permute-start | bytes 6152 | tf_op jit(solution)/shard_map/ppermute | solution.py:332
  159.3 1.4 collective-permute-start.20
  160.7 1.9 %pick_rows.1.prompt = bf16[512,2048]{1,0:T(8,128)(2,1)S(1)} custom-call(bf16[16,2,32,1024]{3,2,1,0:T(8,128)(2,1)S(1)} %bitcast.23, bf16[512,512]{1,0:T(8,128)(2,1)S(1)} %fusion.1.pick, s32[512,1]{1,0:T(8,128)S(1)} %copy.14.usable, bf16[512,2048]{1,0:T(8,128)(2,1)S(1)} %copy-done.1), custom_call_target="tpu_custom_call" | custom-call | flops 1073741824 | bytes 6291456 | tf_op jit(solution)/shard_map/pick_rows/pallas_call | solution.py:280
  162.7 2.5 %finish.1 = bf16[512,2048]{1,0:T(8,128)(2,1)} custom-call(bf16[512,2048]{1,0:T(8,128)(2,1)S(1)} %pick_rows.1.prompt, f32[4,128]{1,0:T(4,128)S(1)} %slot_squares.1.own, f32[4,128]{1,0:T(4,128)S(1)} %collective-permute-done.18.core, f32[4,128]{1,0:T(4,128)S(1)} %collective-permute-done.19.far, f32[4,128]{1,0:T(4,128)S(1)} %collective-permute-done.20.both, ...), custom_call_target="tpu_custom_call" | custom-call | flops 3145728 | bytes 4194304 | tf_op jit(solution)/shard_map/finish/pallas_call | solution.py:314
  (90 shorter events, 18.8 us)
Async XLA Ops:
  6.5 14.1 %copy-start.2 = (bf16[320,1280]{1,0:T(8,128)(2,1)S(1)}, bf16[320,1280]{1,0:T(8,128)(2,1)}, u32[]{:S(2)}) copy-start(bf16[320,1280]{1,0:T(8,128)(2,1)} %refs_5_) | copy-start | bytes 2457604
  6.5 13.8 %copy-start.12 = (s32[1,256]{1,0:T(1,128)S(1)}, s32[1,256]{1,0:T(1,128)}, u32[]{:S(2)}) copy-start(s32[1,256]{1,0:T(1,128)} %param.10) | copy-start | bytes 3076
  6.5 97.9 %all-gather.2.cloned.1.call-start = ((), (), s32[]{:S(2)}) async-start(), calls=%async_computation.2 | async-start | bytes 11141120 | tf_op jit(solution)/shard_map/all_gather | solution.py:383
  7.7 11.0 %collective-permute-start = (bf16[160,1024]{1,0:T(8,128)(2,1)S(1)}, bf16[160,1024]{1,0:T(8,128)(2,1)S(1)}, u32[]{:S(2)}, u32[]{:S(2)}) collective-permute-start(bf16[160,1024]{1,0:T(8,128)(2,1)S(1)} %get-tuple-element.48), channel_id=1, source_target_pairs={{0,4},{4,0},{1,5},{5,1},{2,6},{6,2},{3,7},{7,3},{8,12},{12,8},{9,1... | collective-permute-start | bytes 983048 | tf_op jit(solution)/shard_map/ppermute | solution.py:362
  20.6 41.0 %collective-permute-start.6 = (bf16[320,1280]{1,0:T(8,128)(2,1)S(1)}, bf16[320,1280]{1,0:T(8,128)(2,1)S(1)}, u32[]{:S(2)}, u32[]{:S(2)}) collective-permute-start(bf16[320,1280]{1,0:T(8,128)(2,1)S(1)} %copy-done.2), channel_id=1, source_target_pairs={{0,1},{1,0},{2,3},{3,2},{4,5},{5,4},{6,7},{7,6},{8,9},{9,8},{10,11... | collective-permute-start | bytes 2457608 | tf_op jit(solution)/shard_map/ppermute | solution.py:340
  23.2 26.0 %collective-permute-start.1 = (bf16[160,1280]{1,0:T(8,128)(2,1)}, bf16[160,1280]{1,0:T(8,128)(2,1)S(1)}, u32[]{:S(2)}, u32[]{:S(2)}) collective-permute-start(bf16[160,1280]{1,0:T(8,128)(2,1)} %get-tuple-element.42), channel_id=1, source_target_pairs={{0,2},{2,4},{4,6},{6,0},{1,3},{3,5},{5,7},{7,1},{8,10},{10,12},{12... | collective-permute-start | bytes 1228808 | tf_op jit(solution)/shard_map/ppermute | solution.py:336
  24.5 24.7 %collective-permute-start.2 = (bf16[160,1280]{1,0:T(8,128)(2,1)}, bf16[160,1280]{1,0:T(8,128)(2,1)}, u32[]{:S(2)}, u32[]{:S(2)}) collective-permute-start(bf16[160,1280]{1,0:T(8,128)(2,1)} %get-tuple-element.41), channel_id=1, source_target_pairs={{0,6},{2,0},{4,2},{6,4},{1,7},{3,1},{5,3},{7,5},{8,14},{10,8},{12,... | collective-permute-start | bytes 1228808 | tf_op jit(solution)/shard_map/ppermute | solution.py:336
  25.9 1.7 %copy-start.3 = (bf16[1024,1280]{1,0:T(8,128)(2,1)S(1)}, bf16[1024,1280]{1,0:T(8,128)(2,1)}, u32[]{:S(2)}) copy-start(bf16[1024,1280]{1,0:T(8,128)(2,1)} %refs_11_) | copy-start | bytes 7864324
  39.3 13.1 %copy-start.11 = (f32[1280]{0:T(1024)S(1)}, f32[1280]{0:T(1024)}, u32[]{:S(2)}) copy-start(f32[1280]{0:T(1024)} %param.13) | copy-start | bytes 15364
  39.3 22.4 %copy-start.4 = (bf16[1024,1280]{1,0:T(8,128)(2,1)S(1)}, bf16[1024,1280]{1,0:T(8,128)(2,1)}, u32[]{:S(2)}) copy-start(bf16[1024,1280]{1,0:T(8,128)(2,1)} %refs_11_) | copy-start | bytes 7864324
  49.2 12.5 %collective-permute-start.7 = (bf16[160,1280]{1,0:T(8,128)(2,1)S(1)}, bf16[160,1280]{1,0:T(8,128)(2,1)S(1)}, u32[]{:S(2)}, u32[]{:S(2)}) collective-permute-start(bf16[160,1280]{1,0:T(8,128)(2,1)S(1)} %collective-permute-done.1.refs_7_), channel_id=1, source_target_pairs={{0,1},{1,0},{2,3},{3,2},{4,5},{5,4},{6,7},{7,6},{8,9},{9,8},{10,11... | collective-permute-start | bytes 1228808 | tf_op jit(solution)/shard_map/ppermute | solution.py:340
  49.7 11.9 %collective-permute-start.8 = (bf16[160,1280]{1,0:T(8,128)(2,1)}, bf16[160,1280]{1,0:T(8,128)(2,1)S(1)}, u32[]{:S(2)}, u32[]{:S(2)}) collective-permute-start(bf16[160,1280]{1,0:T(8,128)(2,1)} %collective-permute-done.2.refs_8_), channel_id=1, source_target_pairs={{0,1},{1,0},{2,3},{3,2},{4,5},{5,4},{6,7},{7,6},{8,9},{9,8},{10,11... | collective-permute-start | bytes 1228808 | tf_op jit(solution)/shard_map/ppermute | solution.py:340
  49.9 2.1 %collective-permute-start.3 = (bf16[256,320]{1,0:T(8,128)(2,1)S(1)}, bf16[256,320]{1,0:T(8,128)(2,1)S(1)}, u32[]{:S(2)}, u32[]{:S(2)}) collective-permute-start(bf16[256,320]{1,0:T(8,128)(2,1)S(1)} %get-tuple-element.45), channel_id=1, source_target_pairs={{0,1},{1,0},{2,3},{3,2},{4,5},{5,4},{6,7},{7,6},{8,9},{9,8},{10,11... | collective-permute-start | bytes 491528 | tf_op jit(solution)/shard_map/ppermute | solution.py:332
  50.4 6.5 %collective-permute-start.4 = (bf16[256,320]{1,0:T(8,128)(2,1)S(1)}, bf16[256,320]{1,0:T(8,128)(2,1)S(1)}, u32[]{:S(2)}, u32[]{:S(2)}) collective-permute-start(bf16[256,320]{1,0:T(8,128)(2,1)S(1)} %get-tuple-element.44), channel_id=1, source_target_pairs={{0,2},{1,3},{2,0},{3,1},{4,6},{5,7},{6,4},{7,5},{8,10},{9,11},{10,... | collective-permute-start | bytes 491528 | tf_op jit(solution)/shard_map/ppermute | solution.py:332
  52.0 9.7 %collective-permute-start.5 = (bf16[256,320]{1,0:T(8,128)(2,1)S(1)}, bf16[256,320]{1,0:T(8,128)(2,1)S(1)}, u32[]{:S(2)}, u32[]{:S(2)}) collective-permute-start(bf16[256,320]{1,0:T(8,128)(2,1)S(1)} %get-tuple-element.43), channel_id=1, source_target_pairs={{0,3},{1,2},{2,1},{3,0},{4,7},{5,6},{6,5},{7,4},{8,11},{9,10},{10,... | collective-permute-start | bytes 491528 | tf_op jit(solution)/shard_map/ppermute | solution.py:332
  64.5 17.9 %collective-permute-start.10 = (bf16[64,5120]{1,0:T(8,128)(2,1)S(1)}, bf16[64,5120]{1,0:T(8,128)(2,1)S(1)}, u32[]{:S(2)}, u32[]{:S(2)}) collective-permute-start(bf16[64,5120]{1,0:T(8,128)(2,1)S(1)} %project_and_norm.1.refs_0_), channel_id=1, source_target_pairs={{0,2},{2,4},{4,6},{6,0},{1,3},{3,5},{5,7},{7,1},{8,10},{10,12},{12... | collective-permute-start | bytes 1966088 | tf_op jit(solution)/shard_map/ppermute | solution.py:336
  64.6 17.9 %collective-permute-start.11 = (bf16[64,5120]{1,0:T(8,128)(2,1)S(1)}, bf16[64,5120]{1,0:T(8,128)(2,1)S(1)}, u32[]{:S(2)}, u32[]{:S(2)}) collective-permute-start(bf16[64,5120]{1,0:T(8,128)(2,1)S(1)} %project_and_norm.1.refs_0_), channel_id=1, source_target_pairs={{0,6},{2,0},{4,2},{6,4},{1,7},{3,1},{5,3},{7,5},{8,14},{10,8},{12,... | collective-permute-start | bytes 1966088 | tf_op jit(solution)/shard_map/ppermute | solution.py:336
  68.4 19.0 %all-to-all-start = ((s32[32,1,32]{2,1,0:T(1,128)}), s32[32,1,32]{2,1,0:T(1,128)S(1)}, u32[]{:S(2)}, u32[]{:S(2)}) async-start(s32[32,1,32]{2,1,0:T(1,128)} %bitcast.10), calls=%async_computation | async-start | bytes 32768 | tf_op jit(solution)/shard_map/all_to_all | solution.py:405
  82.5 10.1 %collective-permute-start.14 = (bf16[32,5120]{1,0:T(8,128)(2,1)S(1)}, bf16[32,5120]{1,0:T(8,128)(2,1)S(1)}, u32[]{:S(2)}, u32[]{:S(2)}) collective-permute-start(bf16[32,5120]{1,0:T(8,128)(2,1)S(1)} %slice.16), channel_id=1, source_target_pairs={{0,2},{2,4},{4,6},{6,0},{1,3},{3,5},{5,7},{7,1},{8,10},{10,12},{12... | collective-permute-start | bytes 983048 | tf_op jit(solution)/shard_map/ppermute | solution.py:336
  82.6 11.3 %collective-permute-start.16 = (bf16[32,5120]{1,0:T(8,128)(2,1)S(1)}, bf16[32,5120]{1,0:T(8,128)(2,1)}, u32[]{:S(2)}, u32[]{:S(2)}) collective-permute-start(bf16[32,5120]{1,0:T(8,128)(2,1)S(1)} %slice.17), channel_id=1, source_target_pairs={{0,6},{2,0},{4,2},{6,4},{1,7},{3,1},{5,3},{7,5},{8,14},{10,8},{12,... | collective-permute-start | bytes 983048 | tf_op jit(solution)/shard_map/ppermute | solution.py:336
  86.3 8.8 %collective-permute-start.9 = (bf16[64,5120]{1,0:T(8,128)(2,1)S(1)}, bf16[64,5120]{1,0:T(8,128)(2,1)}, u32[]{:S(2)}, u32[]{:S(2)}) collective-permute-start(bf16[64,5120]{1,0:T(8,128)(2,1)S(1)} %project_and_norm.1.refs_0_), channel_id=1, source_target_pairs={{0,1},{1,0},{2,3},{3,2},{4,5},{5,4},{6,7},{7,6},{8,9},{9,8},{10,11... | collective-permute-start | bytes 1966088 | tf_op jit(solution)/shard_map/ppermute | solution.py:340
  87.4 7.7 %collective-permute-start.12 = (bf16[64,5120]{1,0:T(8,128)(2,1)S(1)}, bf16[64,5120]{1,0:T(8,128)(2,1)}, u32[]{:S(2)}, u32[]{:S(2)}) collective-permute-start(bf16[64,5120]{1,0:T(8,128)(2,1)S(1)} %collective-permute-done.10.refs_2_), channel_id=1, source_target_pairs={{0,1},{1,0},{2,3},{3,2},{4,5},{5,4},{6,7},{7,6},{8,9},{9,8},{10,11... | collective-permute-start | bytes 1966088 | tf_op jit(solution)/shard_map/ppermute | solution.py:340
  87.5 7.6 %collective-permute-start.13 = (bf16[64,5120]{1,0:T(8,128)(2,1)S(1)}, bf16[64,5120]{1,0:T(8,128)(2,1)}, u32[]{:S(2)}, u32[]{:S(2)}) collective-permute-start(bf16[64,5120]{1,0:T(8,128)(2,1)S(1)} %collective-permute-done.11.refs_4_), channel_id=1, source_target_pairs={{0,1},{1,0},{2,3},{3,2},{4,5},{5,4},{6,7},{7,6},{8,9},{9,8},{10,11... | collective-permute-start | bytes 1966088 | tf_op jit(solution)/shard_map/ppermute | solution.py:340
  92.5 3.0 %collective-permute-start.15 = (bf16[32,5120]{1,0:T(8,128)(2,1)S(1)}, bf16[32,5120]{1,0:T(8,128)(2,1)S(1)}, u32[]{:S(2)}, u32[]{:S(2)}) collective-permute-start(bf16[32,5120]{1,0:T(8,128)(2,1)S(1)} %collective-permute-done.14.refs_6_), channel_id=1, source_target_pairs={{0,1},{1,0},{2,3},{3,2},{4,5},{5,4},{6,7},{7,6},{8,9},{9,8},{10,11... | collective-permute-start | bytes 983048 | tf_op jit(solution)/shard_map/ppermute | solution.py:340
  93.9 1.9 %collective-permute-start.17 = (bf16[32,5120]{1,0:T(8,128)(2,1)}, bf16[32,5120]{1,0:T(8,128)(2,1)S(1)}, u32[]{:S(2)}, u32[]{:S(2)}) collective-permute-start(bf16[32,5120]{1,0:T(8,128)(2,1)} %collective-permute-done.16.refs_8_), channel_id=1, source_target_pairs={{0,1},{1,0},{2,3},{3,2},{4,5},{5,4},{6,7},{7,6},{8,9},{9,8},{10,11... | collective-permute-start | bytes 983048 | tf_op jit(solution)/shard_map/ppermute | solution.py:340
  100.4 13.9 %copy-start.10 = (bf16[1024,512]{1,0:T(8,128)(2,1)S(1)}, bf16[1024,512]{1,0:T(8,128)(2,1)}, u32[]{:S(2)}) copy-start(bf16[1024,512]{1,0:T(8,128)(2,1)} %compare_convert_fusion) | copy-start | bytes 3145732
  116.9 38.1 %all-to-all-start.1 = ((bf16[32,32,1024]{2,1,0:T(8,128)(2,1)}), bf16[32,32,1024]{2,1,0:T(8,128)(2,1)S(1)}, u32[]{:S(2)}, u32[]{:S(2)}) async-start(bf16[32,32,1024]{2,1,0:T(8,128)(2,1)} %bitcast.28), calls=%async_computation.1 | async-start | bytes 4194304 | tf_op jit(solution)/shard_map/all_to_all | solution.py:429
  155.1 5.7 %copy-start.1 = (bf16[512,2048]{1,0:T(8,128)(2,1)S(1)}, bf16[512,2048]{1,0:T(8,128)(2,1)}, u32[]{:S(2)}) copy-start(bf16[512,2048]{1,0:T(8,128)(2,1)} %text.3) | copy-start | bytes 6291460
  156.7 6.0 %copy-start.6 = (f32[2048]{0:T(1024)S(1)}, f32[2048]{0:T(1024)}, u32[]{:S(2)}) copy-start(f32[2048]{0:T(1024)} %param.17) | copy-start | bytes 24580
  156.7 5.9 %collective-permute-start.18 = (f32[4,128]{1,0:T(4,128)S(1)}, f32[4,128]{1,0:T(4,128)S(1)}, u32[]{:S(2)}, u32[]{:S(2)}) collective-permute-start(f32[4,128]{1,0:T(4,128)S(1)} %slot_squares.1.own), channel_id=1, source_target_pairs={{0,1},{1,0},{2,3},{3,2},{4,5},{5,4},{6,7},{7,6},{8,9},{9,8},{10,11... | collective-permute-start | bytes 6152 | tf_op jit(solution)/shard_map/ppermute | solution.py:332
  159.0 3.7 %collective-permute-start.19 = (f32[4,128]{1,0:T(4,128)S(1)}, f32[4,128]{1,0:T(4,128)S(1)}, u32[]{:S(2)}, u32[]{:S(2)}) collective-permute-start(f32[4,128]{1,0:T(4,128)S(1)} %slot_squares.1.own), channel_id=1, source_target_pairs={{0,2},{1,3},{2,0},{3,1},{4,6},{5,7},{6,4},{7,5},{8,10},{9,11},{10,... | collective-permute-start | bytes 6152 | tf_op jit(solution)/shard_map/ppermute | solution.py:332
  159.3 3.4 %collective-permute-start.20 = (f32[4,128]{1,0:T(4,128)S(1)}, f32[4,128]{1,0:T(4,128)S(1)}, u32[]{:S(2)}, u32[]{:S(2)}) collective-permute-start(f32[4,128]{1,0:T(4,128)S(1)} %slot_squares.1.own), channel_id=1, source_target_pairs={{0,3},{1,2},{2,1},{3,0},{4,7},{5,6},{6,5},{7,4},{8,11},{9,10},{10,... | collective-permute-start | bytes 6152 | tf_op jit(solution)/shard_map/ppermute | solution.py:332
  (5 other events, 7.5 us)
Sparse Core Ops, SparseCore 0:
  20.5 83.9 all-gather.1

commit v10 on v9

--- a/solution.py
+++ b/solution.py
@@ -17,53 +17,40 @@
 F32 = jnp.float32
 
 
-def project_kernel(patches, weight, projected):
-    projected[0] = lax.dot_general(
-        patches[...], weight[0], (((1,), (1,)), ((), ())), preferred_element_type=F32
-    ).astype(BF)
-
-
-def project(patches, weight):
-    rows, depth = patches.shape
-    count, width, _ = weight.shape
-    return pl.pallas_call(
-        project_kernel,
-        grid=(count,),
-        out_shape=jax.ShapeDtypeStruct((count, rows, width), BF),
-        in_specs=[
-            pl.BlockSpec((rows, depth), lambda i: (0, 0), pipeline_mode=pl.Buffered(1)),
-            pl.BlockSpec((1, width, depth), lambda i: (i, 0, 0)),
-        ],
-        out_specs=pl.BlockSpec((1, rows, width), lambda i: (i, 0, 0)),
-        compiler_params=pltpu.CompilerParams(vmem_limit_bytes=14 * 2**20),
-        cost_estimate=pl.CostEstimate(
-            flops=2 * rows * depth * width * count,
-            bytes_accessed=2 * (rows * depth + count * width * (depth + rows)),
-            transcendentals=0,
-        ),
-        name="project_qkv",
-    )(patches, weight)
-
-
-def attention_kernel(row_ids, column_ids, projected, context, keys, values):
+def attention_kernel(row_ids, column_ids, patches, weight, context, queries, keys, values):
     heads = keys.shape[0]
-    row_count = projected.shape[1]
-    one = jnp.ones((row_count, 128 - HEAD_DIM), BF)
-    for head in range(heads):
-        columns = slice(head * HEAD_DIM, (head + 1) * HEAD_DIM)
-        keys[head] = projected[1, :, columns]
-        values[head] = jnp.concatenate([projected[2, :, columns], one], axis=1)
+    row_count = patches.shape[0]
+    block = min(256, row_count)
+    one = jnp.ones((block, 128 - HEAD_DIM), BF)
+
+    def project(index, carry):
+        rows = pl.ds(pl.multiple_of(index * block, block), block)
+        query, key, value = (
+            lax.dot_general(
+                patches[rows, :], weight[c], (((1,), (1,)), ((), ())), preferred_element_type=F32
+            ).astype(BF)
+            for c in range(3)
+        )
+        for head in range(heads):
+            columns = slice(head * HEAD_DIM, (head + 1) * HEAD_DIM)
+            queries[head, rows, :] = query[:, columns]
+            keys[head, rows, :] = key[:, columns]
+            values[head, rows, :] = jnp.concatenate([value[:, columns], one], axis=1)
+        return carry
+
+    lax.fori_loop(0, row_count // block, project, 0)
     scale = HEAD_DIM ** (-0.5) * LOG2E
-    block = min(256, row_count)
 
     def one_block(index, carry):
         rows = pl.ds(pl.multiple_of(index * block, block), block)
         same_image = row_ids[rows, :] == column_ids[...]
         outs = []
         for head in range(heads):
-            query = projected[0, rows, head * HEAD_DIM : (head + 1) * HEAD_DIM]
             scores = lax.dot_general(
-                query, keys[head], (((1,), (1,)), ((), ())), preferred_element_type=F32
+                queries[head, rows, :],
+                keys[head],
+                (((1,), (1,)), ((), ())),
+                preferred_element_type=F32,
             )
             scores = jnp.where(same_image, scores, -1e30)
             highest = jnp.max(scores, axis=1, keepdims=True)
@@ -76,26 +63,28 @@
     lax.fori_loop(0, row_count // block, one_block, 0)
 
 
-def vision_context(projected, patch_ids):
-    row_count, width = projected.shape[1:]
+def vision_context(patches, weight, patch_ids):
+    row_count, depth = patches.shape
+    width = weight.shape[1]
     heads = width // HEAD_DIM
     return pl.pallas_call(
         attention_kernel,
         out_shape=jax.ShapeDtypeStruct((row_count, width), BF),
-        in_specs=[pl.BlockSpec(memory_space=pltpu.VMEM)] * 3,
+        in_specs=[pl.BlockSpec(memory_space=pltpu.VMEM)] * 4,
         out_specs=pl.BlockSpec(memory_space=pltpu.VMEM),
         scratch_shapes=[
+            pltpu.VMEM((heads, row_count, HEAD_DIM), BF),
             pltpu.VMEM((heads, row_count, HEAD_DIM), BF),
             pltpu.VMEM((heads, row_count, 128), BF),
         ],
         compiler_params=pltpu.CompilerParams(vmem_limit_bytes=20 * 2**20),
         cost_estimate=pl.CostEstimate(
-            flops=4 * heads * row_count * row_count * 256,
-            bytes_accessed=8 * row_count * width,
+            flops=4 * heads * row_count * row_count * 256 + 6 * row_count * depth * width,
+            bytes_accessed=2 * (row_count + 3 * width) * depth,
             transcendentals=heads * row_count * row_count,
         ),
         name="vision_attention",
-    )(patch_ids[:, None], patch_ids[None, :], projected)
+    )(patch_ids[:, None], patch_ids[None, :], patches, weight)
 
 
 def norm_kernel(*refs):
@@ -159,7 +148,7 @@
     return pl.pallas_call(
         stack_kernel,
         grid=(depth // tile,),
-        out_shape=pltpu.HBM((count, depth), BF),
+        out_shape=jax.ShapeDtypeStruct((count, depth), BF),
         in_specs=[pl.BlockSpec((b.shape[0], tile), lambda i: (0, i)) for b in blocks],
         out_specs=pl.BlockSpec((count, tile), lambda i: (0, i)),
         compiler_params=pltpu.CompilerParams(vmem_limit_bytes=10 * 2**20),
@@ -168,6 +157,50 @@
         ),
         name="stack_rows",
     )(*blocks)
+
+
+def merge_kernel(rows, weight, send, outgoing, held, sems, *, first):
+    depth, columns = held.shape
+    steps = sems.shape[0]
+    tile = depth // steps
+    copies = [
+        pltpu.make_async_copy(
+            weight.at[pl.ds(k * tile, tile), pl.ds(first, columns)],
+            held.at[pl.ds(k * tile, tile)],
+            sems.at[k],
+        )
+        for k in range(steps)
+    ]
+    for copy in copies:
+        copy.start()
+    total = jnp.zeros((rows.shape[0], columns), F32)
+    for k, copy in enumerate(copies):
+        copy.wait()
+        part = slice(k * tile, (k + 1) * tile)
+        total += jnp.dot(rows[:, part], held[part, :], preferred_element_type=F32)
+    outgoing[...] = jnp.dot(
+        send[...], total.astype(BF), preferred_element_type=F32
+    ).astype(BF)
+
+
+def merge_and_select(rows, weight, send, first, columns):
+    slots, count = send.shape
+    depth = weight.shape[0]
+    vmem = pl.BlockSpec(memory_space=pltpu.VMEM)
+    return pl.pallas_call(
+        functools.partial(merge_kernel, first=first),
+        out_shape=jax.ShapeDtypeStruct((slots, columns), BF),
+        in_specs=[vmem, pl.BlockSpec(memory_space=pltpu.HBM), vmem],
+        out_specs=vmem,
+        scratch_shapes=[pltpu.VMEM((depth, columns), BF), pltpu.SemaphoreType.DMA((4,))],
+        compiler_params=pltpu.CompilerParams(vmem_limit_bytes=24 * 2**20),
+        cost_estimate=pl.CostEstimate(
+            flops=2 * count * (depth + slots) * columns,
+            bytes_accessed=2 * (count * depth + depth * columns + slots * columns),
+            transcendentals=0,
+        ),
+        name="merge_rows",
+    )(rows, weight, send)
 
 
 def square_sums(block):
@@ -199,20 +232,21 @@
 
 
 def text_kernel(text, usable, squares):
-    squares[...] = jnp.where(usable[...] > 0, 0.0, square_sums(text[...]))
+    total = jnp.where(usable[...] > 0, 0.0, square_sums(text[...]))
+    to_lanes(total, squares.at[pl.ds(pl.program_id(0), 1)])
 
 
 def text_squares(text, usable):
     count, width = text.shape
     return pl.pallas_call(
         text_kernel,
-        grid=(4,),
-        out_shape=jax.ShapeDtypeStruct((count, 1), F32),
+        grid=(count // 128,),
+        out_shape=jax.ShapeDtypeStruct((count // 128, 128), F32),
         in_specs=[
-            pl.BlockSpec((count // 4, width), lambda i: (i, 0)),
-            pl.BlockSpec((count // 4, 1), lambda i: (i, 0)),
+            pl.BlockSpec((128, width), lambda i: (i, 0)),
+            pl.BlockSpec((128, 1), lambda i: (i, 0)),
         ],
-        out_specs=pl.BlockSpec((count // 4, 1), lambda i: (i, 0)),
+        out_specs=pl.BlockSpec((count // 128, 128), lambda i: (0, 0)),
         compiler_params=pltpu.CompilerParams(vmem_limit_bytes=10 * 2**20),
         cost_estimate=pl.CostEstimate(
             flops=2 * count * width, bytes_accessed=2 * count * width, transcendentals=0
@@ -221,7 +255,7 @@
     )(text, usable)
 
 
-def squares_kernel(received, pick, from_text, squares, total):
+def squares_kernel(received, pick, base, squares, total):
     arrived = received[...].reshape(pick.shape[1], received.shape[-1])
     step = pl.program_id(0)
 
@@ -236,15 +270,16 @@
     @pl.when(step == pl.num_programs(0) - 1)
     def _():
         rest = jnp.broadcast_to(total[...], (total.shape[0], 128))
-        chosen = jnp.broadcast_to(from_text[...], (pick.shape[0], 128))
+        chosen = jnp.zeros((pick.shape[0], 128), F32)
         for _ in range(3):
             part = rest.astype(BF)
             chosen += jnp.dot(pick[...], part, preferred_element_type=F32)
             rest = rest - part.astype(F32)
         to_lanes(chosen[:, :1], squares)
-
-
-def slot_squares(received, pick, from_text):
+        squares[...] += base[...]
+
+
+def slot_squares(received, pick, base):
     planes, halves, rows, part = received.shape
     count, slots = pick.shape
     return pl.pallas_call(
@@ -254,18 +289,18 @@
         in_specs=[
             pl.BlockSpec((planes, 1, rows, part), lambda h: (0, h, 0, 0)),
             pl.BlockSpec((count, slots), lambda h: (0, 0), pipeline_mode=pl.Buffered(1)),
-            pl.BlockSpec((count, 1), lambda h: (0, 0), pipeline_mode=pl.Buffered(1)),
+            pl.BlockSpec((count // 128, 128), lambda h: (0, 0)),
         ],
         out_specs=pl.BlockSpec((count // 128, 128), lambda h: (0, 0)),
         scratch_shapes=[pltpu.VMEM((slots, 1), F32)],
-        compiler_params=pltpu.CompilerParams(vmem_limit_bytes=14 * 2**20),
+        compiler_params=pltpu.CompilerParams(vmem_limit_bytes=12 * 2**20),
         cost_estimate=pl.CostEstimate(
             flops=2 * slots * halves * part,
             bytes_accessed=2 * slots * halves * part,
             transcendentals=0,
         ),
         name="slot_squares",
-    )(received, pick, from_text)
+    )(received, pick, base)
 
 
 def pick_kernel(received, pick, usable, text, prompt):
@@ -274,9 +309,10 @@
     prompt[...] = jnp.where(usable[...] > 0, picked, text[...].astype(F32)).astype(BF)
 
 
-def pick_rows(received, pick, usable, text):
+def pick_rows(received, pick, usable, text, index):
     planes, halves, rows, part = received.shape
     count, slots = pick.shape
+    parts = text.shape[1] // (halves * part)
     return pl.pallas_call(
         pick_kernel,
         grid=(halves,),
@@ -285,7 +321,7 @@
             pl.BlockSpec((planes, 1, rows, part), lambda h: (0, h, 0, 0)),
             pl.BlockSpec((count, slots), lambda h: (0, 0), pipeline_mode=pl.Buffered(1)),
             pl.BlockSpec((count, 1), lambda h: (0, 0), pipeline_mode=pl.Buffered(1)),
-            pl.BlockSpec((count, part), lambda h: (0, h)),
+            pl.BlockSpec((count, part), lambda h: (0, h * parts + index)),
         ],
         out_specs=pl.BlockSpec((count, part), lambda h: (0, h)),
         compiler_params=pltpu.CompilerParams(vmem_limit_bytes=14 * 2**20),
@@ -298,34 +334,36 @@
     )(received, pick, usable, text)
 
 
-def finish_kernel(prompt, own, core, far, both, gain, out, inverse, *, width):
+def finish_kernel(first, second, own, core, far, both, gain, out, inverse, *, width):
     @pl.when(pl.program_id(0) == 0)
     def _():
         total = to_column(own[...] + core[...] + far[...] + both[...])
         inverse[...] = lax.rsqrt(total / width + EPSILON)
 
-    out[...] = (prompt[...].astype(F32) * inverse[...] * gain[...]).astype(BF)
-
-
-def finish(prompt, squares, gain):
-    count, width = prompt.shape
-    part = width // 4
+    part = first.shape[1]
+    out[:, :part] = (first[...].astype(F32) * inverse[...] * gain[:, :part]).astype(BF)
+    out[:, part:] = (second[...].astype(F32) * inverse[...] * gain[:, part:]).astype(BF)
+
+
+def finish(first, second, squares, gain):
+    count, width = first.shape
+    part = width // 2
     small = pl.BlockSpec((count // 128, 128), lambda h: (0, 0))
     return pl.pallas_call(
-        functools.partial(finish_kernel, width=4 * width),
-        grid=(4,),
-        out_shape=jax.ShapeDtypeStruct((count, width), BF),
-        in_specs=[pl.BlockSpec((count, part), lambda h: (0, h))]
+        functools.partial(finish_kernel, width=8 * width),
+        grid=(2,),
+        out_shape=jax.ShapeDtypeStruct((count, 2 * width), BF),
+        in_specs=[pl.BlockSpec((count, part), lambda h: (0, h))] * 2
         + [small] * 4
-        + [pl.BlockSpec((1, part), lambda h: (0, h))],
-        out_specs=pl.BlockSpec((count, part), lambda h: (0, h)),
+        + [pl.BlockSpec((1, 2 * part), lambda h: (0, h))],
+        out_specs=pl.BlockSpec((count, 2 * part), lambda h: (0, h)),
         scratch_shapes=[pltpu.VMEM((count, 1), F32)],
-        compiler_params=pltpu.CompilerParams(vmem_limit_bytes=10 * 2**20),
-        cost_estimate=pl.CostEstimate(
-            flops=3 * count * width, bytes_accessed=4 * count * width, transcendentals=count
+        compiler_params=pltpu.CompilerParams(vmem_limit_bytes=12 * 2**20),
+        cost_estimate=pl.CostEstimate(
+            flops=6 * count * width, bytes_accessed=8 * count * width, transcendentals=count
         ),
         name="finish",
-    )(prompt, *squares, gain[None, :])
+    )(first, second, *squares, gain[None, :])
 
 
 def swap_tp(block, k):
@@ -387,8 +425,7 @@
 
     patch_ids = jnp.repeat(image_ids.reshape(-1), MERGE)
     patch_ids, patches, both = lax.optimization_barrier((patch_ids, patches, both))
-    projected = project(patches, jnp.swapaxes(qkv_weight, 1, 2))
-    context = vision_context(projected, patch_ids)
+    context = vision_context(patches, jnp.swapaxes(qkv_weight, 1, 2), patch_ids)
     context, *out_far = lax.optimization_barrier((context, *out_far))
     rows = context.shape[0] // 4
     parts = [
@@ -423,14 +460,17 @@
     wanted = jnp.where(wanted >= 0, wanted + jnp.arange(2)[None, :, None] * 256, -1).reshape(-1)
     send = (wanted[:, None] == row_ids[None, :]).astype(BF)
 
-    image_rows = jnp.dot(stack_rows(blocks), weight, preferred_element_type=F32).astype(BF)
-    image_rows, send = lax.optimization_barrier((image_rows, send))
-    outgoing = jnp.dot(send, image_rows, preferred_element_type=F32).astype(BF)
-    received = lax.all_to_all(outgoing, SEC, split_axis=0, concat_axis=0, tiled=True)
-    received = received.reshape(16, 2, 32, half)
-    squares = slot_squares(received, pick, text_squares(text_rows, usable))
+    rows = stack_rows(blocks)
+    squares = text_squares(text_rows, usable)
+    prompts = []
+    for index in range(2):
+        outgoing = merge_and_select(rows, weight, send, index * half // 2, half // 2)
+        received = lax.all_to_all(outgoing, SEC, split_axis=0, concat_axis=0, tiled=True)
+        received = received.reshape(16, 2, 32, half // 2)
+        squares = slot_squares(received, pick, squares)
+        prompts.append(pick_rows(received, pick, usable, text_rows, index))
     squares = [squares] + [swap_tp(squares, k) for k in (1, 2, 3)]
-    return finish(pick_rows(received, pick, usable, text_rows), squares, llm_gain)
+    return finish(*prompts, squares, llm_gain)
 
 
 def solution(mesh):

time: 173 us -> 185 us (1.069)
  matrix products: 13 us -> 0.61 us
  Pallas kernels: 28.7 us -> 40.4 us
  local copies, waits for them, and re-layouts: 14.8 us -> 22.8 us
  starting transfers between devices: 38.3 us -> 45 us
  other arithmetic: 4.93 us -> 2.8 us
    dot_general x2 -> x0, matrix products: 12.4 us -> none  [the longest x1 9.82 us: on_device(): jnp.dot(stack_rows(blocks), weight, preferred_element_type=F32).astype(BF)]
    unnamed x26 -> x28, local copies, waits for them, and re-layouts: 9.26 us -> 19.6 us
    all_to_all x1 -> x2, waiting for transfers between devices: 27.9 us -> 19.6 us  [on_device(): lax.all_to_all(outgoing, SEC, split_axis=0, concat_axis=0, tiled=True)]
    all_gather x1, waiting for transfers between devices: 4.04 us -> 11.2 us  [on_device(): weight = lax.all_gather(both, ('z', 'x'), axis=0, tiled=True)]
    all_to_all x1 -> x2, starting transfers between devices: 7.71 us -> 12.5 us  [on_device(): lax.all_to_all(outgoing, SEC, split_axis=0, concat_axis=0, tiled=True)]
    pallas_call x1, Pallas kernels: 9.88 us -> 14 us  [vision_context(): pl.pallas_call(attention_kernel, out_shape=jax.ShapeDtypeStruct((row_coun...]
    pallas_call x4 -> x5, Pallas kernels: 12.5 us -> 16 us  [the longest x2 9.89 us: merge_and_select(): pl.pallas_call(functools.partial(merge_kernel, first=first), out_shape=ja...]
    pallas_call x1 -> x2, Pallas kernels: 1.62 us -> 4.48 us  [slot_squares(): pl.pallas_call(squares_kernel, grid=(halves,), out_shape=jax.ShapeDtypeSt...]
  transfers between devices with their start and end apart: 24 -> 25, of which waited for: 10 -> 11; matrix products, arithmetic and copies ran while one was open for 5% -> 2% of each run, Pallas kernels for 14% -> 17%
where the time goes in v10:
time: 185 us; the launch traced here: 184 us
  waiting for transfers between devices  58.8 us (32%)
  starting transfers between devices  45 us (24%)
  Pallas kernels  40.4 us (22%)
  local copies, waits for them, and re-layouts  22.8 us (12%)
  between operations  13.8 us (7%)
  other arithmetic  2.8 us (2%)
    all_to_all x2, waiting for transfers between devices, on_device(): lax.all_to_all(outgoing, SEC, split_axis=0, concat_axis=0, tiled=True)  19.6 us
    unnamed x28, local copies, waits for them, and re-layouts  19.6 us
    pallas_call x1, Pallas kernels, vision_context(): pl.pallas_call(attention_kernel, out_shape=jax.ShapeDtypeStruct((row_coun...  14 us
    all_to_all x2, starting transfers between devices, on_device(): lax.all_to_all(outgoing, SEC, split_axis=0, concat_axis=0, tiled=True)  12.5 us
    all_gather x1, waiting for transfers between devices, on_device(): weight = lax.all_gather(both, ('z', 'x'), axis=0, tiled=True)  11.2 us
    ppermute x6, waiting for transfers between devices, shift_y(): lax.ppermute(block, ('yh', 'yl'), [(i, (i + d) % 4) for i in range(4)])  11.2 us
    ppermute x6, waiting for transfers between devices, swap_tp(): return lax.ppermute(block, TP, [(i, i ^ k) for i in range(4)])  10.3 us
    pallas_call x2, Pallas kernels, merge_and_select(): pl.pallas_call(functools.partial(merge_kernel, first=first), out_shape=ja...  9.89 us
  transfers between devices with their start and end apart: 25, of which 11 were waited for; matrix products, arithmetic and copies ran while one was open for 2% of the time, Pallas kernels for 17%

profile of v10, /device:TPU:1, one launch (start us, length us, event | category | flops | bytes accessed | tf_op | source)
XLA Modules:
  0.0 184.2 jit_solution(17436785584608329691)
XLA Ops:
  7.7 3.8 %collective-permute-start = (bf16[160,1024]{1,0:T(8,128)(2,1)S(1)}, bf16[160,1024]{1,0:T(8,128)(2,1)S(1)}, u32[]{:S(2)}, u32[]{:S(2)}) collective-permute-start(bf16[160,1024]{1,0:T(8,128)(2,1)S(1)} %get-tuple-element.44), channel_id=1, source_target_pairs={{0,4},{4,0},{1,5},{5,1},{2,6},{6,2},{3,7},{7,3},{8,12},{12,8},{9,1... | collective-permute-start | bytes 983048 | tf_op jit(solution)/shard_map/ppermute | solution.py:400
  14.0 4.7 %collective-permute-done = bf16[160,1024]{1,0:T(8,128)(2,1)S(1)} collective-permute-done((bf16[160,1024]{1,0:T(8,128)(2,1)S(1)}, bf16[160,1024]{1,0:T(8,128)(2,1)S(1)}, u32[]{:S(2)}, u32[]{:S(2)}) %collective-permute-start) | collective-permute-done | bytes 327712 | tf_op jit(solution)/shard_map/ppermute | solution.py:400
  25.4 1.7 copy-done.8
  28.9 14.0 %vision_attention.1 = bf16[1024,320]{1,0:T(8,128)(2,1)S(1)} custom-call(s32[1024,1]{1,0:T(8,128)S(1)} %copy.14.row_ids, s32[1,1024]{1,0:T(1,128)S(1)} %bitcast.22, bf16[1024,1280]{1,0:T(8,128)(2,1)S(1)} %copy-done.8, bf16[3,320,1280]{2,1,0:T(8,128)(2,1)S(1)} %bitcast.24), custom_call_target="tpu_custom_call" | custom-call | flops 6811549696 | bytes 5079040 | tf_op jit(solution)/shard_map/vision_attention/pallas_call | solution.py:70
  46.0 4.5 %collective-permute-done.4.refs_3_ = bf16[256,320]{1,0:T(8,128)(2,1)S(1)} collective-permute-done((bf16[256,320]{1,0:T(8,128)(2,1)S(1)}, bf16[256,320]{1,0:T(8,128)(2,1)S(1)}, u32[]{:S(2)}, u32[]{:S(2)}) %collective-permute-start.4) | collective-permute-done | bytes 163872 | tf_op jit(solution)/shard_map/ppermute | solution.py:370
  50.5 4.4 %collective-permute-done.5.refs_4_ = bf16[256,320]{1,0:T(8,128)(2,1)S(1)} collective-permute-done((bf16[256,320]{1,0:T(8,128)(2,1)S(1)}, bf16[256,320]{1,0:T(8,128)(2,1)S(1)}, u32[]{:S(2)}, u32[]{:S(2)}) %collective-permute-start.5) | collective-permute-done | bytes 163872 | tf_op jit(solution)/shard_map/ppermute | solution.py:370
  54.9 1.8 project_and_norm.1.refs_0_
  57.0 2.5 %collective-permute-start.11 = (bf16[64,5120]{1,0:T(8,128)(2,1)S(1)}, bf16[64,5120]{1,0:T(8,128)(2,1)S(1)}, u32[]{:S(2)}, u32[]{:S(2)}) collective-permute-start(bf16[64,5120]{1,0:T(8,128)(2,1)S(1)} %project_and_norm.1.refs_0_), channel_id=1, source_target_pairs={{0,6},{2,0},{4,2},{6,4},{1,7},{3,1},{5,3},{7,5},{8,14},{10,8},{12,... | collective-permute-start | bytes 1966088 | tf_op jit(solution)/shard_map/ppermute | solution.py:374
  59.5 8.2 %all-to-all-start = ((s32[32,1,32]{2,1,0:T(1,128)}), s32[32,1,32]{2,1,0:T(1,128)S(1)}, u32[]{:S(2)}, u32[]{:S(2)}) async-start(s32[32,1,32]{2,1,0:T(1,128)} %bitcast.10), calls=%async_computation | async-start | bytes 32768 | tf_op jit(solution)/shard_map/all_to_all | solution.py:442
  67.7 6.7 %collective-permute-done.10.refs_2_ = bf16[64,5120]{1,0:T(8,128)(2,1)S(1)} collective-permute-done((bf16[64,5120]{1,0:T(8,128)(2,1)S(1)}, bf16[64,5120]{1,0:T(8,128)(2,1)S(1)}, u32[]{:S(2)}, u32[]{:S(2)}) %collective-permute-start.10) | collective-permute-done | bytes 655392 | tf_op jit(solution)/shard_map/ppermute | solution.py:374
  74.6 2.7 %collective-permute-start.16 = (bf16[32,5120]{1,0:T(8,128)(2,1)S(1)}, bf16[32,5120]{1,0:T(8,128)(2,1)}, u32[]{:S(2)}, u32[]{:S(2)}) collective-permute-start(bf16[32,5120]{1,0:T(8,128)(2,1)S(1)} %slice.17), channel_id=1, source_target_pairs={{0,6},{2,0},{4,2},{6,4},{1,7},{3,1},{5,3},{7,5},{8,14},{10,8},{12,... | collective-permute-start | bytes 983048 | tf_op jit(solution)/shard_map/ppermute | solution.py:374
  79.6 4.5 %collective-permute-done.14.refs_6_ = bf16[32,5120]{1,0:T(8,128)(2,1)} collective-permute-done((bf16[32,5120]{1,0:T(8,128)(2,1)S(1)}, bf16[32,5120]{1,0:T(8,128)(2,1)}, u32[]{:S(2)}, u32[]{:S(2)}) %collective-permute-start.14) | collective-permute-done | bytes 327712 | tf_op jit(solution)/shard_map/ppermute | solution.py:374
  84.1 1.8 collective-permute-start.15
  87.9 3.0 %stack_rows.1.rows = bf16[512,5120]{1,0:T(8,128)(2,1)S(1)} custom-call(bf16[64,5120]{1,0:T(8,128)(2,1)S(1)} %project_and_norm.1.refs_0_, bf16[64,5120]{1,0:T(8,128)(2,1)} %collective-permute-done.9.refs_1_, bf16[64,5120]{1,0:T(8,128)(2,1)S(1)} %collective-permute-done.10.refs_2_, bf16[64,5120]{1,0:T(8,128)(2,1)} %collective-permute-done.12.refs_3_, ...), custom_call_target="tpu_custom_call" | custom-call | bytes 10485760 | tf_op jit(solution)/shard_map/stack_rows/pallas_call | solution.py:148
  90.9 2.3 %copy-done = bf16[512,5120]{1,0:T(8,128)(2,1)} copy-done((bf16[512,5120]{1,0:T(8,128)(2,1)}, bf16[512,5120]{1,0:T(8,128)(2,1)S(1)}, u32[]{:S(2)}) %copy-start) | copy-done | bytes 5242904
  93.2 11.2 %all-gather.2.cloned.1.call-done.weight = bf16[5120,1024]{1,0:T(8,128)(2,1)} async-done(((bf16[320,1024]{1,0:T(8,128)(2,1)}), bf16[5120,1024]{1,0:T(8,128)(2,1)}) %all-gather.2.cloned.1.call-update) | async-done | bytes 10485776 | tf_op jit(solution)/shard_map/all_gather | solution.py:421
  104.4 2.5 %copy-done.1 = bf16[512,5120]{1,0:T(8,128)(2,1)S(1)} copy-done((bf16[512,5120]{1,0:T(8,128)(2,1)S(1)}, bf16[512,5120]{1,0:T(8,128)(2,1)}, u32[]{:S(2)}) %copy-start.1) | copy-done | bytes 5242904
  106.9 4.0 %copy-done.3 = bf16[5120,1024]{1,0:T(8,128)(2,1)S(1)} copy-done((bf16[5120,1024]{1,0:T(8,128)(2,1)S(1)}, bf16[5120,1024]{1,0:T(8,128)(2,1)}, u32[]{:S(2)}) %copy-start.3) | copy-done | bytes 10485784
  110.9 5.4 %merge_rows.2 = bf16[1024,512]{1,0:T(8,128)(2,1)} custom-call(bf16[512,5120]{1,0:T(8,128)(2,1)S(1)} %copy-done.1, bf16[5120,1024]{1,0:T(8,128)(2,1)S(1)} %copy-done.3, bf16[1024,512]{1,0:T(8,128)(2,1)S(1)} %compare_convert_fusion.send), custom_call_target="tpu_custom_call" | custom-call | flops 3221225472 | bytes 11534336 | tf_op jit(solution)/shard_map/merge_rows/pallas_call | solution.py:190
  116.3 7.9 %all-to-all-start.1 = ((bf16[32,32,512]{2,1,0:T(8,128)(2,1)}), bf16[32,32,512]{2,1,0:T(8,128)(2,1)}, u32[]{:S(2)}, u32[]{:S(2)}) async-start(bf16[32,32,512]{2,1,0:T(8,128)(2,1)} %bitcast.12), calls=%async_computation.1 | async-start | bytes 2097152 | tf_op jit(solution)/shard_map/all_to_all | solution.py:468
  124.2 2.5 %copy-done.2 = bf16[512,5120]{1,0:T(8,128)(2,1)S(1)} copy-done((bf16[512,5120]{1,0:T(8,128)(2,1)S(1)}, bf16[512,5120]{1,0:T(8,128)(2,1)}, u32[]{:S(2)}) %copy-start.2) | copy-done | bytes 5242904
  126.7 4.0 %copy-done.4 = bf16[5120,1024]{1,0:T(8,128)(2,1)S(1)} copy-done((bf16[5120,1024]{1,0:T(8,128)(2,1)S(1)}, bf16[5120,1024]{1,0:T(8,128)(2,1)}, u32[]{:S(2)}) %copy-start.4) | copy-done | bytes 10485784
  130.7 4.5 %merge_rows.3 = bf16[1024,512]{1,0:T(8,128)(2,1)S(1)} custom-call(bf16[512,5120]{1,0:T(8,128)(2,1)S(1)} %copy-done.2, bf16[5120,1024]{1,0:T(8,128)(2,1)S(1)} %copy-done.4, bf16[1024,512]{1,0:T(8,128)(2,1)S(1)} %compare_convert_fusion.send), custom_call_target="tpu_custom_call" | custom-call | flops 3221225472 | bytes 11534336 | tf_op jit(solution)/shard_map/merge_rows/pallas_call | solution.py:190
  136.1 6.2 %all-to-all-done.1 = bf16[32,32,512]{2,1,0:T(8,128)(2,1)} async-done(((bf16[32,32,512]{2,1,0:T(8,128)(2,1)}), bf16[32,32,512]{2,1,0:T(8,128)(2,1)}, u32[]{:S(2)}, u32[]{:S(2)}) %all-to-all-start.1) | async-done | bytes 1048608 | tf_op jit(solution)/shard_map/all_to_all | solution.py:468
  142.3 4.7 %all-to-all-start.2 = ((bf16[32,32,512]{2,1,0:T(8,128)(2,1)}), bf16[32,32,512]{2,1,0:T(8,128)(2,1)}, u32[]{:S(2)}, u32[]{:S(2)}) async-start(bf16[32,32,512]{2,1,0:T(8,128)(2,1)} %bitcast.20), calls=%async_computation.2 | async-start | bytes 2097152 | tf_op jit(solution)/shard_map/all_to_all | solution.py:468
  148.3 2.2 %slot_squares.2.base = f32[4,128]{1,0:T(4,128)S(1)} custom-call(bf16[16,2,32,512]{3,2,1,0:T(8,128)(2,1)} %bitcast.13.received, bf16[512,512]{1,0:T(8,128)(2,1)S(1)} %fusion.1.pick, f32[4,128]{1,0:T(4,128)S(1)} %text_squares.1.base), custom_call_target="tpu_custom_call" | custom-call | flops 1048576 | bytes 1048576 | tf_op jit(solution)/shard_map/slot_squares/pallas_call | solution.py:285
  150.5 13.5 %all-to-all-done.2 = bf16[32,32,512]{2,1,0:T(8,128)(2,1)} async-done(((bf16[32,32,512]{2,1,0:T(8,128)(2,1)}), bf16[32,32,512]{2,1,0:T(8,128)(2,1)}, u32[]{:S(2)}, u32[]{:S(2)}) %all-to-all-start.2) | async-done | bytes 1048608 | tf_op jit(solution)/shard_map/all_to_all | solution.py:468
  164.0 2.2 %slot_squares.3.own = f32[4,128]{1,0:T(4,128)S(1)} custom-call(bf16[16,2,32,512]{3,2,1,0:T(8,128)(2,1)} %bitcast.15.received, bf16[512,512]{1,0:T(8,128)(2,1)S(1)} %fusion.1.pick, f32[4,128]{1,0:T(4,128)S(1)} %slot_squares.2.base), custom_call_target="tpu_custom_call" | custom-call | flops 1048576 | bytes 1048576 | tf_op jit(solution)/shard_map/slot_squares/pallas_call | solution.py:285
  166.2 3.3 %collective-permute-start.18 = (f32[4,128]{1,0:T(4,128)S(1)}, f32[4,128]{1,0:T(4,128)S(1)}, u32[]{:S(2)}, u32[]{:S(2)}) collective-permute-start(f32[4,128]{1,0:T(4,128)S(1)} %slot_squares.3.own), channel_id=1, source_target_pairs={{0,1},{1,0},{2,3},{3,2},{4,5},{5,4},{6,7},{7,6},{8,9},{9,8},{10,11... | collective-permute-start | bytes 6152 | tf_op jit(solution)/shard_map/ppermute | solution.py:370
  171.3 2.0 %pick_rows.3.second = bf16[512,1024]{1,0:T(8,128)(2,1)S(1)} custom-call(bf16[16,2,32,512]{3,2,1,0:T(8,128)(2,1)} %bitcast.15.received, bf16[512,512]{1,0:T(8,128)(2,1)S(1)} %fusion.1.pick, s32[512,1]{1,0:T(8,128)S(1)} %copy.15.usable, bf16[512,2048]{1,0:T(8,128)(2,1)S(1)} %copy-done.5), custom_call_target="tpu_custom_call" | custom-call | flops 536870912 | bytes 3145728 | tf_op jit(solution)/shard_map/pick_rows/pallas_call | solution.py:316
  173.3 2.0 %pick_rows.2.first = bf16[512,1024]{1,0:T(8,128)(2,1)S(1)} custom-call(bf16[16,2,32,512]{3,2,1,0:T(8,128)(2,1)} %bitcast.13.received, bf16[512,512]{1,0:T(8,128)(2,1)S(1)} %fusion.1.pick, s32[512,1]{1,0:T(8,128)S(1)} %copy.15.usable, bf16[512,2048]{1,0:T(8,128)(2,1)S(1)} %copy-done.5), custom_call_target="tpu_custom_call" | custom-call | flops 536870912 | bytes 3145728 | tf_op jit(solution)/shard_map/pick_rows/pallas_call | solution.py:316
  175.4 2.0 %finish.1 = bf16[512,2048]{1,0:T(8,128)(2,1)} custom-call(bf16[512,1024]{1,0:T(8,128)(2,1)S(1)} %pick_rows.2.first, bf16[512,1024]{1,0:T(8,128)(2,1)S(1)} %pick_rows.3.second, f32[4,128]{1,0:T(4,128)S(1)} %slot_squares.3.own, f32[4,128]{1,0:T(4,128)S(1)} %collective-permute-done.18.core, f32[4,128]{1,0:T(4,128)S(1)} %collective-permute-done.19.far, ...), custom_call_target="tpu_custom_call" | custom-call | flops 3145728 | bytes 4194304 | tf_op jit(solution)/shard_map/finish/pallas_call | solution.py:352
  (95 shorter events, 23.6 us)
Async XLA Ops:
  6.5 13.8 %copy-start.13 = (s32[1,256]{1,0:T(1,128)S(1)}, s32[1,256]{1,0:T(1,128)}, u32[]{:S(2)}) copy-start(s32[1,256]{1,0:T(1,128)} %param.10) | copy-start | bytes 3076
  6.5 97.9 %all-gather.2.cloned.1.call-start = ((), (), s32[]{:S(2)}) async-start(), calls=%async_computation.3 | async-start | bytes 11141120 | tf_op jit(solution)/shard_map/all_gather | solution.py:421
  6.5 14.3 %copy-start.7 = (bf16[320,1280]{1,0:T(8,128)(2,1)S(1)}, bf16[320,1280]{1,0:T(8,128)(2,1)}, u32[]{:S(2)}) copy-start(bf16[320,1280]{1,0:T(8,128)(2,1)} %refs_5_) | copy-start | bytes 2457604
  7.7 11.0 %collective-permute-start = (bf16[160,1024]{1,0:T(8,128)(2,1)S(1)}, bf16[160,1024]{1,0:T(8,128)(2,1)S(1)}, u32[]{:S(2)}, u32[]{:S(2)}) collective-permute-start(bf16[160,1024]{1,0:T(8,128)(2,1)S(1)} %get-tuple-element.44), channel_id=1, source_target_pairs={{0,4},{4,0},{1,5},{5,1},{2,6},{6,2},{3,7},{7,3},{8,12},{12,8},{9,1... | collective-permute-start | bytes 983048 | tf_op jit(solution)/shard_map/ppermute | solution.py:400
  20.8 34.1 %collective-permute-start.6 = (bf16[320,1280]{1,0:T(8,128)(2,1)S(1)}, bf16[320,1280]{1,0:T(8,128)(2,1)S(1)}, u32[]{:S(2)}, u32[]{:S(2)}) collective-permute-start(bf16[320,1280]{1,0:T(8,128)(2,1)S(1)} %copy-done.7), channel_id=1, source_target_pairs={{0,1},{1,0},{2,3},{3,2},{4,5},{5,4},{6,7},{7,6},{8,9},{9,8},{10,11... | collective-permute-start | bytes 2457608 | tf_op jit(solution)/shard_map/ppermute | solution.py:378
  22.5 20.5 %collective-permute-start.1 = (bf16[160,1280]{1,0:T(8,128)(2,1)S(1)}, bf16[160,1280]{1,0:T(8,128)(2,1)S(1)}, u32[]{:S(2)}, u32[]{:S(2)}) collective-permute-start(bf16[160,1280]{1,0:T(8,128)(2,1)S(1)} %get-tuple-element.38), channel_id=1, source_target_pairs={{0,2},{2,4},{4,6},{6,0},{1,3},{3,5},{5,7},{7,1},{8,10},{10,12},{12... | collective-permute-start | bytes 1228808 | tf_op jit(solution)/shard_map/ppermute | solution.py:374
  23.9 19.1 %collective-permute-start.2 = (bf16[160,1280]{1,0:T(8,128)(2,1)S(1)}, bf16[160,1280]{1,0:T(8,128)(2,1)S(1)}, u32[]{:S(2)}, u32[]{:S(2)}) collective-permute-start(bf16[160,1280]{1,0:T(8,128)(2,1)S(1)} %get-tuple-element.37), channel_id=1, source_target_pairs={{0,6},{2,0},{4,2},{6,4},{1,7},{3,1},{5,3},{7,5},{8,14},{10,8},{12,... | collective-permute-start | bytes 1228808 | tf_op jit(solution)/shard_map/ppermute | solution.py:374
  28.9 17.2 %copy-start.12 = (f32[1280]{0:T(1024)S(1)}, f32[1280]{0:T(1024)}, u32[]{:S(2)}) copy-start(f32[1280]{0:T(1024)} %param.13) | copy-start | bytes 15364
  28.9 26.0 %copy-start.9 = (bf16[1024,1280]{1,0:T(8,128)(2,1)S(1)}, bf16[1024,1280]{1,0:T(8,128)(2,1)}, u32[]{:S(2)}) copy-start(bf16[1024,1280]{1,0:T(8,128)(2,1)} %refs_11_) | copy-start | bytes 7864324
  42.9 12.0 %collective-permute-start.7 = (bf16[160,1280]{1,0:T(8,128)(2,1)S(1)}, bf16[160,1280]{1,0:T(8,128)(2,1)S(1)}, u32[]{:S(2)}, u32[]{:S(2)}) collective-permute-start(bf16[160,1280]{1,0:T(8,128)(2,1)S(1)} %collective-permute-done.1.refs_7_), channel_id=1, source_target_pairs={{0,1},{1,0},{2,3},{3,2},{4,5},{5,4},{6,7},{7,6},{8,9},{9,8},{10,11... | collective-permute-start | bytes 1228808 | tf_op jit(solution)/shard_map/ppermute | solution.py:378
  43.4 11.5 %collective-permute-start.8 = (bf16[160,1280]{1,0:T(8,128)(2,1)S(1)}, bf16[160,1280]{1,0:T(8,128)(2,1)S(1)}, u32[]{:S(2)}, u32[]{:S(2)}) collective-permute-start(bf16[160,1280]{1,0:T(8,128)(2,1)S(1)} %collective-permute-done.2.refs_8_), channel_id=1, source_target_pairs={{0,1},{1,0},{2,3},{3,2},{4,5},{5,4},{6,7},{7,6},{8,9},{9,8},{10,11... | collective-permute-start | bytes 1228808 | tf_op jit(solution)/shard_map/ppermute | solution.py:378
  43.6 2.0 %collective-permute-start.3 = (bf16[256,320]{1,0:T(8,128)(2,1)S(1)}, bf16[256,320]{1,0:T(8,128)(2,1)S(1)}, u32[]{:S(2)}, u32[]{:S(2)}) collective-permute-start(bf16[256,320]{1,0:T(8,128)(2,1)S(1)} %get-tuple-element.41), channel_id=1, source_target_pairs={{0,1},{1,0},{2,3},{3,2},{4,5},{5,4},{6,7},{7,6},{8,9},{9,8},{10,11... | collective-permute-start | bytes 491528 | tf_op jit(solution)/shard_map/ppermute | solution.py:370
  44.1 6.5 %collective-permute-start.4 = (bf16[256,320]{1,0:T(8,128)(2,1)S(1)}, bf16[256,320]{1,0:T(8,128)(2,1)S(1)}, u32[]{:S(2)}, u32[]{:S(2)}) collective-permute-start(bf16[256,320]{1,0:T(8,128)(2,1)S(1)} %get-tuple-element.40), channel_id=1, source_target_pairs={{0,2},{1,3},{2,0},{3,1},{4,6},{5,7},{6,4},{7,5},{8,10},{9,11},{10,... | collective-permute-start | bytes 491528 | tf_op jit(solution)/shard_map/ppermute | solution.py:370
  45.6 9.3 %collective-permute-start.5 = (bf16[256,320]{1,0:T(8,128)(2,1)S(1)}, bf16[256,320]{1,0:T(8,128)(2,1)S(1)}, u32[]{:S(2)}, u32[]{:S(2)}) collective-permute-start(bf16[256,320]{1,0:T(8,128)(2,1)S(1)} %get-tuple-element.39), channel_id=1, source_target_pairs={{0,3},{1,2},{2,1},{3,0},{4,7},{5,6},{6,5},{7,4},{8,11},{9,10},{10,... | collective-permute-start | bytes 491528 | tf_op jit(solution)/shard_map/ppermute | solution.py:370
  56.8 17.6 %collective-permute-start.10 = (bf16[64,5120]{1,0:T(8,128)(2,1)S(1)}, bf16[64,5120]{1,0:T(8,128)(2,1)S(1)}, u32[]{:S(2)}, u32[]{:S(2)}) collective-permute-start(bf16[64,5120]{1,0:T(8,128)(2,1)S(1)} %project_and_norm.1.refs_0_), channel_id=1, source_target_pairs={{0,2},{2,4},{4,6},{6,0},{1,3},{3,5},{5,7},{7,1},{8,10},{10,12},{12... | collective-permute-start | bytes 1966088 | tf_op jit(solution)/shard_map/ppermute | solution.py:374
  57.0 17.5 %collective-permute-start.11 = (bf16[64,5120]{1,0:T(8,128)(2,1)S(1)}, bf16[64,5120]{1,0:T(8,128)(2,1)S(1)}, u32[]{:S(2)}, u32[]{:S(2)}) collective-permute-start(bf16[64,5120]{1,0:T(8,128)(2,1)S(1)} %project_and_norm.1.refs_0_), channel_id=1, source_target_pairs={{0,6},{2,0},{4,2},{6,4},{1,7},{3,1},{5,3},{7,5},{8,14},{10,8},{12,... | collective-permute-start | bytes 1966088 | tf_op jit(solution)/shard_map/ppermute | solution.py:374
  59.5 19.5 %all-to-all-start = ((s32[32,1,32]{2,1,0:T(1,128)}), s32[32,1,32]{2,1,0:T(1,128)S(1)}, u32[]{:S(2)}, u32[]{:S(2)}) async-start(s32[32,1,32]{2,1,0:T(1,128)} %bitcast.10), calls=%async_computation | async-start | bytes 32768 | tf_op jit(solution)/shard_map/all_to_all | solution.py:442
  74.4 9.7 %collective-permute-start.14 = (bf16[32,5120]{1,0:T(8,128)(2,1)S(1)}, bf16[32,5120]{1,0:T(8,128)(2,1)}, u32[]{:S(2)}, u32[]{:S(2)}) collective-permute-start(bf16[32,5120]{1,0:T(8,128)(2,1)S(1)} %slice.16), channel_id=1, source_target_pairs={{0,2},{2,4},{4,6},{6,0},{1,3},{3,5},{5,7},{7,1},{8,10},{10,12},{12... | collective-permute-start | bytes 983048 | tf_op jit(solution)/shard_map/ppermute | solution.py:374
  74.6 11.4 %collective-permute-start.16 = (bf16[32,5120]{1,0:T(8,128)(2,1)S(1)}, bf16[32,5120]{1,0:T(8,128)(2,1)}, u32[]{:S(2)}, u32[]{:S(2)}) collective-permute-start(bf16[32,5120]{1,0:T(8,128)(2,1)S(1)} %slice.17), channel_id=1, source_target_pairs={{0,6},{2,0},{4,2},{6,4},{1,7},{3,1},{5,3},{7,5},{8,14},{10,8},{12,... | collective-permute-start | bytes 983048 | tf_op jit(solution)/shard_map/ppermute | solution.py:374
  77.5 8.7 %collective-permute-start.9 = (bf16[64,5120]{1,0:T(8,128)(2,1)S(1)}, bf16[64,5120]{1,0:T(8,128)(2,1)}, u32[]{:S(2)}, u32[]{:S(2)}) collective-permute-start(bf16[64,5120]{1,0:T(8,128)(2,1)S(1)} %project_and_norm.1.refs_0_), channel_id=1, source_target_pairs={{0,1},{1,0},{2,3},{3,2},{4,5},{5,4},{6,7},{7,6},{8,9},{9,8},{10,11... | collective-permute-start | bytes 1966088 | tf_op jit(solution)/shard_map/ppermute | solution.py:378
  79.0 7.2 %collective-permute-start.12 = (bf16[64,5120]{1,0:T(8,128)(2,1)S(1)}, bf16[64,5120]{1,0:T(8,128)(2,1)}, u32[]{:S(2)}, u32[]{:S(2)}) collective-permute-start(bf16[64,5120]{1,0:T(8,128)(2,1)S(1)} %collective-permute-done.10.refs_2_), channel_id=1, source_target_pairs={{0,1},{1,0},{2,3},{3,2},{4,5},{5,4},{6,7},{7,6},{8,9},{9,8},{10,11... | collective-permute-start | bytes 1966088 | tf_op jit(solution)/shard_map/ppermute | solution.py:378
  79.1 7.1 %collective-permute-start.13 = (bf16[64,5120]{1,0:T(8,128)(2,1)S(1)}, bf16[64,5120]{1,0:T(8,128)(2,1)}, u32[]{:S(2)}, u32[]{:S(2)}) collective-permute-start(bf16[64,5120]{1,0:T(8,128)(2,1)S(1)} %collective-permute-done.11.refs_4_), channel_id=1, source_target_pairs={{0,1},{1,0},{2,3},{3,2},{4,5},{5,4},{6,7},{7,6},{8,9},{9,8},{10,11... | collective-permute-start | bytes 1966088 | tf_op jit(solution)/shard_map/ppermute | solution.py:378
  84.1 3.3 %collective-permute-start.15 = (bf16[32,5120]{1,0:T(8,128)(2,1)}, bf16[32,5120]{1,0:T(8,128)(2,1)S(1)}, u32[]{:S(2)}, u32[]{:S(2)}) collective-permute-start(bf16[32,5120]{1,0:T(8,128)(2,1)} %collective-permute-done.14.refs_6_), channel_id=1, source_target_pairs={{0,1},{1,0},{2,3},{3,2},{4,5},{5,4},{6,7},{7,6},{8,9},{9,8},{10,11... | collective-permute-start | bytes 983048 | tf_op jit(solution)/shard_map/ppermute | solution.py:378
  86.0 1.9 %collective-permute-start.17 = (bf16[32,5120]{1,0:T(8,128)(2,1)}, bf16[32,5120]{1,0:T(8,128)(2,1)S(1)}, u32[]{:S(2)}, u32[]{:S(2)}) collective-permute-start(bf16[32,5120]{1,0:T(8,128)(2,1)} %collective-permute-done.16.refs_8_), channel_id=1, source_target_pairs={{0,1},{1,0},{2,3},{3,2},{4,5},{5,4},{6,7},{7,6},{8,9},{9,8},{10,11... | collective-permute-start | bytes 983048 | tf_op jit(solution)/shard_map/ppermute | solution.py:378
  106.9 4.0 %copy-start.3 = (bf16[5120,1024]{1,0:T(8,128)(2,1)S(1)}, bf16[5120,1024]{1,0:T(8,128)(2,1)}, u32[]{:S(2)}) copy-start(bf16[5120,1024]{1,0:T(8,128)(2,1)} %all-gather.2.cloned.1.call-done.weight) | copy-start | bytes 31457284
  116.3 26.0 %all-to-all-start.1 = ((bf16[32,32,512]{2,1,0:T(8,128)(2,1)}), bf16[32,32,512]{2,1,0:T(8,128)(2,1)}, u32[]{:S(2)}, u32[]{:S(2)}) async-start(bf16[32,32,512]{2,1,0:T(8,128)(2,1)} %bitcast.12), calls=%async_computation.1 | async-start | bytes 2097152 | tf_op jit(solution)/shard_map/all_to_all | solution.py:468
  126.7 4.0 %copy-start.4 = (bf16[5120,1024]{1,0:T(8,128)(2,1)S(1)}, bf16[5120,1024]{1,0:T(8,128)(2,1)}, u32[]{:S(2)}) copy-start(bf16[5120,1024]{1,0:T(8,128)(2,1)} %all-gather.2.cloned.1.call-done.weight) | copy-start | bytes 31457284
  136.1 11.0 %copy-start.5 = (bf16[512,2048]{1,0:T(8,128)(2,1)S(1)}, bf16[512,2048]{1,0:T(8,128)(2,1)}, u32[]{:S(2)}) copy-start(bf16[512,2048]{1,0:T(8,128)(2,1)} %text.5) | copy-start | bytes 6291460
  142.3 21.7 %all-to-all-start.2 = ((bf16[32,32,512]{2,1,0:T(8,128)(2,1)}), bf16[32,32,512]{2,1,0:T(8,128)(2,1)}, u32[]{:S(2)}, u32[]{:S(2)}) async-start(bf16[32,32,512]{2,1,0:T(8,128)(2,1)} %bitcast.20), calls=%async_computation.2 | async-start | bytes 2097152 | tf_op jit(solution)/shard_map/all_to_all | solution.py:468
  166.2 9.2 %collective-permute-start.18 = (f32[4,128]{1,0:T(4,128)S(1)}, f32[4,128]{1,0:T(4,128)S(1)}, u32[]{:S(2)}, u32[]{:S(2)}) collective-permute-start(f32[4,128]{1,0:T(4,128)S(1)} %slot_squares.3.own), channel_id=1, source_target_pairs={{0,1},{1,0},{2,3},{3,2},{4,5},{5,4},{6,7},{7,6},{8,9},{9,8},{10,11... | collective-permute-start | bytes 6152 | tf_op jit(solution)/shard_map/ppermute | solution.py:370
  169.6 5.8 %collective-permute-start.19 = (f32[4,128]{1,0:T(4,128)S(1)}, f32[4,128]{1,0:T(4,128)S(1)}, u32[]{:S(2)}, u32[]{:S(2)}) collective-permute-start(f32[4,128]{1,0:T(4,128)S(1)} %slot_squares.3.own), channel_id=1, source_target_pairs={{0,2},{1,3},{2,0},{3,1},{4,6},{5,7},{6,4},{7,5},{8,10},{9,11},{10,... | collective-permute-start | bytes 6152 | tf_op jit(solution)/shard_map/ppermute | solution.py:370
  169.9 5.5 %collective-permute-start.20 = (f32[4,128]{1,0:T(4,128)S(1)}, f32[4,128]{1,0:T(4,128)S(1)}, u32[]{:S(2)}, u32[]{:S(2)}) collective-permute-start(f32[4,128]{1,0:T(4,128)S(1)} %slot_squares.3.own), channel_id=1, source_target_pairs={{0,3},{1,2},{2,1},{3,0},{4,7},{5,6},{6,5},{7,4},{8,11},{9,10},{10,... | collective-permute-start | bytes 6152 | tf_op jit(solution)/shard_map/ppermute | solution.py:370
  (7 other events, 13.8 us)
Sparse Core Ops, SparseCore 0:
  20.4 83.9 all-gather.1

commit v11 on v10

--- a/solution.py
+++ b/solution.py
@@ -159,15 +159,13 @@
     )(*blocks)
 
 
-def merge_kernel(rows, weight, send, outgoing, held, sems, *, first):
+def merge_kernel(rows, weight, send, outgoing, held, sems):
     depth, columns = held.shape
     steps = sems.shape[0]
     tile = depth // steps
     copies = [
         pltpu.make_async_copy(
-            weight.at[pl.ds(k * tile, tile), pl.ds(first, columns)],
-            held.at[pl.ds(k * tile, tile)],
-            sems.at[k],
+            weight.at[pl.ds(k * tile, tile)], held.at[pl.ds(k * tile, tile)], sems.at[k]
         )
         for k in range(steps)
     ]
@@ -183,17 +181,17 @@
     ).astype(BF)
 
 
-def merge_and_select(rows, weight, send, first, columns):
+def merge_and_select(rows, weight, send):
     slots, count = send.shape
-    depth = weight.shape[0]
+    depth, columns = weight.shape
     vmem = pl.BlockSpec(memory_space=pltpu.VMEM)
     return pl.pallas_call(
-        functools.partial(merge_kernel, first=first),
+        merge_kernel,
         out_shape=jax.ShapeDtypeStruct((slots, columns), BF),
         in_specs=[vmem, pl.BlockSpec(memory_space=pltpu.HBM), vmem],
         out_specs=vmem,
         scratch_shapes=[pltpu.VMEM((depth, columns), BF), pltpu.SemaphoreType.DMA((4,))],
-        compiler_params=pltpu.CompilerParams(vmem_limit_bytes=24 * 2**20),
+        compiler_params=pltpu.CompilerParams(vmem_limit_bytes=44 * 2**20),
         cost_estimate=pl.CostEstimate(
             flops=2 * count * (depth + slots) * columns,
             bytes_accessed=2 * (count * depth + depth * columns + slots * columns),
@@ -309,10 +307,9 @@
     prompt[...] = jnp.where(usable[...] > 0, picked, text[...].astype(F32)).astype(BF)
 
 
-def pick_rows(received, pick, usable, text, index):
+def pick_rows(received, pick, usable, text):
     planes, halves, rows, part = received.shape
     count, slots = pick.shape
-    parts = text.shape[1] // (halves * part)
     return pl.pallas_call(
         pick_kernel,
         grid=(halves,),
@@ -321,7 +318,7 @@
             pl.BlockSpec((planes, 1, rows, part), lambda h: (0, h, 0, 0)),
             pl.BlockSpec((count, slots), lambda h: (0, 0), pipeline_mode=pl.Buffered(1)),
             pl.BlockSpec((count, 1), lambda h: (0, 0), pipeline_mode=pl.Buffered(1)),
-            pl.BlockSpec((count, part), lambda h: (0, h * parts + index)),
+            pl.BlockSpec((count, part), lambda h: (0, h)),
         ],
         out_specs=pl.BlockSpec((count, part), lambda h: (0, h)),
         compiler_params=pltpu.CompilerParams(vmem_limit_bytes=14 * 2**20),
@@ -334,36 +331,34 @@
     )(received, pick, usable, text)
 
 
-def finish_kernel(first, second, own, core, far, both, gain, out, inverse, *, width):
+def finish_kernel(prompt, own, core, far, both, gain, out, inverse, *, width):
     @pl.when(pl.program_id(0) == 0)
     def _():
         total = to_column(own[...] + core[...] + far[...] + both[...])
         inverse[...] = lax.rsqrt(total / width + EPSILON)
 
-    part = first.shape[1]
-    out[:, :part] = (first[...].astype(F32) * inverse[...] * gain[:, :part]).astype(BF)
-    out[:, part:] = (second[...].astype(F32) * inverse[...] * gain[:, part:]).astype(BF)
-
-
-def finish(first, second, squares, gain):
-    count, width = first.shape
-    part = width // 2
+    out[...] = (prompt[...].astype(F32) * inverse[...] * gain[...]).astype(BF)
+
+
+def finish(prompt, squares, gain):
+    count, width = prompt.shape
+    part = width // 4
     small = pl.BlockSpec((count // 128, 128), lambda h: (0, 0))
     return pl.pallas_call(
-        functools.partial(finish_kernel, width=8 * width),
-        grid=(2,),
-        out_shape=jax.ShapeDtypeStruct((count, 2 * width), BF),
-        in_specs=[pl.BlockSpec((count, part), lambda h: (0, h))] * 2
+        functools.partial(finish_kernel, width=4 * width),
+        grid=(4,),
+        out_shape=jax.ShapeDtypeStruct((count, width), BF),
+        in_specs=[pl.BlockSpec((count, part), lambda h: (0, h))]
         + [small] * 4
-        + [pl.BlockSpec((1, 2 * part), lambda h: (0, h))],
-        out_specs=pl.BlockSpec((count, 2 * part), lambda h: (0, h)),
+        + [pl.BlockSpec((1, part), lambda h: (0, h))],
+        out_specs=pl.BlockSpec((count, part), lambda h: (0, h)),
         scratch_shapes=[pltpu.VMEM((count, 1), F32)],
-        compiler_params=pltpu.CompilerParams(vmem_limit_bytes=12 * 2**20),
-        cost_estimate=pl.CostEstimate(
-            flops=6 * count * width, bytes_accessed=8 * count * width, transcendentals=count
+        compiler_params=pltpu.CompilerParams(vmem_limit_bytes=10 * 2**20),
+        cost_estimate=pl.CostEstimate(
+            flops=3 * count * width, bytes_accessed=4 * count * width, transcendentals=count
         ),
         name="finish",
-    )(first, second, *squares, gain[None, :])
+    )(prompt, *squares, gain[None, :])
 
 
 def swap_tp(block, k):
@@ -460,17 +455,12 @@
     wanted = jnp.where(wanted >= 0, wanted + jnp.arange(2)[None, :, None] * 256, -1).reshape(-1)
     send = (wanted[:, None] == row_ids[None, :]).astype(BF)
 
-    rows = stack_rows(blocks)
-    squares = text_squares(text_rows, usable)
-    prompts = []
-    for index in range(2):
-        outgoing = merge_and_select(rows, weight, send, index * half // 2, half // 2)
-        received = lax.all_to_all(outgoing, SEC, split_axis=0, concat_axis=0, tiled=True)
-        received = received.reshape(16, 2, 32, half // 2)
-        squares = slot_squares(received, pick, squares)
-        prompts.append(pick_rows(received, pick, usable, text_rows, index))
+    outgoing = merge_and_select(stack_rows(blocks), weight, send)
+    received = lax.all_to_all(outgoing, SEC, split_axis=0, concat_axis=0, tiled=True)
+    received = received.reshape(16, 2, 32, half)
+    squares = slot_squares(received, pick, text_squares(text_rows, usable))
     squares = [squares] + [swap_tp(squares, k) for k in (1, 2, 3)]
-    return finish(*prompts, squares, llm_gain)
+    return finish(pick_rows(received, pick, usable, text_rows), squares, llm_gain)
 
 
 def solution(mesh):

time: 185 us -> 173 us (0.935)
  local copies, waits for them, and re-layouts: 22.8 us -> 14.2 us
  waiting for transfers between devices: 58.8 us -> 66.7 us
  starting transfers between devices: 45 us -> 39.1 us
  Pallas kernels: 40.4 us -> 35.3 us
    unnamed x28 -> x24, local copies, waits for them, and re-layouts: 19.6 us -> 11.1 us
    all_to_all x2 -> x1, waiting for transfers between devices: 19.6 us -> 27.5 us  [on_device(): lax.all_to_all(outgoing, SEC, split_axis=0, concat_axis=0, tiled=True)]
    all_to_all x2 -> x1, starting transfers between devices: 12.5 us -> 7.71 us  [on_device(): lax.all_to_all(outgoing, SEC, split_axis=0, concat_axis=0, tiled=True)]
    pallas_call x2 -> x1, Pallas kernels: 4.48 us -> 1.61 us  [slot_squares(): pl.pallas_call(squares_kernel, grid=(halves,), out_shape=jax.ShapeDtypeSt...]
    pallas_call x2 -> x1, Pallas kernels: 4.07 us -> 1.88 us  [pick_rows(): pl.pallas_call(pick_kernel, grid=(halves,), out_shape=jax.ShapeDtypeStruc...]
    pallas_call x3 -> x2, Pallas kernels: 11.8 us -> 11.8 us  [the longest x1 9.33 us: merge_and_select(): pl.pallas_call(merge_kernel, out_shape=jax.ShapeDtypeStruct((slots, colum...]
  transfers between devices with their start and end apart: 25 -> 24, of which waited for: 11 -> 10; matrix products, arithmetic and copies ran while one was open for 2% -> 2% of each run, Pallas kernels for 17% -> 13%
where the time goes in v11:
time: 173 us
  waiting for transfers between devices  66.7 us (39%)
  starting transfers between devices  39.1 us (23%)
  Pallas kernels  35.3 us (20%)
  local copies, waits for them, and re-layouts  14.2 us (8%)
  between operations  13.8 us (8%)
  other arithmetic  2.8 us (2%)
    all_to_all x1, waiting for transfers between devices, on_device(): lax.all_to_all(outgoing, SEC, split_axis=0, concat_axis=0, tiled=True)  27.5 us
    pallas_call x1, Pallas kernels, vision_context(): pl.pallas_call(attention_kernel, out_shape=jax.ShapeDtypeStruct((row_coun...  14.1 us
    ppermute x6, waiting for transfers between devices, shift_y(): lax.ppermute(block, ('yh', 'yl'), [(i, (i + d) % 4) for i in range(4)])  11.3 us
    all_gather x1, waiting for transfers between devices, on_device(): weight = lax.all_gather(both, ('z', 'x'), axis=0, tiled=True)  11.2 us
    unnamed x24, local copies, waits for them, and re-layouts  11.1 us
    ppermute x6, waiting for transfers between devices, swap_tp(): return lax.ppermute(block, TP, [(i, i ^ k) for i in range(4)])  10.3 us
    pallas_call x1, Pallas kernels, merge_and_select(): pl.pallas_call(merge_kernel, out_shape=jax.ShapeDtypeStruct((slots, colum...  9.33 us
    ppermute x6, starting transfers between devices, shift_y(): lax.ppermute(block, ('yh', 'yl'), [(i, (i + d) % 4) for i in range(4)])  8.5 us
  transfers between devices with their start and end apart: 24, of which 10 were waited for; matrix products, arithmetic and copies ran while one was open for 2% of the time, Pallas kernels for 13%

profile of v11, /device:TPU:1, one launch (start us, length us, event | category | flops | bytes accessed | tf_op | source)
XLA Modules:
  0.0 172.6 jit_solution(15845685807017206923)
XLA Ops:
  7.7 3.8 %collective-permute-start = (bf16[160,1024]{1,0:T(8,128)(2,1)S(1)}, bf16[160,1024]{1,0:T(8,128)(2,1)S(1)}, u32[]{:S(2)}, u32[]{:S(2)}) collective-permute-start(bf16[160,1024]{1,0:T(8,128)(2,1)S(1)} %get-tuple-element.44), channel_id=1, source_target_pairs={{0,4},{4,0},{1,5},{5,1},{2,6},{6,2},{3,7},{7,3},{8,12},{12,8},{9,1... | collective-permute-start | bytes 983048 | tf_op jit(solution)/shard_map/ppermute | solution.py:395
  13.9 4.7 %collective-permute-done = bf16[160,1024]{1,0:T(8,128)(2,1)S(1)} collective-permute-done((bf16[160,1024]{1,0:T(8,128)(2,1)S(1)}, bf16[160,1024]{1,0:T(8,128)(2,1)S(1)}, u32[]{:S(2)}, u32[]{:S(2)}) %collective-permute-start) | collective-permute-done | bytes 327712 | tf_op jit(solution)/shard_map/ppermute | solution.py:395
  20.8 1.6 collective-permute-start.6
  22.4 1.4 collective-permute-start.1
  23.8 1.5 collective-permute-start.2
  25.4 1.7 %copy-done.5 = bf16[1024,1280]{1,0:T(8,128)(2,1)S(1)} copy-done((bf16[1024,1280]{1,0:T(8,128)(2,1)S(1)}, bf16[1024,1280]{1,0:T(8,128)(2,1)}, u32[]{:S(2)}) %copy-start.5) | copy-done | bytes 2621464
  27.1 1.7 copy-done.9
  28.8 14.1 %vision_attention.1 = bf16[1024,320]{1,0:T(8,128)(2,1)S(1)} custom-call(s32[1024,1]{1,0:T(8,128)S(1)} %copy.13.row_ids, s32[1,1024]{1,0:T(1,128)S(1)} %bitcast.22, bf16[1024,1280]{1,0:T(8,128)(2,1)S(1)} %copy-done.5, bf16[3,320,1280]{2,1,0:T(8,128)(2,1)S(1)} %bitcast.24), custom_call_target="tpu_custom_call" | custom-call | flops 6811549696 | bytes 5079040 | tf_op jit(solution)/shard_map/vision_attention/pallas_call | solution.py:70
  44.2 1.4 collective-permute-done.3.refs_2_
  46.0 4.5 %collective-permute-done.4.refs_3_ = bf16[256,320]{1,0:T(8,128)(2,1)S(1)} collective-permute-done((bf16[256,320]{1,0:T(8,128)(2,1)S(1)}, bf16[256,320]{1,0:T(8,128)(2,1)S(1)}, u32[]{:S(2)}, u32[]{:S(2)}) %collective-permute-start.4) | collective-permute-done | bytes 163872 | tf_op jit(solution)/shard_map/ppermute | solution.py:365
  50.5 4.4 %collective-permute-done.5.refs_4_ = bf16[256,320]{1,0:T(8,128)(2,1)S(1)} collective-permute-done((bf16[256,320]{1,0:T(8,128)(2,1)S(1)}, bf16[256,320]{1,0:T(8,128)(2,1)S(1)}, u32[]{:S(2)}, u32[]{:S(2)}) %collective-permute-start.5) | collective-permute-done | bytes 163872 | tf_op jit(solution)/shard_map/ppermute | solution.py:365
  54.9 1.8 %project_and_norm.1.refs_0_ = bf16[64,5120]{1,0:T(8,128)(2,1)S(1)} custom-call(s32[1]{0:T(128)} %bitcast.3.refs_0_, bf16[256,320]{1,0:T(8,128)(2,1)S(1)} %get-tuple-element.42.refs_1_, bf16[256,320]{1,0:T(8,128)(2,1)S(1)} %collective-permute-done.3.refs_2_, bf16[256,320]{1,0:T(8,128)(2,1)S(1)} %collective-permute-done.4.refs_3_, ...), custom_call_target="tpu_custom_call" | custom-call | flops 838860800 | bytes 5242880 | tf_op jit(solution)/shard_map/project_and_norm/pallas_call | solution.py:115
  56.9 2.5 %collective-permute-start.11 = (bf16[64,5120]{1,0:T(8,128)(2,1)S(1)}, bf16[64,5120]{1,0:T(8,128)(2,1)S(1)}, u32[]{:S(2)}, u32[]{:S(2)}) collective-permute-start(bf16[64,5120]{1,0:T(8,128)(2,1)S(1)} %project_and_norm.1.refs_0_), channel_id=1, source_target_pairs={{0,6},{2,0},{4,2},{6,4},{1,7},{3,1},{5,3},{7,5},{8,14},{10,8},{12,... | collective-permute-start | bytes 1966088 | tf_op jit(solution)/shard_map/ppermute | solution.py:369
  59.5 8.2 %all-to-all-start = ((s32[32,1,32]{2,1,0:T(1,128)}), s32[32,1,32]{2,1,0:T(1,128)S(1)}, u32[]{:S(2)}, u32[]{:S(2)}) async-start(s32[32,1,32]{2,1,0:T(1,128)} %bitcast.10), calls=%async_computation | async-start | bytes 32768 | tf_op jit(solution)/shard_map/all_to_all | solution.py:437
  67.7 6.7 %collective-permute-done.10.refs_2_ = bf16[64,5120]{1,0:T(8,128)(2,1)S(1)} collective-permute-done((bf16[64,5120]{1,0:T(8,128)(2,1)S(1)}, bf16[64,5120]{1,0:T(8,128)(2,1)S(1)}, u32[]{:S(2)}, u32[]{:S(2)}) %collective-permute-start.10) | collective-permute-done | bytes 655392 | tf_op jit(solution)/shard_map/ppermute | solution.py:369
  74.5 2.7 %collective-permute-start.16 = (bf16[32,5120]{1,0:T(8,128)(2,1)S(1)}, bf16[32,5120]{1,0:T(8,128)(2,1)}, u32[]{:S(2)}, u32[]{:S(2)}) collective-permute-start(bf16[32,5120]{1,0:T(8,128)(2,1)S(1)} %slice.17), channel_id=1, source_target_pairs={{0,6},{2,0},{4,2},{6,4},{1,7},{3,1},{5,3},{7,5},{8,14},{10,8},{12,... | collective-permute-start | bytes 983048 | tf_op jit(solution)/shard_map/ppermute | solution.py:369
  77.5 1.5 collective-permute-start.9
  79.6 4.6 %collective-permute-done.14.refs_6_ = bf16[32,5120]{1,0:T(8,128)(2,1)} collective-permute-done((bf16[32,5120]{1,0:T(8,128)(2,1)S(1)}, bf16[32,5120]{1,0:T(8,128)(2,1)}, u32[]{:S(2)}, u32[]{:S(2)}) %collective-permute-start.14) | collective-permute-done | bytes 327712 | tf_op jit(solution)/shard_map/ppermute | solution.py:369
  84.1 1.8 %collective-permute-start.15 = (bf16[32,5120]{1,0:T(8,128)(2,1)}, bf16[32,5120]{1,0:T(8,128)(2,1)S(1)}, u32[]{:S(2)}, u32[]{:S(2)}) collective-permute-start(bf16[32,5120]{1,0:T(8,128)(2,1)} %collective-permute-done.14.refs_6_), channel_id=1, source_target_pairs={{0,1},{1,0},{2,3},{3,2},{4,5},{5,4},{6,7},{7,6},{8,9},{9,8},{10,11... | collective-permute-start | bytes 983048 | tf_op jit(solution)/shard_map/ppermute | solution.py:373
  87.8 3.0 %stack_rows.1.rows = bf16[512,5120]{1,0:T(8,128)(2,1)S(1)} custom-call(bf16[64,5120]{1,0:T(8,128)(2,1)S(1)} %project_and_norm.1.refs_0_, bf16[64,5120]{1,0:T(8,128)(2,1)} %collective-permute-done.9.refs_1_, bf16[64,5120]{1,0:T(8,128)(2,1)S(1)} %collective-permute-done.10.refs_2_, bf16[64,5120]{1,0:T(8,128)(2,1)} %collective-permute-done.12.refs_3_, ...), custom_call_target="tpu_custom_call" | custom-call | bytes 10485760 | tf_op jit(solution)/shard_map/stack_rows/pallas_call | solution.py:148
  90.9 2.3 %copy-done.2 = bf16[512,5120]{1,0:T(8,128)(2,1)} copy-done((bf16[512,5120]{1,0:T(8,128)(2,1)}, bf16[512,5120]{1,0:T(8,128)(2,1)S(1)}, u32[]{:S(2)}) %copy-start.2) | copy-done | bytes 5242904
  93.2 11.2 %all-gather.2.cloned.1.call-done.weight = bf16[5120,1024]{1,0:T(8,128)(2,1)} async-done(((bf16[320,1024]{1,0:T(8,128)(2,1)}), bf16[5120,1024]{1,0:T(8,128)(2,1)}) %all-gather.2.cloned.1.call-update) | async-done | bytes 10485776 | tf_op jit(solution)/shard_map/all_gather | solution.py:416
  104.4 2.5 %copy-done.3 = bf16[512,5120]{1,0:T(8,128)(2,1)S(1)} copy-done((bf16[512,5120]{1,0:T(8,128)(2,1)S(1)}, bf16[512,5120]{1,0:T(8,128)(2,1)}, u32[]{:S(2)}) %copy-start.3) | copy-done | bytes 5242904
  106.9 9.3 %merge_rows.1 = bf16[1024,1024]{1,0:T(8,128)(2,1)S(1)} custom-call(bf16[512,5120]{1,0:T(8,128)(2,1)S(1)} %copy-done.3, bf16[5120,1024]{1,0:T(8,128)(2,1)} %all-gather.2.cloned.1.call-done.weight, bf16[1024,512]{1,0:T(8,128)(2,1)S(1)} %compare_convert_fusion.send), custom_call_target="tpu_custom_call" | custom-call | flops 6442450944 | bytes 17825792 | tf_op jit(solution)/shard_map/merge_rows/pallas_call | solution.py:188
  117.5 7.7 %all-to-all-start.1 = ((bf16[32,32,1024]{2,1,0:T(8,128)(2,1)}), bf16[32,32,1024]{2,1,0:T(8,128)(2,1)S(1)}, u32[]{:S(2)}, u32[]{:S(2)}) async-start(bf16[32,32,1024]{2,1,0:T(8,128)(2,1)} %bitcast.20), calls=%async_computation.1 | async-start | bytes 4194304 | tf_op jit(solution)/shard_map/all_to_all | solution.py:459
  125.4 1.6 copy-done
  128.1 27.5 %all-to-all-done.1 = bf16[32,32,1024]{2,1,0:T(8,128)(2,1)S(1)} async-done(((bf16[32,32,1024]{2,1,0:T(8,128)(2,1)}), bf16[32,32,1024]{2,1,0:T(8,128)(2,1)S(1)}, u32[]{:S(2)}, u32[]{:S(2)}) %all-to-all-start.1) | async-done | bytes 2097184 | tf_op jit(solution)/shard_map/all_to_all | solution.py:459
  155.7 1.6 slot_squares.1.own
  157.3 2.3 %collective-permute-start.18 = (f32[4,128]{1,0:T(4,128)S(1)}, f32[4,128]{1,0:T(4,128)S(1)}, u32[]{:S(2)}, u32[]{:S(2)}) collective-permute-start(f32[4,128]{1,0:T(4,128)S(1)} %slot_squares.1.own), channel_id=1, source_target_pairs={{0,1},{1,0},{2,3},{3,2},{4,5},{5,4},{6,7},{7,6},{8,9},{9,8},{10,11... | collective-permute-start | bytes 6152 | tf_op jit(solution)/shard_map/ppermute | solution.py:365
  159.9 1.4 collective-permute-start.20
  161.3 1.9 %pick_rows.1.prompt = bf16[512,2048]{1,0:T(8,128)(2,1)S(1)} custom-call(bf16[16,2,32,1024]{3,2,1,0:T(8,128)(2,1)S(1)} %bitcast.19, bf16[512,512]{1,0:T(8,128)(2,1)S(1)} %fusion.1.pick, s32[512,1]{1,0:T(8,128)S(1)} %copy.14.usable, bf16[512,2048]{1,0:T(8,128)(2,1)S(1)} %copy-done.1), custom_call_target="tpu_custom_call" | custom-call | flops 1073741824 | bytes 6291456 | tf_op jit(solution)/shard_map/pick_rows/pallas_call | solution.py:313
  163.3 2.5 %finish.1 = bf16[512,2048]{1,0:T(8,128)(2,1)} custom-call(bf16[512,2048]{1,0:T(8,128)(2,1)S(1)} %pick_rows.1.prompt, f32[4,128]{1,0:T(4,128)S(1)} %slot_squares.1.own, f32[4,128]{1,0:T(4,128)S(1)} %collective-permute-done.18.core, f32[4,128]{1,0:T(4,128)S(1)} %collective-permute-done.19.far, f32[4,128]{1,0:T(4,128)S(1)} %collective-permute-done.20.both, ...), custom_call_target="tpu_custom_call" | custom-call | flops 3145728 | bytes 4194304 | tf_op jit(solution)/shard_map/finish/pallas_call | solution.py:347
  (86 shorter events, 13.3 us)
Async XLA Ops:
  6.5 97.9 %all-gather.2.cloned.1.call-start = ((), (), s32[]{:S(2)}) async-start(), calls=%async_computation.2 | async-start | bytes 11141120 | tf_op jit(solution)/shard_map/all_gather | solution.py:416
  6.5 13.8 %copy-start.11 = (s32[1,256]{1,0:T(1,128)S(1)}, s32[1,256]{1,0:T(1,128)}, u32[]{:S(2)}) copy-start(s32[1,256]{1,0:T(1,128)} %param.10) | copy-start | bytes 3076
  7.7 13.1 %copy-start.4 = (bf16[320,1280]{1,0:T(8,128)(2,1)S(1)}, bf16[320,1280]{1,0:T(8,128)(2,1)}, u32[]{:S(2)}) copy-start(bf16[320,1280]{1,0:T(8,128)(2,1)} %refs_5_) | copy-start | bytes 2457604
  7.7 11.0 %collective-permute-start = (bf16[160,1024]{1,0:T(8,128)(2,1)S(1)}, bf16[160,1024]{1,0:T(8,128)(2,1)S(1)}, u32[]{:S(2)}, u32[]{:S(2)}) collective-permute-start(bf16[160,1024]{1,0:T(8,128)(2,1)S(1)} %get-tuple-element.44), channel_id=1, source_target_pairs={{0,4},{4,0},{1,5},{5,1},{2,6},{6,2},{3,7},{7,3},{8,12},{12,8},{9,1... | collective-permute-start | bytes 983048 | tf_op jit(solution)/shard_map/ppermute | solution.py:395
  20.8 34.1 %collective-permute-start.6 = (bf16[320,1280]{1,0:T(8,128)(2,1)S(1)}, bf16[320,1280]{1,0:T(8,128)(2,1)S(1)}, u32[]{:S(2)}, u32[]{:S(2)}) collective-permute-start(bf16[320,1280]{1,0:T(8,128)(2,1)S(1)} %copy-done.4), channel_id=1, source_target_pairs={{0,1},{1,0},{2,3},{3,2},{4,5},{5,4},{6,7},{7,6},{8,9},{9,8},{10,11... | collective-permute-start | bytes 2457608 | tf_op jit(solution)/shard_map/ppermute | solution.py:373
  22.4 20.5 %collective-permute-start.1 = (bf16[160,1280]{1,0:T(8,128)(2,1)S(1)}, bf16[160,1280]{1,0:T(8,128)(2,1)S(1)}, u32[]{:S(2)}, u32[]{:S(2)}) collective-permute-start(bf16[160,1280]{1,0:T(8,128)(2,1)S(1)} %get-tuple-element.38), channel_id=1, source_target_pairs={{0,2},{2,4},{4,6},{6,0},{1,3},{3,5},{5,7},{7,1},{8,10},{10,12},{12... | collective-permute-start | bytes 1228808 | tf_op jit(solution)/shard_map/ppermute | solution.py:369
  23.8 19.1 %collective-permute-start.2 = (bf16[160,1280]{1,0:T(8,128)(2,1)S(1)}, bf16[160,1280]{1,0:T(8,128)(2,1)S(1)}, u32[]{:S(2)}, u32[]{:S(2)}) collective-permute-start(bf16[160,1280]{1,0:T(8,128)(2,1)S(1)} %get-tuple-element.37), channel_id=1, source_target_pairs={{0,6},{2,0},{4,2},{6,4},{1,7},{3,1},{5,3},{7,5},{8,14},{10,8},{12,... | collective-permute-start | bytes 1228808 | tf_op jit(solution)/shard_map/ppermute | solution.py:369
  28.8 17.2 %copy-start.10 = (f32[1280]{0:T(1024)S(1)}, f32[1280]{0:T(1024)}, u32[]{:S(2)}) copy-start(f32[1280]{0:T(1024)} %param.13) | copy-start | bytes 15364
  28.8 26.0 %copy-start.6 = (bf16[1024,1280]{1,0:T(8,128)(2,1)S(1)}, bf16[1024,1280]{1,0:T(8,128)(2,1)}, u32[]{:S(2)}) copy-start(bf16[1024,1280]{1,0:T(8,128)(2,1)} %refs_11_) | copy-start | bytes 7864324
  42.9 12.0 %collective-permute-start.7 = (bf16[160,1280]{1,0:T(8,128)(2,1)S(1)}, bf16[160,1280]{1,0:T(8,128)(2,1)S(1)}, u32[]{:S(2)}, u32[]{:S(2)}) collective-permute-start(bf16[160,1280]{1,0:T(8,128)(2,1)S(1)} %collective-permute-done.1.refs_7_), channel_id=1, source_target_pairs={{0,1},{1,0},{2,3},{3,2},{4,5},{5,4},{6,7},{7,6},{8,9},{9,8},{10,11... | collective-permute-start | bytes 1228808 | tf_op jit(solution)/shard_map/ppermute | solution.py:373
  43.3 11.5 %collective-permute-start.8 = (bf16[160,1280]{1,0:T(8,128)(2,1)S(1)}, bf16[160,1280]{1,0:T(8,128)(2,1)S(1)}, u32[]{:S(2)}, u32[]{:S(2)}) collective-permute-start(bf16[160,1280]{1,0:T(8,128)(2,1)S(1)} %collective-permute-done.2.refs_8_), channel_id=1, source_target_pairs={{0,1},{1,0},{2,3},{3,2},{4,5},{5,4},{6,7},{7,6},{8,9},{9,8},{10,11... | collective-permute-start | bytes 1228808 | tf_op jit(solution)/shard_map/ppermute | solution.py:373
  43.6 2.0 %collective-permute-start.3 = (bf16[256,320]{1,0:T(8,128)(2,1)S(1)}, bf16[256,320]{1,0:T(8,128)(2,1)S(1)}, u32[]{:S(2)}, u32[]{:S(2)}) collective-permute-start(bf16[256,320]{1,0:T(8,128)(2,1)S(1)} %get-tuple-element.41), channel_id=1, source_target_pairs={{0,1},{1,0},{2,3},{3,2},{4,5},{5,4},{6,7},{7,6},{8,9},{9,8},{10,11... | collective-permute-start | bytes 491528 | tf_op jit(solution)/shard_map/ppermute | solution.py:365
  44.0 6.5 %collective-permute-start.4 = (bf16[256,320]{1,0:T(8,128)(2,1)S(1)}, bf16[256,320]{1,0:T(8,128)(2,1)S(1)}, u32[]{:S(2)}, u32[]{:S(2)}) collective-permute-start(bf16[256,320]{1,0:T(8,128)(2,1)S(1)} %get-tuple-element.40), channel_id=1, source_target_pairs={{0,2},{1,3},{2,0},{3,1},{4,6},{5,7},{6,4},{7,5},{8,10},{9,11},{10,... | collective-permute-start | bytes 491528 | tf_op jit(solution)/shard_map/ppermute | solution.py:365
  45.6 9.3 %collective-permute-start.5 = (bf16[256,320]{1,0:T(8,128)(2,1)S(1)}, bf16[256,320]{1,0:T(8,128)(2,1)S(1)}, u32[]{:S(2)}, u32[]{:S(2)}) collective-permute-start(bf16[256,320]{1,0:T(8,128)(2,1)S(1)} %get-tuple-element.39), channel_id=1, source_target_pairs={{0,3},{1,2},{2,1},{3,0},{4,7},{5,6},{6,5},{7,4},{8,11},{9,10},{10,... | collective-permute-start | bytes 491528 | tf_op jit(solution)/shard_map/ppermute | solution.py:365
  56.7 17.6 %collective-permute-start.10 = (bf16[64,5120]{1,0:T(8,128)(2,1)S(1)}, bf16[64,5120]{1,0:T(8,128)(2,1)S(1)}, u32[]{:S(2)}, u32[]{:S(2)}) collective-permute-start(bf16[64,5120]{1,0:T(8,128)(2,1)S(1)} %project_and_norm.1.refs_0_), channel_id=1, source_target_pairs={{0,2},{2,4},{4,6},{6,0},{1,3},{3,5},{5,7},{7,1},{8,10},{10,12},{12... | collective-permute-start | bytes 1966088 | tf_op jit(solution)/shard_map/ppermute | solution.py:369
  56.9 17.5 %collective-permute-start.11 = (bf16[64,5120]{1,0:T(8,128)(2,1)S(1)}, bf16[64,5120]{1,0:T(8,128)(2,1)S(1)}, u32[]{:S(2)}, u32[]{:S(2)}) collective-permute-start(bf16[64,5120]{1,0:T(8,128)(2,1)S(1)} %project_and_norm.1.refs_0_), channel_id=1, source_target_pairs={{0,6},{2,0},{4,2},{6,4},{1,7},{3,1},{5,3},{7,5},{8,14},{10,8},{12,... | collective-permute-start | bytes 1966088 | tf_op jit(solution)/shard_map/ppermute | solution.py:369
  59.5 19.5 %all-to-all-start = ((s32[32,1,32]{2,1,0:T(1,128)}), s32[32,1,32]{2,1,0:T(1,128)S(1)}, u32[]{:S(2)}, u32[]{:S(2)}) async-start(s32[32,1,32]{2,1,0:T(1,128)} %bitcast.10), calls=%async_computation | async-start | bytes 32768 | tf_op jit(solution)/shard_map/all_to_all | solution.py:437
  74.4 9.7 %collective-permute-start.14 = (bf16[32,5120]{1,0:T(8,128)(2,1)S(1)}, bf16[32,5120]{1,0:T(8,128)(2,1)}, u32[]{:S(2)}, u32[]{:S(2)}) collective-permute-start(bf16[32,5120]{1,0:T(8,128)(2,1)S(1)} %slice.16), channel_id=1, source_target_pairs={{0,2},{2,4},{4,6},{6,0},{1,3},{3,5},{5,7},{7,1},{8,10},{10,12},{12... | collective-permute-start | bytes 983048 | tf_op jit(solution)/shard_map/ppermute | solution.py:369
  74.5 11.4 %collective-permute-start.16 = (bf16[32,5120]{1,0:T(8,128)(2,1)S(1)}, bf16[32,5120]{1,0:T(8,128)(2,1)}, u32[]{:S(2)}, u32[]{:S(2)}) collective-permute-start(bf16[32,5120]{1,0:T(8,128)(2,1)S(1)} %slice.17), channel_id=1, source_target_pairs={{0,6},{2,0},{4,2},{6,4},{1,7},{3,1},{5,3},{7,5},{8,14},{10,8},{12,... | collective-permute-start | bytes 983048 | tf_op jit(solution)/shard_map/ppermute | solution.py:369
  77.5 8.7 %collective-permute-start.9 = (bf16[64,5120]{1,0:T(8,128)(2,1)S(1)}, bf16[64,5120]{1,0:T(8,128)(2,1)}, u32[]{:S(2)}, u32[]{:S(2)}) collective-permute-start(bf16[64,5120]{1,0:T(8,128)(2,1)S(1)} %project_and_norm.1.refs_0_), channel_id=1, source_target_pairs={{0,1},{1,0},{2,3},{3,2},{4,5},{5,4},{6,7},{7,6},{8,9},{9,8},{10,11... | collective-permute-start | bytes 1966088 | tf_op jit(solution)/shard_map/ppermute | solution.py:373
  79.0 7.2 %collective-permute-start.12 = (bf16[64,5120]{1,0:T(8,128)(2,1)S(1)}, bf16[64,5120]{1,0:T(8,128)(2,1)}, u32[]{:S(2)}, u32[]{:S(2)}) collective-permute-start(bf16[64,5120]{1,0:T(8,128)(2,1)S(1)} %collective-permute-done.10.refs_2_), channel_id=1, source_target_pairs={{0,1},{1,0},{2,3},{3,2},{4,5},{5,4},{6,7},{7,6},{8,9},{9,8},{10,11... | collective-permute-start | bytes 1966088 | tf_op jit(solution)/shard_map/ppermute | solution.py:373
  79.1 7.1 %collective-permute-start.13 = (bf16[64,5120]{1,0:T(8,128)(2,1)S(1)}, bf16[64,5120]{1,0:T(8,128)(2,1)}, u32[]{:S(2)}, u32[]{:S(2)}) collective-permute-start(bf16[64,5120]{1,0:T(8,128)(2,1)S(1)} %collective-permute-done.11.refs_4_), channel_id=1, source_target_pairs={{0,1},{1,0},{2,3},{3,2},{4,5},{5,4},{6,7},{7,6},{8,9},{9,8},{10,11... | collective-permute-start | bytes 1966088 | tf_op jit(solution)/shard_map/ppermute | solution.py:373
  84.1 3.3 %collective-permute-start.15 = (bf16[32,5120]{1,0:T(8,128)(2,1)}, bf16[32,5120]{1,0:T(8,128)(2,1)S(1)}, u32[]{:S(2)}, u32[]{:S(2)}) collective-permute-start(bf16[32,5120]{1,0:T(8,128)(2,1)} %collective-permute-done.14.refs_6_), channel_id=1, source_target_pairs={{0,1},{1,0},{2,3},{3,2},{4,5},{5,4},{6,7},{7,6},{8,9},{9,8},{10,11... | collective-permute-start | bytes 983048 | tf_op jit(solution)/shard_map/ppermute | solution.py:373
  85.9 1.9 %collective-permute-start.17 = (bf16[32,5120]{1,0:T(8,128)(2,1)}, bf16[32,5120]{1,0:T(8,128)(2,1)S(1)}, u32[]{:S(2)}, u32[]{:S(2)}) collective-permute-start(bf16[32,5120]{1,0:T(8,128)(2,1)} %collective-permute-done.16.refs_8_), channel_id=1, source_target_pairs={{0,1},{1,0},{2,3},{3,2},{4,5},{5,4},{6,7},{7,6},{8,9},{9,8},{10,11... | collective-permute-start | bytes 983048 | tf_op jit(solution)/shard_map/ppermute | solution.py:373
  90.9 2.3 %copy-start.2 = (bf16[512,5120]{1,0:T(8,128)(2,1)}, bf16[512,5120]{1,0:T(8,128)(2,1)S(1)}, u32[]{:S(2)}) copy-start(bf16[512,5120]{1,0:T(8,128)(2,1)S(1)} %stack_rows.1.rows) | copy-start | bytes 15728644
  104.4 2.5 %copy-start.3 = (bf16[512,5120]{1,0:T(8,128)(2,1)S(1)}, bf16[512,5120]{1,0:T(8,128)(2,1)}, u32[]{:S(2)}) copy-start(bf16[512,5120]{1,0:T(8,128)(2,1)} %copy-done.2) | copy-start | bytes 15728644
  117.5 38.1 %all-to-all-start.1 = ((bf16[32,32,1024]{2,1,0:T(8,128)(2,1)}), bf16[32,32,1024]{2,1,0:T(8,128)(2,1)S(1)}, u32[]{:S(2)}, u32[]{:S(2)}) async-start(bf16[32,32,1024]{2,1,0:T(8,128)(2,1)} %bitcast.20), calls=%async_computation.1 | async-start | bytes 4194304 | tf_op jit(solution)/shard_map/all_to_all | solution.py:459
  155.7 5.6 %copy-start.1 = (bf16[512,2048]{1,0:T(8,128)(2,1)S(1)}, bf16[512,2048]{1,0:T(8,128)(2,1)}, u32[]{:S(2)}) copy-start(bf16[512,2048]{1,0:T(8,128)(2,1)} %text.3) | copy-start | bytes 6291460
  157.3 5.9 %copy-start.8 = (f32[2048]{0:T(1024)S(1)}, f32[2048]{0:T(1024)}, u32[]{:S(2)}) copy-start(f32[2048]{0:T(1024)} %param.17) | copy-start | bytes 24580
  157.3 5.9 %collective-permute-start.18 = (f32[4,128]{1,0:T(4,128)S(1)}, f32[4,128]{1,0:T(4,128)S(1)}, u32[]{:S(2)}, u32[]{:S(2)}) collective-permute-start(f32[4,128]{1,0:T(4,128)S(1)} %slot_squares.1.own), channel_id=1, source_target_pairs={{0,1},{1,0},{2,3},{3,2},{4,5},{5,4},{6,7},{7,6},{8,9},{9,8},{10,11... | collective-permute-start | bytes 6152 | tf_op jit(solution)/shard_map/ppermute | solution.py:365
  159.6 3.6 %collective-permute-start.19 = (f32[4,128]{1,0:T(4,128)S(1)}, f32[4,128]{1,0:T(4,128)S(1)}, u32[]{:S(2)}, u32[]{:S(2)}) collective-permute-start(f32[4,128]{1,0:T(4,128)S(1)} %slot_squares.1.own), channel_id=1, source_target_pairs={{0,2},{1,3},{2,0},{3,1},{4,6},{5,7},{6,4},{7,5},{8,10},{9,11},{10,... | collective-permute-start | bytes 6152 | tf_op jit(solution)/shard_map/ppermute | solution.py:365
  159.9 3.3 %collective-permute-start.20 = (f32[4,128]{1,0:T(4,128)S(1)}, f32[4,128]{1,0:T(4,128)S(1)}, u32[]{:S(2)}, u32[]{:S(2)}) collective-permute-start(f32[4,128]{1,0:T(4,128)S(1)} %slot_squares.1.own), channel_id=1, source_target_pairs={{0,3},{1,2},{2,1},{3,0},{4,7},{5,6},{6,5},{7,4},{8,11},{9,10},{10,... | collective-permute-start | bytes 6152 | tf_op jit(solution)/shard_map/ppermute | solution.py:365
  (4 other events, 6.4 us)
Sparse Core Ops, SparseCore 0:
  20.4 83.9 all-gather.1

commit v12 on v11

--- a/solution.py
+++ b/solution.py
@@ -148,7 +148,7 @@
     return pl.pallas_call(
         stack_kernel,
         grid=(depth // tile,),
-        out_shape=jax.ShapeDtypeStruct((count, depth), BF),
+        out_shape=pltpu.HBM((count, depth), BF),
         in_specs=[pl.BlockSpec((b.shape[0], tile), lambda i: (0, i)) for b in blocks],
         out_specs=pl.BlockSpec((count, tile), lambda i: (0, i)),
         compiler_params=pltpu.CompilerParams(vmem_limit_bytes=10 * 2**20),
@@ -159,38 +159,56 @@
     )(*blocks)
 
 
-def merge_kernel(rows, weight, send, outgoing, held, sems):
-    depth, columns = held.shape
-    steps = sems.shape[0]
+def merge_kernel(rows, weight, send, outgoing, rows_held, weight_held, sent, sems):
+    depth = weight_held.shape[0]
+    steps = sems.shape[0] // 2
     tile = depth // steps
-    copies = [
-        pltpu.make_async_copy(
-            weight.at[pl.ds(k * tile, tile)], held.at[pl.ds(k * tile, tile)], sems.at[k]
-        )
-        for k in range(steps)
-    ]
+    copies = []
+    for k in range(steps):
+        part = pl.ds(k * tile, tile)
+        copies += [
+            pltpu.make_async_copy(rows.at[:, part], rows_held.at[:, part], sems.at[2 * k]),
+            pltpu.make_async_copy(weight.at[part], weight_held.at[part], sems.at[2 * k + 1]),
+        ]
     for copy in copies:
         copy.start()
-    total = jnp.zeros((rows.shape[0], columns), F32)
-    for k, copy in enumerate(copies):
+    total = jnp.zeros((rows_held.shape[0], weight_held.shape[1]), F32)
+    for k in range(steps):
+        copies[2 * k].wait()
+        copies[2 * k + 1].wait()
+        part = slice(k * tile, (k + 1) * tile)
+        total += jnp.dot(
+            rows_held[:, part], weight_held[part, :], preferred_element_type=F32
+        )
+    image = total.astype(BF)
+    pieces = 4
+    count = sent.shape[0] // pieces
+    copies = []
+    for k in range(pieces):
+        part = pl.ds(k * count, count)
+        sent[part, :] = jnp.dot(send[part, :], image, preferred_element_type=F32).astype(BF)
+        copy = pltpu.make_async_copy(sent.at[part], outgoing.at[part], sems.at[k])
+        copy.start()
+        copies.append(copy)
+    for copy in copies:
         copy.wait()
-        part = slice(k * tile, (k + 1) * tile)
-        total += jnp.dot(rows[:, part], held[part, :], preferred_element_type=F32)
-    outgoing[...] = jnp.dot(
-        send[...], total.astype(BF), preferred_element_type=F32
-    ).astype(BF)
 
 
 def merge_and_select(rows, weight, send):
     slots, count = send.shape
     depth, columns = weight.shape
-    vmem = pl.BlockSpec(memory_space=pltpu.VMEM)
+    hbm = pl.BlockSpec(memory_space=pltpu.HBM)
     return pl.pallas_call(
         merge_kernel,
-        out_shape=jax.ShapeDtypeStruct((slots, columns), BF),
-        in_specs=[vmem, pl.BlockSpec(memory_space=pltpu.HBM), vmem],
-        out_specs=vmem,
-        scratch_shapes=[pltpu.VMEM((depth, columns), BF), pltpu.SemaphoreType.DMA((4,))],
+        out_shape=pltpu.HBM((slots, columns), BF),
+        in_specs=[hbm, hbm, pl.BlockSpec(memory_space=pltpu.VMEM)],
+        out_specs=hbm,
+        scratch_shapes=[
+            pltpu.VMEM((count, depth), BF),
+            pltpu.VMEM((depth, columns), BF),
+            pltpu.VMEM((slots, columns), BF),
+            pltpu.SemaphoreType.DMA((8,)),
+        ],
         compiler_params=pltpu.CompilerParams(vmem_limit_bytes=44 * 2**20),
         cost_estimate=pl.CostEstimate(
             flops=2 * count * (depth + slots) * columns,

time: 173 us -> 174 us (level)
  Pallas kernels: 35.3 us -> 38.1 us
  other arithmetic: 2.8 us -> 4.86 us
  waiting for transfers between devices: 66.7 us -> 64.8 us
    pallas_call x2, Pallas kernels: 12.4 us -> 15.1 us  [the longest x1 10.4 us: merge_and_select(): pl.pallas_call(merge_kernel, out_shape=pltpu.HBM((slots, columns), BF), i...]
    unnamed x24 -> x22, local copies, waits for them, and re-layouts: 11.1 us -> 8.76 us
  transfers between devices with their start and end apart: 24 -> 24, of which waited for: 10 -> 10; matrix products, arithmetic and copies ran while one was open for 2% -> 4% of each run, Pallas kernels for 13% -> 14%
where the time goes in v12:
time: 174 us
  waiting for transfers between devices  64.8 us (37%)
  starting transfers between devices  39 us (22%)
  Pallas kernels  38.1 us (22%)
  between operations  13.7 us (8%)
  local copies, waits for them, and re-layouts  12.5 us (7%)
  other arithmetic  4.86 us (3%)
    all_to_all x1, waiting for transfers between devices, on_device(): lax.all_to_all(outgoing, SEC, split_axis=0, concat_axis=0, tiled=True)  27.5 us
    pallas_call x1, Pallas kernels, vision_context(): pl.pallas_call(attention_kernel, out_shape=jax.ShapeDtypeStruct((row_coun...  14.1 us
    all_gather x1, waiting for transfers between devices, on_device(): weight = lax.all_gather(both, ('z', 'x'), axis=0, tiled=True)  12 us
    pallas_call x1, Pallas kernels, merge_and_select(): pl.pallas_call(merge_kernel, out_shape=pltpu.HBM((slots, columns), BF), i...  10.4 us
    ppermute x6, waiting for transfers between devices, swap_tp(): return lax.ppermute(block, TP, [(i, i ^ k) for i in range(4)])  10.3 us
    ppermute x6, waiting for transfers between devices, shift_y(): lax.ppermute(block, ('yh', 'yl'), [(i, (i + d) % 4) for i in range(4)])  9.54 us
    unnamed x22, local copies, waits for them, and re-layouts  8.76 us
    ppermute x6, starting transfers between devices, shift_y(): lax.ppermute(block, ('yh', 'yl'), [(i, (i + d) % 4) for i in range(4)])  8.5 us
  transfers between devices with their start and end apart: 24, of which 10 were waited for; matrix products, arithmetic and copies ran while one was open for 4% of the time, Pallas kernels for 14%

profile of v12, /device:TPU:1, one launch (start us, length us, event | category | flops | bytes accessed | tf_op | source)
XLA Modules:
  0.0 173.6 jit_solution(9855785396827533489)
XLA Ops:
  7.7 3.8 %collective-permute-start = (bf16[160,1024]{1,0:T(8,128)(2,1)S(1)}, bf16[160,1024]{1,0:T(8,128)(2,1)S(1)}, u32[]{:S(2)}, u32[]{:S(2)}) collective-permute-start(bf16[160,1024]{1,0:T(8,128)(2,1)S(1)} %get-tuple-element.44), channel_id=1, source_target_pairs={{0,4},{4,0},{1,5},{5,1},{2,6},{6,2},{3,7},{7,3},{8,12},{12,8},{9,1... | collective-permute-start | bytes 983048 | tf_op jit(solution)/shard_map/ppermute | solution.py:413
  13.9 4.7 %collective-permute-done = bf16[160,1024]{1,0:T(8,128)(2,1)S(1)} collective-permute-done((bf16[160,1024]{1,0:T(8,128)(2,1)S(1)}, bf16[160,1024]{1,0:T(8,128)(2,1)S(1)}, u32[]{:S(2)}, u32[]{:S(2)}) %collective-permute-start) | collective-permute-done | bytes 327712 | tf_op jit(solution)/shard_map/ppermute | solution.py:413
  20.8 1.6 collective-permute-start.6
  22.4 1.4 collective-permute-start.1
  23.9 1.5 collective-permute-start.2
  25.4 1.7 %copy-done.4 = bf16[1024,1280]{1,0:T(8,128)(2,1)S(1)} copy-done((bf16[1024,1280]{1,0:T(8,128)(2,1)S(1)}, bf16[1024,1280]{1,0:T(8,128)(2,1)}, u32[]{:S(2)}) %copy-start.4) | copy-done | bytes 2621464
  27.1 1.7 copy-done.8
  28.8 14.1 %vision_attention.1 = bf16[1024,320]{1,0:T(8,128)(2,1)S(1)} custom-call(s32[1024,1]{1,0:T(8,128)S(1)} %copy.13.row_ids, s32[1,1024]{1,0:T(1,128)S(1)} %bitcast.21, bf16[1024,1280]{1,0:T(8,128)(2,1)S(1)} %copy-done.4, bf16[3,320,1280]{2,1,0:T(8,128)(2,1)S(1)} %bitcast.23), custom_call_target="tpu_custom_call" | custom-call | flops 6811549696 | bytes 5079040 | tf_op jit(solution)/shard_map/vision_attention/pallas_call | solution.py:70
  44.2 1.4 collective-permute-done.3.refs_2_
  46.1 4.5 %collective-permute-done.4.refs_3_ = bf16[256,320]{1,0:T(8,128)(2,1)S(1)} collective-permute-done((bf16[256,320]{1,0:T(8,128)(2,1)S(1)}, bf16[256,320]{1,0:T(8,128)(2,1)S(1)}, u32[]{:S(2)}, u32[]{:S(2)}) %collective-permute-start.4) | collective-permute-done | bytes 163872 | tf_op jit(solution)/shard_map/ppermute | solution.py:383
  50.5 4.4 %collective-permute-done.5.refs_4_ = bf16[256,320]{1,0:T(8,128)(2,1)S(1)} collective-permute-done((bf16[256,320]{1,0:T(8,128)(2,1)S(1)}, bf16[256,320]{1,0:T(8,128)(2,1)S(1)}, u32[]{:S(2)}, u32[]{:S(2)}) %collective-permute-start.5) | collective-permute-done | bytes 163872 | tf_op jit(solution)/shard_map/ppermute | solution.py:383
  54.9 1.8 %project_and_norm.1.refs_0_ = bf16[64,5120]{1,0:T(8,128)(2,1)S(1)} custom-call(s32[1]{0:T(128)} %bitcast.3.refs_0_, bf16[256,320]{1,0:T(8,128)(2,1)S(1)} %get-tuple-element.42.refs_1_, bf16[256,320]{1,0:T(8,128)(2,1)S(1)} %collective-permute-done.3.refs_2_, bf16[256,320]{1,0:T(8,128)(2,1)S(1)} %collective-permute-done.4.refs_3_, ...), custom_call_target="tpu_custom_call" | custom-call | flops 838860800 | bytes 5242880 | tf_op jit(solution)/shard_map/project_and_norm/pallas_call | solution.py:115
  57.0 2.5 %collective-permute-start.11 = (bf16[64,5120]{1,0:T(8,128)(2,1)S(1)}, bf16[64,5120]{1,0:T(8,128)(2,1)S(1)}, u32[]{:S(2)}, u32[]{:S(2)}) collective-permute-start(bf16[64,5120]{1,0:T(8,128)(2,1)S(1)} %project_and_norm.1.refs_0_), channel_id=1, source_target_pairs={{0,6},{2,0},{4,2},{6,4},{1,7},{3,1},{5,3},{7,5},{8,14},{10,8},{12,... | collective-permute-start | bytes 1966088 | tf_op jit(solution)/shard_map/ppermute | solution.py:387
  60.6 8.2 %all-to-all-start = ((s32[32,1,32]{2,1,0:T(1,128)}), s32[32,1,32]{2,1,0:T(1,128)S(1)}, u32[]{:S(2)}, u32[]{:S(2)}) async-start(s32[32,1,32]{2,1,0:T(1,128)} %bitcast.10), calls=%async_computation | async-start | bytes 32768 | tf_op jit(solution)/shard_map/all_to_all | solution.py:455
  68.8 5.6 %collective-permute-done.10.refs_2_ = bf16[64,5120]{1,0:T(8,128)(2,1)S(1)} collective-permute-done((bf16[64,5120]{1,0:T(8,128)(2,1)S(1)}, bf16[64,5120]{1,0:T(8,128)(2,1)S(1)}, u32[]{:S(2)}, u32[]{:S(2)}) %collective-permute-start.10) | collective-permute-done | bytes 655392 | tf_op jit(solution)/shard_map/ppermute | solution.py:387
  74.5 2.7 %collective-permute-start.16 = (bf16[32,5120]{1,0:T(8,128)(2,1)S(1)}, bf16[32,5120]{1,0:T(8,128)(2,1)}, u32[]{:S(2)}, u32[]{:S(2)}) collective-permute-start(bf16[32,5120]{1,0:T(8,128)(2,1)S(1)} %slice.17), channel_id=1, source_target_pairs={{0,6},{2,0},{4,2},{6,4},{1,7},{3,1},{5,3},{7,5},{8,14},{10,8},{12,... | collective-permute-start | bytes 983048 | tf_op jit(solution)/shard_map/ppermute | solution.py:387
  78.2 1.4 collective-permute-start.9
  80.2 3.9 %collective-permute-done.14.refs_6_ = bf16[32,5120]{1,0:T(8,128)(2,1)S(1)} collective-permute-done((bf16[32,5120]{1,0:T(8,128)(2,1)S(1)}, bf16[32,5120]{1,0:T(8,128)(2,1)S(1)}, u32[]{:S(2)}, u32[]{:S(2)}) %collective-permute-start.14) | collective-permute-done | bytes 327712 | tf_op jit(solution)/shard_map/ppermute | solution.py:387
  84.2 1.7 collective-permute-start.15
  87.8 4.7 %stack_rows.1.rows = bf16[512,5120]{1,0:T(8,128)(2,1)} custom-call(bf16[64,5120]{1,0:T(8,128)(2,1)S(1)} %project_and_norm.1.refs_0_, bf16[64,5120]{1,0:T(8,128)(2,1)} %collective-permute-done.9.refs_1_, bf16[64,5120]{1,0:T(8,128)(2,1)S(1)} %collective-permute-done.10.refs_2_, bf16[64,5120]{1,0:T(8,128)(2,1)} %collective-permute-done.12.refs_3_, ...), custom_call_target="tpu_custom_call" | custom-call | bytes 10485760 | tf_op jit(solution)/shard_map/stack_rows/pallas_call | solution.py:148
  92.4 12.0 %all-gather.2.cloned.1.call-done.weight = bf16[5120,1024]{1,0:T(8,128)(2,1)} async-done(((bf16[320,1024]{1,0:T(8,128)(2,1)}), bf16[5120,1024]{1,0:T(8,128)(2,1)}) %all-gather.2.cloned.1.call-update) | async-done | bytes 10485776 | tf_op jit(solution)/shard_map/all_gather | solution.py:434
  104.4 2.5 %copy-done.2 = bf16[512,5120]{1,0:T(8,128)(2,1)S(1)} copy-done((bf16[512,5120]{1,0:T(8,128)(2,1)S(1)}, bf16[512,5120]{1,0:T(8,128)(2,1)}, u32[]{:S(2)}) %copy-start.2) | copy-done | bytes 5242904
  106.9 1.2 copy-done.6
  108.1 10.4 %merge_rows.1 = bf16[1024,1024]{1,0:T(8,128)(2,1)} custom-call(bf16[512,5120]{1,0:T(8,128)(2,1)S(1)} %copy-done.2, bf16[5120,1024]{1,0:T(8,128)(2,1)} %all-gather.2.cloned.1.call-done.weight, bf16[1024,512]{1,0:T(8,128)(2,1)S(1)} %copy-done.6), custom_call_target="tpu_custom_call" | custom-call | flops 6442450944 | bytes 17825792 | tf_op jit(solution)/shard_map/merge_rows/pallas_call | solution.py:201
  118.5 7.7 %all-to-all-start.1 = ((bf16[32,32,1024]{2,1,0:T(8,128)(2,1)}), bf16[32,32,1024]{2,1,0:T(8,128)(2,1)S(1)}, u32[]{:S(2)}, u32[]{:S(2)}) async-start(bf16[32,32,1024]{2,1,0:T(8,128)(2,1)} %bitcast.24), calls=%async_computation.1 | async-start | bytes 4194304 | tf_op jit(solution)/shard_map/all_to_all | solution.py:477
  126.4 1.6 copy-done
  129.1 27.5 %all-to-all-done.1 = bf16[32,32,1024]{2,1,0:T(8,128)(2,1)S(1)} async-done(((bf16[32,32,1024]{2,1,0:T(8,128)(2,1)}), bf16[32,32,1024]{2,1,0:T(8,128)(2,1)S(1)}, u32[]{:S(2)}, u32[]{:S(2)}) %all-to-all-start.1) | async-done | bytes 2097184 | tf_op jit(solution)/shard_map/all_to_all | solution.py:477
  156.7 1.6 slot_squares.1.own
  158.3 2.3 %collective-permute-start.18 = (f32[4,128]{1,0:T(4,128)S(1)}, f32[4,128]{1,0:T(4,128)S(1)}, u32[]{:S(2)}, u32[]{:S(2)}) collective-permute-start(f32[4,128]{1,0:T(4,128)S(1)} %slot_squares.1.own), channel_id=1, source_target_pairs={{0,1},{1,0},{2,3},{3,2},{4,5},{5,4},{6,7},{7,6},{8,9},{9,8},{10,11... | collective-permute-start | bytes 6152 | tf_op jit(solution)/shard_map/ppermute | solution.py:383
  160.9 1.4 collective-permute-start.20
  162.3 1.9 %pick_rows.1.prompt = bf16[512,2048]{1,0:T(8,128)(2,1)S(1)} custom-call(bf16[16,2,32,1024]{3,2,1,0:T(8,128)(2,1)S(1)} %bitcast.19, bf16[512,512]{1,0:T(8,128)(2,1)S(1)} %fusion.1.pick, s32[512,1]{1,0:T(8,128)S(1)} %copy.14.usable, bf16[512,2048]{1,0:T(8,128)(2,1)S(1)} %copy-done.1), custom_call_target="tpu_custom_call" | custom-call | flops 1073741824 | bytes 6291456 | tf_op jit(solution)/shard_map/pick_rows/pallas_call | solution.py:331
  164.3 2.5 %finish.1 = bf16[512,2048]{1,0:T(8,128)(2,1)} custom-call(bf16[512,2048]{1,0:T(8,128)(2,1)S(1)} %pick_rows.1.prompt, f32[4,128]{1,0:T(4,128)S(1)} %slot_squares.1.own, f32[4,128]{1,0:T(4,128)S(1)} %collective-permute-done.18.core, f32[4,128]{1,0:T(4,128)S(1)} %collective-permute-done.19.far, f32[4,128]{1,0:T(4,128)S(1)} %collective-permute-done.20.both, ...), custom_call_target="tpu_custom_call" | custom-call | flops 3145728 | bytes 4194304 | tf_op jit(solution)/shard_map/finish/pallas_call | solution.py:365
  (84 shorter events, 13.8 us)
Async XLA Ops:
  6.5 97.9 %all-gather.2.cloned.1.call-start = ((), (), s32[]{:S(2)}) async-start(), calls=%async_computation.2 | async-start | bytes 11141120 | tf_op jit(solution)/shard_map/all_gather | solution.py:434
  6.5 13.8 %copy-start.10 = (s32[1,256]{1,0:T(1,128)S(1)}, s32[1,256]{1,0:T(1,128)}, u32[]{:S(2)}) copy-start(s32[1,256]{1,0:T(1,128)} %param.10) | copy-start | bytes 3076
  7.7 13.1 %copy-start.3 = (bf16[320,1280]{1,0:T(8,128)(2,1)S(1)}, bf16[320,1280]{1,0:T(8,128)(2,1)}, u32[]{:S(2)}) copy-start(bf16[320,1280]{1,0:T(8,128)(2,1)} %refs_5_) | copy-start | bytes 2457604
  7.7 11.0 %collective-permute-start = (bf16[160,1024]{1,0:T(8,128)(2,1)S(1)}, bf16[160,1024]{1,0:T(8,128)(2,1)S(1)}, u32[]{:S(2)}, u32[]{:S(2)}) collective-permute-start(bf16[160,1024]{1,0:T(8,128)(2,1)S(1)} %get-tuple-element.44), channel_id=1, source_target_pairs={{0,4},{4,0},{1,5},{5,1},{2,6},{6,2},{3,7},{7,3},{8,12},{12,8},{9,1... | collective-permute-start | bytes 983048 | tf_op jit(solution)/shard_map/ppermute | solution.py:413
  20.8 34.1 %collective-permute-start.6 = (bf16[320,1280]{1,0:T(8,128)(2,1)S(1)}, bf16[320,1280]{1,0:T(8,128)(2,1)S(1)}, u32[]{:S(2)}, u32[]{:S(2)}) collective-permute-start(bf16[320,1280]{1,0:T(8,128)(2,1)S(1)} %copy-done.3), channel_id=1, source_target_pairs={{0,1},{1,0},{2,3},{3,2},{4,5},{5,4},{6,7},{7,6},{8,9},{9,8},{10,11... | collective-permute-start | bytes 2457608 | tf_op jit(solution)/shard_map/ppermute | solution.py:391
  22.4 20.5 %collective-permute-start.1 = (bf16[160,1280]{1,0:T(8,128)(2,1)S(1)}, bf16[160,1280]{1,0:T(8,128)(2,1)S(1)}, u32[]{:S(2)}, u32[]{:S(2)}) collective-permute-start(bf16[160,1280]{1,0:T(8,128)(2,1)S(1)} %get-tuple-element.38), channel_id=1, source_target_pairs={{0,2},{2,4},{4,6},{6,0},{1,3},{3,5},{5,7},{7,1},{8,10},{10,12},{12... | collective-permute-start | bytes 1228808 | tf_op jit(solution)/shard_map/ppermute | solution.py:387
  23.9 19.1 %collective-permute-start.2 = (bf16[160,1280]{1,0:T(8,128)(2,1)S(1)}, bf16[160,1280]{1,0:T(8,128)(2,1)S(1)}, u32[]{:S(2)}, u32[]{:S(2)}) collective-permute-start(bf16[160,1280]{1,0:T(8,128)(2,1)S(1)} %get-tuple-element.37), channel_id=1, source_target_pairs={{0,6},{2,0},{4,2},{6,4},{1,7},{3,1},{5,3},{7,5},{8,14},{10,8},{12,... | collective-permute-start | bytes 1228808 | tf_op jit(solution)/shard_map/ppermute | solution.py:387
  25.4 1.7 %copy-start.4 = (bf16[1024,1280]{1,0:T(8,128)(2,1)S(1)}, bf16[1024,1280]{1,0:T(8,128)(2,1)}, u32[]{:S(2)}) copy-start(bf16[1024,1280]{1,0:T(8,128)(2,1)} %refs_11_) | copy-start | bytes 7864324
  28.8 17.2 %copy-start.9 = (f32[1280]{0:T(1024)S(1)}, f32[1280]{0:T(1024)}, u32[]{:S(2)}) copy-start(f32[1280]{0:T(1024)} %param.13) | copy-start | bytes 15364
  28.8 26.1 %copy-start.5 = (bf16[1024,1280]{1,0:T(8,128)(2,1)S(1)}, bf16[1024,1280]{1,0:T(8,128)(2,1)}, u32[]{:S(2)}) copy-start(bf16[1024,1280]{1,0:T(8,128)(2,1)} %refs_11_) | copy-start | bytes 7864324
  43.0 12.0 %collective-permute-start.7 = (bf16[160,1280]{1,0:T(8,128)(2,1)S(1)}, bf16[160,1280]{1,0:T(8,128)(2,1)S(1)}, u32[]{:S(2)}, u32[]{:S(2)}) collective-permute-start(bf16[160,1280]{1,0:T(8,128)(2,1)S(1)} %collective-permute-done.1.refs_7_), channel_id=1, source_target_pairs={{0,1},{1,0},{2,3},{3,2},{4,5},{5,4},{6,7},{7,6},{8,9},{9,8},{10,11... | collective-permute-start | bytes 1228808 | tf_op jit(solution)/shard_map/ppermute | solution.py:391
  43.4 11.5 %collective-permute-start.8 = (bf16[160,1280]{1,0:T(8,128)(2,1)S(1)}, bf16[160,1280]{1,0:T(8,128)(2,1)S(1)}, u32[]{:S(2)}, u32[]{:S(2)}) collective-permute-start(bf16[160,1280]{1,0:T(8,128)(2,1)S(1)} %collective-permute-done.2.refs_8_), channel_id=1, source_target_pairs={{0,1},{1,0},{2,3},{3,2},{4,5},{5,4},{6,7},{7,6},{8,9},{9,8},{10,11... | collective-permute-start | bytes 1228808 | tf_op jit(solution)/shard_map/ppermute | solution.py:391
  43.6 2.0 %collective-permute-start.3 = (bf16[256,320]{1,0:T(8,128)(2,1)S(1)}, bf16[256,320]{1,0:T(8,128)(2,1)S(1)}, u32[]{:S(2)}, u32[]{:S(2)}) collective-permute-start(bf16[256,320]{1,0:T(8,128)(2,1)S(1)} %get-tuple-element.41), channel_id=1, source_target_pairs={{0,1},{1,0},{2,3},{3,2},{4,5},{5,4},{6,7},{7,6},{8,9},{9,8},{10,11... | collective-permute-start | bytes 491528 | tf_op jit(solution)/shard_map/ppermute | solution.py:383
  44.1 6.5 %collective-permute-start.4 = (bf16[256,320]{1,0:T(8,128)(2,1)S(1)}, bf16[256,320]{1,0:T(8,128)(2,1)S(1)}, u32[]{:S(2)}, u32[]{:S(2)}) collective-permute-start(bf16[256,320]{1,0:T(8,128)(2,1)S(1)} %get-tuple-element.40), channel_id=1, source_target_pairs={{0,2},{1,3},{2,0},{3,1},{4,6},{5,7},{6,4},{7,5},{8,10},{9,11},{10,... | collective-permute-start | bytes 491528 | tf_op jit(solution)/shard_map/ppermute | solution.py:383
  45.7 9.3 %collective-permute-start.5 = (bf16[256,320]{1,0:T(8,128)(2,1)S(1)}, bf16[256,320]{1,0:T(8,128)(2,1)S(1)}, u32[]{:S(2)}, u32[]{:S(2)}) collective-permute-start(bf16[256,320]{1,0:T(8,128)(2,1)S(1)} %get-tuple-element.39), channel_id=1, source_target_pairs={{0,3},{1,2},{2,1},{3,0},{4,7},{5,6},{6,5},{7,4},{8,11},{9,10},{10,... | collective-permute-start | bytes 491528 | tf_op jit(solution)/shard_map/ppermute | solution.py:383
  56.8 17.6 %collective-permute-start.10 = (bf16[64,5120]{1,0:T(8,128)(2,1)S(1)}, bf16[64,5120]{1,0:T(8,128)(2,1)S(1)}, u32[]{:S(2)}, u32[]{:S(2)}) collective-permute-start(bf16[64,5120]{1,0:T(8,128)(2,1)S(1)} %project_and_norm.1.refs_0_), channel_id=1, source_target_pairs={{0,2},{2,4},{4,6},{6,0},{1,3},{3,5},{5,7},{7,1},{8,10},{10,12},{12... | collective-permute-start | bytes 1966088 | tf_op jit(solution)/shard_map/ppermute | solution.py:387
  57.0 17.5 %collective-permute-start.11 = (bf16[64,5120]{1,0:T(8,128)(2,1)S(1)}, bf16[64,5120]{1,0:T(8,128)(2,1)S(1)}, u32[]{:S(2)}, u32[]{:S(2)}) collective-permute-start(bf16[64,5120]{1,0:T(8,128)(2,1)S(1)} %project_and_norm.1.refs_0_), channel_id=1, source_target_pairs={{0,6},{2,0},{4,2},{6,4},{1,7},{3,1},{5,3},{7,5},{8,14},{10,8},{12,... | collective-permute-start | bytes 1966088 | tf_op jit(solution)/shard_map/ppermute | solution.py:387
  60.6 19.0 %all-to-all-start = ((s32[32,1,32]{2,1,0:T(1,128)}), s32[32,1,32]{2,1,0:T(1,128)S(1)}, u32[]{:S(2)}, u32[]{:S(2)}) async-start(s32[32,1,32]{2,1,0:T(1,128)} %bitcast.10), calls=%async_computation | async-start | bytes 32768 | tf_op jit(solution)/shard_map/all_to_all | solution.py:455
  74.4 9.7 %collective-permute-start.14 = (bf16[32,5120]{1,0:T(8,128)(2,1)S(1)}, bf16[32,5120]{1,0:T(8,128)(2,1)S(1)}, u32[]{:S(2)}, u32[]{:S(2)}) collective-permute-start(bf16[32,5120]{1,0:T(8,128)(2,1)S(1)} %slice.16), channel_id=1, source_target_pairs={{0,2},{2,4},{4,6},{6,0},{1,3},{3,5},{5,7},{7,1},{8,10},{10,12},{12... | collective-permute-start | bytes 983048 | tf_op jit(solution)/shard_map/ppermute | solution.py:387
  74.5 11.3 %collective-permute-start.16 = (bf16[32,5120]{1,0:T(8,128)(2,1)S(1)}, bf16[32,5120]{1,0:T(8,128)(2,1)}, u32[]{:S(2)}, u32[]{:S(2)}) collective-permute-start(bf16[32,5120]{1,0:T(8,128)(2,1)S(1)} %slice.17), channel_id=1, source_target_pairs={{0,6},{2,0},{4,2},{6,4},{1,7},{3,1},{5,3},{7,5},{8,14},{10,8},{12,... | collective-permute-start | bytes 983048 | tf_op jit(solution)/shard_map/ppermute | solution.py:387
  78.2 8.9 %collective-permute-start.9 = (bf16[64,5120]{1,0:T(8,128)(2,1)S(1)}, bf16[64,5120]{1,0:T(8,128)(2,1)}, u32[]{:S(2)}, u32[]{:S(2)}) collective-permute-start(bf16[64,5120]{1,0:T(8,128)(2,1)S(1)} %project_and_norm.1.refs_0_), channel_id=1, source_target_pairs={{0,1},{1,0},{2,3},{3,2},{4,5},{5,4},{6,7},{7,6},{8,9},{9,8},{10,11... | collective-permute-start | bytes 1966088 | tf_op jit(solution)/shard_map/ppermute | solution.py:391
  79.6 7.4 %collective-permute-start.12 = (bf16[64,5120]{1,0:T(8,128)(2,1)S(1)}, bf16[64,5120]{1,0:T(8,128)(2,1)}, u32[]{:S(2)}, u32[]{:S(2)}) collective-permute-start(bf16[64,5120]{1,0:T(8,128)(2,1)S(1)} %collective-permute-done.10.refs_2_), channel_id=1, source_target_pairs={{0,1},{1,0},{2,3},{3,2},{4,5},{5,4},{6,7},{7,6},{8,9},{9,8},{10,11... | collective-permute-start | bytes 1966088 | tf_op jit(solution)/shard_map/ppermute | solution.py:391
  79.7 7.3 %collective-permute-start.13 = (bf16[64,5120]{1,0:T(8,128)(2,1)S(1)}, bf16[64,5120]{1,0:T(8,128)(2,1)}, u32[]{:S(2)}, u32[]{:S(2)}) collective-permute-start(bf16[64,5120]{1,0:T(8,128)(2,1)S(1)} %collective-permute-done.11.refs_4_), channel_id=1, source_target_pairs={{0,1},{1,0},{2,3},{3,2},{4,5},{5,4},{6,7},{7,6},{8,9},{9,8},{10,11... | collective-permute-start | bytes 1966088 | tf_op jit(solution)/shard_map/ppermute | solution.py:391
  84.2 3.3 %collective-permute-start.15 = (bf16[32,5120]{1,0:T(8,128)(2,1)S(1)}, bf16[32,5120]{1,0:T(8,128)(2,1)S(1)}, u32[]{:S(2)}, u32[]{:S(2)}) collective-permute-start(bf16[32,5120]{1,0:T(8,128)(2,1)S(1)} %collective-permute-done.14.refs_6_), channel_id=1, source_target_pairs={{0,1},{1,0},{2,3},{3,2},{4,5},{5,4},{6,7},{7,6},{8,9},{9,8},{10,11... | collective-permute-start | bytes 983048 | tf_op jit(solution)/shard_map/ppermute | solution.py:391
  85.8 1.9 %collective-permute-start.17 = (bf16[32,5120]{1,0:T(8,128)(2,1)}, bf16[32,5120]{1,0:T(8,128)(2,1)S(1)}, u32[]{:S(2)}, u32[]{:S(2)}) collective-permute-start(bf16[32,5120]{1,0:T(8,128)(2,1)} %collective-permute-done.16.refs_8_), channel_id=1, source_target_pairs={{0,1},{1,0},{2,3},{3,2},{4,5},{5,4},{6,7},{7,6},{8,9},{9,8},{10,11... | collective-permute-start | bytes 983048 | tf_op jit(solution)/shard_map/ppermute | solution.py:391
  104.4 2.5 %copy-start.2 = (bf16[512,5120]{1,0:T(8,128)(2,1)S(1)}, bf16[512,5120]{1,0:T(8,128)(2,1)}, u32[]{:S(2)}) copy-start(bf16[512,5120]{1,0:T(8,128)(2,1)} %stack_rows.1.rows) | copy-start | bytes 15728644
  118.5 38.2 %all-to-all-start.1 = ((bf16[32,32,1024]{2,1,0:T(8,128)(2,1)}), bf16[32,32,1024]{2,1,0:T(8,128)(2,1)S(1)}, u32[]{:S(2)}, u32[]{:S(2)}) async-start(bf16[32,32,1024]{2,1,0:T(8,128)(2,1)} %bitcast.24), calls=%async_computation.1 | async-start | bytes 4194304 | tf_op jit(solution)/shard_map/all_to_all | solution.py:477
  156.7 5.6 %copy-start.1 = (bf16[512,2048]{1,0:T(8,128)(2,1)S(1)}, bf16[512,2048]{1,0:T(8,128)(2,1)}, u32[]{:S(2)}) copy-start(bf16[512,2048]{1,0:T(8,128)(2,1)} %text.3) | copy-start | bytes 6291460
  158.3 6.0 %copy-start.7 = (f32[2048]{0:T(1024)S(1)}, f32[2048]{0:T(1024)}, u32[]{:S(2)}) copy-start(f32[2048]{0:T(1024)} %param.17) | copy-start | bytes 24580
  158.3 5.9 %collective-permute-start.18 = (f32[4,128]{1,0:T(4,128)S(1)}, f32[4,128]{1,0:T(4,128)S(1)}, u32[]{:S(2)}, u32[]{:S(2)}) collective-permute-start(f32[4,128]{1,0:T(4,128)S(1)} %slot_squares.1.own), channel_id=1, source_target_pairs={{0,1},{1,0},{2,3},{3,2},{4,5},{5,4},{6,7},{7,6},{8,9},{9,8},{10,11... | collective-permute-start | bytes 6152 | tf_op jit(solution)/shard_map/ppermute | solution.py:383
  160.6 3.7 %collective-permute-start.19 = (f32[4,128]{1,0:T(4,128)S(1)}, f32[4,128]{1,0:T(4,128)S(1)}, u32[]{:S(2)}, u32[]{:S(2)}) collective-permute-start(f32[4,128]{1,0:T(4,128)S(1)} %slot_squares.1.own), channel_id=1, source_target_pairs={{0,2},{1,3},{2,0},{3,1},{4,6},{5,7},{6,4},{7,5},{8,10},{9,11},{10,... | collective-permute-start | bytes 6152 | tf_op jit(solution)/shard_map/ppermute | solution.py:383
  160.9 3.4 %collective-permute-start.20 = (f32[4,128]{1,0:T(4,128)S(1)}, f32[4,128]{1,0:T(4,128)S(1)}, u32[]{:S(2)}, u32[]{:S(2)}) collective-permute-start(f32[4,128]{1,0:T(4,128)S(1)} %slot_squares.1.own), channel_id=1, source_target_pairs={{0,3},{1,2},{2,1},{3,0},{4,7},{5,6},{6,5},{7,4},{8,11},{9,10},{10,... | collective-permute-start | bytes 6152 | tf_op jit(solution)/shard_map/ppermute | solution.py:383
  (3 other events, 4.5 us)
Sparse Core Ops, SparseCore 0:
  20.4 83.9 all-gather.1

commit v13 on v12

--- a/solution.py
+++ b/solution.py
@@ -159,9 +159,9 @@
     )(*blocks)
 
 
-def merge_kernel(rows, weight, send, outgoing, rows_held, weight_held, sent, sems):
+def merge_kernel(rows, weight, send, outgoing, rows_held, weight_held, send_held, sent, sems):
     depth = weight_held.shape[0]
-    steps = sems.shape[0] // 2
+    steps = (sems.shape[0] - 1) // 2
     tile = depth // steps
     copies = []
     for k in range(steps):
@@ -170,6 +170,7 @@
             pltpu.make_async_copy(rows.at[:, part], rows_held.at[:, part], sems.at[2 * k]),
             pltpu.make_async_copy(weight.at[part], weight_held.at[part], sems.at[2 * k + 1]),
         ]
+    copies.append(pltpu.make_async_copy(send, send_held, sems.at[2 * steps]))
     for copy in copies:
         copy.start()
     total = jnp.zeros((rows_held.shape[0], weight_held.shape[1]), F32)
@@ -181,12 +182,15 @@
             rows_held[:, part], weight_held[part, :], preferred_element_type=F32
         )
     image = total.astype(BF)
+    copies[-1].wait()
     pieces = 4
     count = sent.shape[0] // pieces
     copies = []
     for k in range(pieces):
         part = pl.ds(k * count, count)
-        sent[part, :] = jnp.dot(send[part, :], image, preferred_element_type=F32).astype(BF)
+        sent[part, :] = jnp.dot(
+            send_held[part, :], image, preferred_element_type=F32
+        ).astype(BF)
         copy = pltpu.make_async_copy(sent.at[part], outgoing.at[part], sems.at[k])
         copy.start()
         copies.append(copy)
@@ -201,15 +205,16 @@
     return pl.pallas_call(
         merge_kernel,
         out_shape=pltpu.HBM((slots, columns), BF),
-        in_specs=[hbm, hbm, pl.BlockSpec(memory_space=pltpu.VMEM)],
+        in_specs=[hbm, hbm, hbm],
         out_specs=hbm,
         scratch_shapes=[
             pltpu.VMEM((count, depth), BF),
             pltpu.VMEM((depth, columns), BF),
+            pltpu.VMEM((slots, count), BF),
             pltpu.VMEM((slots, columns), BF),
-            pltpu.SemaphoreType.DMA((8,)),
+            pltpu.SemaphoreType.DMA((9,)),
         ],
-        compiler_params=pltpu.CompilerParams(vmem_limit_bytes=44 * 2**20),
+        compiler_params=pltpu.CompilerParams(vmem_limit_bytes=60 * 2**20),
         cost_estimate=pl.CostEstimate(
             flops=2 * count * (depth + slots) * columns,
             bytes_accessed=2 * (count * depth + depth * columns + slots * columns),

time: 174 us -> 171 us (0.983)
  local copies, waits for them, and re-layouts: 12.5 us -> 8.81 us
    unnamed x22 -> x18, local copies, waits for them, and re-layouts: 8.76 us -> 5.05 us
where the time goes in v13:
time: 171 us
  waiting for transfers between devices  64.6 us (38%)
  starting transfers between devices  39 us (23%)
  Pallas kernels  39 us (23%)
  between operations  13.7 us (8%)
  local copies, waits for them, and re-layouts  8.81 us (5%)
  other arithmetic  4.94 us (3%)
    all_to_all x1, waiting for transfers between devices, on_device(): lax.all_to_all(outgoing, SEC, split_axis=0, concat_axis=0, tiled=True)  27.5 us
    pallas_call x1, Pallas kernels, vision_context(): pl.pallas_call(attention_kernel, out_shape=jax.ShapeDtypeStruct((row_coun...  14.1 us
    all_gather x1, waiting for transfers between devices, on_device(): weight = lax.all_gather(both, ('z', 'x'), axis=0, tiled=True)  11.9 us
    pallas_call x1, Pallas kernels, merge_and_select(): pl.pallas_call(merge_kernel, out_shape=pltpu.HBM((slots, columns), BF), i...  11.1 us
    ppermute x6, waiting for transfers between devices, swap_tp(): return lax.ppermute(block, TP, [(i, i ^ k) for i in range(4)])  10.3 us
    ppermute x6, waiting for transfers between devices, shift_y(): lax.ppermute(block, ('yh', 'yl'), [(i, (i + d) % 4) for i in range(4)])  9.44 us
    ppermute x6, starting transfers between devices, shift_y(): lax.ppermute(block, ('yh', 'yl'), [(i, (i + d) % 4) for i in range(4)])  8.5 us
    all_to_all x1, starting transfers between devices, on_device(): table = lax.all_to_all(table, SEC, split_axis=0, concat_axis=0, tiled=True)  8.16 us
  transfers between devices with their start and end apart: 24, of which 10 were waited for; matrix products, arithmetic and copies ran while one was open for 4% of the time, Pallas kernels for 14%

profile of v13, /device:TPU:1, one launch (start us, length us, event | category | flops | bytes accessed | tf_op | source)
XLA Modules:
  0.0 170.6 jit_solution(13186670298185488255)
XLA Ops:
  6.5 1.1 constant_dynamic-slice_fusion.4
  7.7 3.8 %collective-permute-start = (bf16[160,1024]{1,0:T(8,128)(2,1)S(1)}, bf16[160,1024]{1,0:T(8,128)(2,1)S(1)}, u32[]{:S(2)}, u32[]{:S(2)}) collective-permute-start(bf16[160,1024]{1,0:T(8,128)(2,1)S(1)} %get-tuple-element.44), channel_id=1, source_target_pairs={{0,4},{4,0},{1,5},{5,1},{2,6},{6,2},{3,7},{7,3},{8,12},{12,8},{9,1... | collective-permute-start | bytes 983048 | tf_op jit(solution)/shard_map/ppermute | solution.py:418
  13.9 4.7 %collective-permute-done = bf16[160,1024]{1,0:T(8,128)(2,1)S(1)} collective-permute-done((bf16[160,1024]{1,0:T(8,128)(2,1)S(1)}, bf16[160,1024]{1,0:T(8,128)(2,1)S(1)}, u32[]{:S(2)}, u32[]{:S(2)}) %collective-permute-start) | collective-permute-done | bytes 327712 | tf_op jit(solution)/shard_map/ppermute | solution.py:418
  20.8 1.6 collective-permute-start.6
  22.4 1.4 collective-permute-start.1
  23.8 1.5 collective-permute-start.2
  25.4 1.7 %copy-done.3 = bf16[1024,1280]{1,0:T(8,128)(2,1)S(1)} copy-done((bf16[1024,1280]{1,0:T(8,128)(2,1)S(1)}, bf16[1024,1280]{1,0:T(8,128)(2,1)}, u32[]{:S(2)}) %copy-start.3) | copy-done | bytes 2621464
  27.1 1.7 copy-done.6
  28.8 14.1 %vision_attention.1 = bf16[1024,320]{1,0:T(8,128)(2,1)S(1)} custom-call(s32[1024,1]{1,0:T(8,128)S(1)} %copy.13.row_ids, s32[1,1024]{1,0:T(1,128)S(1)} %bitcast.21, bf16[1024,1280]{1,0:T(8,128)(2,1)S(1)} %copy-done.3, bf16[3,320,1280]{2,1,0:T(8,128)(2,1)S(1)} %bitcast.23), custom_call_target="tpu_custom_call" | custom-call | flops 6811549696 | bytes 5079040 | tf_op jit(solution)/shard_map/vision_attention/pallas_call | solution.py:70
  44.2 1.4 collective-permute-done.3.refs_2_
  46.0 4.5 %collective-permute-done.4.refs_3_ = bf16[256,320]{1,0:T(8,128)(2,1)S(1)} collective-permute-done((bf16[256,320]{1,0:T(8,128)(2,1)S(1)}, bf16[256,320]{1,0:T(8,128)(2,1)S(1)}, u32[]{:S(2)}, u32[]{:S(2)}) %collective-permute-start.4) | collective-permute-done | bytes 163872 | tf_op jit(solution)/shard_map/ppermute | solution.py:388
  50.5 4.4 %collective-permute-done.5.refs_4_ = bf16[256,320]{1,0:T(8,128)(2,1)S(1)} collective-permute-done((bf16[256,320]{1,0:T(8,128)(2,1)S(1)}, bf16[256,320]{1,0:T(8,128)(2,1)S(1)}, u32[]{:S(2)}, u32[]{:S(2)}) %collective-permute-start.5) | collective-permute-done | bytes 163872 | tf_op jit(solution)/shard_map/ppermute | solution.py:388
  54.9 1.8 %project_and_norm.1.refs_0_ = bf16[64,5120]{1,0:T(8,128)(2,1)S(1)} custom-call(s32[1]{0:T(128)} %bitcast.3.refs_0_, bf16[256,320]{1,0:T(8,128)(2,1)S(1)} %get-tuple-element.42.refs_1_, bf16[256,320]{1,0:T(8,128)(2,1)S(1)} %collective-permute-done.3.refs_2_, bf16[256,320]{1,0:T(8,128)(2,1)S(1)} %collective-permute-done.4.refs_3_, ...), custom_call_target="tpu_custom_call" | custom-call | flops 838860800 | bytes 5242880 | tf_op jit(solution)/shard_map/project_and_norm/pallas_call | solution.py:115
  57.0 2.5 %collective-permute-start.11 = (bf16[64,5120]{1,0:T(8,128)(2,1)S(1)}, bf16[64,5120]{1,0:T(8,128)(2,1)S(1)}, u32[]{:S(2)}, u32[]{:S(2)}) collective-permute-start(bf16[64,5120]{1,0:T(8,128)(2,1)S(1)} %project_and_norm.1.refs_0_), channel_id=1, source_target_pairs={{0,6},{2,0},{4,2},{6,4},{1,7},{3,1},{5,3},{7,5},{8,14},{10,8},{12,... | collective-permute-start | bytes 1966088 | tf_op jit(solution)/shard_map/ppermute | solution.py:392
  60.7 8.2 %all-to-all-start = ((s32[32,1,32]{2,1,0:T(1,128)}), s32[32,1,32]{2,1,0:T(1,128)S(1)}, u32[]{:S(2)}, u32[]{:S(2)}) async-start(s32[32,1,32]{2,1,0:T(1,128)} %bitcast.10), calls=%async_computation | async-start | bytes 32768 | tf_op jit(solution)/shard_map/all_to_all | solution.py:460
  68.9 5.5 %collective-permute-done.10.refs_2_ = bf16[64,5120]{1,0:T(8,128)(2,1)S(1)} collective-permute-done((bf16[64,5120]{1,0:T(8,128)(2,1)S(1)}, bf16[64,5120]{1,0:T(8,128)(2,1)S(1)}, u32[]{:S(2)}, u32[]{:S(2)}) %collective-permute-start.10) | collective-permute-done | bytes 655392 | tf_op jit(solution)/shard_map/ppermute | solution.py:392
  74.5 2.7 %collective-permute-start.16 = (bf16[32,5120]{1,0:T(8,128)(2,1)S(1)}, bf16[32,5120]{1,0:T(8,128)(2,1)}, u32[]{:S(2)}, u32[]{:S(2)}) collective-permute-start(bf16[32,5120]{1,0:T(8,128)(2,1)S(1)} %slice.17), channel_id=1, source_target_pairs={{0,6},{2,0},{4,2},{6,4},{1,7},{3,1},{5,3},{7,5},{8,14},{10,8},{12,... | collective-permute-start | bytes 983048 | tf_op jit(solution)/shard_map/ppermute | solution.py:392
  78.2 1.4 collective-permute-start.9
  80.2 3.9 %collective-permute-done.14.refs_6_ = bf16[32,5120]{1,0:T(8,128)(2,1)S(1)} collective-permute-done((bf16[32,5120]{1,0:T(8,128)(2,1)S(1)}, bf16[32,5120]{1,0:T(8,128)(2,1)S(1)}, u32[]{:S(2)}, u32[]{:S(2)}) %collective-permute-start.14) | collective-permute-done | bytes 327712 | tf_op jit(solution)/shard_map/ppermute | solution.py:392
  84.1 1.7 collective-permute-start.15
  85.8 1.2 compare_convert_fusion.send
  87.7 4.8 %stack_rows.1.rows = bf16[512,5120]{1,0:T(8,128)(2,1)} custom-call(bf16[64,5120]{1,0:T(8,128)(2,1)S(1)} %project_and_norm.1.refs_0_, bf16[64,5120]{1,0:T(8,128)(2,1)} %collective-permute-done.9.refs_1_, bf16[64,5120]{1,0:T(8,128)(2,1)S(1)} %collective-permute-done.10.refs_2_, bf16[64,5120]{1,0:T(8,128)(2,1)} %collective-permute-done.12.refs_3_, ...), custom_call_target="tpu_custom_call" | custom-call | bytes 10485760 | tf_op jit(solution)/shard_map/stack_rows/pallas_call | solution.py:148
  92.5 11.9 %all-gather.2.cloned.1.call-done.weight = bf16[5120,1024]{1,0:T(8,128)(2,1)} async-done(((bf16[320,1024]{1,0:T(8,128)(2,1)}), bf16[5120,1024]{1,0:T(8,128)(2,1)}) %all-gather.2.cloned.1.call-update) | async-done | bytes 10485776 | tf_op jit(solution)/shard_map/all_gather | solution.py:439
  104.4 11.1 %merge_rows.1 = bf16[1024,1024]{1,0:T(8,128)(2,1)} custom-call(bf16[512,5120]{1,0:T(8,128)(2,1)} %stack_rows.1.rows, bf16[5120,1024]{1,0:T(8,128)(2,1)} %all-gather.2.cloned.1.call-done.weight, bf16[1024,512]{1,0:T(8,128)(2,1)} %compare_convert_fusion.send), custom_call_target="tpu_custom_call" | custom-call | flops 6442450944 | bytes 17825792 | tf_op jit(solution)/shard_map/merge_rows/pallas_call | solution.py:205
  115.5 7.7 %all-to-all-start.1 = ((bf16[32,32,1024]{2,1,0:T(8,128)(2,1)}), bf16[32,32,1024]{2,1,0:T(8,128)(2,1)S(1)}, u32[]{:S(2)}, u32[]{:S(2)}) async-start(bf16[32,32,1024]{2,1,0:T(8,128)(2,1)} %bitcast.24), calls=%async_computation.1 | async-start | bytes 4194304 | tf_op jit(solution)/shard_map/all_to_all | solution.py:482
  123.4 1.6 copy-done
  126.1 27.5 %all-to-all-done.1 = bf16[32,32,1024]{2,1,0:T(8,128)(2,1)S(1)} async-done(((bf16[32,32,1024]{2,1,0:T(8,128)(2,1)}), bf16[32,32,1024]{2,1,0:T(8,128)(2,1)S(1)}, u32[]{:S(2)}, u32[]{:S(2)}) %all-to-all-start.1) | async-done | bytes 2097184 | tf_op jit(solution)/shard_map/all_to_all | solution.py:482
  153.7 1.6 slot_squares.1.own
  155.3 2.3 %collective-permute-start.18 = (f32[4,128]{1,0:T(4,128)S(1)}, f32[4,128]{1,0:T(4,128)S(1)}, u32[]{:S(2)}, u32[]{:S(2)}) collective-permute-start(f32[4,128]{1,0:T(4,128)S(1)} %slot_squares.1.own), channel_id=1, source_target_pairs={{0,1},{1,0},{2,3},{3,2},{4,5},{5,4},{6,7},{7,6},{8,9},{9,8},{10,11... | collective-permute-start | bytes 6152 | tf_op jit(solution)/shard_map/ppermute | solution.py:388
  157.9 1.4 collective-permute-start.20
  159.3 1.9 %pick_rows.1.prompt = bf16[512,2048]{1,0:T(8,128)(2,1)S(1)} custom-call(bf16[16,2,32,1024]{3,2,1,0:T(8,128)(2,1)S(1)} %bitcast.19, bf16[512,512]{1,0:T(8,128)(2,1)S(1)} %fusion.1.pick, s32[512,1]{1,0:T(8,128)S(1)} %copy.14.usable, bf16[512,2048]{1,0:T(8,128)(2,1)S(1)} %copy-done.1), custom_call_target="tpu_custom_call" | custom-call | flops 1073741824 | bytes 6291456 | tf_op jit(solution)/shard_map/pick_rows/pallas_call | solution.py:336
  161.3 2.5 %finish.1 = bf16[512,2048]{1,0:T(8,128)(2,1)} custom-call(bf16[512,2048]{1,0:T(8,128)(2,1)S(1)} %pick_rows.1.prompt, f32[4,128]{1,0:T(4,128)S(1)} %slot_squares.1.own, f32[4,128]{1,0:T(4,128)S(1)} %collective-permute-done.18.core, f32[4,128]{1,0:T(4,128)S(1)} %collective-permute-done.19.far, f32[4,128]{1,0:T(4,128)S(1)} %collective-permute-done.20.both, ...), custom_call_target="tpu_custom_call" | custom-call | flops 3145728 | bytes 4194304 | tf_op jit(solution)/shard_map/finish/pallas_call | solution.py:370
  (80 shorter events, 11.5 us)
Async XLA Ops:
  6.5 97.8 %all-gather.2.cloned.1.call-start = ((), (), s32[]{:S(2)}) async-start(), calls=%async_computation.2 | async-start | bytes 11141120 | tf_op jit(solution)/shard_map/all_gather | solution.py:439
  6.5 13.8 %copy-start.8 = (s32[1,256]{1,0:T(1,128)S(1)}, s32[1,256]{1,0:T(1,128)}, u32[]{:S(2)}) copy-start(s32[1,256]{1,0:T(1,128)} %param.10) | copy-start | bytes 3076
  7.7 13.1 %copy-start.2 = (bf16[320,1280]{1,0:T(8,128)(2,1)S(1)}, bf16[320,1280]{1,0:T(8,128)(2,1)}, u32[]{:S(2)}) copy-start(bf16[320,1280]{1,0:T(8,128)(2,1)} %refs_5_) | copy-start | bytes 2457604
  7.7 11.0 %collective-permute-start = (bf16[160,1024]{1,0:T(8,128)(2,1)S(1)}, bf16[160,1024]{1,0:T(8,128)(2,1)S(1)}, u32[]{:S(2)}, u32[]{:S(2)}) collective-permute-start(bf16[160,1024]{1,0:T(8,128)(2,1)S(1)} %get-tuple-element.44), channel_id=1, source_target_pairs={{0,4},{4,0},{1,5},{5,1},{2,6},{6,2},{3,7},{7,3},{8,12},{12,8},{9,1... | collective-permute-start | bytes 983048 | tf_op jit(solution)/shard_map/ppermute | solution.py:418
  20.8 34.1 %collective-permute-start.6 = (bf16[320,1280]{1,0:T(8,128)(2,1)S(1)}, bf16[320,1280]{1,0:T(8,128)(2,1)S(1)}, u32[]{:S(2)}, u32[]{:S(2)}) collective-permute-start(bf16[320,1280]{1,0:T(8,128)(2,1)S(1)} %copy-done.2), channel_id=1, source_target_pairs={{0,1},{1,0},{2,3},{3,2},{4,5},{5,4},{6,7},{7,6},{8,9},{9,8},{10,11... | collective-permute-start | bytes 2457608 | tf_op jit(solution)/shard_map/ppermute | solution.py:396
  22.4 20.5 %collective-permute-start.1 = (bf16[160,1280]{1,0:T(8,128)(2,1)S(1)}, bf16[160,1280]{1,0:T(8,128)(2,1)S(1)}, u32[]{:S(2)}, u32[]{:S(2)}) collective-permute-start(bf16[160,1280]{1,0:T(8,128)(2,1)S(1)} %get-tuple-element.38), channel_id=1, source_target_pairs={{0,2},{2,4},{4,6},{6,0},{1,3},{3,5},{5,7},{7,1},{8,10},{10,12},{12... | collective-permute-start | bytes 1228808 | tf_op jit(solution)/shard_map/ppermute | solution.py:392
  23.8 19.1 %collective-permute-start.2 = (bf16[160,1280]{1,0:T(8,128)(2,1)S(1)}, bf16[160,1280]{1,0:T(8,128)(2,1)S(1)}, u32[]{:S(2)}, u32[]{:S(2)}) collective-permute-start(bf16[160,1280]{1,0:T(8,128)(2,1)S(1)} %get-tuple-element.37), channel_id=1, source_target_pairs={{0,6},{2,0},{4,2},{6,4},{1,7},{3,1},{5,3},{7,5},{8,14},{10,8},{12,... | collective-permute-start | bytes 1228808 | tf_op jit(solution)/shard_map/ppermute | solution.py:392
  25.4 1.7 %copy-start.3 = (bf16[1024,1280]{1,0:T(8,128)(2,1)S(1)}, bf16[1024,1280]{1,0:T(8,128)(2,1)}, u32[]{:S(2)}) copy-start(bf16[1024,1280]{1,0:T(8,128)(2,1)} %refs_11_) | copy-start | bytes 7864324
  27.1 1.7 copy-start.6
  28.8 17.2 %copy-start.7 = (f32[1280]{0:T(1024)S(1)}, f32[1280]{0:T(1024)}, u32[]{:S(2)}) copy-start(f32[1280]{0:T(1024)} %param.13) | copy-start | bytes 15364
  28.8 26.1 %copy-start.4 = (bf16[1024,1280]{1,0:T(8,128)(2,1)S(1)}, bf16[1024,1280]{1,0:T(8,128)(2,1)}, u32[]{:S(2)}) copy-start(bf16[1024,1280]{1,0:T(8,128)(2,1)} %refs_11_) | copy-start | bytes 7864324
  43.0 12.0 %collective-permute-start.7 = (bf16[160,1280]{1,0:T(8,128)(2,1)S(1)}, bf16[160,1280]{1,0:T(8,128)(2,1)S(1)}, u32[]{:S(2)}, u32[]{:S(2)}) collective-permute-start(bf16[160,1280]{1,0:T(8,128)(2,1)S(1)} %collective-permute-done.1.refs_7_), channel_id=1, source_target_pairs={{0,1},{1,0},{2,3},{3,2},{4,5},{5,4},{6,7},{7,6},{8,9},{9,8},{10,11... | collective-permute-start | bytes 1228808 | tf_op jit(solution)/shard_map/ppermute | solution.py:396
  43.4 11.5 %collective-permute-start.8 = (bf16[160,1280]{1,0:T(8,128)(2,1)S(1)}, bf16[160,1280]{1,0:T(8,128)(2,1)S(1)}, u32[]{:S(2)}, u32[]{:S(2)}) collective-permute-start(bf16[160,1280]{1,0:T(8,128)(2,1)S(1)} %collective-permute-done.2.refs_8_), channel_id=1, source_target_pairs={{0,1},{1,0},{2,3},{3,2},{4,5},{5,4},{6,7},{7,6},{8,9},{9,8},{10,11... | collective-permute-start | bytes 1228808 | tf_op jit(solution)/shard_map/ppermute | solution.py:396
  43.6 2.0 %collective-permute-start.3 = (bf16[256,320]{1,0:T(8,128)(2,1)S(1)}, bf16[256,320]{1,0:T(8,128)(2,1)S(1)}, u32[]{:S(2)}, u32[]{:S(2)}) collective-permute-start(bf16[256,320]{1,0:T(8,128)(2,1)S(1)} %get-tuple-element.41), channel_id=1, source_target_pairs={{0,1},{1,0},{2,3},{3,2},{4,5},{5,4},{6,7},{7,6},{8,9},{9,8},{10,11... | collective-permute-start | bytes 491528 | tf_op jit(solution)/shard_map/ppermute | solution.py:388
  44.1 6.5 %collective-permute-start.4 = (bf16[256,320]{1,0:T(8,128)(2,1)S(1)}, bf16[256,320]{1,0:T(8,128)(2,1)S(1)}, u32[]{:S(2)}, u32[]{:S(2)}) collective-permute-start(bf16[256,320]{1,0:T(8,128)(2,1)S(1)} %get-tuple-element.40), channel_id=1, source_target_pairs={{0,2},{1,3},{2,0},{3,1},{4,6},{5,7},{6,4},{7,5},{8,10},{9,11},{10,... | collective-permute-start | bytes 491528 | tf_op jit(solution)/shard_map/ppermute | solution.py:388
  45.7 9.3 %collective-permute-start.5 = (bf16[256,320]{1,0:T(8,128)(2,1)S(1)}, bf16[256,320]{1,0:T(8,128)(2,1)S(1)}, u32[]{:S(2)}, u32[]{:S(2)}) collective-permute-start(bf16[256,320]{1,0:T(8,128)(2,1)S(1)} %get-tuple-element.39), channel_id=1, source_target_pairs={{0,3},{1,2},{2,1},{3,0},{4,7},{5,6},{6,5},{7,4},{8,11},{9,10},{10,... | collective-permute-start | bytes 491528 | tf_op jit(solution)/shard_map/ppermute | solution.py:388
  56.8 17.6 %collective-permute-start.10 = (bf16[64,5120]{1,0:T(8,128)(2,1)S(1)}, bf16[64,5120]{1,0:T(8,128)(2,1)S(1)}, u32[]{:S(2)}, u32[]{:S(2)}) collective-permute-start(bf16[64,5120]{1,0:T(8,128)(2,1)S(1)} %project_and_norm.1.refs_0_), channel_id=1, source_target_pairs={{0,2},{2,4},{4,6},{6,0},{1,3},{3,5},{5,7},{7,1},{8,10},{10,12},{12... | collective-permute-start | bytes 1966088 | tf_op jit(solution)/shard_map/ppermute | solution.py:392
  57.0 17.5 %collective-permute-start.11 = (bf16[64,5120]{1,0:T(8,128)(2,1)S(1)}, bf16[64,5120]{1,0:T(8,128)(2,1)S(1)}, u32[]{:S(2)}, u32[]{:S(2)}) collective-permute-start(bf16[64,5120]{1,0:T(8,128)(2,1)S(1)} %project_and_norm.1.refs_0_), channel_id=1, source_target_pairs={{0,6},{2,0},{4,2},{6,4},{1,7},{3,1},{5,3},{7,5},{8,14},{10,8},{12,... | collective-permute-start | bytes 1966088 | tf_op jit(solution)/shard_map/ppermute | solution.py:392
  60.7 19.0 %all-to-all-start = ((s32[32,1,32]{2,1,0:T(1,128)}), s32[32,1,32]{2,1,0:T(1,128)S(1)}, u32[]{:S(2)}, u32[]{:S(2)}) async-start(s32[32,1,32]{2,1,0:T(1,128)} %bitcast.10), calls=%async_computation | async-start | bytes 32768 | tf_op jit(solution)/shard_map/all_to_all | solution.py:460
  74.4 9.7 %collective-permute-start.14 = (bf16[32,5120]{1,0:T(8,128)(2,1)S(1)}, bf16[32,5120]{1,0:T(8,128)(2,1)S(1)}, u32[]{:S(2)}, u32[]{:S(2)}) collective-permute-start(bf16[32,5120]{1,0:T(8,128)(2,1)S(1)} %slice.16), channel_id=1, source_target_pairs={{0,2},{2,4},{4,6},{6,0},{1,3},{3,5},{5,7},{7,1},{8,10},{10,12},{12... | collective-permute-start | bytes 983048 | tf_op jit(solution)/shard_map/ppermute | solution.py:392
  74.5 11.3 %collective-permute-start.16 = (bf16[32,5120]{1,0:T(8,128)(2,1)S(1)}, bf16[32,5120]{1,0:T(8,128)(2,1)}, u32[]{:S(2)}, u32[]{:S(2)}) collective-permute-start(bf16[32,5120]{1,0:T(8,128)(2,1)S(1)} %slice.17), channel_id=1, source_target_pairs={{0,6},{2,0},{4,2},{6,4},{1,7},{3,1},{5,3},{7,5},{8,14},{10,8},{12,... | collective-permute-start | bytes 983048 | tf_op jit(solution)/shard_map/ppermute | solution.py:392
  78.2 8.8 %collective-permute-start.9 = (bf16[64,5120]{1,0:T(8,128)(2,1)S(1)}, bf16[64,5120]{1,0:T(8,128)(2,1)}, u32[]{:S(2)}, u32[]{:S(2)}) collective-permute-start(bf16[64,5120]{1,0:T(8,128)(2,1)S(1)} %project_and_norm.1.refs_0_), channel_id=1, source_target_pairs={{0,1},{1,0},{2,3},{3,2},{4,5},{5,4},{6,7},{7,6},{8,9},{9,8},{10,11... | collective-permute-start | bytes 1966088 | tf_op jit(solution)/shard_map/ppermute | solution.py:396
  79.6 7.4 %collective-permute-start.12 = (bf16[64,5120]{1,0:T(8,128)(2,1)S(1)}, bf16[64,5120]{1,0:T(8,128)(2,1)}, u32[]{:S(2)}, u32[]{:S(2)}) collective-permute-start(bf16[64,5120]{1,0:T(8,128)(2,1)S(1)} %collective-permute-done.10.refs_2_), channel_id=1, source_target_pairs={{0,1},{1,0},{2,3},{3,2},{4,5},{5,4},{6,7},{7,6},{8,9},{9,8},{10,11... | collective-permute-start | bytes 1966088 | tf_op jit(solution)/shard_map/ppermute | solution.py:396
  79.7 7.3 %collective-permute-start.13 = (bf16[64,5120]{1,0:T(8,128)(2,1)S(1)}, bf16[64,5120]{1,0:T(8,128)(2,1)}, u32[]{:S(2)}, u32[]{:S(2)}) collective-permute-start(bf16[64,5120]{1,0:T(8,128)(2,1)S(1)} %collective-permute-done.11.refs_4_), channel_id=1, source_target_pairs={{0,1},{1,0},{2,3},{3,2},{4,5},{5,4},{6,7},{7,6},{8,9},{9,8},{10,11... | collective-permute-start | bytes 1966088 | tf_op jit(solution)/shard_map/ppermute | solution.py:396
  84.1 3.3 %collective-permute-start.15 = (bf16[32,5120]{1,0:T(8,128)(2,1)S(1)}, bf16[32,5120]{1,0:T(8,128)(2,1)S(1)}, u32[]{:S(2)}, u32[]{:S(2)}) collective-permute-start(bf16[32,5120]{1,0:T(8,128)(2,1)S(1)} %collective-permute-done.14.refs_6_), channel_id=1, source_target_pairs={{0,1},{1,0},{2,3},{3,2},{4,5},{5,4},{6,7},{7,6},{8,9},{9,8},{10,11... | collective-permute-start | bytes 983048 | tf_op jit(solution)/shard_map/ppermute | solution.py:396
  85.8 1.9 %collective-permute-start.17 = (bf16[32,5120]{1,0:T(8,128)(2,1)}, bf16[32,5120]{1,0:T(8,128)(2,1)S(1)}, u32[]{:S(2)}, u32[]{:S(2)}) collective-permute-start(bf16[32,5120]{1,0:T(8,128)(2,1)} %collective-permute-done.16.refs_8_), channel_id=1, source_target_pairs={{0,1},{1,0},{2,3},{3,2},{4,5},{5,4},{6,7},{7,6},{8,9},{9,8},{10,11... | collective-permute-start | bytes 983048 | tf_op jit(solution)/shard_map/ppermute | solution.py:396
  115.5 38.2 %all-to-all-start.1 = ((bf16[32,32,1024]{2,1,0:T(8,128)(2,1)}), bf16[32,32,1024]{2,1,0:T(8,128)(2,1)S(1)}, u32[]{:S(2)}, u32[]{:S(2)}) async-start(bf16[32,32,1024]{2,1,0:T(8,128)(2,1)} %bitcast.24), calls=%async_computation.1 | async-start | bytes 4194304 | tf_op jit(solution)/shard_map/all_to_all | solution.py:482
  153.7 5.7 %copy-start.1 = (bf16[512,2048]{1,0:T(8,128)(2,1)S(1)}, bf16[512,2048]{1,0:T(8,128)(2,1)}, u32[]{:S(2)}) copy-start(bf16[512,2048]{1,0:T(8,128)(2,1)} %text.3) | copy-start | bytes 6291460
  155.3 6.0 %copy-start.5 = (f32[2048]{0:T(1024)S(1)}, f32[2048]{0:T(1024)}, u32[]{:S(2)}) copy-start(f32[2048]{0:T(1024)} %param.17) | copy-start | bytes 24580
  155.3 6.0 %collective-permute-start.18 = (f32[4,128]{1,0:T(4,128)S(1)}, f32[4,128]{1,0:T(4,128)S(1)}, u32[]{:S(2)}, u32[]{:S(2)}) collective-permute-start(f32[4,128]{1,0:T(4,128)S(1)} %slot_squares.1.own), channel_id=1, source_target_pairs={{0,1},{1,0},{2,3},{3,2},{4,5},{5,4},{6,7},{7,6},{8,9},{9,8},{10,11... | collective-permute-start | bytes 6152 | tf_op jit(solution)/shard_map/ppermute | solution.py:388
  157.6 3.7 %collective-permute-start.19 = (f32[4,128]{1,0:T(4,128)S(1)}, f32[4,128]{1,0:T(4,128)S(1)}, u32[]{:S(2)}, u32[]{:S(2)}) collective-permute-start(f32[4,128]{1,0:T(4,128)S(1)} %slot_squares.1.own), channel_id=1, source_target_pairs={{0,2},{1,3},{2,0},{3,1},{4,6},{5,7},{6,4},{7,5},{8,10},{9,11},{10,... | collective-permute-start | bytes 6152 | tf_op jit(solution)/shard_map/ppermute | solution.py:388
  157.9 3.4 %collective-permute-start.20 = (f32[4,128]{1,0:T(4,128)S(1)}, f32[4,128]{1,0:T(4,128)S(1)}, u32[]{:S(2)}, u32[]{:S(2)}) collective-permute-start(f32[4,128]{1,0:T(4,128)S(1)} %slot_squares.1.own), channel_id=1, source_target_pairs={{0,3},{1,2},{2,1},{3,0},{4,7},{5,6},{6,5},{7,4},{8,11},{9,10},{10,... | collective-permute-start | bytes 6152 | tf_op jit(solution)/shard_map/ppermute | solution.py:388
  (1 other events, 1.6 us)
Sparse Core Ops, SparseCore 0:
  20.4 83.9 all-gather.1

commit v14 on v13

--- a/solution.py
+++ b/solution.py
@@ -413,7 +413,6 @@
     core = lax.axis_index("c")
 
     half = merge_weight.shape[1] // 2
-    own = lax.dynamic_slice_in_dim(merge_weight, yh * half, half, 1)
     other = lax.dynamic_slice_in_dim(merge_weight, (1 - yh) * half, half, 1)
     arrived = lax.ppermute(other, "yh", [(0, 1), (1, 0)])
 
@@ -428,12 +427,12 @@
     pick = (slot[:, None] == jnp.arange(512)[None, :]).astype(BF)
     names = jnp.where(usable, image_refs % 256 + 1, 0).astype(BF)
     table = jnp.dot(names[None, :], pick, preferred_element_type=F32).astype(jnp.int32)
-    table = jnp.broadcast_to(table.reshape(16, 1, 32), (16, 2, 32)).reshape(32, 32)
     usable = usable.astype(jnp.int32)[:, None]
 
-    arrived, table, pick, usable, out_weight = lax.optimization_barrier(
-        (arrived, table, pick, usable, out_weight)
+    arrived, table, pick, usable, out_weight, merge_weight = lax.optimization_barrier(
+        (arrived, table, pick, usable, out_weight, merge_weight)
     )
+    own = lax.dynamic_slice_in_dim(merge_weight, yh * half, half, 1)
     is_own = (jnp.arange(2) == yh)[:, None, None]
     both = jnp.where(is_own, own[None], arrived[None]).reshape(-1, half)
     weight = lax.all_gather(both, ("z", "x"), axis=0, tiled=True)
@@ -454,6 +453,7 @@
     merged = project_and_norm(tp, parts, out_blocks, patches, merge_gain)
 
     table, merged = lax.optimization_barrier((table, merged))
+    table = jnp.broadcast_to(table.reshape(16, 1, 32), (16, 2, 32)).reshape(32, 32)
     after, before = shift_y(merged, 1), shift_y(merged, -1)
     count = merged.shape[0] // 2
     far = [shift_y(after[:count], 1), shift_y(before[count:], -1)]
@@ -478,10 +478,12 @@
     wanted = jnp.where(wanted >= 0, wanted + jnp.arange(2)[None, :, None] * 256, -1).reshape(-1)
     send = (wanted[:, None] == row_ids[None, :]).astype(BF)
 
+    from_text = text_squares(text_rows, usable)
+    from_text, send = lax.optimization_barrier((from_text, send))
     outgoing = merge_and_select(stack_rows(blocks), weight, send)
     received = lax.all_to_all(outgoing, SEC, split_axis=0, concat_axis=0, tiled=True)
     received = received.reshape(16, 2, 32, half)
-    squares = slot_squares(received, pick, text_squares(text_rows, usable))
+    squares = slot_squares(received, pick, from_text)
     squares = [squares] + [swap_tp(squares, k) for k in (1, 2, 3)]
     return finish(pick_rows(received, pick, usable, text_rows), squares, llm_gain)
 

time: 171 us -> 170 us (level)
  blocking collectives: 0 us -> 37.1 us
  waiting for transfers between devices: 64.6 us -> 28.1 us
  starting transfers between devices: 39 us -> 32.1 us
  local copies, waits for them, and re-layouts: 8.81 us -> 11.2 us
    all_to_all x0 -> x1, blocking collectives: none -> 37.1 us  [on_device(): lax.all_to_all(outgoing, SEC, split_axis=0, concat_axis=0, tiled=True)]
    all_to_all x1 -> x0, waiting for transfers between devices: 27.5 us -> none  [on_device(): lax.all_to_all(outgoing, SEC, split_axis=0, concat_axis=0, tiled=True)]
    all_to_all x1 -> x0, starting transfers between devices: 7.72 us -> none  [on_device(): lax.all_to_all(outgoing, SEC, split_axis=0, concat_axis=0, tiled=True)]
    ppermute x6, waiting for transfers between devices: 9.44 us -> 4.9 us  [shift_y(): lax.ppermute(block, ('yh', 'yl'), [(i, (i + d) % 4) for i in range(4)])]
    all_gather x1, waiting for transfers between devices: 11.9 us -> 7.87 us  [on_device(): weight = lax.all_gather(both, ('z', 'x'), axis=0, tiled=True)]
    slice x2, local copies, waits for them, and re-layouts: 0.05 us -> 3.47 us  [on_device(): far = [shift_y(after[:count], 1), shift_y(before[count:], -1)]]
    unnamed x18 -> x20, local copies, waits for them, and re-layouts: 5.05 us -> 4.56 us
  transfers between devices with their start and end apart: 24 -> 23, of which waited for: 10 -> 7; matrix products, arithmetic and copies ran while one was open for 4% -> 7% of each run, Pallas kernels for 14% -> 15%
where the time goes in v14:
time: 170 us; the launch traced here: 169 us
  Pallas kernels  40.3 us (24%)
  blocking collectives  37.1 us (22%)
  starting transfers between devices  32.1 us (19%)
  waiting for transfers between devices  28.1 us (17%)
  between operations  13.7 us (8%)
  local copies, waits for them, and re-layouts  11.2 us (7%)
  other arithmetic  5.72 us (3%)
    all_to_all x1, blocking collectives, on_device(): lax.all_to_all(outgoing, SEC, split_axis=0, concat_axis=0, tiled=True)  37.1 us
    pallas_call x1, Pallas kernels, vision_context(): pl.pallas_call(attention_kernel, out_shape=jax.ShapeDtypeStruct((row_coun...  14.1 us
    pallas_call x1, Pallas kernels, merge_and_select(): pl.pallas_call(merge_kernel, out_shape=pltpu.HBM((slots, columns), BF), i...  11.1 us
    ppermute x6, waiting for transfers between devices, swap_tp(): return lax.ppermute(block, TP, [(i, i ^ k) for i in range(4)])  10.3 us
    ppermute x6, starting transfers between devices, shift_y(): lax.ppermute(block, ('yh', 'yl'), [(i, (i + d) % 4) for i in range(4)])  8.32 us
    all_to_all x1, starting transfers between devices, on_device(): table = lax.all_to_all(table, SEC, split_axis=0, concat_axis=0, tiled=True)  8.27 us
    all_gather x1, waiting for transfers between devices, on_device(): weight = lax.all_gather(both, ('z', 'x'), axis=0, tiled=True)  7.87 us
    ppermute x8, starting transfers between devices, swap_core(): return lax.ppermute(block, 'c', [(0, 1), (1, 0)])  6.73 us
  transfers between devices with their start and end apart: 23, of which 7 were waited for; matrix products, arithmetic and copies ran while one was open for 7% of the time, Pallas kernels for 15%

profile of v14, /device:TPU:1, one launch (start us, length us, event | category | flops | bytes accessed | tf_op | source)
XLA Modules:
  0.0 168.9 jit_solution(7215537898345533139)
XLA Ops:
  7.7 3.8 %collective-permute-start = (bf16[160,1024]{1,0:T(8,128)(2,1)S(1)}, bf16[160,1024]{1,0:T(8,128)(2,1)S(1)}, u32[]{:S(2)}, u32[]{:S(2)}) collective-permute-start(bf16[160,1024]{1,0:T(8,128)(2,1)S(1)} %constant_dynamic-slice_fusion.5), channel_id=1, source_target_pairs={{0,4},{4,0},{1,5},{5,1},{2,6},{6,2},{3,7},{7,3},{8,12},{12,8},{9,1... | collective-permute-start | bytes 983048 | tf_op jit(solution)/shard_map/ppermute | solution.py:417
  13.9 4.8 %collective-permute-done = bf16[160,1024]{1,0:T(8,128)(2,1)S(1)} collective-permute-done((bf16[160,1024]{1,0:T(8,128)(2,1)S(1)}, bf16[160,1024]{1,0:T(8,128)(2,1)S(1)}, u32[]{:S(2)}, u32[]{:S(2)}) %collective-permute-start) | collective-permute-done | bytes 327712 | tf_op jit(solution)/shard_map/ppermute | solution.py:417
  20.2 1.6 collective-permute-start.6
  21.8 1.4 collective-permute-start.1
  23.3 1.5 collective-permute-start.2
  24.8 1.7 %copy-done.4 = bf16[1024,1280]{1,0:T(8,128)(2,1)S(1)} copy-done((bf16[1024,1280]{1,0:T(8,128)(2,1)S(1)}, bf16[1024,1280]{1,0:T(8,128)(2,1)}, u32[]{:S(2)}) %copy-start.4) | copy-done | bytes 2621464
  26.6 1.7 %copy-done.7 = bf16[3,1280,320]{1,2,0:T(8,128)(2,1)S(1)} copy-done((bf16[3,1280,320]{1,2,0:T(8,128)(2,1)S(1)}, bf16[3,1280,320]{1,2,0:T(8,128)(2,1)}, u32[]{:S(2)}) %copy-start.7) | copy-done | bytes 2457624
  28.2 14.1 %vision_attention.1 = bf16[1024,320]{1,0:T(8,128)(2,1)S(1)} custom-call(s32[1024,1]{1,0:T(8,128)S(1)} %copy.13.row_ids, s32[1,1024]{1,0:T(1,128)S(1)} %bitcast.21, bf16[1024,1280]{1,0:T(8,128)(2,1)S(1)} %copy-done.4, bf16[3,320,1280]{2,1,0:T(8,128)(2,1)S(1)} %bitcast.23), custom_call_target="tpu_custom_call" | custom-call | flops 6811549696 | bytes 5079040 | tf_op jit(solution)/shard_map/vision_attention/pallas_call | solution.py:70
  43.6 1.4 collective-permute-done.3.refs_2_
  45.5 4.5 %collective-permute-done.4.refs_3_ = bf16[256,320]{1,0:T(8,128)(2,1)S(1)} collective-permute-done((bf16[256,320]{1,0:T(8,128)(2,1)S(1)}, bf16[256,320]{1,0:T(8,128)(2,1)S(1)}, u32[]{:S(2)}, u32[]{:S(2)}) %collective-permute-start.4) | collective-permute-done | bytes 163872 | tf_op jit(solution)/shard_map/ppermute | solution.py:388
  49.9 4.4 %collective-permute-done.5.refs_4_ = bf16[256,320]{1,0:T(8,128)(2,1)S(1)} collective-permute-done((bf16[256,320]{1,0:T(8,128)(2,1)S(1)}, bf16[256,320]{1,0:T(8,128)(2,1)S(1)}, u32[]{:S(2)}, u32[]{:S(2)}) %collective-permute-start.5) | collective-permute-done | bytes 163872 | tf_op jit(solution)/shard_map/ppermute | solution.py:388
  54.4 2.7 %project_and_norm.1.refs_0_ = bf16[64,5120]{1,0:T(8,128)(2,1)} custom-call(s32[1]{0:T(128)} %bitcast.3.refs_0_, bf16[256,320]{1,0:T(8,128)(2,1)S(1)} %get-tuple-element.48.refs_1_, bf16[256,320]{1,0:T(8,128)(2,1)S(1)} %collective-permute-done.3.refs_2_, bf16[256,320]{1,0:T(8,128)(2,1)S(1)} %collective-permute-done.4.refs_3_, ...), custom_call_target="tpu_custom_call" | custom-call | flops 838860800 | bytes 5242880 | tf_op jit(solution)/shard_map/project_and_norm/pallas_call | solution.py:115
  57.2 2.5 %collective-permute-start.11 = (bf16[64,5120]{1,0:T(8,128)(2,1)}, bf16[64,5120]{1,0:T(8,128)(2,1)}, u32[]{:S(2)}, u32[]{:S(2)}) collective-permute-start(bf16[64,5120]{1,0:T(8,128)(2,1)} %project_and_norm.1.refs_0_), channel_id=1, source_target_pairs={{0,6},{2,0},{4,2},{6,4},{1,7},{3,1},{5,3},{7,5},{8,14},{10,8},{12,... | collective-permute-start | bytes 1966088 | tf_op jit(solution)/shard_map/ppermute | solution.py:392
  61.6 8.3 %all-to-all-start = ((s32[32,1,32]{2,1,0:T(1,128)}), s32[32,1,32]{2,1,0:T(1,128)}, u32[]{:S(2)}, u32[]{:S(2)}) async-start(s32[32,1,32]{2,1,0:T(1,128)} %bitcast.10), calls=%async_computation | async-start | bytes 32768 | tf_op jit(solution)/shard_map/all_to_all | solution.py:460
  69.9 4.9 %collective-permute-done.10.refs_2_ = bf16[64,5120]{1,0:T(8,128)(2,1)} collective-permute-done((bf16[64,5120]{1,0:T(8,128)(2,1)}, bf16[64,5120]{1,0:T(8,128)(2,1)}, u32[]{:S(2)}, u32[]{:S(2)}) %collective-permute-start.10) | collective-permute-done | bytes 655392 | tf_op jit(solution)/shard_map/ppermute | solution.py:392
  74.8 1.7 %slice.16 = bf16[32,5120]{1,0:T(8,128)(2,1)} slice(bf16[64,5120]{1,0:T(8,128)(2,1)} %collective-permute-done.10.refs_2_), slice={[0:32], [0:5120]} | slice | bytes 655360 | tf_op jit(solution)/shard_map/slice | solution.py:459
  76.5 1.7 %slice.17 = bf16[32,5120]{1,0:T(8,128)(2,1)} slice(bf16[64,5120]{1,0:T(8,128)(2,1)} %collective-permute-done.11.refs_4_), slice={[32:64], [0:5120]} | slice | bytes 655360 | tf_op jit(solution)/shard_map/slice | solution.py:459
  78.2 2.7 %collective-permute-start.16 = (bf16[32,5120]{1,0:T(8,128)(2,1)}, bf16[32,5120]{1,0:T(8,128)(2,1)}, u32[]{:S(2)}, u32[]{:S(2)}) collective-permute-start(bf16[32,5120]{1,0:T(8,128)(2,1)} %slice.17), channel_id=1, source_target_pairs={{0,6},{2,0},{4,2},{6,4},{1,7},{3,1},{5,3},{7,5},{8,14},{10,8},{12,... | collective-permute-start | bytes 983048 | tf_op jit(solution)/shard_map/ppermute | solution.py:392
  81.3 1.1 text_squares.1.base
  82.5 1.6 collective-permute-start.9
  84.6 1.3 broadcast_add_fusion
  86.7 1.4 collective-permute-start.15
  89.2 1.2 compare_convert_fusion.send
  90.6 5.3 %stack_rows.1.rows = bf16[512,5120]{1,0:T(8,128)(2,1)} custom-call(bf16[64,5120]{1,0:T(8,128)(2,1)} %project_and_norm.1.refs_0_, bf16[64,5120]{1,0:T(8,128)(2,1)} %collective-permute-done.9.refs_1_, bf16[64,5120]{1,0:T(8,128)(2,1)} %collective-permute-done.10.refs_2_, bf16[64,5120]{1,0:T(8,128)(2,1)} %collective-permute-done.12.refs_3_, ...), custom_call_target="tpu_custom_call" | custom-call | bytes 10485760 | tf_op jit(solution)/shard_map/stack_rows/pallas_call | solution.py:148
  95.9 7.9 %all-gather.2.cloned.1.call-done.weight = bf16[5120,1024]{1,0:T(8,128)(2,1)} async-done(((bf16[320,1024]{1,0:T(8,128)(2,1)}), bf16[5120,1024]{1,0:T(8,128)(2,1)}) %all-gather.2.cloned.1.call-update) | async-done | bytes 10485776 | tf_op jit(solution)/shard_map/all_gather | solution.py:438
  103.8 11.1 %merge_rows.1 = bf16[1024,1024]{1,0:T(8,128)(2,1)} custom-call(bf16[512,5120]{1,0:T(8,128)(2,1)} %stack_rows.1.rows, bf16[5120,1024]{1,0:T(8,128)(2,1)} %all-gather.2.cloned.1.call-done.weight, bf16[1024,512]{1,0:T(8,128)(2,1)} %compare_convert_fusion.send), custom_call_target="tpu_custom_call" | custom-call | flops 6442450944 | bytes 17825792 | tf_op jit(solution)/shard_map/merge_rows/pallas_call | solution.py:205
  115.0 37.1 %all_to_all.21 = bf16[32,32,1024]{2,1,0:T(8,128)(2,1)S(1)} all-to-all(bf16[32,32,1024]{2,1,0:T(8,128)(2,1)} %bitcast.24), channel_id=1, replica_groups=mesh['z'=4,'x'=4,'yh'=2,'yl'=2,'c'=2] {'z','x','yh'}, dimensions={0} | all-to-all | bytes 4194304 | tf_op jit(solution)/shard_map/all_to_all | solution.py:484
  152.0 1.6 slot_squares.1.own
  153.7 2.2 %collective-permute-start.18 = (f32[4,128]{1,0:T(4,128)S(1)}, f32[4,128]{1,0:T(4,128)S(1)}, u32[]{:S(2)}, u32[]{:S(2)}) collective-permute-start(f32[4,128]{1,0:T(4,128)S(1)} %slot_squares.1.own), channel_id=1, source_target_pairs={{0,1},{1,0},{2,3},{3,2},{4,5},{5,4},{6,7},{7,6},{8,9},{9,8},{10,11... | collective-permute-start | bytes 6152 | tf_op jit(solution)/shard_map/ppermute | solution.py:388
  156.2 1.4 collective-permute-start.20
  157.6 1.9 %pick_rows.1.prompt = bf16[512,2048]{1,0:T(8,128)(2,1)S(1)} custom-call(bf16[16,2,32,1024]{3,2,1,0:T(8,128)(2,1)S(1)} %bitcast.19, bf16[512,512]{1,0:T(8,128)(2,1)S(1)} %fusion.1.pick, s32[512,1]{1,0:T(8,128)S(1)} %copy.14.usable, bf16[512,2048]{1,0:T(8,128)(2,1)S(1)} %copy-done.1), custom_call_target="tpu_custom_call" | custom-call | flops 1073741824 | bytes 6291456 | tf_op jit(solution)/shard_map/pick_rows/pallas_call | solution.py:336
  159.6 2.5 %finish.1 = bf16[512,2048]{1,0:T(8,128)(2,1)} custom-call(bf16[512,2048]{1,0:T(8,128)(2,1)S(1)} %pick_rows.1.prompt, f32[4,128]{1,0:T(4,128)S(1)} %slot_squares.1.own, f32[4,128]{1,0:T(4,128)S(1)} %collective-permute-done.18.core, f32[4,128]{1,0:T(4,128)S(1)} %collective-permute-done.19.far, f32[4,128]{1,0:T(4,128)S(1)} %collective-permute-done.20.both, ...), custom_call_target="tpu_custom_call" | custom-call | flops 3145728 | bytes 4194304 | tf_op jit(solution)/shard_map/finish/pallas_call | solution.py:370
  (84 shorter events, 12.0 us)
Async XLA Ops:
  6.5 97.3 %all-gather.2.cloned.1.call-start = ((), (), s32[]{:S(2)}) async-start(), calls=%async_computation.2 | async-start | bytes 11141120 | tf_op jit(solution)/shard_map/all_gather | solution.py:438
  7.7 12.1 %copy-start.9 = (s32[1,256]{1,0:T(1,128)S(1)}, s32[1,256]{1,0:T(1,128)}, u32[]{:S(2)}) copy-start(s32[1,256]{1,0:T(1,128)} %param.10) | copy-start | bytes 3076
  7.7 11.0 %collective-permute-start = (bf16[160,1024]{1,0:T(8,128)(2,1)S(1)}, bf16[160,1024]{1,0:T(8,128)(2,1)S(1)}, u32[]{:S(2)}, u32[]{:S(2)}) collective-permute-start(bf16[160,1024]{1,0:T(8,128)(2,1)S(1)} %constant_dynamic-slice_fusion.5), channel_id=1, source_target_pairs={{0,4},{4,0},{1,5},{5,1},{2,6},{6,2},{3,7},{7,3},{8,12},{12,8},{9,1... | collective-permute-start | bytes 983048 | tf_op jit(solution)/shard_map/ppermute | solution.py:417
  13.2 7.0 %copy-start.2 = (bf16[320,1280]{1,0:T(8,128)(2,1)S(1)}, bf16[320,1280]{1,0:T(8,128)(2,1)}, u32[]{:S(2)}) copy-start(bf16[320,1280]{1,0:T(8,128)(2,1)} %refs_5_) | copy-start | bytes 2457604
  20.2 34.1 %collective-permute-start.6 = (bf16[320,1280]{1,0:T(8,128)(2,1)S(1)}, bf16[320,1280]{1,0:T(8,128)(2,1)S(1)}, u32[]{:S(2)}, u32[]{:S(2)}) collective-permute-start(bf16[320,1280]{1,0:T(8,128)(2,1)S(1)} %copy-done.2), channel_id=1, source_target_pairs={{0,1},{1,0},{2,3},{3,2},{4,5},{5,4},{6,7},{7,6},{8,9},{9,8},{10,11... | collective-permute-start | bytes 2457608 | tf_op jit(solution)/shard_map/ppermute | solution.py:396
  21.8 20.5 %collective-permute-start.1 = (bf16[160,1280]{1,0:T(8,128)(2,1)S(1)}, bf16[160,1280]{1,0:T(8,128)(2,1)S(1)}, u32[]{:S(2)}, u32[]{:S(2)}) collective-permute-start(bf16[160,1280]{1,0:T(8,128)(2,1)S(1)} %get-tuple-element.44), channel_id=1, source_target_pairs={{0,2},{2,4},{4,6},{6,0},{1,3},{3,5},{5,7},{7,1},{8,10},{10,12},{12... | collective-permute-start | bytes 1228808 | tf_op jit(solution)/shard_map/ppermute | solution.py:392
  23.3 19.1 %collective-permute-start.2 = (bf16[160,1280]{1,0:T(8,128)(2,1)S(1)}, bf16[160,1280]{1,0:T(8,128)(2,1)S(1)}, u32[]{:S(2)}, u32[]{:S(2)}) collective-permute-start(bf16[160,1280]{1,0:T(8,128)(2,1)S(1)} %get-tuple-element.43), channel_id=1, source_target_pairs={{0,6},{2,0},{4,2},{6,4},{1,7},{3,1},{5,3},{7,5},{8,14},{10,8},{12,... | collective-permute-start | bytes 1228808 | tf_op jit(solution)/shard_map/ppermute | solution.py:392
  24.8 1.7 %copy-start.4 = (bf16[1024,1280]{1,0:T(8,128)(2,1)S(1)}, bf16[1024,1280]{1,0:T(8,128)(2,1)}, u32[]{:S(2)}) copy-start(bf16[1024,1280]{1,0:T(8,128)(2,1)} %refs_11_) | copy-start | bytes 7864324
  26.6 1.7 %copy-start.7 = (bf16[3,1280,320]{1,2,0:T(8,128)(2,1)S(1)}, bf16[3,1280,320]{1,2,0:T(8,128)(2,1)}, u32[]{:S(2)}) copy-start(bf16[3,1280,320]{1,2,0:T(8,128)(2,1)} %param.11) | copy-start | bytes 7372804
  28.2 17.2 %copy-start.8 = (f32[1280]{0:T(1024)S(1)}, f32[1280]{0:T(1024)}, u32[]{:S(2)}) copy-start(f32[1280]{0:T(1024)} %param.13) | copy-start | bytes 15364
  28.2 26.1 %copy-start.5 = (bf16[1024,1280]{1,0:T(8,128)(2,1)S(1)}, bf16[1024,1280]{1,0:T(8,128)(2,1)}, u32[]{:S(2)}) copy-start(bf16[1024,1280]{1,0:T(8,128)(2,1)} %refs_11_) | copy-start | bytes 7864324
  42.3 12.0 %copy-start.3 = (bf16[320,1280]{1,0:T(8,128)(2,1)S(1)}, bf16[320,1280]{1,0:T(8,128)(2,1)}, u32[]{:S(2)}) copy-start(bf16[320,1280]{1,0:T(8,128)(2,1)} %refs_5_) | copy-start | bytes 2457604
  42.4 12.0 %collective-permute-start.7 = (bf16[160,1280]{1,0:T(8,128)(2,1)S(1)}, bf16[160,1280]{1,0:T(8,128)(2,1)S(1)}, u32[]{:S(2)}, u32[]{:S(2)}) collective-permute-start(bf16[160,1280]{1,0:T(8,128)(2,1)S(1)} %collective-permute-done.1.refs_7_), channel_id=1, source_target_pairs={{0,1},{1,0},{2,3},{3,2},{4,5},{5,4},{6,7},{7,6},{8,9},{9,8},{10,11... | collective-permute-start | bytes 1228808 | tf_op jit(solution)/shard_map/ppermute | solution.py:396
  42.8 11.5 %collective-permute-start.8 = (bf16[160,1280]{1,0:T(8,128)(2,1)S(1)}, bf16[160,1280]{1,0:T(8,128)(2,1)S(1)}, u32[]{:S(2)}, u32[]{:S(2)}) collective-permute-start(bf16[160,1280]{1,0:T(8,128)(2,1)S(1)} %collective-permute-done.2.refs_8_), channel_id=1, source_target_pairs={{0,1},{1,0},{2,3},{3,2},{4,5},{5,4},{6,7},{7,6},{8,9},{9,8},{10,11... | collective-permute-start | bytes 1228808 | tf_op jit(solution)/shard_map/ppermute | solution.py:396
  43.0 2.0 %collective-permute-start.3 = (bf16[256,320]{1,0:T(8,128)(2,1)S(1)}, bf16[256,320]{1,0:T(8,128)(2,1)S(1)}, u32[]{:S(2)}, u32[]{:S(2)}) collective-permute-start(bf16[256,320]{1,0:T(8,128)(2,1)S(1)} %get-tuple-element.47), channel_id=1, source_target_pairs={{0,1},{1,0},{2,3},{3,2},{4,5},{5,4},{6,7},{7,6},{8,9},{9,8},{10,11... | collective-permute-start | bytes 491528 | tf_op jit(solution)/shard_map/ppermute | solution.py:388
  43.5 6.5 %collective-permute-start.4 = (bf16[256,320]{1,0:T(8,128)(2,1)S(1)}, bf16[256,320]{1,0:T(8,128)(2,1)S(1)}, u32[]{:S(2)}, u32[]{:S(2)}) collective-permute-start(bf16[256,320]{1,0:T(8,128)(2,1)S(1)} %get-tuple-element.46), channel_id=1, source_target_pairs={{0,2},{1,3},{2,0},{3,1},{4,6},{5,7},{6,4},{7,5},{8,10},{9,11},{10,... | collective-permute-start | bytes 491528 | tf_op jit(solution)/shard_map/ppermute | solution.py:388
  45.1 9.3 %collective-permute-start.5 = (bf16[256,320]{1,0:T(8,128)(2,1)S(1)}, bf16[256,320]{1,0:T(8,128)(2,1)S(1)}, u32[]{:S(2)}, u32[]{:S(2)}) collective-permute-start(bf16[256,320]{1,0:T(8,128)(2,1)S(1)} %get-tuple-element.45), channel_id=1, source_target_pairs={{0,3},{1,2},{2,1},{3,0},{4,7},{5,6},{6,5},{7,4},{8,11},{9,10},{10,... | collective-permute-start | bytes 491528 | tf_op jit(solution)/shard_map/ppermute | solution.py:388
  54.4 27.0 %copy-start.1 = (bf16[512,2048]{1,0:T(8,128)(2,1)S(1)}, bf16[512,2048]{1,0:T(8,128)(2,1)}, u32[]{:S(2)}) copy-start(bf16[512,2048]{1,0:T(8,128)(2,1)} %text.3) | copy-start | bytes 6291460
  57.0 17.7 %collective-permute-start.10 = (bf16[64,5120]{1,0:T(8,128)(2,1)}, bf16[64,5120]{1,0:T(8,128)(2,1)}, u32[]{:S(2)}, u32[]{:S(2)}) collective-permute-start(bf16[64,5120]{1,0:T(8,128)(2,1)} %project_and_norm.1.refs_0_), channel_id=1, source_target_pairs={{0,2},{2,4},{4,6},{6,0},{1,3},{3,5},{5,7},{7,1},{8,10},{10,12},{12... | collective-permute-start | bytes 1966088 | tf_op jit(solution)/shard_map/ppermute | solution.py:392
  57.2 19.3 %collective-permute-start.11 = (bf16[64,5120]{1,0:T(8,128)(2,1)}, bf16[64,5120]{1,0:T(8,128)(2,1)}, u32[]{:S(2)}, u32[]{:S(2)}) collective-permute-start(bf16[64,5120]{1,0:T(8,128)(2,1)} %project_and_norm.1.refs_0_), channel_id=1, source_target_pairs={{0,6},{2,0},{4,2},{6,4},{1,7},{3,1},{5,3},{7,5},{8,14},{10,8},{12,... | collective-permute-start | bytes 1966088 | tf_op jit(solution)/shard_map/ppermute | solution.py:392
  61.6 22.5 %all-to-all-start = ((s32[32,1,32]{2,1,0:T(1,128)}), s32[32,1,32]{2,1,0:T(1,128)}, u32[]{:S(2)}, u32[]{:S(2)}) async-start(s32[32,1,32]{2,1,0:T(1,128)} %bitcast.10), calls=%async_computation | async-start | bytes 32768 | tf_op jit(solution)/shard_map/all_to_all | solution.py:460
  76.5 10.2 %collective-permute-start.14 = (bf16[32,5120]{1,0:T(8,128)(2,1)}, bf16[32,5120]{1,0:T(8,128)(2,1)}, u32[]{:S(2)}, u32[]{:S(2)}) collective-permute-start(bf16[32,5120]{1,0:T(8,128)(2,1)} %slice.16), channel_id=1, source_target_pairs={{0,2},{2,4},{4,6},{6,0},{1,3},{3,5},{5,7},{7,1},{8,10},{10,12},{12... | collective-permute-start | bytes 983048 | tf_op jit(solution)/shard_map/ppermute | solution.py:392
  78.2 9.9 %collective-permute-start.16 = (bf16[32,5120]{1,0:T(8,128)(2,1)}, bf16[32,5120]{1,0:T(8,128)(2,1)}, u32[]{:S(2)}, u32[]{:S(2)}) collective-permute-start(bf16[32,5120]{1,0:T(8,128)(2,1)} %slice.17), channel_id=1, source_target_pairs={{0,6},{2,0},{4,2},{6,4},{1,7},{3,1},{5,3},{7,5},{8,14},{10,8},{12,... | collective-permute-start | bytes 983048 | tf_op jit(solution)/shard_map/ppermute | solution.py:392
  82.5 7.9 %collective-permute-start.9 = (bf16[64,5120]{1,0:T(8,128)(2,1)}, bf16[64,5120]{1,0:T(8,128)(2,1)}, u32[]{:S(2)}, u32[]{:S(2)}) collective-permute-start(bf16[64,5120]{1,0:T(8,128)(2,1)} %project_and_norm.1.refs_0_), channel_id=1, source_target_pairs={{0,1},{1,0},{2,3},{3,2},{4,5},{5,4},{6,7},{7,6},{8,9},{9,8},{10,11... | collective-permute-start | bytes 1966088 | tf_op jit(solution)/shard_map/ppermute | solution.py:396
  84.1 6.3 %collective-permute-start.12 = (bf16[64,5120]{1,0:T(8,128)(2,1)}, bf16[64,5120]{1,0:T(8,128)(2,1)}, u32[]{:S(2)}, u32[]{:S(2)}) collective-permute-start(bf16[64,5120]{1,0:T(8,128)(2,1)} %collective-permute-done.10.refs_2_), channel_id=1, source_target_pairs={{0,1},{1,0},{2,3},{3,2},{4,5},{5,4},{6,7},{7,6},{8,9},{9,8},{10,11... | collective-permute-start | bytes 1966088 | tf_op jit(solution)/shard_map/ppermute | solution.py:396
  84.2 6.2 %collective-permute-start.13 = (bf16[64,5120]{1,0:T(8,128)(2,1)}, bf16[64,5120]{1,0:T(8,128)(2,1)}, u32[]{:S(2)}, u32[]{:S(2)}) collective-permute-start(bf16[64,5120]{1,0:T(8,128)(2,1)} %collective-permute-done.11.refs_4_), channel_id=1, source_target_pairs={{0,1},{1,0},{2,3},{3,2},{4,5},{5,4},{6,7},{7,6},{8,9},{9,8},{10,11... | collective-permute-start | bytes 1966088 | tf_op jit(solution)/shard_map/ppermute | solution.py:396
  86.7 3.6 %collective-permute-start.15 = (bf16[32,5120]{1,0:T(8,128)(2,1)}, bf16[32,5120]{1,0:T(8,128)(2,1)S(1)}, u32[]{:S(2)}, u32[]{:S(2)}) collective-permute-start(bf16[32,5120]{1,0:T(8,128)(2,1)} %collective-permute-done.14.refs_6_), channel_id=1, source_target_pairs={{0,1},{1,0},{2,3},{3,2},{4,5},{5,4},{6,7},{7,6},{8,9},{9,8},{10,11... | collective-permute-start | bytes 983048 | tf_op jit(solution)/shard_map/ppermute | solution.py:396
  88.2 2.5 %collective-permute-start.17 = (bf16[32,5120]{1,0:T(8,128)(2,1)}, bf16[32,5120]{1,0:T(8,128)(2,1)S(1)}, u32[]{:S(2)}, u32[]{:S(2)}) collective-permute-start(bf16[32,5120]{1,0:T(8,128)(2,1)} %collective-permute-done.16.refs_8_), channel_id=1, source_target_pairs={{0,1},{1,0},{2,3},{3,2},{4,5},{5,4},{6,7},{7,6},{8,9},{9,8},{10,11... | collective-permute-start | bytes 983048 | tf_op jit(solution)/shard_map/ppermute | solution.py:396
  153.7 5.9 %copy-start.6 = (f32[2048]{0:T(1024)S(1)}, f32[2048]{0:T(1024)}, u32[]{:S(2)}) copy-start(f32[2048]{0:T(1024)} %param.17) | copy-start | bytes 24580
  153.7 5.8 %collective-permute-start.18 = (f32[4,128]{1,0:T(4,128)S(1)}, f32[4,128]{1,0:T(4,128)S(1)}, u32[]{:S(2)}, u32[]{:S(2)}) collective-permute-start(f32[4,128]{1,0:T(4,128)S(1)} %slot_squares.1.own), channel_id=1, source_target_pairs={{0,1},{1,0},{2,3},{3,2},{4,5},{5,4},{6,7},{7,6},{8,9},{9,8},{10,11... | collective-permute-start | bytes 6152 | tf_op jit(solution)/shard_map/ppermute | solution.py:388
  155.9 3.6 %collective-permute-start.19 = (f32[4,128]{1,0:T(4,128)S(1)}, f32[4,128]{1,0:T(4,128)S(1)}, u32[]{:S(2)}, u32[]{:S(2)}) collective-permute-start(f32[4,128]{1,0:T(4,128)S(1)} %slot_squares.1.own), channel_id=1, source_target_pairs={{0,2},{1,3},{2,0},{3,1},{4,6},{5,7},{6,4},{7,5},{8,10},{9,11},{10,... | collective-permute-start | bytes 6152 | tf_op jit(solution)/shard_map/ppermute | solution.py:388
  156.2 3.3 %collective-permute-start.20 = (f32[4,128]{1,0:T(4,128)S(1)}, f32[4,128]{1,0:T(4,128)S(1)}, u32[]{:S(2)}, u32[]{:S(2)}) collective-permute-start(f32[4,128]{1,0:T(4,128)S(1)} %slot_squares.1.own), channel_id=1, source_target_pairs={{0,3},{1,2},{2,1},{3,0},{4,7},{5,6},{6,5},{7,4},{8,11},{9,10},{10,... | collective-permute-start | bytes 6152 | tf_op jit(solution)/shard_map/ppermute | solution.py:388
  (1 other events, 1.1 us)
Sparse Core Ops, SparseCore 0:
  19.8 83.9 all-gather.1

commit v15 on v14

--- a/solution.py
+++ b/solution.py
@@ -160,41 +160,60 @@
 
 
 def merge_kernel(rows, weight, send, outgoing, rows_held, weight_held, send_held, sent, sems):
-    depth = weight_held.shape[0]
-    steps = (sems.shape[0] - 1) // 2
-    tile = depth // steps
+    depth, columns = weight_held.shape
+    half = columns // 2
+    left, right = pl.ds(0, half), pl.ds(half, half)
+    edges = [depth * k // 40 for k in (0, 5, 15, 27, 40)]
+    steps = len(edges) - 1
     copies = []
     for k in range(steps):
-        part = pl.ds(k * tile, tile)
+        part = pl.ds(edges[k], edges[k + 1] - edges[k])
         copies += [
             pltpu.make_async_copy(rows.at[:, part], rows_held.at[:, part], sems.at[2 * k]),
-            pltpu.make_async_copy(weight.at[part], weight_held.at[part], sems.at[2 * k + 1]),
+            pltpu.make_async_copy(
+                weight.at[part, left], weight_held.at[part, left], sems.at[2 * k + 1]
+            ),
         ]
-    copies.append(pltpu.make_async_copy(send, send_held, sems.at[2 * steps]))
+    copies += [
+        pltpu.make_async_copy(send, send_held, sems.at[2 * steps]),
+        pltpu.make_async_copy(
+            weight.at[:, right], weight_held.at[:, right], sems.at[2 * steps + 1]
+        ),
+    ]
     for copy in copies:
         copy.start()
-    total = jnp.zeros((rows_held.shape[0], weight_held.shape[1]), F32)
+    total = jnp.zeros((rows_held.shape[0], half), F32)
     for k in range(steps):
         copies[2 * k].wait()
         copies[2 * k + 1].wait()
-        part = slice(k * tile, (k + 1) * tile)
+        part = slice(edges[k], edges[k + 1])
         total += jnp.dot(
-            rows_held[:, part], weight_held[part, :], preferred_element_type=F32
+            rows_held[:, part], weight_held[part, :half], preferred_element_type=F32
         )
-    image = total.astype(BF)
-    copies[-1].wait()
-    pieces = 4
+    copies[2 * steps].wait()
+    sent[:, :half] = jnp.dot(
+        send_held[...], total.astype(BF), preferred_element_type=F32
+    ).astype(BF)
+    first = pltpu.make_async_copy(sent.at[:, left], outgoing.at[:, left], sems.at[0])
+    first.start()
+    copies[2 * steps + 1].wait()
+    image = jnp.dot(
+        rows_held[...], weight_held[:, half:], preferred_element_type=F32
+    ).astype(BF)
+    pieces = 2
     count = sent.shape[0] // pieces
-    copies = []
+    writes = [first]
     for k in range(pieces):
         part = pl.ds(k * count, count)
-        sent[part, :] = jnp.dot(
+        sent[part, half:] = jnp.dot(
             send_held[part, :], image, preferred_element_type=F32
         ).astype(BF)
-        copy = pltpu.make_async_copy(sent.at[part], outgoing.at[part], sems.at[k])
+        copy = pltpu.make_async_copy(
+            sent.at[part, right], outgoing.at[part, right], sems.at[k + 1]
+        )
         copy.start()
-        copies.append(copy)
-    for copy in copies:
+        writes.append(copy)
+    for copy in writes:
         copy.wait()
 
 
@@ -212,7 +231,7 @@
             pltpu.VMEM((depth, columns), BF),
             pltpu.VMEM((slots, count), BF),
             pltpu.VMEM((slots, columns), BF),
-            pltpu.SemaphoreType.DMA((9,)),
+            pltpu.SemaphoreType.DMA((10,)),
         ],
         compiler_params=pltpu.CompilerParams(vmem_limit_bytes=60 * 2**20),
         cost_estimate=pl.CostEstimate(

time: 170 us -> 169 us (level)
  no operation moved by 1% of the time
where the time goes in v15:
time: 169 us; the launch traced here: 168 us
  Pallas kernels  39.5 us (23%)
  blocking collectives  37.1 us (22%)
  starting transfers between devices  32.1 us (19%)
  waiting for transfers between devices  28.1 us (17%)
  between operations  13.7 us (8%)
  local copies, waits for them, and re-layouts  11.2 us (7%)
  other arithmetic  5.72 us (3%)
    all_to_all x1, blocking collectives, on_device(): lax.all_to_all(outgoing, SEC, split_axis=0, concat_axis=0, tiled=True)  37.1 us
    pallas_call x1, Pallas kernels, vision_context(): pl.pallas_call(attention_kernel, out_shape=jax.ShapeDtypeStruct((row_coun...  14.1 us
    ppermute x6, waiting for transfers between devices, swap_tp(): return lax.ppermute(block, TP, [(i, i ^ k) for i in range(4)])  10.3 us
    pallas_call x1, Pallas kernels, merge_and_select(): pl.pallas_call(merge_kernel, out_shape=pltpu.HBM((slots, columns), BF), i...  10.3 us
    ppermute x6, starting transfers between devices, shift_y(): lax.ppermute(block, ('yh', 'yl'), [(i, (i + d) % 4) for i in range(4)])  8.32 us
    all_to_all x1, starting transfers between devices, on_device(): table = lax.all_to_all(table, SEC, split_axis=0, concat_axis=0, tiled=True)  8.27 us
    all_gather x1, waiting for transfers between devices, on_device(): weight = lax.all_gather(both, ('z', 'x'), axis=0, tiled=True)  7.87 us
    ppermute x8, starting transfers between devices, swap_core(): return lax.ppermute(block, 'c', [(0, 1), (1, 0)])  6.73 us
  transfers between devices with their start and end apart: 23, of which 7 were waited for; matrix products, arithmetic and copies ran while one was open for 7% of the time, Pallas kernels for 15%

profile of v15, /device:TPU:1, one launch (start us, length us, event | category | flops | bytes accessed | tf_op | source)
XLA Modules:
  0.0 168.0 jit_solution(8295699103081483644)
XLA Ops:
  7.7 3.8 %collective-permute-start = (bf16[160,1024]{1,0:T(8,128)(2,1)S(1)}, bf16[160,1024]{1,0:T(8,128)(2,1)S(1)}, u32[]{:S(2)}, u32[]{:S(2)}) collective-permute-start(bf16[160,1024]{1,0:T(8,128)(2,1)S(1)} %constant_dynamic-slice_fusion.5), channel_id=1, source_target_pairs={{0,4},{4,0},{1,5},{5,1},{2,6},{6,2},{3,7},{7,3},{8,12},{12,8},{9,1... | collective-permute-start | bytes 983048 | tf_op jit(solution)/shard_map/ppermute | solution.py:436
  13.9 4.8 %collective-permute-done = bf16[160,1024]{1,0:T(8,128)(2,1)S(1)} collective-permute-done((bf16[160,1024]{1,0:T(8,128)(2,1)S(1)}, bf16[160,1024]{1,0:T(8,128)(2,1)S(1)}, u32[]{:S(2)}, u32[]{:S(2)}) %collective-permute-start) | collective-permute-done | bytes 327712 | tf_op jit(solution)/shard_map/ppermute | solution.py:436
  20.2 1.6 collective-permute-start.6
  21.8 1.4 collective-permute-start.1
  23.3 1.5 collective-permute-start.2
  24.8 1.7 %copy-done.4 = bf16[1024,1280]{1,0:T(8,128)(2,1)S(1)} copy-done((bf16[1024,1280]{1,0:T(8,128)(2,1)S(1)}, bf16[1024,1280]{1,0:T(8,128)(2,1)}, u32[]{:S(2)}) %copy-start.4) | copy-done | bytes 2621464
  26.6 1.7 %copy-done.7 = bf16[3,1280,320]{1,2,0:T(8,128)(2,1)S(1)} copy-done((bf16[3,1280,320]{1,2,0:T(8,128)(2,1)S(1)}, bf16[3,1280,320]{1,2,0:T(8,128)(2,1)}, u32[]{:S(2)}) %copy-start.7) | copy-done | bytes 2457624
  28.2 14.1 %vision_attention.1 = bf16[1024,320]{1,0:T(8,128)(2,1)S(1)} custom-call(s32[1024,1]{1,0:T(8,128)S(1)} %copy.13.row_ids, s32[1,1024]{1,0:T(1,128)S(1)} %bitcast.21, bf16[1024,1280]{1,0:T(8,128)(2,1)S(1)} %copy-done.4, bf16[3,320,1280]{2,1,0:T(8,128)(2,1)S(1)} %bitcast.23), custom_call_target="tpu_custom_call" | custom-call | flops 6811549696 | bytes 5079040 | tf_op jit(solution)/shard_map/vision_attention/pallas_call | solution.py:70
  43.6 1.4 collective-permute-done.3.refs_2_
  45.5 4.5 %collective-permute-done.4.refs_3_ = bf16[256,320]{1,0:T(8,128)(2,1)S(1)} collective-permute-done((bf16[256,320]{1,0:T(8,128)(2,1)S(1)}, bf16[256,320]{1,0:T(8,128)(2,1)S(1)}, u32[]{:S(2)}, u32[]{:S(2)}) %collective-permute-start.4) | collective-permute-done | bytes 163872 | tf_op jit(solution)/shard_map/ppermute | solution.py:407
  49.9 4.4 %collective-permute-done.5.refs_4_ = bf16[256,320]{1,0:T(8,128)(2,1)S(1)} collective-permute-done((bf16[256,320]{1,0:T(8,128)(2,1)S(1)}, bf16[256,320]{1,0:T(8,128)(2,1)S(1)}, u32[]{:S(2)}, u32[]{:S(2)}) %collective-permute-start.5) | collective-permute-done | bytes 163872 | tf_op jit(solution)/shard_map/ppermute | solution.py:407
  54.4 2.7 %project_and_norm.1.refs_0_ = bf16[64,5120]{1,0:T(8,128)(2,1)} custom-call(s32[1]{0:T(128)} %bitcast.3.refs_0_, bf16[256,320]{1,0:T(8,128)(2,1)S(1)} %get-tuple-element.48.refs_1_, bf16[256,320]{1,0:T(8,128)(2,1)S(1)} %collective-permute-done.3.refs_2_, bf16[256,320]{1,0:T(8,128)(2,1)S(1)} %collective-permute-done.4.refs_3_, ...), custom_call_target="tpu_custom_call" | custom-call | flops 838860800 | bytes 5242880 | tf_op jit(solution)/shard_map/project_and_norm/pallas_call | solution.py:115
  57.2 2.5 %collective-permute-start.11 = (bf16[64,5120]{1,0:T(8,128)(2,1)}, bf16[64,5120]{1,0:T(8,128)(2,1)}, u32[]{:S(2)}, u32[]{:S(2)}) collective-permute-start(bf16[64,5120]{1,0:T(8,128)(2,1)} %project_and_norm.1.refs_0_), channel_id=1, source_target_pairs={{0,6},{2,0},{4,2},{6,4},{1,7},{3,1},{5,3},{7,5},{8,14},{10,8},{12,... | collective-permute-start | bytes 1966088 | tf_op jit(solution)/shard_map/ppermute | solution.py:411
  61.6 8.3 %all-to-all-start = ((s32[32,1,32]{2,1,0:T(1,128)}), s32[32,1,32]{2,1,0:T(1,128)}, u32[]{:S(2)}, u32[]{:S(2)}) async-start(s32[32,1,32]{2,1,0:T(1,128)} %bitcast.10), calls=%async_computation | async-start | bytes 32768 | tf_op jit(solution)/shard_map/all_to_all | solution.py:479
  69.9 4.9 %collective-permute-done.10.refs_2_ = bf16[64,5120]{1,0:T(8,128)(2,1)} collective-permute-done((bf16[64,5120]{1,0:T(8,128)(2,1)}, bf16[64,5120]{1,0:T(8,128)(2,1)}, u32[]{:S(2)}, u32[]{:S(2)}) %collective-permute-start.10) | collective-permute-done | bytes 655392 | tf_op jit(solution)/shard_map/ppermute | solution.py:411
  74.8 1.7 %slice.16 = bf16[32,5120]{1,0:T(8,128)(2,1)} slice(bf16[64,5120]{1,0:T(8,128)(2,1)} %collective-permute-done.10.refs_2_), slice={[0:32], [0:5120]} | slice | bytes 655360 | tf_op jit(solution)/shard_map/slice | solution.py:478
  76.5 1.7 %slice.17 = bf16[32,5120]{1,0:T(8,128)(2,1)} slice(bf16[64,5120]{1,0:T(8,128)(2,1)} %collective-permute-done.11.refs_4_), slice={[32:64], [0:5120]} | slice | bytes 655360 | tf_op jit(solution)/shard_map/slice | solution.py:478
  78.2 2.7 %collective-permute-start.16 = (bf16[32,5120]{1,0:T(8,128)(2,1)}, bf16[32,5120]{1,0:T(8,128)(2,1)}, u32[]{:S(2)}, u32[]{:S(2)}) collective-permute-start(bf16[32,5120]{1,0:T(8,128)(2,1)} %slice.17), channel_id=1, source_target_pairs={{0,6},{2,0},{4,2},{6,4},{1,7},{3,1},{5,3},{7,5},{8,14},{10,8},{12,... | collective-permute-start | bytes 983048 | tf_op jit(solution)/shard_map/ppermute | solution.py:411
  81.3 1.1 text_squares.1.base
  82.5 1.6 collective-permute-start.9
  84.6 1.3 broadcast_add_fusion
  86.7 1.4 collective-permute-start.15
  89.2 1.2 compare_convert_fusion.send
  90.6 5.3 %stack_rows.1.rows = bf16[512,5120]{1,0:T(8,128)(2,1)} custom-call(bf16[64,5120]{1,0:T(8,128)(2,1)} %project_and_norm.1.refs_0_, bf16[64,5120]{1,0:T(8,128)(2,1)} %collective-permute-done.9.refs_1_, bf16[64,5120]{1,0:T(8,128)(2,1)} %collective-permute-done.10.refs_2_, bf16[64,5120]{1,0:T(8,128)(2,1)} %collective-permute-done.12.refs_3_, ...), custom_call_target="tpu_custom_call" | custom-call | bytes 10485760 | tf_op jit(solution)/shard_map/stack_rows/pallas_call | solution.py:148
  95.9 7.9 %all-gather.2.cloned.1.call-done.weight = bf16[5120,1024]{1,0:T(8,128)(2,1)} async-done(((bf16[320,1024]{1,0:T(8,128)(2,1)}), bf16[5120,1024]{1,0:T(8,128)(2,1)}) %all-gather.2.cloned.1.call-update) | async-done | bytes 10485776 | tf_op jit(solution)/shard_map/all_gather | solution.py:457
  103.8 10.3 %merge_rows.1 = bf16[1024,1024]{1,0:T(8,128)(2,1)} custom-call(bf16[512,5120]{1,0:T(8,128)(2,1)} %stack_rows.1.rows, bf16[5120,1024]{1,0:T(8,128)(2,1)} %all-gather.2.cloned.1.call-done.weight, bf16[1024,512]{1,0:T(8,128)(2,1)} %compare_convert_fusion.send), custom_call_target="tpu_custom_call" | custom-call | flops 6442450944 | bytes 17825792 | tf_op jit(solution)/shard_map/merge_rows/pallas_call | solution.py:224
  114.1 37.1 %all_to_all.21 = bf16[32,32,1024]{2,1,0:T(8,128)(2,1)S(1)} all-to-all(bf16[32,32,1024]{2,1,0:T(8,128)(2,1)} %bitcast.24), channel_id=1, replica_groups=mesh['z'=4,'x'=4,'yh'=2,'yl'=2,'c'=2] {'z','x','yh'}, dimensions={0} | all-to-all | bytes 4194304 | tf_op jit(solution)/shard_map/all_to_all | solution.py:503
  151.2 1.6 slot_squares.1.own
  152.8 2.2 %collective-permute-start.18 = (f32[4,128]{1,0:T(4,128)S(1)}, f32[4,128]{1,0:T(4,128)S(1)}, u32[]{:S(2)}, u32[]{:S(2)}) collective-permute-start(f32[4,128]{1,0:T(4,128)S(1)} %slot_squares.1.own), channel_id=1, source_target_pairs={{0,1},{1,0},{2,3},{3,2},{4,5},{5,4},{6,7},{7,6},{8,9},{9,8},{10,11... | collective-permute-start | bytes 6152 | tf_op jit(solution)/shard_map/ppermute | solution.py:407
  155.4 1.4 collective-permute-start.20
  156.8 1.9 %pick_rows.1.prompt = bf16[512,2048]{1,0:T(8,128)(2,1)S(1)} custom-call(bf16[16,2,32,1024]{3,2,1,0:T(8,128)(2,1)S(1)} %bitcast.19, bf16[512,512]{1,0:T(8,128)(2,1)S(1)} %fusion.1.pick, s32[512,1]{1,0:T(8,128)S(1)} %copy.14.usable, bf16[512,2048]{1,0:T(8,128)(2,1)S(1)} %copy-done.1), custom_call_target="tpu_custom_call" | custom-call | flops 1073741824 | bytes 6291456 | tf_op jit(solution)/shard_map/pick_rows/pallas_call | solution.py:355
  158.7 2.5 %finish.1 = bf16[512,2048]{1,0:T(8,128)(2,1)} custom-call(bf16[512,2048]{1,0:T(8,128)(2,1)S(1)} %pick_rows.1.prompt, f32[4,128]{1,0:T(4,128)S(1)} %slot_squares.1.own, f32[4,128]{1,0:T(4,128)S(1)} %collective-permute-done.18.core, f32[4,128]{1,0:T(4,128)S(1)} %collective-permute-done.19.far, f32[4,128]{1,0:T(4,128)S(1)} %collective-permute-done.20.both, ...), custom_call_target="tpu_custom_call" | custom-call | flops 3145728 | bytes 4194304 | tf_op jit(solution)/shard_map/finish/pallas_call | solution.py:389
  (84 shorter events, 12.0 us)
Async XLA Ops:
  6.5 97.3 %all-gather.2.cloned.1.call-start = ((), (), s32[]{:S(2)}) async-start(), calls=%async_computation.2 | async-start | bytes 11141120 | tf_op jit(solution)/shard_map/all_gather | solution.py:457
  7.7 12.1 %copy-start.9 = (s32[1,256]{1,0:T(1,128)S(1)}, s32[1,256]{1,0:T(1,128)}, u32[]{:S(2)}) copy-start(s32[1,256]{1,0:T(1,128)} %param.10) | copy-start | bytes 3076
  7.7 11.0 %collective-permute-start = (bf16[160,1024]{1,0:T(8,128)(2,1)S(1)}, bf16[160,1024]{1,0:T(8,128)(2,1)S(1)}, u32[]{:S(2)}, u32[]{:S(2)}) collective-permute-start(bf16[160,1024]{1,0:T(8,128)(2,1)S(1)} %constant_dynamic-slice_fusion.5), channel_id=1, source_target_pairs={{0,4},{4,0},{1,5},{5,1},{2,6},{6,2},{3,7},{7,3},{8,12},{12,8},{9,1... | collective-permute-start | bytes 983048 | tf_op jit(solution)/shard_map/ppermute | solution.py:436
  13.2 7.0 %copy-start.2 = (bf16[320,1280]{1,0:T(8,128)(2,1)S(1)}, bf16[320,1280]{1,0:T(8,128)(2,1)}, u32[]{:S(2)}) copy-start(bf16[320,1280]{1,0:T(8,128)(2,1)} %refs_5_) | copy-start | bytes 2457604
  20.2 34.1 %collective-permute-start.6 = (bf16[320,1280]{1,0:T(8,128)(2,1)S(1)}, bf16[320,1280]{1,0:T(8,128)(2,1)S(1)}, u32[]{:S(2)}, u32[]{:S(2)}) collective-permute-start(bf16[320,1280]{1,0:T(8,128)(2,1)S(1)} %copy-done.2), channel_id=1, source_target_pairs={{0,1},{1,0},{2,3},{3,2},{4,5},{5,4},{6,7},{7,6},{8,9},{9,8},{10,11... | collective-permute-start | bytes 2457608 | tf_op jit(solution)/shard_map/ppermute | solution.py:415
  21.8 20.5 %collective-permute-start.1 = (bf16[160,1280]{1,0:T(8,128)(2,1)S(1)}, bf16[160,1280]{1,0:T(8,128)(2,1)S(1)}, u32[]{:S(2)}, u32[]{:S(2)}) collective-permute-start(bf16[160,1280]{1,0:T(8,128)(2,1)S(1)} %get-tuple-element.44), channel_id=1, source_target_pairs={{0,2},{2,4},{4,6},{6,0},{1,3},{3,5},{5,7},{7,1},{8,10},{10,12},{12... | collective-permute-start | bytes 1228808 | tf_op jit(solution)/shard_map/ppermute | solution.py:411
  23.3 19.1 %collective-permute-start.2 = (bf16[160,1280]{1,0:T(8,128)(2,1)S(1)}, bf16[160,1280]{1,0:T(8,128)(2,1)S(1)}, u32[]{:S(2)}, u32[]{:S(2)}) collective-permute-start(bf16[160,1280]{1,0:T(8,128)(2,1)S(1)} %get-tuple-element.43), channel_id=1, source_target_pairs={{0,6},{2,0},{4,2},{6,4},{1,7},{3,1},{5,3},{7,5},{8,14},{10,8},{12,... | collective-permute-start | bytes 1228808 | tf_op jit(solution)/shard_map/ppermute | solution.py:411
  24.8 1.7 %copy-start.4 = (bf16[1024,1280]{1,0:T(8,128)(2,1)S(1)}, bf16[1024,1280]{1,0:T(8,128)(2,1)}, u32[]{:S(2)}) copy-start(bf16[1024,1280]{1,0:T(8,128)(2,1)} %refs_11_) | copy-start | bytes 7864324
  26.6 1.7 %copy-start.7 = (bf16[3,1280,320]{1,2,0:T(8,128)(2,1)S(1)}, bf16[3,1280,320]{1,2,0:T(8,128)(2,1)}, u32[]{:S(2)}) copy-start(bf16[3,1280,320]{1,2,0:T(8,128)(2,1)} %param.11) | copy-start | bytes 7372804
  28.2 17.2 %copy-start.8 = (f32[1280]{0:T(1024)S(1)}, f32[1280]{0:T(1024)}, u32[]{:S(2)}) copy-start(f32[1280]{0:T(1024)} %param.13) | copy-start | bytes 15364
  28.2 26.1 %copy-start.5 = (bf16[1024,1280]{1,0:T(8,128)(2,1)S(1)}, bf16[1024,1280]{1,0:T(8,128)(2,1)}, u32[]{:S(2)}) copy-start(bf16[1024,1280]{1,0:T(8,128)(2,1)} %refs_11_) | copy-start | bytes 7864324
  42.3 12.0 %copy-start.3 = (bf16[320,1280]{1,0:T(8,128)(2,1)S(1)}, bf16[320,1280]{1,0:T(8,128)(2,1)}, u32[]{:S(2)}) copy-start(bf16[320,1280]{1,0:T(8,128)(2,1)} %refs_5_) | copy-start | bytes 2457604
  42.4 12.0 %collective-permute-start.7 = (bf16[160,1280]{1,0:T(8,128)(2,1)S(1)}, bf16[160,1280]{1,0:T(8,128)(2,1)S(1)}, u32[]{:S(2)}, u32[]{:S(2)}) collective-permute-start(bf16[160,1280]{1,0:T(8,128)(2,1)S(1)} %collective-permute-done.1.refs_7_), channel_id=1, source_target_pairs={{0,1},{1,0},{2,3},{3,2},{4,5},{5,4},{6,7},{7,6},{8,9},{9,8},{10,11... | collective-permute-start | bytes 1228808 | tf_op jit(solution)/shard_map/ppermute | solution.py:415
  42.8 11.5 %collective-permute-start.8 = (bf16[160,1280]{1,0:T(8,128)(2,1)S(1)}, bf16[160,1280]{1,0:T(8,128)(2,1)S(1)}, u32[]{:S(2)}, u32[]{:S(2)}) collective-permute-start(bf16[160,1280]{1,0:T(8,128)(2,1)S(1)} %collective-permute-done.2.refs_8_), channel_id=1, source_target_pairs={{0,1},{1,0},{2,3},{3,2},{4,5},{5,4},{6,7},{7,6},{8,9},{9,8},{10,11... | collective-permute-start | bytes 1228808 | tf_op jit(solution)/shard_map/ppermute | solution.py:415
  43.0 2.0 %collective-permute-start.3 = (bf16[256,320]{1,0:T(8,128)(2,1)S(1)}, bf16[256,320]{1,0:T(8,128)(2,1)S(1)}, u32[]{:S(2)}, u32[]{:S(2)}) collective-permute-start(bf16[256,320]{1,0:T(8,128)(2,1)S(1)} %get-tuple-element.47), channel_id=1, source_target_pairs={{0,1},{1,0},{2,3},{3,2},{4,5},{5,4},{6,7},{7,6},{8,9},{9,8},{10,11... | collective-permute-start | bytes 491528 | tf_op jit(solution)/shard_map/ppermute | solution.py:407
  43.5 6.5 %collective-permute-start.4 = (bf16[256,320]{1,0:T(8,128)(2,1)S(1)}, bf16[256,320]{1,0:T(8,128)(2,1)S(1)}, u32[]{:S(2)}, u32[]{:S(2)}) collective-permute-start(bf16[256,320]{1,0:T(8,128)(2,1)S(1)} %get-tuple-element.46), channel_id=1, source_target_pairs={{0,2},{1,3},{2,0},{3,1},{4,6},{5,7},{6,4},{7,5},{8,10},{9,11},{10,... | collective-permute-start | bytes 491528 | tf_op jit(solution)/shard_map/ppermute | solution.py:407
  45.1 9.3 %collective-permute-start.5 = (bf16[256,320]{1,0:T(8,128)(2,1)S(1)}, bf16[256,320]{1,0:T(8,128)(2,1)S(1)}, u32[]{:S(2)}, u32[]{:S(2)}) collective-permute-start(bf16[256,320]{1,0:T(8,128)(2,1)S(1)} %get-tuple-element.45), channel_id=1, source_target_pairs={{0,3},{1,2},{2,1},{3,0},{4,7},{5,6},{6,5},{7,4},{8,11},{9,10},{10,... | collective-permute-start | bytes 491528 | tf_op jit(solution)/shard_map/ppermute | solution.py:407
  54.4 27.0 %copy-start.1 = (bf16[512,2048]{1,0:T(8,128)(2,1)S(1)}, bf16[512,2048]{1,0:T(8,128)(2,1)}, u32[]{:S(2)}) copy-start(bf16[512,2048]{1,0:T(8,128)(2,1)} %text.3) | copy-start | bytes 6291460
  57.0 17.7 %collective-permute-start.10 = (bf16[64,5120]{1,0:T(8,128)(2,1)}, bf16[64,5120]{1,0:T(8,128)(2,1)}, u32[]{:S(2)}, u32[]{:S(2)}) collective-permute-start(bf16[64,5120]{1,0:T(8,128)(2,1)} %project_and_norm.1.refs_0_), channel_id=1, source_target_pairs={{0,2},{2,4},{4,6},{6,0},{1,3},{3,5},{5,7},{7,1},{8,10},{10,12},{12... | collective-permute-start | bytes 1966088 | tf_op jit(solution)/shard_map/ppermute | solution.py:411
  57.2 19.3 %collective-permute-start.11 = (bf16[64,5120]{1,0:T(8,128)(2,1)}, bf16[64,5120]{1,0:T(8,128)(2,1)}, u32[]{:S(2)}, u32[]{:S(2)}) collective-permute-start(bf16[64,5120]{1,0:T(8,128)(2,1)} %project_and_norm.1.refs_0_), channel_id=1, source_target_pairs={{0,6},{2,0},{4,2},{6,4},{1,7},{3,1},{5,3},{7,5},{8,14},{10,8},{12,... | collective-permute-start | bytes 1966088 | tf_op jit(solution)/shard_map/ppermute | solution.py:411
  61.6 22.5 %all-to-all-start = ((s32[32,1,32]{2,1,0:T(1,128)}), s32[32,1,32]{2,1,0:T(1,128)}, u32[]{:S(2)}, u32[]{:S(2)}) async-start(s32[32,1,32]{2,1,0:T(1,128)} %bitcast.10), calls=%async_computation | async-start | bytes 32768 | tf_op jit(solution)/shard_map/all_to_all | solution.py:479
  76.5 10.2 %collective-permute-start.14 = (bf16[32,5120]{1,0:T(8,128)(2,1)}, bf16[32,5120]{1,0:T(8,128)(2,1)}, u32[]{:S(2)}, u32[]{:S(2)}) collective-permute-start(bf16[32,5120]{1,0:T(8,128)(2,1)} %slice.16), channel_id=1, source_target_pairs={{0,2},{2,4},{4,6},{6,0},{1,3},{3,5},{5,7},{7,1},{8,10},{10,12},{12... | collective-permute-start | bytes 983048 | tf_op jit(solution)/shard_map/ppermute | solution.py:411
  78.2 9.9 %collective-permute-start.16 = (bf16[32,5120]{1,0:T(8,128)(2,1)}, bf16[32,5120]{1,0:T(8,128)(2,1)}, u32[]{:S(2)}, u32[]{:S(2)}) collective-permute-start(bf16[32,5120]{1,0:T(8,128)(2,1)} %slice.17), channel_id=1, source_target_pairs={{0,6},{2,0},{4,2},{6,4},{1,7},{3,1},{5,3},{7,5},{8,14},{10,8},{12,... | collective-permute-start | bytes 983048 | tf_op jit(solution)/shard_map/ppermute | solution.py:411
  82.5 7.9 %collective-permute-start.9 = (bf16[64,5120]{1,0:T(8,128)(2,1)}, bf16[64,5120]{1,0:T(8,128)(2,1)}, u32[]{:S(2)}, u32[]{:S(2)}) collective-permute-start(bf16[64,5120]{1,0:T(8,128)(2,1)} %project_and_norm.1.refs_0_), channel_id=1, source_target_pairs={{0,1},{1,0},{2,3},{3,2},{4,5},{5,4},{6,7},{7,6},{8,9},{9,8},{10,11... | collective-permute-start | bytes 1966088 | tf_op jit(solution)/shard_map/ppermute | solution.py:415
  84.1 6.3 %collective-permute-start.12 = (bf16[64,5120]{1,0:T(8,128)(2,1)}, bf16[64,5120]{1,0:T(8,128)(2,1)}, u32[]{:S(2)}, u32[]{:S(2)}) collective-permute-start(bf16[64,5120]{1,0:T(8,128)(2,1)} %collective-permute-done.10.refs_2_), channel_id=1, source_target_pairs={{0,1},{1,0},{2,3},{3,2},{4,5},{5,4},{6,7},{7,6},{8,9},{9,8},{10,11... | collective-permute-start | bytes 1966088 | tf_op jit(solution)/shard_map/ppermute | solution.py:415
  84.2 6.2 %collective-permute-start.13 = (bf16[64,5120]{1,0:T(8,128)(2,1)}, bf16[64,5120]{1,0:T(8,128)(2,1)}, u32[]{:S(2)}, u32[]{:S(2)}) collective-permute-start(bf16[64,5120]{1,0:T(8,128)(2,1)} %collective-permute-done.11.refs_4_), channel_id=1, source_target_pairs={{0,1},{1,0},{2,3},{3,2},{4,5},{5,4},{6,7},{7,6},{8,9},{9,8},{10,11... | collective-permute-start | bytes 1966088 | tf_op jit(solution)/shard_map/ppermute | solution.py:415
  86.7 3.6 %collective-permute-start.15 = (bf16[32,5120]{1,0:T(8,128)(2,1)}, bf16[32,5120]{1,0:T(8,128)(2,1)S(1)}, u32[]{:S(2)}, u32[]{:S(2)}) collective-permute-start(bf16[32,5120]{1,0:T(8,128)(2,1)} %collective-permute-done.14.refs_6_), channel_id=1, source_target_pairs={{0,1},{1,0},{2,3},{3,2},{4,5},{5,4},{6,7},{7,6},{8,9},{9,8},{10,11... | collective-permute-start | bytes 983048 | tf_op jit(solution)/shard_map/ppermute | solution.py:415
  88.2 2.5 %collective-permute-start.17 = (bf16[32,5120]{1,0:T(8,128)(2,1)}, bf16[32,5120]{1,0:T(8,128)(2,1)S(1)}, u32[]{:S(2)}, u32[]{:S(2)}) collective-permute-start(bf16[32,5120]{1,0:T(8,128)(2,1)} %collective-permute-done.16.refs_8_), channel_id=1, source_target_pairs={{0,1},{1,0},{2,3},{3,2},{4,5},{5,4},{6,7},{7,6},{8,9},{9,8},{10,11... | collective-permute-start | bytes 983048 | tf_op jit(solution)/shard_map/ppermute | solution.py:415
  152.8 5.9 %copy-start.6 = (f32[2048]{0:T(1024)S(1)}, f32[2048]{0:T(1024)}, u32[]{:S(2)}) copy-start(f32[2048]{0:T(1024)} %param.17) | copy-start | bytes 24580
  152.8 5.9 %collective-permute-start.18 = (f32[4,128]{1,0:T(4,128)S(1)}, f32[4,128]{1,0:T(4,128)S(1)}, u32[]{:S(2)}, u32[]{:S(2)}) collective-permute-start(f32[4,128]{1,0:T(4,128)S(1)} %slot_squares.1.own), channel_id=1, source_target_pairs={{0,1},{1,0},{2,3},{3,2},{4,5},{5,4},{6,7},{7,6},{8,9},{9,8},{10,11... | collective-permute-start | bytes 6152 | tf_op jit(solution)/shard_map/ppermute | solution.py:407
  155.1 3.6 %collective-permute-start.19 = (f32[4,128]{1,0:T(4,128)S(1)}, f32[4,128]{1,0:T(4,128)S(1)}, u32[]{:S(2)}, u32[]{:S(2)}) collective-permute-start(f32[4,128]{1,0:T(4,128)S(1)} %slot_squares.1.own), channel_id=1, source_target_pairs={{0,2},{1,3},{2,0},{3,1},{4,6},{5,7},{6,4},{7,5},{8,10},{9,11},{10,... | collective-permute-start | bytes 6152 | tf_op jit(solution)/shard_map/ppermute | solution.py:407
  155.4 3.3 %collective-permute-start.20 = (f32[4,128]{1,0:T(4,128)S(1)}, f32[4,128]{1,0:T(4,128)S(1)}, u32[]{:S(2)}, u32[]{:S(2)}) collective-permute-start(f32[4,128]{1,0:T(4,128)S(1)} %slot_squares.1.own), channel_id=1, source_target_pairs={{0,3},{1,2},{2,1},{3,0},{4,7},{5,6},{6,5},{7,4},{8,11},{9,10},{10,... | collective-permute-start | bytes 6152 | tf_op jit(solution)/shard_map/ppermute | solution.py:407
  (1 other events, 1.1 us)
Sparse Core Ops, SparseCore 0:
  19.8 83.9 all-gather.1

commit v16 on v15

--- a/solution.py
+++ b/solution.py
@@ -163,7 +163,7 @@
     depth, columns = weight_held.shape
     half = columns // 2
     left, right = pl.ds(0, half), pl.ds(half, half)
-    edges = [depth * k // 40 for k in (0, 5, 15, 27, 40)]
+    edges = [depth * k // 40 for k in (0, 3, 10, 22, 40)]
     steps = len(edges) - 1
     copies = []
     for k in range(steps):

time: 169 us -> 169 us (level)
  no operation moved by 1% of the time
where the time goes in v16:
time: 169 us; the launch traced here: 168 us
  Pallas kernels  39.7 us (23%)
  blocking collectives  37.1 us (22%)
  starting transfers between devices  32.1 us (19%)
  waiting for transfers between devices  28.1 us (17%)
  between operations  13.7 us (8%)
  local copies, waits for them, and re-layouts  11.2 us (7%)
  other arithmetic  5.72 us (3%)
    all_to_all x1, blocking collectives, on_device(): lax.all_to_all(outgoing, SEC, split_axis=0, concat_axis=0, tiled=True)  37.1 us
    pallas_call x1, Pallas kernels, vision_context(): pl.pallas_call(attention_kernel, out_shape=jax.ShapeDtypeStruct((row_coun...  14.1 us
    pallas_call x1, Pallas kernels, merge_and_select(): pl.pallas_call(merge_kernel, out_shape=pltpu.HBM((slots, columns), BF), i...  10.5 us
    ppermute x6, waiting for transfers between devices, swap_tp(): return lax.ppermute(block, TP, [(i, i ^ k) for i in range(4)])  10.3 us
    ppermute x6, starting transfers between devices, shift_y(): lax.ppermute(block, ('yh', 'yl'), [(i, (i + d) % 4) for i in range(4)])  8.32 us
    all_to_all x1, starting transfers between devices, on_device(): table = lax.all_to_all(table, SEC, split_axis=0, concat_axis=0, tiled=True)  8.27 us
    all_gather x1, waiting for transfers between devices, on_device(): weight = lax.all_gather(both, ('z', 'x'), axis=0, tiled=True)  7.87 us
    ppermute x8, starting transfers between devices, swap_core(): return lax.ppermute(block, 'c', [(0, 1), (1, 0)])  6.73 us
  transfers between devices with their start and end apart: 23, of which 7 were waited for; matrix products, arithmetic and copies ran while one was open for 7% of the time, Pallas kernels for 15%

profile of v16, /device:TPU:1, one launch (start us, length us, event | category | flops | bytes accessed | tf_op | source)
XLA Modules:
  0.0 168.3 jit_solution(944280210297747507)
XLA Ops:
  7.7 3.8 %collective-permute-start = (bf16[160,1024]{1,0:T(8,128)(2,1)S(1)}, bf16[160,1024]{1,0:T(8,128)(2,1)S(1)}, u32[]{:S(2)}, u32[]{:S(2)}) collective-permute-start(bf16[160,1024]{1,0:T(8,128)(2,1)S(1)} %constant_dynamic-slice_fusion.5), channel_id=1, source_target_pairs={{0,4},{4,0},{1,5},{5,1},{2,6},{6,2},{3,7},{7,3},{8,12},{12,8},{9,1... | collective-permute-start | bytes 983048 | tf_op jit(solution)/shard_map/ppermute | solution.py:436
  13.9 4.8 %collective-permute-done = bf16[160,1024]{1,0:T(8,128)(2,1)S(1)} collective-permute-done((bf16[160,1024]{1,0:T(8,128)(2,1)S(1)}, bf16[160,1024]{1,0:T(8,128)(2,1)S(1)}, u32[]{:S(2)}, u32[]{:S(2)}) %collective-permute-start) | collective-permute-done | bytes 327712 | tf_op jit(solution)/shard_map/ppermute | solution.py:436
  20.2 1.6 collective-permute-start.6
  21.8 1.4 collective-permute-start.1
  23.3 1.5 collective-permute-start.2
  24.8 1.7 %copy-done.4 = bf16[1024,1280]{1,0:T(8,128)(2,1)S(1)} copy-done((bf16[1024,1280]{1,0:T(8,128)(2,1)S(1)}, bf16[1024,1280]{1,0:T(8,128)(2,1)}, u32[]{:S(2)}) %copy-start.4) | copy-done | bytes 2621464
  26.6 1.7 %copy-done.7 = bf16[3,1280,320]{1,2,0:T(8,128)(2,1)S(1)} copy-done((bf16[3,1280,320]{1,2,0:T(8,128)(2,1)S(1)}, bf16[3,1280,320]{1,2,0:T(8,128)(2,1)}, u32[]{:S(2)}) %copy-start.7) | copy-done | bytes 2457624
  28.2 14.1 %vision_attention.1 = bf16[1024,320]{1,0:T(8,128)(2,1)S(1)} custom-call(s32[1024,1]{1,0:T(8,128)S(1)} %copy.13.row_ids, s32[1,1024]{1,0:T(1,128)S(1)} %bitcast.21, bf16[1024,1280]{1,0:T(8,128)(2,1)S(1)} %copy-done.4, bf16[3,320,1280]{2,1,0:T(8,128)(2,1)S(1)} %bitcast.23), custom_call_target="tpu_custom_call" | custom-call | flops 6811549696 | bytes 5079040 | tf_op jit(solution)/shard_map/vision_attention/pallas_call | solution.py:70
  43.6 1.4 collective-permute-done.3.refs_2_
  45.5 4.5 %collective-permute-done.4.refs_3_ = bf16[256,320]{1,0:T(8,128)(2,1)S(1)} collective-permute-done((bf16[256,320]{1,0:T(8,128)(2,1)S(1)}, bf16[256,320]{1,0:T(8,128)(2,1)S(1)}, u32[]{:S(2)}, u32[]{:S(2)}) %collective-permute-start.4) | collective-permute-done | bytes 163872 | tf_op jit(solution)/shard_map/ppermute | solution.py:407
  49.9 4.4 %collective-permute-done.5.refs_4_ = bf16[256,320]{1,0:T(8,128)(2,1)S(1)} collective-permute-done((bf16[256,320]{1,0:T(8,128)(2,1)S(1)}, bf16[256,320]{1,0:T(8,128)(2,1)S(1)}, u32[]{:S(2)}, u32[]{:S(2)}) %collective-permute-start.5) | collective-permute-done | bytes 163872 | tf_op jit(solution)/shard_map/ppermute | solution.py:407
  54.4 2.7 %project_and_norm.1.refs_0_ = bf16[64,5120]{1,0:T(8,128)(2,1)} custom-call(s32[1]{0:T(128)} %bitcast.3.refs_0_, bf16[256,320]{1,0:T(8,128)(2,1)S(1)} %get-tuple-element.48.refs_1_, bf16[256,320]{1,0:T(8,128)(2,1)S(1)} %collective-permute-done.3.refs_2_, bf16[256,320]{1,0:T(8,128)(2,1)S(1)} %collective-permute-done.4.refs_3_, ...), custom_call_target="tpu_custom_call" | custom-call | flops 838860800 | bytes 5242880 | tf_op jit(solution)/shard_map/project_and_norm/pallas_call | solution.py:115
  57.2 2.5 %collective-permute-start.11 = (bf16[64,5120]{1,0:T(8,128)(2,1)}, bf16[64,5120]{1,0:T(8,128)(2,1)}, u32[]{:S(2)}, u32[]{:S(2)}) collective-permute-start(bf16[64,5120]{1,0:T(8,128)(2,1)} %project_and_norm.1.refs_0_), channel_id=1, source_target_pairs={{0,6},{2,0},{4,2},{6,4},{1,7},{3,1},{5,3},{7,5},{8,14},{10,8},{12,... | collective-permute-start | bytes 1966088 | tf_op jit(solution)/shard_map/ppermute | solution.py:411
  61.6 8.3 %all-to-all-start = ((s32[32,1,32]{2,1,0:T(1,128)}), s32[32,1,32]{2,1,0:T(1,128)}, u32[]{:S(2)}, u32[]{:S(2)}) async-start(s32[32,1,32]{2,1,0:T(1,128)} %bitcast.10), calls=%async_computation | async-start | bytes 32768 | tf_op jit(solution)/shard_map/all_to_all | solution.py:479
  69.9 4.9 %collective-permute-done.10.refs_2_ = bf16[64,5120]{1,0:T(8,128)(2,1)} collective-permute-done((bf16[64,5120]{1,0:T(8,128)(2,1)}, bf16[64,5120]{1,0:T(8,128)(2,1)}, u32[]{:S(2)}, u32[]{:S(2)}) %collective-permute-start.10) | collective-permute-done | bytes 655392 | tf_op jit(solution)/shard_map/ppermute | solution.py:411
  74.8 1.7 %slice.16 = bf16[32,5120]{1,0:T(8,128)(2,1)} slice(bf16[64,5120]{1,0:T(8,128)(2,1)} %collective-permute-done.10.refs_2_), slice={[0:32], [0:5120]} | slice | bytes 655360 | tf_op jit(solution)/shard_map/slice | solution.py:478
  76.5 1.7 %slice.17 = bf16[32,5120]{1,0:T(8,128)(2,1)} slice(bf16[64,5120]{1,0:T(8,128)(2,1)} %collective-permute-done.11.refs_4_), slice={[32:64], [0:5120]} | slice | bytes 655360 | tf_op jit(solution)/shard_map/slice | solution.py:478
  78.2 2.7 %collective-permute-start.16 = (bf16[32,5120]{1,0:T(8,128)(2,1)}, bf16[32,5120]{1,0:T(8,128)(2,1)}, u32[]{:S(2)}, u32[]{:S(2)}) collective-permute-start(bf16[32,5120]{1,0:T(8,128)(2,1)} %slice.17), channel_id=1, source_target_pairs={{0,6},{2,0},{4,2},{6,4},{1,7},{3,1},{5,3},{7,5},{8,14},{10,8},{12,... | collective-permute-start | bytes 983048 | tf_op jit(solution)/shard_map/ppermute | solution.py:411
  81.3 1.1 text_squares.1.base
  82.5 1.6 collective-permute-start.9
  84.6 1.3 broadcast_add_fusion
  86.7 1.4 collective-permute-start.15
  89.2 1.2 compare_convert_fusion.send
  90.6 5.3 %stack_rows.1.rows = bf16[512,5120]{1,0:T(8,128)(2,1)} custom-call(bf16[64,5120]{1,0:T(8,128)(2,1)} %project_and_norm.1.refs_0_, bf16[64,5120]{1,0:T(8,128)(2,1)} %collective-permute-done.9.refs_1_, bf16[64,5120]{1,0:T(8,128)(2,1)} %collective-permute-done.10.refs_2_, bf16[64,5120]{1,0:T(8,128)(2,1)} %collective-permute-done.12.refs_3_, ...), custom_call_target="tpu_custom_call" | custom-call | bytes 10485760 | tf_op jit(solution)/shard_map/stack_rows/pallas_call | solution.py:148
  95.9 7.9 %all-gather.2.cloned.1.call-done.weight = bf16[5120,1024]{1,0:T(8,128)(2,1)} async-done(((bf16[320,1024]{1,0:T(8,128)(2,1)}), bf16[5120,1024]{1,0:T(8,128)(2,1)}) %all-gather.2.cloned.1.call-update) | async-done | bytes 10485776 | tf_op jit(solution)/shard_map/all_gather | solution.py:457
  103.8 10.5 %merge_rows.1 = bf16[1024,1024]{1,0:T(8,128)(2,1)} custom-call(bf16[512,5120]{1,0:T(8,128)(2,1)} %stack_rows.1.rows, bf16[5120,1024]{1,0:T(8,128)(2,1)} %all-gather.2.cloned.1.call-done.weight, bf16[1024,512]{1,0:T(8,128)(2,1)} %compare_convert_fusion.send), custom_call_target="tpu_custom_call" | custom-call | flops 6442450944 | bytes 17825792 | tf_op jit(solution)/shard_map/merge_rows/pallas_call | solution.py:224
  114.4 37.1 %all_to_all.21 = bf16[32,32,1024]{2,1,0:T(8,128)(2,1)S(1)} all-to-all(bf16[32,32,1024]{2,1,0:T(8,128)(2,1)} %bitcast.24), channel_id=1, replica_groups=mesh['z'=4,'x'=4,'yh'=2,'yl'=2,'c'=2] {'z','x','yh'}, dimensions={0} | all-to-all | bytes 4194304 | tf_op jit(solution)/shard_map/all_to_all | solution.py:503
  151.4 1.6 slot_squares.1.own
  153.1 2.2 %collective-permute-start.18 = (f32[4,128]{1,0:T(4,128)S(1)}, f32[4,128]{1,0:T(4,128)S(1)}, u32[]{:S(2)}, u32[]{:S(2)}) collective-permute-start(f32[4,128]{1,0:T(4,128)S(1)} %slot_squares.1.own), channel_id=1, source_target_pairs={{0,1},{1,0},{2,3},{3,2},{4,5},{5,4},{6,7},{7,6},{8,9},{9,8},{10,11... | collective-permute-start | bytes 6152 | tf_op jit(solution)/shard_map/ppermute | solution.py:407
  155.6 1.4 collective-permute-start.20
  157.0 1.9 %pick_rows.1.prompt = bf16[512,2048]{1,0:T(8,128)(2,1)S(1)} custom-call(bf16[16,2,32,1024]{3,2,1,0:T(8,128)(2,1)S(1)} %bitcast.19, bf16[512,512]{1,0:T(8,128)(2,1)S(1)} %fusion.1.pick, s32[512,1]{1,0:T(8,128)S(1)} %copy.14.usable, bf16[512,2048]{1,0:T(8,128)(2,1)S(1)} %copy-done.1), custom_call_target="tpu_custom_call" | custom-call | flops 1073741824 | bytes 6291456 | tf_op jit(solution)/shard_map/pick_rows/pallas_call | solution.py:355
  159.0 2.5 %finish.1 = bf16[512,2048]{1,0:T(8,128)(2,1)} custom-call(bf16[512,2048]{1,0:T(8,128)(2,1)S(1)} %pick_rows.1.prompt, f32[4,128]{1,0:T(4,128)S(1)} %slot_squares.1.own, f32[4,128]{1,0:T(4,128)S(1)} %collective-permute-done.18.core, f32[4,128]{1,0:T(4,128)S(1)} %collective-permute-done.19.far, f32[4,128]{1,0:T(4,128)S(1)} %collective-permute-done.20.both, ...), custom_call_target="tpu_custom_call" | custom-call | flops 3145728 | bytes 4194304 | tf_op jit(solution)/shard_map/finish/pallas_call | solution.py:389
  (84 shorter events, 12.0 us)
Async XLA Ops:
  6.5 97.3 %all-gather.2.cloned.1.call-start = ((), (), s32[]{:S(2)}) async-start(), calls=%async_computation.2 | async-start | bytes 11141120 | tf_op jit(solution)/shard_map/all_gather | solution.py:457
  7.7 12.1 %copy-start.9 = (s32[1,256]{1,0:T(1,128)S(1)}, s32[1,256]{1,0:T(1,128)}, u32[]{:S(2)}) copy-start(s32[1,256]{1,0:T(1,128)} %param.10) | copy-start | bytes 3076
  7.7 11.0 %collective-permute-start = (bf16[160,1024]{1,0:T(8,128)(2,1)S(1)}, bf16[160,1024]{1,0:T(8,128)(2,1)S(1)}, u32[]{:S(2)}, u32[]{:S(2)}) collective-permute-start(bf16[160,1024]{1,0:T(8,128)(2,1)S(1)} %constant_dynamic-slice_fusion.5), channel_id=1, source_target_pairs={{0,4},{4,0},{1,5},{5,1},{2,6},{6,2},{3,7},{7,3},{8,12},{12,8},{9,1... | collective-permute-start | bytes 983048 | tf_op jit(solution)/shard_map/ppermute | solution.py:436
  13.2 7.0 %copy-start.2 = (bf16[320,1280]{1,0:T(8,128)(2,1)S(1)}, bf16[320,1280]{1,0:T(8,128)(2,1)}, u32[]{:S(2)}) copy-start(bf16[320,1280]{1,0:T(8,128)(2,1)} %refs_5_) | copy-start | bytes 2457604
  20.2 34.1 %collective-permute-start.6 = (bf16[320,1280]{1,0:T(8,128)(2,1)S(1)}, bf16[320,1280]{1,0:T(8,128)(2,1)S(1)}, u32[]{:S(2)}, u32[]{:S(2)}) collective-permute-start(bf16[320,1280]{1,0:T(8,128)(2,1)S(1)} %copy-done.2), channel_id=1, source_target_pairs={{0,1},{1,0},{2,3},{3,2},{4,5},{5,4},{6,7},{7,6},{8,9},{9,8},{10,11... | collective-permute-start | bytes 2457608 | tf_op jit(solution)/shard_map/ppermute | solution.py:415
  21.8 20.5 %collective-permute-start.1 = (bf16[160,1280]{1,0:T(8,128)(2,1)S(1)}, bf16[160,1280]{1,0:T(8,128)(2,1)S(1)}, u32[]{:S(2)}, u32[]{:S(2)}) collective-permute-start(bf16[160,1280]{1,0:T(8,128)(2,1)S(1)} %get-tuple-element.44), channel_id=1, source_target_pairs={{0,2},{2,4},{4,6},{6,0},{1,3},{3,5},{5,7},{7,1},{8,10},{10,12},{12... | collective-permute-start | bytes 1228808 | tf_op jit(solution)/shard_map/ppermute | solution.py:411
  23.3 19.1 %collective-permute-start.2 = (bf16[160,1280]{1,0:T(8,128)(2,1)S(1)}, bf16[160,1280]{1,0:T(8,128)(2,1)S(1)}, u32[]{:S(2)}, u32[]{:S(2)}) collective-permute-start(bf16[160,1280]{1,0:T(8,128)(2,1)S(1)} %get-tuple-element.43), channel_id=1, source_target_pairs={{0,6},{2,0},{4,2},{6,4},{1,7},{3,1},{5,3},{7,5},{8,14},{10,8},{12,... | collective-permute-start | bytes 1228808 | tf_op jit(solution)/shard_map/ppermute | solution.py:411
  24.8 1.7 %copy-start.4 = (bf16[1024,1280]{1,0:T(8,128)(2,1)S(1)}, bf16[1024,1280]{1,0:T(8,128)(2,1)}, u32[]{:S(2)}) copy-start(bf16[1024,1280]{1,0:T(8,128)(2,1)} %refs_11_) | copy-start | bytes 7864324
  26.6 1.7 %copy-start.7 = (bf16[3,1280,320]{1,2,0:T(8,128)(2,1)S(1)}, bf16[3,1280,320]{1,2,0:T(8,128)(2,1)}, u32[]{:S(2)}) copy-start(bf16[3,1280,320]{1,2,0:T(8,128)(2,1)} %param.11) | copy-start | bytes 7372804
  28.2 17.2 %copy-start.8 = (f32[1280]{0:T(1024)S(1)}, f32[1280]{0:T(1024)}, u32[]{:S(2)}) copy-start(f32[1280]{0:T(1024)} %param.13) | copy-start | bytes 15364
  28.2 26.1 %copy-start.5 = (bf16[1024,1280]{1,0:T(8,128)(2,1)S(1)}, bf16[1024,1280]{1,0:T(8,128)(2,1)}, u32[]{:S(2)}) copy-start(bf16[1024,1280]{1,0:T(8,128)(2,1)} %refs_11_) | copy-start | bytes 7864324
  42.3 12.0 %copy-start.3 = (bf16[320,1280]{1,0:T(8,128)(2,1)S(1)}, bf16[320,1280]{1,0:T(8,128)(2,1)}, u32[]{:S(2)}) copy-start(bf16[320,1280]{1,0:T(8,128)(2,1)} %refs_5_) | copy-start | bytes 2457604
  42.4 12.0 %collective-permute-start.7 = (bf16[160,1280]{1,0:T(8,128)(2,1)S(1)}, bf16[160,1280]{1,0:T(8,128)(2,1)S(1)}, u32[]{:S(2)}, u32[]{:S(2)}) collective-permute-start(bf16[160,1280]{1,0:T(8,128)(2,1)S(1)} %collective-permute-done.1.refs_7_), channel_id=1, source_target_pairs={{0,1},{1,0},{2,3},{3,2},{4,5},{5,4},{6,7},{7,6},{8,9},{9,8},{10,11... | collective-permute-start | bytes 1228808 | tf_op jit(solution)/shard_map/ppermute | solution.py:415
  42.8 11.5 %collective-permute-start.8 = (bf16[160,1280]{1,0:T(8,128)(2,1)S(1)}, bf16[160,1280]{1,0:T(8,128)(2,1)S(1)}, u32[]{:S(2)}, u32[]{:S(2)}) collective-permute-start(bf16[160,1280]{1,0:T(8,128)(2,1)S(1)} %collective-permute-done.2.refs_8_), channel_id=1, source_target_pairs={{0,1},{1,0},{2,3},{3,2},{4,5},{5,4},{6,7},{7,6},{8,9},{9,8},{10,11... | collective-permute-start | bytes 1228808 | tf_op jit(solution)/shard_map/ppermute | solution.py:415
  43.0 2.0 %collective-permute-start.3 = (bf16[256,320]{1,0:T(8,128)(2,1)S(1)}, bf16[256,320]{1,0:T(8,128)(2,1)S(1)}, u32[]{:S(2)}, u32[]{:S(2)}) collective-permute-start(bf16[256,320]{1,0:T(8,128)(2,1)S(1)} %get-tuple-element.47), channel_id=1, source_target_pairs={{0,1},{1,0},{2,3},{3,2},{4,5},{5,4},{6,7},{7,6},{8,9},{9,8},{10,11... | collective-permute-start | bytes 491528 | tf_op jit(solution)/shard_map/ppermute | solution.py:407
  43.5 6.5 %collective-permute-start.4 = (bf16[256,320]{1,0:T(8,128)(2,1)S(1)}, bf16[256,320]{1,0:T(8,128)(2,1)S(1)}, u32[]{:S(2)}, u32[]{:S(2)}) collective-permute-start(bf16[256,320]{1,0:T(8,128)(2,1)S(1)} %get-tuple-element.46), channel_id=1, source_target_pairs={{0,2},{1,3},{2,0},{3,1},{4,6},{5,7},{6,4},{7,5},{8,10},{9,11},{10,... | collective-permute-start | bytes 491528 | tf_op jit(solution)/shard_map/ppermute | solution.py:407
  45.1 9.3 %collective-permute-start.5 = (bf16[256,320]{1,0:T(8,128)(2,1)S(1)}, bf16[256,320]{1,0:T(8,128)(2,1)S(1)}, u32[]{:S(2)}, u32[]{:S(2)}) collective-permute-start(bf16[256,320]{1,0:T(8,128)(2,1)S(1)} %get-tuple-element.45), channel_id=1, source_target_pairs={{0,3},{1,2},{2,1},{3,0},{4,7},{5,6},{6,5},{7,4},{8,11},{9,10},{10,... | collective-permute-start | bytes 491528 | tf_op jit(solution)/shard_map/ppermute | solution.py:407
  54.4 27.0 %copy-start.1 = (bf16[512,2048]{1,0:T(8,128)(2,1)S(1)}, bf16[512,2048]{1,0:T(8,128)(2,1)}, u32[]{:S(2)}) copy-start(bf16[512,2048]{1,0:T(8,128)(2,1)} %text.3) | copy-start | bytes 6291460
  57.0 17.7 %collective-permute-start.10 = (bf16[64,5120]{1,0:T(8,128)(2,1)}, bf16[64,5120]{1,0:T(8,128)(2,1)}, u32[]{:S(2)}, u32[]{:S(2)}) collective-permute-start(bf16[64,5120]{1,0:T(8,128)(2,1)} %project_and_norm.1.refs_0_), channel_id=1, source_target_pairs={{0,2},{2,4},{4,6},{6,0},{1,3},{3,5},{5,7},{7,1},{8,10},{10,12},{12... | collective-permute-start | bytes 1966088 | tf_op jit(solution)/shard_map/ppermute | solution.py:411
  57.2 19.3 %collective-permute-start.11 = (bf16[64,5120]{1,0:T(8,128)(2,1)}, bf16[64,5120]{1,0:T(8,128)(2,1)}, u32[]{:S(2)}, u32[]{:S(2)}) collective-permute-start(bf16[64,5120]{1,0:T(8,128)(2,1)} %project_and_norm.1.refs_0_), channel_id=1, source_target_pairs={{0,6},{2,0},{4,2},{6,4},{1,7},{3,1},{5,3},{7,5},{8,14},{10,8},{12,... | collective-permute-start | bytes 1966088 | tf_op jit(solution)/shard_map/ppermute | solution.py:411
  61.6 22.5 %all-to-all-start = ((s32[32,1,32]{2,1,0:T(1,128)}), s32[32,1,32]{2,1,0:T(1,128)}, u32[]{:S(2)}, u32[]{:S(2)}) async-start(s32[32,1,32]{2,1,0:T(1,128)} %bitcast.10), calls=%async_computation | async-start | bytes 32768 | tf_op jit(solution)/shard_map/all_to_all | solution.py:479
  76.5 10.2 %collective-permute-start.14 = (bf16[32,5120]{1,0:T(8,128)(2,1)}, bf16[32,5120]{1,0:T(8,128)(2,1)}, u32[]{:S(2)}, u32[]{:S(2)}) collective-permute-start(bf16[32,5120]{1,0:T(8,128)(2,1)} %slice.16), channel_id=1, source_target_pairs={{0,2},{2,4},{4,6},{6,0},{1,3},{3,5},{5,7},{7,1},{8,10},{10,12},{12... | collective-permute-start | bytes 983048 | tf_op jit(solution)/shard_map/ppermute | solution.py:411
  78.2 9.9 %collective-permute-start.16 = (bf16[32,5120]{1,0:T(8,128)(2,1)}, bf16[32,5120]{1,0:T(8,128)(2,1)}, u32[]{:S(2)}, u32[]{:S(2)}) collective-permute-start(bf16[32,5120]{1,0:T(8,128)(2,1)} %slice.17), channel_id=1, source_target_pairs={{0,6},{2,0},{4,2},{6,4},{1,7},{3,1},{5,3},{7,5},{8,14},{10,8},{12,... | collective-permute-start | bytes 983048 | tf_op jit(solution)/shard_map/ppermute | solution.py:411
  82.5 7.9 %collective-permute-start.9 = (bf16[64,5120]{1,0:T(8,128)(2,1)}, bf16[64,5120]{1,0:T(8,128)(2,1)}, u32[]{:S(2)}, u32[]{:S(2)}) collective-permute-start(bf16[64,5120]{1,0:T(8,128)(2,1)} %project_and_norm.1.refs_0_), channel_id=1, source_target_pairs={{0,1},{1,0},{2,3},{3,2},{4,5},{5,4},{6,7},{7,6},{8,9},{9,8},{10,11... | collective-permute-start | bytes 1966088 | tf_op jit(solution)/shard_map/ppermute | solution.py:415
  84.1 6.3 %collective-permute-start.12 = (bf16[64,5120]{1,0:T(8,128)(2,1)}, bf16[64,5120]{1,0:T(8,128)(2,1)}, u32[]{:S(2)}, u32[]{:S(2)}) collective-permute-start(bf16[64,5120]{1,0:T(8,128)(2,1)} %collective-permute-done.10.refs_2_), channel_id=1, source_target_pairs={{0,1},{1,0},{2,3},{3,2},{4,5},{5,4},{6,7},{7,6},{8,9},{9,8},{10,11... | collective-permute-start | bytes 1966088 | tf_op jit(solution)/shard_map/ppermute | solution.py:415
  84.2 6.2 %collective-permute-start.13 = (bf16[64,5120]{1,0:T(8,128)(2,1)}, bf16[64,5120]{1,0:T(8,128)(2,1)}, u32[]{:S(2)}, u32[]{:S(2)}) collective-permute-start(bf16[64,5120]{1,0:T(8,128)(2,1)} %collective-permute-done.11.refs_4_), channel_id=1, source_target_pairs={{0,1},{1,0},{2,3},{3,2},{4,5},{5,4},{6,7},{7,6},{8,9},{9,8},{10,11... | collective-permute-start | bytes 1966088 | tf_op jit(solution)/shard_map/ppermute | solution.py:415
  86.7 3.6 %collective-permute-start.15 = (bf16[32,5120]{1,0:T(8,128)(2,1)}, bf16[32,5120]{1,0:T(8,128)(2,1)S(1)}, u32[]{:S(2)}, u32[]{:S(2)}) collective-permute-start(bf16[32,5120]{1,0:T(8,128)(2,1)} %collective-permute-done.14.refs_6_), channel_id=1, source_target_pairs={{0,1},{1,0},{2,3},{3,2},{4,5},{5,4},{6,7},{7,6},{8,9},{9,8},{10,11... | collective-permute-start | bytes 983048 | tf_op jit(solution)/shard_map/ppermute | solution.py:415
  88.2 2.5 %collective-permute-start.17 = (bf16[32,5120]{1,0:T(8,128)(2,1)}, bf16[32,5120]{1,0:T(8,128)(2,1)S(1)}, u32[]{:S(2)}, u32[]{:S(2)}) collective-permute-start(bf16[32,5120]{1,0:T(8,128)(2,1)} %collective-permute-done.16.refs_8_), channel_id=1, source_target_pairs={{0,1},{1,0},{2,3},{3,2},{4,5},{5,4},{6,7},{7,6},{8,9},{9,8},{10,11... | collective-permute-start | bytes 983048 | tf_op jit(solution)/shard_map/ppermute | solution.py:415
  153.1 5.9 %copy-start.6 = (f32[2048]{0:T(1024)S(1)}, f32[2048]{0:T(1024)}, u32[]{:S(2)}) copy-start(f32[2048]{0:T(1024)} %param.17) | copy-start | bytes 24580
  153.1 5.9 %collective-permute-start.18 = (f32[4,128]{1,0:T(4,128)S(1)}, f32[4,128]{1,0:T(4,128)S(1)}, u32[]{:S(2)}, u32[]{:S(2)}) collective-permute-start(f32[4,128]{1,0:T(4,128)S(1)} %slot_squares.1.own), channel_id=1, source_target_pairs={{0,1},{1,0},{2,3},{3,2},{4,5},{5,4},{6,7},{7,6},{8,9},{9,8},{10,11... | collective-permute-start | bytes 6152 | tf_op jit(solution)/shard_map/ppermute | solution.py:407
  155.3 3.6 %collective-permute-start.19 = (f32[4,128]{1,0:T(4,128)S(1)}, f32[4,128]{1,0:T(4,128)S(1)}, u32[]{:S(2)}, u32[]{:S(2)}) collective-permute-start(f32[4,128]{1,0:T(4,128)S(1)} %slot_squares.1.own), channel_id=1, source_target_pairs={{0,2},{1,3},{2,0},{3,1},{4,6},{5,7},{6,4},{7,5},{8,10},{9,11},{10,... | collective-permute-start | bytes 6152 | tf_op jit(solution)/shard_map/ppermute | solution.py:407
  155.6 3.3 %collective-permute-start.20 = (f32[4,128]{1,0:T(4,128)S(1)}, f32[4,128]{1,0:T(4,128)S(1)}, u32[]{:S(2)}, u32[]{:S(2)}) collective-permute-start(f32[4,128]{1,0:T(4,128)S(1)} %slot_squares.1.own), channel_id=1, source_target_pairs={{0,3},{1,2},{2,1},{3,0},{4,7},{5,6},{6,5},{7,4},{8,11},{9,10},{10,... | collective-permute-start | bytes 6152 | tf_op jit(solution)/shard_map/ppermute | solution.py:407
  (1 other events, 1.1 us)
Sparse Core Ops, SparseCore 0:
  19.8 83.9 all-gather.1
